TPU v7x, 32 devices: a whole 2x2x4 slice. The times are simulated.
32 devices in a mesh: groups: 2 (over y), wide: 4 (over x, core), narrow: 4 (over z).
Axes of the slice: x: 2, y: 2, z: 4, core: 2. Of those that a mesh axis runs over, the one named last changes fastest.
Arguments:
- inputs: bfloat16 [512, 6144], P(('groups', 'narrow'), 'wide'), parts along dimension 0, may hold values from -6 to 6
- up_weight: bfloat16 [6144, 12288], P('wide', 'narrow'), may hold values from -0.078125 to 0.078125
- down_weight: bfloat16 [12288, 6144], P('narrow', 'wide'), may hold values from -0.0546875 to 0.0546875
- out_grad: bfloat16 [512, 6144], P(('groups', 'narrow'), 'wide'), parts along dimension 0, may hold values from -6 to 6
Outputs:
- input_grad: bfloat16 [512, 6144], P(('groups', 'narrow'), 'wide'), parts along dimension 0
- up_grad: float32 [12288, 12288], P(('groups', 'wide'), 'narrow'), parts along dimension 0
- down_grad: float32 [24576, 6144], P(('groups', 'narrow'), 'wide'), parts along dimension 0
There are 2 independent parts, one for each index of `groups`. A program takes and returns all parts, laid end to end along the dimension named above; an argument that names none is the same for every part. Nothing has to cross between parts.
All inputs are finite; a program needn't handle non-finite values.
Results may differ from a plain program's by a relative error of at most 0.018.
Values may be sent and summed in bfloat16 or wider, within the bound.
No kernel may reach another device: no remote copies, remote signals or barrier semaphores. Data moves between devices by JAX's collectives and lax.ppermute only.
A program may use at most 128 MiB of HBM per device.

v0:
```python
import jax
import jax.numpy as jnp
from jax import lax
from jax.sharding import PartitionSpec as P


def gelu_parts(hidden):
    normal_cdf = 0.5 * (1.0 + jax.scipy.special.erf(hidden * 0.7071067811865476))
    normal_pdf = jnp.exp(-0.5 * hidden * hidden) * 0.3989422804014327
    return (hidden * normal_cdf, normal_cdf + hidden * normal_pdf)


def per_device(inputs, up_weight, down_weight, out_grad):
    gathered_inputs, gathered_grads = (
        lax.all_gather(inputs, "narrow", axis=0, tiled=True),
        lax.all_gather(out_grad, "narrow", axis=0, tiled=True),
    )
    row_total = gathered_inputs.shape[0]
    row_block = gathered_inputs
    hidden = lax.psum_scatter(
        jnp.dot(row_block, up_weight, preferred_element_type=jnp.float32).astype(jnp.bfloat16),
        "wide",
        scatter_dimension=0,
        tiled=True,
    ).astype(jnp.float32)
    row_block = gathered_grads
    grad_hidden = lax.psum_scatter(
        lax.dot_general(
            row_block, down_weight, (((1,), (1,)), ((), ())), preferred_element_type=jnp.float32
        ).astype(jnp.bfloat16),
        "wide",
        scatter_dimension=0,
        tiled=True,
    ).astype(jnp.float32)
    gelu_value, gelu_slope = gelu_parts(hidden)
    grad_rows = (grad_hidden * gelu_slope).astype(jnp.bfloat16)
    grad_act, activation = (
        lax.all_gather(grad_rows, "wide", axis=0, tiled=True),
        lax.all_gather(gelu_value.astype(jnp.bfloat16), "wide", axis=0, tiled=True),
    )
    row_block = grad_act
    input_grad = lax.psum_scatter(
        lax.dot_general(
            row_block, up_weight, (((1,), (1,)), ((), ())), preferred_element_type=jnp.float32
        ).astype(jnp.bfloat16),
        "narrow",
        scatter_dimension=0,
        tiled=True,
    )
    loss_scale = row_total ** (-0.5)
    up_grad = (
        lax.dot_general(
            gathered_inputs, grad_act, (((0,), (0,)), ((), ())), preferred_element_type=jnp.float32
        )
        * loss_scale
    )
    down_grad = (
        lax.dot_general(
            activation, gathered_grads, (((0,), (0,)), ((), ())), preferred_element_type=jnp.float32
        )
        * loss_scale
    )
    return (input_grad, up_grad, down_grad)


def solution(mesh):
    placed = (
        P(("groups", "narrow"), "wide"),
        P("wide", "narrow"),
        P("narrow", "wide"),
        P(("groups", "narrow"), "wide"),
    )
    return jax.shard_map(
        per_device,
        mesh=mesh,
        in_specs=placed,
        out_specs=(
            P(("groups", "narrow"), "wide"),
            P(("groups", "wide"), "narrow"),
            P(("groups", "narrow"), "wide"),
        ),
        check_vma=False,
    )
```

profile of v0, /device:TPU:0, one launch (start us, length us, event | category | flops | bytes accessed | tf_op | source)
XLA Modules:
  0.0 174.9 jit_solution(6244585226750307225)
XLA Ops:
  7.2 0.0 copy-start.1
  7.2 0.0 reduce-scatter.4.cloned.1.call-start
  7.2 21.6 %all_gather.12 = bf16[256,1536]{1,0:T(8,128)(2,1)S(1)} all-gather(bf16[64,1536]{1,0:T(8,128)(2,1)} %param.7), channel_id=1, replica_groups=mesh['groups'=2,'wide'=4,'narrow'=4] {'narrow'}, dimensions={0}, use_global_device_ids=true | all-gather | bytes 983040 | tf_op jit(solution)/shard_map/all_gather | solution.py:16
  28.9 10.9 %convolution_convert_fusion.1 = bf16[256,3072]{1,0:T(8,128)(2,1)} fusion(bf16[256,1536]{1,0:T(8,128)(2,1)S(1)} %all_gather.12, bf16[3072,1536]{1,0:T(8,128)(2,1)} %param.6), kind=kOutput, calls=%fused_computation.3 | convolution fusion | flops 2416705536 | bytes 11796480 | tf_op jit(solution)/shard_map/dot_general | solution.py:28
  39.7 0.0 reduce-scatter.4.cloned.1.call-update
  39.7 0.0 reduce-scatter.6.cloned.1.call-start
  39.8 0.0 copy-done.1
  39.8 17.7 %all_gather.13 = bf16[256,1536]{1,0:T(8,128)(2,1)S(1)} all-gather(bf16[64,1536]{1,0:T(8,128)(2,1)S(1)} %copy-done.1), channel_id=1, replica_groups=mesh['groups'=2,'wide'=4,'narrow'=4] {'narrow'}, dimensions={0}, use_global_device_ids=true | all-gather | bytes 983040 | tf_op jit(solution)/shard_map/all_gather | solution.py:15
  57.5 7.4 %convolution_convert_fusion = bf16[256,3072]{1,0:T(8,128)(2,1)} fusion(bf16[256,1536]{1,0:T(8,128)(2,1)S(1)} %all_gather.13, bf16[1536,3072]{1,0:T(8,128)(2,1)} %param.5), kind=kOutput, calls=%fused_computation.2 | convolution fusion | flops 2416705536 | bytes 11796480 | tf_op jit(solution)/shard_map/dot_general | solution.py:21
  64.9 0.0 reduce-scatter.6.cloned.1.call-update
  64.9 0.0 all-gather.3.cloned.1.call-start
  65.0 2.4 %reduce-scatter.4.cloned.1.call-done = bf16[64,3072]{1,0:T(8,128)(2,1)} async-done(((bf16[256,3072]{1,0:T(8,128)(2,1)}), bf16[64,3072]{1,0:T(8,128)(2,1)}) %reduce-scatter.4.cloned.1.call-update) | async-done | bytes 393232 | tf_op jit(solution)/shard_map/reduce_scatter | solution.py:27
  67.4 31.5 %reduce-scatter.6.cloned.1.call-done = bf16[64,3072]{1,0:T(8,128)(2,1)} async-done(((bf16[256,3072]{1,0:T(8,128)(2,1)}), bf16[64,3072]{1,0:T(8,128)(2,1)}) %reduce-scatter.6.cloned.1.call-update) | async-done | bytes 393232 | tf_op jit(solution)/shard_map/reduce_scatter | solution.py:20
  98.9 2.4 %fusion.8 = (bf16[64,3072]{1,0:T(8,128)(2,1)}, bf16[64,3072]{1,0:T(8,128)(2,1)}) fusion(bf16[64,3072]{1,0:T(8,128)(2,1)} %reduce-scatter.6.cloned.1.call-done, bf16[64,3072]{1,0:T(8,128)(2,1)} %reduce-scatter.4.cloned.1.call-done), kind=kLoop, calls=%fused_computation.18 | loop fusion | flops 2752512 | bytes 1572864 | tf_op jit(solution)/shard_map/convert_element_type | solution.py:39
  101.3 0.0 all-gather.3.cloned.1.call-update
  101.3 0.0 all-gather.5.cloned.1.call-start
  101.3 0.5 all-gather.5.cloned.1.call-update
  101.9 0.0 reduce-scatter.8.cloned.1.call-start
  101.9 19.2 %all-gather.3.cloned.1.call-done = bf16[256,3072]{1,0:T(8,128)(2,1)} async-done(((bf16[64,3072]{1,0:T(8,128)(2,1)}), bf16[256,3072]{1,0:T(8,128)(2,1)}) %all-gather.3.cloned.1.call-update) | async-done | bytes 1572880 | tf_op jit(solution)/shard_map/all_gather | solution.py:38
  121.1 0.0 copy-start
  121.1 7.8 %convolution_convert_fusion.2 = bf16[256,1536]{1,0:T(8,128)(2,1)} fusion(bf16[256,3072]{1,0:T(8,128)(2,1)} %all-gather.3.cloned.1.call-done, bf16[1536,3072]{1,0:T(8,128)(2,1)} %param.5), kind=kOutput, calls=%fused_computation.4 | convolution fusion | flops 2416312320 | bytes 11796480 | tf_op jit(solution)/shard_map/dot_general | solution.py:43
  128.9 0.0 reduce-scatter.8.cloned.1.call-update
  128.9 0.0 copy-done
  129.0 8.3 %multiply_bitcast_fusion = f32[1536,3072]{0,1:T(8,128)} fusion(bf16[256,3072]{1,0:T(8,128)(2,1)S(1)} %copy-done, bf16[256,1536]{1,0:T(8,128)(2,1)S(1)} %all_gather.13), kind=kOutput, calls=%fused_computation | convolution fusion | flops 2420637696 | bytes 21233664 | tf_op jit(solution)/shard_map/dot_general | solution.py:52
  137.3 18.7 %copy.7 = f32[1536,3072]{1,0:T(8,128)} copy(f32[1536,3072]{0,1:T(8,128)} %multiply_bitcast_fusion) | data formatting | bytes 37748736
  155.9 0.0 all-gather.5.cloned.1.call-done
  155.9 9.7 %convolution_multiply_fusion = f32[3072,1536]{1,0:T(8,128)} fusion(bf16[256,3072]{1,0:T(8,128)(2,1)} %all-gather.5.cloned.1.call-done, bf16[256,1536]{1,0:T(8,128)(2,1)S(1)} %all_gather.12), kind=kOutput, calls=%fused_computation.1 | convolution fusion | flops 2420637696 | bytes 21233664 | tf_op jit(solution)/shard_map/dot_general | solution.py:58
  165.7 2.7 %reduce-scatter.8.cloned.1.call-done = bf16[64,1536]{1,0:T(8,128)(2,1)} async-done(((bf16[256,1536]{1,0:T(8,128)(2,1)}), bf16[64,1536]{1,0:T(8,128)(2,1)}) %reduce-scatter.8.cloned.1.call-update) | async-done | bytes 196624 | tf_op jit(solution)/shard_map/reduce_scatter | solution.py:42
Async XLA Ops:
  7.2 32.6 %copy-start.1 = (bf16[64,1536]{1,0:T(8,128)(2,1)S(1)}, bf16[64,1536]{1,0:T(8,128)(2,1)}, u32[]{:S(2)}) copy-start(bf16[64,1536]{1,0:T(8,128)(2,1)} %param.4) | copy-start | bytes 589828
  7.2 60.2 %reduce-scatter.4.cloned.1.call-start = ((), (), s32[]{:S(2)}) async-start(), calls=%async_computation.3 | async-start | bytes 1966080 | tf_op jit(solution)/shard_map/reduce_scatter | solution.py:27
  39.7 59.1 %reduce-scatter.6.cloned.1.call-start = ((), (), s32[]{:S(2)}) async-start(), calls=%async_computation.4 | async-start | bytes 1966080 | tf_op jit(solution)/shard_map/reduce_scatter | solution.py:20
  64.9 56.2 %all-gather.3.cloned.1.call-start = ((), (), s32[]{:S(2)}) async-start(), calls=%async_computation.5 | async-start | bytes 1966080 | tf_op jit(solution)/shard_map/all_gather | solution.py:38
  101.3 54.6 %all-gather.5.cloned.1.call-start = ((), (), s32[]{:S(2)}) async-start(), calls=%async_computation.7 | async-start | bytes 1966080 | tf_op jit(solution)/shard_map/all_gather | solution.py:39
  101.9 66.5 %reduce-scatter.8.cloned.1.call-start = ((), (), s32[]{:S(2)}) async-start(), calls=%async_computation.6 | async-start | bytes 983040 | tf_op jit(solution)/shard_map/reduce_scatter | solution.py:42
  121.1 7.8 %copy-start = (bf16[256,3072]{1,0:T(8,128)(2,1)S(1)}, bf16[256,3072]{1,0:T(8,128)(2,1)}, u32[]{:S(2)}) copy-start(bf16[256,3072]{1,0:T(8,128)(2,1)} %all-gather.3.cloned.1.call-done) | copy-start | bytes 4718596
Sparse Core Ops, SparseCore 0:
  39.9 27.4 reduce-scatter.3
  70.7 28.1 reduce-scatter.5
  101.4 19.6 all-gather.2
  122.5 19.6 all-gather.4
  145.0 23.3 reduce-scatter.7
where the time goes:
time: 175 us
  waiting for transfers between devices  56.4 us (32%)
  matrix products  44 us (25%)
  blocking collectives  39.4 us (23%)
  local copies, waits for them, and re-layouts  18.7 us (11%)
  between operations  13.8 us (8%)
  other arithmetic  2.4 us (1%)
    reduce_scatter x1, waiting for transfers between devices, per_device(): lax.psum_scatter(jnp.dot(row_block, up_weight, preferred_element_type=jnp...  31.5 us
    all_gather x1, blocking collectives, per_device(): lax.all_gather(out_grad, 'narrow', axis=0, tiled=True)  21.6 us
    all_gather x1, waiting for transfers between devices, per_device(): lax.all_gather(grad_rows, 'wide', axis=0, tiled=True)  19.2 us
    unnamed x5, local copies, waits for them, and re-layouts  18.7 us
    all_gather x1, blocking collectives, per_device(): lax.all_gather(inputs, 'narrow', axis=0, tiled=True)  17.7 us
    dot_general x1, matrix products, per_device(): lax.dot_general(row_block, down_weight, (((1,), (1,)), ((), ())), preferr...  10.9 us
    dot_general x1, matrix products, per_device(): lax.dot_general(activation, gathered_grads, (((0,), (0,)), ((), ())), pre...  9.72 us
    dot_general x1, matrix products, per_device(): lax.dot_general(gathered_inputs, grad_act, (((0,), (0,)), ((), ())), pref...  8.3 us
  transfers between devices with their start and end apart: 5, of which 4 were waited for; matrix products, arithmetic and copies ran while one was open for 30% of the time, Pallas kernels for 0%

commit v1 on v0

v1 whole, which is shorter than its diff:
```python
import functools

import jax
import jax.numpy as jnp
from jax import lax
from jax.experimental import pallas as pl
from jax.experimental.pallas import tpu as pltpu
from jax.sharding import PartitionSpec as P

F32, BF16 = jnp.float32, jnp.bfloat16
MIB = 1 << 20
VMEM = pltpu.VMEM
NN = (((1,), (0,)), ((), ()))
NT = (((1,), (1,)), ((), ()))
TN = (((0,), (0,)), ((), ()))


def dot(a, b, dims):
    return lax.dot_general(a, b, dims, preferred_element_type=F32)


def call(body, outs, args, flops, bytes_accessed, limit=24 * MIB, transcendentals=0, scratch=(), name=None):
    return pl.pallas_call(
        body,
        out_shape=outs,
        in_specs=[pl.BlockSpec(memory_space=pltpu.SMEM if a.dtype == jnp.int32 else VMEM) for a in args],
        out_specs=jax.tree.map(lambda _: pl.BlockSpec(memory_space=VMEM), outs),
        scratch_shapes=scratch,
        compiler_params=pltpu.CompilerParams(vmem_limit_bytes=limit),
        cost_estimate=pl.CostEstimate(flops=flops, bytes_accessed=bytes_accessed, transcendentals=transcendentals),
        name=name,
    )(*args)


def hidden_products(core, tokens, up_weight, down_weight):
    _, rows, features = tokens.shape
    half = up_weight.shape[1] // 2
    tile = 512 if half % 512 == 0 else half

    def body(core_ref, tokens_ref, up_ref, down_ref, give_ref, keep_ref):
        me = core_ref[0]
        for out_ref, base in ((give_ref, (1 - me) * half), (keep_ref, me * half)):
            for start in range(0, half, tile):
                units = pl.ds(pl.multiple_of(base + start, tile), tile)
                out_ref[0, :, start : start + tile] = dot(tokens_ref[0], up_ref[:, units], NN).astype(BF16)
                out_ref[1, :, start : start + tile] = dot(tokens_ref[1], down_ref[units, :], NT).astype(BF16)

    out = jax.ShapeDtypeStruct((2, rows, half), BF16)
    weights = [pltpu.with_memory_space_constraint(w, VMEM) for w in (up_weight, down_weight)]
    return call(
        body, (out, out), (core, tokens, *weights), 8 * rows * features * half, 4 * 2 * features * half, name="hidden_products"
    )


def input_product(core, mine, other, up_weight):
    rows, half = mine.shape
    features = up_weight.shape[0]
    tile = 512 if features % 512 == 0 else features

    def body(core_ref, mine_ref, other_ref, up_ref, out_ref):
        me = core_ref[0]
        own_units = pl.ds(pl.multiple_of(me * half, half), half)
        other_units = pl.ds(pl.multiple_of((1 - me) * half, half), half)
        for start in range(0, features, tile):
            part = slice(start, start + tile)
            out_ref[:, part] = (
                dot(mine_ref[...], up_ref[part, own_units], NT) + dot(other_ref[...], up_ref[part, other_units], NT)
            ).astype(BF16)

    weight = pltpu.with_memory_space_constraint(up_weight, VMEM)
    return call(
        body,
        jax.ShapeDtypeStruct((rows, features), BF16),
        (core, mine, other, weight),
        4 * rows * features * half,
        4 * features * half,
        name="input_product",
    )


def gelu_kernel(own, peer):
    _, rows, half = own.shape

    def body(own_ref, peer_ref, out_ref):
        hidden = own_ref[0].astype(F32) + peer_ref[0].astype(F32)
        grad_hidden = own_ref[1].astype(F32) + peer_ref[1].astype(F32)
        cdf = 0.5 * (1.0 + lax.erf(hidden * 0.7071067811865476))
        pdf = jnp.exp(-0.5 * hidden * hidden) * 0.3989422804014327
        out_ref[0] = (grad_hidden * (cdf + hidden * pdf)).astype(BF16)
        out_ref[1] = (hidden * cdf).astype(BF16)

    return call(
        body, jax.ShapeDtypeStruct((2, rows, half), BF16), (own, peer), 40 * rows * half, 12 * rows * half, name="gelu"
    )


def weight_grad(core, left_chunks, right_chunks, which, left_split, right_split, scale, name):
    def flat(chunks, split):
        return [a for pair in chunks for a in pair] if split else list(chunks)

    left, right = flat(left_chunks, left_split), flat(right_chunks, right_split)
    count = len(left_chunks)
    rows = left[0].shape[1]
    wide_left = left[0].shape[2] * (2 if left_split else 1)
    wide_right = right[0].shape[2] * (2 if right_split else 1)
    tokens = rows * count
    tile = 256 if wide_left % 256 == 0 else 128

    def fill(me, refs, split, scratch, index):
        for chunk in range(count):
            at = slice(chunk * rows, (chunk + 1) * rows)
            if split:
                half = scratch.shape[1] // 2
                scratch[at, pl.ds(pl.multiple_of(me * half, half), half)] = refs[2 * chunk][index]
                scratch[at, pl.ds(pl.multiple_of((1 - me) * half, half), half)] = refs[2 * chunk + 1][index]
            else:
                scratch[at, :] = refs[chunk][index]

    def body(core_ref, *refs):
        left_refs, right_refs = refs[: len(left)], refs[len(left) : len(left) + len(right)]
        out_ref, left_all, right_all = refs[len(left) + len(right) :]

        @pl.when(pl.program_id(0) == 0)
        def _():
            fill(core_ref[0], left_refs, left_split, left_all, which[0])
            fill(core_ref[0], right_refs, right_split, right_all, which[1])

        part = pl.ds(pl.multiple_of(pl.program_id(0) * tile, tile), tile)
        out_ref[...] = dot(left_all[:, part], right_all[...], TN) * scale

    return pl.pallas_call(
        body,
        grid=(wide_left // tile,),
        out_shape=jax.ShapeDtypeStruct((wide_left, wide_right), F32),
        in_specs=[pl.BlockSpec(memory_space=pltpu.SMEM)] + [pl.BlockSpec(memory_space=VMEM)] * (len(left) + len(right)),
        out_specs=pl.BlockSpec((tile, wide_right), lambda i: (i, 0)),
        scratch_shapes=[VMEM((tokens, wide_left), BF16), VMEM((tokens, wide_right), BF16)],
        compiler_params=pltpu.CompilerParams(vmem_limit_bytes=24 * MIB),
        cost_estimate=pl.CostEstimate(
            flops=2 * tokens * wide_left * wide_right, bytes_accessed=4 * wide_left * wide_right, transcendentals=0
        ),
        name=name,
    )(core, *left, *right)


def per_device(wide, narrow, inputs, up_weight, down_weight, out_grad):
    rows = inputs.shape[0]
    chips = wide // 2
    place = lax.axis_index("narrow")
    core = (lax.axis_index("wide") % 2).astype(jnp.int32).reshape(1)

    def swap_cores(x):
        return lax.ppermute(x, "wide", [(i, i ^ 1) for i in range(wide)])

    tokens = jnp.stack([inputs, out_grad])

    below, above = [tokens], [tokens]
    for step in range(1, narrow):
        below.append(lax.ppermute(below[-1], "narrow", [(i, i + 1) for i in range(step - 1, narrow - 1)]))
        above.append(lax.ppermute(above[-1], "narrow", [(i + 1, i) for i in range(0, narrow - step)]))

    chunks = [tokens]
    for step in range(1, narrow):
        value = None
        for d in range(1, step + 1):
            if any(i - (i ^ step) == d for i in range(narrow)):
                value = below[d] if value is None else jnp.where(place - (place ^ step) == d, below[d], value)
            if any((i ^ step) - i == d for i in range(narrow)):
                value = above[d] if value is None else jnp.where((place ^ step) - place == d, above[d], value)
        chunks.append(value)

    mine, other, returned = [], [], None
    for step, chunk in enumerate(chunks):
        give, keep = hidden_products(core, chunk, up_weight, down_weight)
        got = swap_cores(give)
        partial = (keep.astype(F32) + got.astype(F32)).astype(BF16)
        hop = 1
        while hop < chips:
            peer = lax.ppermute(partial, "wide", [(i, i ^ (2 * hop)) for i in range(wide)])
            if 2 * hop < chips:
                partial = (partial.astype(F32) + peer.astype(F32)).astype(BF16)
            hop *= 2
        own_half = gelu_kernel(partial, peer)
        other_half = swap_cores(own_half)
        mine.append(own_half)
        other.append(other_half)
        share = input_product(core, own_half[0], other_half[0], up_weight)
        if step:
            share = lax.ppermute(share, "narrow", [(i, i ^ step) for i in range(narrow)])
        returned = share.astype(F32) if returned is None else returned + share.astype(F32)
    scale = (rows * narrow) ** -0.5
    acts = list(zip(mine, other))
    up_grad = weight_grad(core, chunks, acts, (0, 0), False, True, scale, "up_grad")
    down_grad = weight_grad(core, acts, chunks, (1, 1), True, False, scale, "down_grad")
    return returned.astype(BF16), up_grad, down_grad


def solution(mesh):
    placed = (
        P(("groups", "narrow"), "wide"),
        P("wide", "narrow"),
        P("narrow", "wide"),
        P(("groups", "narrow"), "wide"),
    )
    return jax.shard_map(
        functools.partial(per_device, mesh.shape["wide"], mesh.shape["narrow"]),
        mesh=mesh,
        in_specs=placed,
        out_specs=(
            P(("groups", "narrow"), "wide"),
            P(("groups", "wide"), "narrow"),
            P(("groups", "narrow"), "wide"),
        ),
        check_vma=False,
    )
```

time: 175 us -> 129 us (0.74)
  Pallas kernels: 0 us -> 49.4 us
  matrix products: 44 us -> 0 us
  blocking collectives: 39.4 us -> 0 us
  starting transfers between devices: 0.2 us -> 23.5 us
  waiting for transfers between devices: 56.4 us -> 37.6 us
  between operations: 13.8 us -> 1.05 us
  local copies, waits for them, and re-layouts: 18.7 us -> 14.8 us
    pallas_call x0 -> x14, Pallas kernels: none -> 49.4 us  [the longest x12 31.4 us: call(): pl.pallas_call(body, out_shape=outs, in_specs=[pl.BlockSpec(memory_space=...]
    dot_general x5 -> x0, matrix products: 44 us -> none  [the longest x1 10.9 us: per_device(): lax.dot_general(row_block, down_weight, (((1,), (1,)), ((), ())), preferr...]
    all_gather x2 -> x0, blocking collectives: 39.4 us -> none  [the longest x1 21.6 us: per_device(): lax.all_gather(out_grad, 'narrow', axis=0, tiled=True)]
    ppermute x0 -> x21, waiting for transfers between devices: none -> 37.6 us  [the longest x3 20.7 us: per_device(): lax.ppermute(above[-1], 'narrow', [(i + 1, i) for i in range(0, narrow -...]
    reduce_scatter x3 -> x0, waiting for transfers between devices: 36.6 us -> none  [the longest x1 31.5 us: per_device(): lax.psum_scatter(jnp.dot(row_block, up_weight, preferred_element_type=jnp...]
    ppermute x0 -> x21, starting transfers between devices: none -> 23.5 us  [the longest x3 7.13 us: per_device(): lax.ppermute(below[-1], 'narrow', [(i, i + 1) for i in range(step - 1, na...]
    all_gather x2 -> x0, waiting for transfers between devices: 19.2 us -> none  [the longest x1 19.2 us: per_device(): lax.all_gather(grad_rows, 'wide', axis=0, tiled=True)]
    unnamed x5 -> x14, local copies, waits for them, and re-layouts: 18.7 us -> 14.7 us
  transfers between devices with their start and end apart: 5 -> 21, of which waited for: 4 -> 5; matrix products, arithmetic and copies ran while one was open for 30% -> 1% of each run, Pallas kernels for 0% -> 38%
where the time goes in v1:
time: 129 us
  Pallas kernels  49.4 us (38%)
  waiting for transfers between devices  37.6 us (29%)
  starting transfers between devices  23.5 us (18%)
  local copies, waits for them, and re-layouts  14.8 us (11%)
  other arithmetic  2.38 us (2%)
    pallas_call x12, Pallas kernels, call(): pl.pallas_call(body, out_shape=outs, in_specs=[pl.BlockSpec(memory_space=...  31.4 us
    ppermute x3, waiting for transfers between devices, per_device(): lax.ppermute(above[-1], 'narrow', [(i + 1, i) for i in range(0, narrow -...  20.7 us
    pallas_call x2, Pallas kernels, weight_grad(): pl.pallas_call(body, grid=(wide_left // tile,), out_shape=jax.ShapeDtypeS...  18 us
    ppermute x4, waiting for transfers between devices, per_device(): lax.ppermute(partial, 'wide', [(i, i ^ 2 * hop) for i in range(wide)])  16.8 us
    unnamed x14, local copies, waits for them, and re-layouts  14.7 us
    ppermute x3, starting transfers between devices, per_device(): lax.ppermute(below[-1], 'narrow', [(i, i + 1) for i in range(step - 1, na...  7.13 us
    ppermute x4, starting transfers between devices, per_device(): lax.ppermute(partial, 'wide', [(i, i ^ 2 * hop) for i in range(wide)])  5.71 us
    ppermute x3, starting transfers between devices, per_device(): lax.ppermute(share, 'narrow', [(i, i ^ step) for i in range(narrow)])  5.46 us
  transfers between devices with their start and end apart: 21, of which 5 were waited for; matrix products, arithmetic and copies ran while one was open for 1% of the time, Pallas kernels for 38%

profile of v1, /device:TPU:0, one launch (start us, length us, event | category | flops | bytes accessed | tf_op | source)
XLA Modules:
  0.0 128.8 jit_solution(10113509490502582386)
XLA Ops:
  0.6 1.1 pad_maximum_fusion.tokens_ref.refs_0_.refs_8_
  1.7 1.3 %collective-permute-start.3 = (bf16[2,64,1536]{2,1,0:T(8,128)(2,1)S(1)}, bf16[2,64,1536]{2,1,0:T(8,128)(2,1)S(1)}, u32[]{:S(2)}, u32[]{:S(2)}) collective-permute-start(bf16[2,64,1536]{2,1,0:T(8,128)(2,1)S(1)} %pad_maximum_fusion.tokens_ref.refs_0_.refs_8_), channel_id=1, source_target_pairs={{1,0},{2,1},{3,2},{5,4},{6,5},{7,6},{9,8},{10,9},{11,10},{13,12},{... | collective-permute-start | bytes 1179656 | tf_op jit(solution)/shard_map/ppermute | solution.py:160
  3.0 5.6 %collective-permute-start.4 = (bf16[2,64,1536]{2,1,0:T(8,128)(2,1)S(1)}, bf16[2,64,1536]{2,1,0:T(8,128)(2,1)S(1)}, u32[]{:S(2)}, u32[]{:S(2)}) collective-permute-start(bf16[2,64,1536]{2,1,0:T(8,128)(2,1)S(1)} %pad_maximum_fusion.tokens_ref.refs_0_.refs_8_), channel_id=1, source_target_pairs={{0,1},{1,2},{2,3},{4,5},{5,6},{6,7},{8,9},{9,10},{10,11},{12,13},{... | collective-permute-start | bytes 1179656 | tf_op jit(solution)/shard_map/ppermute | solution.py:159
  8.6 3.7 %copy-done = bf16[1536,3072]{1,0:T(8,128)(2,1)S(1)} copy-done((bf16[1536,3072]{1,0:T(8,128)(2,1)S(1)}, bf16[1536,3072]{1,0:T(8,128)(2,1)}, u32[]{:S(2)}) %copy-start) | copy-done | bytes 9437208
  12.3 3.7 %copy-done.2 = bf16[3072,1536]{1,0:T(8,128)(2,1)S(1)} copy-done((bf16[3072,1536]{1,0:T(8,128)(2,1)S(1)}, bf16[3072,1536]{1,0:T(8,128)(2,1)}, u32[]{:S(2)}) %copy-start.2) | copy-done | bytes 9437208
  16.0 4.6 %hidden_products.4 = (bf16[2,64,1536]{2,1,0:T(8,128)(2,1)S(1)}, bf16[2,64,1536]{2,1,0:T(8,128)(2,1)S(1)}) custom-call(s32[1]{0:T(128)} %bitcast.core_ref, bf16[2,64,1536]{2,1,0:T(8,128)(2,1)S(1)} %pad_maximum_fusion.tokens_ref.refs_0_.refs_8_, bf16[1536,3072]{1,0:T(8,128)(2,1)S(1)} %copy-done, bf16[3072,1536]{1,0:T(8,128)(2,1)S(1)} %copy-done.2), custom_call_target="tpu_custom_call" | custom-call | flops 1207959552 | bytes 18874368 | tf_op jit(solution)/shard_map/hidden_products/pallas_call | solution.py:23
  20.7 1.4 %collective-permute-start.9 = (bf16[2,64,1536]{2,1,0:T(8,128)(2,1)S(1)}, bf16[2,64,1536]{2,1,0:T(8,128)(2,1)S(1)}, u32[]{:S(2)}, u32[]{:S(2)}) collective-permute-start(bf16[2,64,1536]{2,1,0:T(8,128)(2,1)S(1)} %collective-permute-done.3), channel_id=1, source_target_pairs={{1,0},{2,1},{5,4},{6,5},{9,8},{10,9},{13,12},{14,13},{17,16},{18,1... | collective-permute-start | bytes 1179656 | tf_op jit(solution)/shard_map/ppermute | solution.py:160
  22.1 0.7 collective-permute-start.10
  22.9 2.0 %collective-permute-start.1 = (bf16[2,64,1536]{2,1,0:T(8,128)(2,1)S(1)}, bf16[2,64,1536]{2,1,0:T(8,128)(2,1)S(1)}, u32[]{:S(2)}, u32[]{:S(2)}) collective-permute-start(bf16[2,64,1536]{2,1,0:T(8,128)(2,1)S(1)} %add_convert_fusion.3.own_ref), channel_id=1, source_target_pairs={{0,8},{4,12},{8,0},{12,4},{1,9},{5,13},{9,1},{13,5},{2,10},{6,14},... | collective-permute-start | bytes 1179656 | tf_op jit(solution)/shard_map/ppermute | solution.py:179
  24.9 9.4 %collective-permute-done.9 = bf16[2,64,1536]{2,1,0:T(8,128)(2,1)S(1)} collective-permute-done((bf16[2,64,1536]{2,1,0:T(8,128)(2,1)S(1)}, bf16[2,64,1536]{2,1,0:T(8,128)(2,1)S(1)}, u32[]{:S(2)}, u32[]{:S(2)}) %collective-permute-start.9) | collective-permute-done | bytes 393248 | tf_op jit(solution)/shard_map/ppermute | solution.py:160
  34.4 3.7 %copy-done.1 = bf16[1536,3072]{1,0:T(8,128)(2,1)S(1)} copy-done((bf16[1536,3072]{1,0:T(8,128)(2,1)S(1)}, bf16[1536,3072]{1,0:T(8,128)(2,1)}, u32[]{:S(2)}) %copy-start.1) | copy-done | bytes 9437208
  38.1 3.7 %copy-done.3 = bf16[3072,1536]{1,0:T(8,128)(2,1)S(1)} copy-done((bf16[3072,1536]{1,0:T(8,128)(2,1)S(1)}, bf16[3072,1536]{1,0:T(8,128)(2,1)}, u32[]{:S(2)}) %copy-start.3) | copy-done | bytes 9437208
  41.8 4.6 %hidden_products.6 = (bf16[2,64,1536]{2,1,0:T(8,128)(2,1)S(1)}, bf16[2,64,1536]{2,1,0:T(8,128)(2,1)S(1)}) custom-call(s32[1]{0:T(128)} %bitcast.core_ref, bf16[2,64,1536]{2,1,0:T(8,128)(2,1)S(1)} %broadcast_select_fusion.tokens_ref.refs_2_.refs_10_, bf16[1536,3072]{1,0:T(8,128)(2,1)S(1)} %copy-done.1, bf16[3072,1536]{1,0:T(8,128)(2,1)S(1)} %copy-done.3), custom_call_target="tpu_custom_call" | custom-call | flops 1207959552 | bytes 18874368 | tf_op jit(solution)/shard_map/hidden_products/pallas_call | solution.py:23
  47.3 1.3 collective-permute-start.15
  48.5 0.9 collective-permute-start.16
  49.4 11.3 %collective-permute-done.15 = bf16[2,64,1536]{2,1,0:T(8,128)(2,1)S(1)} collective-permute-done((bf16[2,64,1536]{2,1,0:T(8,128)(2,1)S(1)}, bf16[2,64,1536]{2,1,0:T(8,128)(2,1)S(1)}, u32[]{:S(2)}, u32[]{:S(2)}) %collective-permute-start.15) | collective-permute-done | bytes 393248 | tf_op jit(solution)/shard_map/ppermute | solution.py:160
  60.9 4.6 %hidden_products.5 = (bf16[2,64,1536]{2,1,0:T(8,128)(2,1)S(1)}, bf16[2,64,1536]{2,1,0:T(8,128)(2,1)S(1)}) custom-call(s32[1]{0:T(128)} %bitcast.core_ref, bf16[2,64,1536]{2,1,0:T(8,128)(2,1)S(1)} %get-tuple-element.19.tokens_ref.refs_1_.refs_9_, bf16[1536,3072]{1,0:T(8,128)(2,1)S(1)} %bitcast.20, bf16[3072,1536]{1,0:T(8,128)(2,1)S(1)} %copy-done.3), custom_call_target="tpu_custom_call" | custom-call | flops 1207959552 | bytes 18874368 | tf_op jit(solution)/shard_map/hidden_products/pallas_call | solution.py:23
  65.7 1.6 %collective-permute-start.12 = (bf16[2,64,1536]{2,1,0:T(8,128)(2,1)S(1)}, bf16[2,64,1536]{2,1,0:T(8,128)(2,1)S(1)}, u32[]{:S(2)}, u32[]{:S(2)}) collective-permute-start(bf16[2,64,1536]{2,1,0:T(8,128)(2,1)S(1)} %add_convert_fusion.1.own_ref), channel_id=1, source_target_pairs={{0,8},{4,12},{8,0},{12,4},{1,9},{5,13},{9,1},{13,5},{2,10},{6,14},... | collective-permute-start | bytes 1179656 | tf_op jit(solution)/shard_map/ppermute | solution.py:179
  67.3 4.6 %hidden_products.7 = (bf16[2,64,1536]{2,1,0:T(8,128)(2,1)S(1)}, bf16[2,64,1536]{2,1,0:T(8,128)(2,1)S(1)}) custom-call(s32[1]{0:T(128)} %bitcast.core_ref, bf16[2,64,1536]{2,1,0:T(8,128)(2,1)S(1)} %get-tuple-element.20.tokens_ref.refs_3_.refs_11_, bf16[1536,3072]{1,0:T(8,128)(2,1)S(1)} %bitcast.20, bf16[3072,1536]{1,0:T(8,128)(2,1)S(1)} %copy-done.3), custom_call_target="tpu_custom_call" | custom-call | flops 1207959552 | bytes 18874368 | tf_op jit(solution)/shard_map/hidden_products/pallas_call | solution.py:23
  72.2 3.0 %input_product.4 = bf16[64,1536]{1,0:T(8,128)(2,1)S(1)} custom-call(s32[1]{0:T(128)} %bitcast.core_ref, bf16[64,1536]{1,0:T(8,128)(2,1)S(1)} %slice_bitcast_fusion.7.mine_ref, bf16[64,1536]{1,0:T(8,128)(2,1)S(1)} %slice_bitcast_fusion.6.other_ref, bf16[1536,3072]{1,0:T(8,128)(2,1)S(1)} %bitcast.20), custom_call_target="tpu_custom_call" | custom-call | flops 603979776 | bytes 9437184 | tf_op jit(solution)/shard_map/input_product/pallas_call | solution.py:23
  75.9 1.4 %collective-permute-done.12.peer_ref = bf16[2,64,1536]{2,1,0:T(8,128)(2,1)S(1)} collective-permute-done((bf16[2,64,1536]{2,1,0:T(8,128)(2,1)S(1)}, bf16[2,64,1536]{2,1,0:T(8,128)(2,1)S(1)}, u32[]{:S(2)}, u32[]{:S(2)}) %collective-permute-start.12) | collective-permute-done | bytes 393248 | tf_op jit(solution)/shard_map/ppermute | solution.py:179
  77.8 1.6 %collective-permute-start.18 = (bf16[2,64,1536]{2,1,0:T(8,128)(2,1)S(1)}, bf16[2,64,1536]{2,1,0:T(8,128)(2,1)S(1)}, u32[]{:S(2)}, u32[]{:S(2)}) collective-permute-start(bf16[2,64,1536]{2,1,0:T(8,128)(2,1)S(1)} %add_convert_fusion.own_ref), channel_id=1, source_target_pairs={{0,8},{4,12},{8,0},{12,4},{1,9},{5,13},{9,1},{13,5},{2,10},{6,14},... | collective-permute-start | bytes 1179656 | tf_op jit(solution)/shard_map/ppermute | solution.py:179
  79.3 7.9 %collective-permute-done.6.peer_ref = bf16[2,64,1536]{2,1,0:T(8,128)(2,1)S(1)} collective-permute-done((bf16[2,64,1536]{2,1,0:T(8,128)(2,1)S(1)}, bf16[2,64,1536]{2,1,0:T(8,128)(2,1)S(1)}, u32[]{:S(2)}, u32[]{:S(2)}) %collective-permute-start.6) | collective-permute-done | bytes 393248 | tf_op jit(solution)/shard_map/ppermute | solution.py:179
  87.6 7.5 %collective-permute-done.18.peer_ref = bf16[2,64,1536]{2,1,0:T(8,128)(2,1)S(1)} collective-permute-done((bf16[2,64,1536]{2,1,0:T(8,128)(2,1)S(1)}, bf16[2,64,1536]{2,1,0:T(8,128)(2,1)S(1)}, u32[]{:S(2)}, u32[]{:S(2)}) %collective-permute-start.18) | collective-permute-done | bytes 393248 | tf_op jit(solution)/shard_map/ppermute | solution.py:179
  95.5 3.0 %input_product.6 = bf16[64,1536]{1,0:T(8,128)(2,1)S(1)} custom-call(s32[1]{0:T(128)} %bitcast.core_ref, bf16[64,1536]{1,0:T(8,128)(2,1)S(1)} %slice_bitcast_fusion.3.mine_ref, bf16[64,1536]{1,0:T(8,128)(2,1)S(1)} %slice_bitcast_fusion.2.other_ref, bf16[1536,3072]{1,0:T(8,128)(2,1)S(1)} %bitcast.20), custom_call_target="tpu_custom_call" | custom-call | flops 603979776 | bytes 9437184 | tf_op jit(solution)/shard_map/input_product/pallas_call | solution.py:23
  98.5 2.8 %collective-permute-start.14 = (bf16[64,1536]{1,0:T(8,128)(2,1)S(1)}, bf16[64,1536]{1,0:T(8,128)(2,1)S(1)}, u32[]{:S(2)}, u32[]{:S(2)}) collective-permute-start(bf16[64,1536]{1,0:T(8,128)(2,1)S(1)} %input_product.6), channel_id=1, source_target_pairs={{0,2},{1,3},{2,0},{3,1},{4,6},{5,7},{6,4},{7,5},{8,10},{9,11},{10,... | collective-permute-start | bytes 589832 | tf_op jit(solution)/shard_map/ppermute | solution.py:189
  101.4 3.0 %input_product.5 = bf16[64,1536]{1,0:T(8,128)(2,1)S(1)} custom-call(s32[1]{0:T(128)} %bitcast.core_ref, bf16[64,1536]{1,0:T(8,128)(2,1)S(1)} %slice_bitcast_fusion.5.mine_ref, bf16[64,1536]{1,0:T(8,128)(2,1)S(1)} %slice_bitcast_fusion.4.other_ref, bf16[1536,3072]{1,0:T(8,128)(2,1)S(1)} %bitcast.20), custom_call_target="tpu_custom_call" | custom-call | flops 603979776 | bytes 9437184 | tf_op jit(solution)/shard_map/input_product/pallas_call | solution.py:23
  104.3 2.5 %collective-permute-start.8 = (bf16[64,1536]{1,0:T(8,128)(2,1)S(1)}, bf16[64,1536]{1,0:T(8,128)(2,1)S(1)}, u32[]{:S(2)}, u32[]{:S(2)}) collective-permute-start(bf16[64,1536]{1,0:T(8,128)(2,1)S(1)} %input_product.5), channel_id=1, source_target_pairs={{0,1},{1,0},{2,3},{3,2},{4,5},{5,4},{6,7},{7,6},{8,9},{9,8},{10,11... | collective-permute-start | bytes 589832 | tf_op jit(solution)/shard_map/ppermute | solution.py:189
  106.9 3.0 %input_product.7 = bf16[64,1536]{1,0:T(8,128)(2,1)S(1)} custom-call(s32[1]{0:T(128)} %bitcast.core_ref, bf16[64,1536]{1,0:T(8,128)(2,1)S(1)} %slice_bitcast_fusion.1.mine_ref, bf16[64,1536]{1,0:T(8,128)(2,1)S(1)} %slice_bitcast_fusion.other_ref, bf16[1536,3072]{1,0:T(8,128)(2,1)S(1)} %bitcast.20), custom_call_target="tpu_custom_call" | custom-call | flops 603979776 | bytes 9437184 | tf_op jit(solution)/shard_map/input_product/pallas_call | solution.py:23
  110.0 10.0 %down_grad.1 = f32[3072,1536]{1,0:T(8,128)} custom-call(s32[1]{0:T(128)} %bitcast.core_ref, bf16[2,64,1536]{2,1,0:T(8,128)(2,1)S(1)} %gelu.4.refs_4_.refs_0_, bf16[2,64,1536]{2,1,0:T(8,128)(2,1)S(1)} %collective-permute-done.2.refs_5_.refs_1_, bf16[2,64,1536]{2,1,0:T(8,128)(2,1)S(1)} %gelu.5.refs_6_.refs_2_, ...), custom_call_target="tpu_custom_call" | custom-call | flops 2415919104 | bytes 18874368 | tf_op jit(solution)/shard_map/down_grad/pallas_call | solution.py:131
  120.0 8.0 %up_grad.1 = f32[1536,3072]{1,0:T(8,128)} custom-call(s32[1]{0:T(128)} %bitcast.core_ref, bf16[2,64,1536]{2,1,0:T(8,128)(2,1)S(1)} %pad_maximum_fusion.tokens_ref.refs_0_.refs_8_, bf16[2,64,1536]{2,1,0:T(8,128)(2,1)S(1)} %get-tuple-element.19.tokens_ref.refs_1_.refs_9_, bf16[2,64,1536]{2,1,0:T(8,128)(2,1)S(1)} %broadcast_select_fusion.tokens_ref.refs_2_.refs_10_, ...), custom_call_target="tpu_custom_call" | custom-call | flops 2415919104 | bytes 18874368 | tf_op jit(solution)/shard_map/up_grad/pallas_call | solution.py:131
  128.0 0.8 add_convert_fusion.4
  (55 shorter events, 3.7 us)
Async XLA Ops:
  1.7 19.0 %collective-permute-start.3 = (bf16[2,64,1536]{2,1,0:T(8,128)(2,1)S(1)}, bf16[2,64,1536]{2,1,0:T(8,128)(2,1)S(1)}, u32[]{:S(2)}, u32[]{:S(2)}) collective-permute-start(bf16[2,64,1536]{2,1,0:T(8,128)(2,1)S(1)} %pad_maximum_fusion.tokens_ref.refs_0_.refs_8_), channel_id=1, source_target_pairs={{1,0},{2,1},{3,2},{5,4},{6,5},{7,6},{9,8},{10,9},{11,10},{13,12},{... | collective-permute-start | bytes 1179656 | tf_op jit(solution)/shard_map/ppermute | solution.py:160
  3.0 19.1 %collective-permute-start.4 = (bf16[2,64,1536]{2,1,0:T(8,128)(2,1)S(1)}, bf16[2,64,1536]{2,1,0:T(8,128)(2,1)S(1)}, u32[]{:S(2)}, u32[]{:S(2)}) collective-permute-start(bf16[2,64,1536]{2,1,0:T(8,128)(2,1)S(1)} %pad_maximum_fusion.tokens_ref.refs_0_.refs_8_), channel_id=1, source_target_pairs={{0,1},{1,2},{2,3},{4,5},{5,6},{6,7},{8,9},{9,10},{10,11},{12,13},{... | collective-permute-start | bytes 1179656 | tf_op jit(solution)/shard_map/ppermute | solution.py:159
  8.6 3.7 %copy-start = (bf16[1536,3072]{1,0:T(8,128)(2,1)S(1)}, bf16[1536,3072]{1,0:T(8,128)(2,1)}, u32[]{:S(2)}) copy-start(bf16[1536,3072]{1,0:T(8,128)(2,1)} %up_ref.15) | copy-start | bytes 28311556
  12.3 3.7 %copy-start.2 = (bf16[3072,1536]{1,0:T(8,128)(2,1)S(1)}, bf16[3072,1536]{1,0:T(8,128)(2,1)}, u32[]{:S(2)}) copy-start(bf16[3072,1536]{1,0:T(8,128)(2,1)} %down_ref.7) | copy-start | bytes 28311556
  20.6 40.3 %slice-start = ((s8[9437184]{0:T(1024)(128)(4,1)}), s8[1048576]{0:T(1024)(128)(4,1)S(1)}, s32[]{:S(2)}) async-start(s8[9437184]{0:T(1024)(128)(4,1)} %bitcast.19), calls=%async_computation | async-start | bytes 2097152
  20.6 2.2 %collective-permute-start = (bf16[2,64,1536]{2,1,0:T(8,128)(2,1)S(1)}, bf16[2,64,1536]{2,1,0:T(8,128)(2,1)S(1)}, u32[]{:S(2)}, u32[]{:S(2)}) collective-permute-start(bf16[2,64,1536]{2,1,0:T(8,128)(2,1)S(1)} %get-tuple-element.12), channel_id=1, source_target_pairs={{0,4},{4,0},{8,12},{12,8},{1,5},{5,1},{9,13},{13,9},{2,6},{6,2},{1... | collective-permute-start | bytes 1179656 | tf_op jit(solution)/shard_map/ppermute | solution.py:153
  20.7 13.6 %collective-permute-start.9 = (bf16[2,64,1536]{2,1,0:T(8,128)(2,1)S(1)}, bf16[2,64,1536]{2,1,0:T(8,128)(2,1)S(1)}, u32[]{:S(2)}, u32[]{:S(2)}) collective-permute-start(bf16[2,64,1536]{2,1,0:T(8,128)(2,1)S(1)} %collective-permute-done.3), channel_id=1, source_target_pairs={{1,0},{2,1},{5,4},{6,5},{9,8},{10,9},{13,12},{14,13},{17,16},{18,1... | collective-permute-start | bytes 1179656 | tf_op jit(solution)/shard_map/ppermute | solution.py:160
  22.1 12.2 %collective-permute-start.10 = (bf16[2,64,1536]{2,1,0:T(8,128)(2,1)S(1)}, bf16[2,64,1536]{2,1,0:T(8,128)(2,1)S(1)}, u32[]{:S(2)}, u32[]{:S(2)}) collective-permute-start(bf16[2,64,1536]{2,1,0:T(8,128)(2,1)S(1)} %collective-permute-done.4), channel_id=1, source_target_pairs={{1,2},{2,3},{5,6},{6,7},{9,10},{10,11},{13,14},{14,15},{17,18},{18... | collective-permute-start | bytes 1179656 | tf_op jit(solution)/shard_map/ppermute | solution.py:159
  22.9 23.5 %collective-permute-start.1 = (bf16[2,64,1536]{2,1,0:T(8,128)(2,1)S(1)}, bf16[2,64,1536]{2,1,0:T(8,128)(2,1)S(1)}, u32[]{:S(2)}, u32[]{:S(2)}) collective-permute-start(bf16[2,64,1536]{2,1,0:T(8,128)(2,1)S(1)} %add_convert_fusion.3.own_ref), channel_id=1, source_target_pairs={{0,8},{4,12},{8,0},{12,4},{1,9},{5,13},{9,1},{13,5},{2,10},{6,14},... | collective-permute-start | bytes 1179656 | tf_op jit(solution)/shard_map/ppermute | solution.py:179
  34.4 3.7 %copy-start.1 = (bf16[1536,3072]{1,0:T(8,128)(2,1)S(1)}, bf16[1536,3072]{1,0:T(8,128)(2,1)}, u32[]{:S(2)}) copy-start(bf16[1536,3072]{1,0:T(8,128)(2,1)} %up_ref.15) | copy-start | bytes 28311556
  38.1 3.7 %copy-start.3 = (bf16[3072,1536]{1,0:T(8,128)(2,1)S(1)}, bf16[3072,1536]{1,0:T(8,128)(2,1)}, u32[]{:S(2)}) copy-start(bf16[3072,1536]{1,0:T(8,128)(2,1)} %down_ref.7) | copy-start | bytes 28311556
  41.8 19.1 %slice-start.1 = ((s8[9437184]{0:T(1024)(128)(4,1)}), s8[4194304]{0:T(1024)(128)(4,1)S(1)}, s32[]{:S(2)}) async-start(s8[9437184]{0:T(1024)(128)(4,1)} %bitcast.19), calls=%async_computation.1 | async-start | bytes 8388608
  41.8 19.2 %slice-start.2 = ((s8[9437184]{0:T(1024)(128)(4,1)}), s8[4194304]{0:T(1024)(128)(4,1)S(1)}, s32[]{:S(2)}) async-start(s8[9437184]{0:T(1024)(128)(4,1)} %bitcast.19), calls=%async_computation.2 | async-start | bytes 8388608
  46.3 19.3 %collective-permute-start.11 = (bf16[2,64,1536]{2,1,0:T(8,128)(2,1)S(1)}, bf16[2,64,1536]{2,1,0:T(8,128)(2,1)S(1)}, u32[]{:S(2)}, u32[]{:S(2)}) collective-permute-start(bf16[2,64,1536]{2,1,0:T(8,128)(2,1)S(1)} %get-tuple-element.16), channel_id=1, source_target_pairs={{0,4},{4,0},{8,12},{12,8},{1,5},{5,1},{9,13},{13,9},{2,6},{6,2},{1... | collective-permute-start | bytes 1179656 | tf_op jit(solution)/shard_map/ppermute | solution.py:153
  46.7 25.5 %collective-permute-start.2 = (bf16[2,64,1536]{2,1,0:T(8,128)(2,1)S(1)}, bf16[2,64,1536]{2,1,0:T(8,128)(2,1)S(1)}, u32[]{:S(2)}, u32[]{:S(2)}) collective-permute-start(bf16[2,64,1536]{2,1,0:T(8,128)(2,1)S(1)} %gelu.4.refs_4_.refs_0_), channel_id=1, source_target_pairs={{0,4},{4,0},{8,12},{12,8},{1,5},{5,1},{9,13},{13,9},{2,6},{6,2},{1... | collective-permute-start | bytes 1179656 | tf_op jit(solution)/shard_map/ppermute | solution.py:153
  47.3 13.5 %collective-permute-start.15 = (bf16[2,64,1536]{2,1,0:T(8,128)(2,1)S(1)}, bf16[2,64,1536]{2,1,0:T(8,128)(2,1)S(1)}, u32[]{:S(2)}, u32[]{:S(2)}) collective-permute-start(bf16[2,64,1536]{2,1,0:T(8,128)(2,1)S(1)} %collective-permute-done.9), channel_id=1, source_target_pairs={{1,0},{5,4},{9,8},{13,12},{17,16},{21,20},{25,24},{29,28}} | collective-permute-start | bytes 1179656 | tf_op jit(solution)/shard_map/ppermute | solution.py:160
  48.5 12.2 %collective-permute-start.16 = (bf16[2,64,1536]{2,1,0:T(8,128)(2,1)S(1)}, bf16[2,64,1536]{2,1,0:T(8,128)(2,1)S(1)}, u32[]{:S(2)}, u32[]{:S(2)}) collective-permute-start(bf16[2,64,1536]{2,1,0:T(8,128)(2,1)S(1)} %collective-permute-done.10), channel_id=1, source_target_pairs={{2,3},{6,7},{10,11},{14,15},{18,19},{22,23},{26,27},{30,31}} | collective-permute-start | bytes 1179656 | tf_op jit(solution)/shard_map/ppermute | solution.py:159
  65.6 9.6 %collective-permute-start.5 = (bf16[2,64,1536]{2,1,0:T(8,128)(2,1)S(1)}, bf16[2,64,1536]{2,1,0:T(8,128)(2,1)S(1)}, u32[]{:S(2)}, u32[]{:S(2)}) collective-permute-start(bf16[2,64,1536]{2,1,0:T(8,128)(2,1)S(1)} %get-tuple-element.14), channel_id=1, source_target_pairs={{0,4},{4,0},{8,12},{12,8},{1,5},{5,1},{9,13},{13,9},{2,6},{6,2},{1... | collective-permute-start | bytes 1179656 | tf_op jit(solution)/shard_map/ppermute | solution.py:153
  65.7 11.6 %collective-permute-start.12 = (bf16[2,64,1536]{2,1,0:T(8,128)(2,1)S(1)}, bf16[2,64,1536]{2,1,0:T(8,128)(2,1)S(1)}, u32[]{:S(2)}, u32[]{:S(2)}) collective-permute-start(bf16[2,64,1536]{2,1,0:T(8,128)(2,1)S(1)} %add_convert_fusion.1.own_ref), channel_id=1, source_target_pairs={{0,8},{4,12},{8,0},{12,4},{1,9},{5,13},{9,1},{13,5},{2,10},{6,14},... | collective-permute-start | bytes 1179656 | tf_op jit(solution)/shard_map/ppermute | solution.py:179
  71.9 5.7 %collective-permute-start.17 = (bf16[2,64,1536]{2,1,0:T(8,128)(2,1)S(1)}, bf16[2,64,1536]{2,1,0:T(8,128)(2,1)S(1)}, u32[]{:S(2)}, u32[]{:S(2)}) collective-permute-start(bf16[2,64,1536]{2,1,0:T(8,128)(2,1)S(1)} %get-tuple-element.18), channel_id=1, source_target_pairs={{0,4},{4,0},{8,12},{12,8},{1,5},{5,1},{9,13},{13,9},{2,6},{6,2},{1... | collective-permute-start | bytes 1179656 | tf_op jit(solution)/shard_map/ppermute | solution.py:153
  75.3 12.0 %collective-permute-start.6 = (bf16[2,64,1536]{2,1,0:T(8,128)(2,1)S(1)}, bf16[2,64,1536]{2,1,0:T(8,128)(2,1)S(1)}, u32[]{:S(2)}, u32[]{:S(2)}) collective-permute-start(bf16[2,64,1536]{2,1,0:T(8,128)(2,1)S(1)} %add_convert_fusion.2.own_ref), channel_id=1, source_target_pairs={{0,8},{4,12},{8,0},{12,4},{1,9},{5,13},{9,1},{13,5},{2,10},{6,14},... | collective-permute-start | bytes 1179656 | tf_op jit(solution)/shard_map/ppermute | solution.py:179
  77.6 17.9 %collective-permute-start.13 = (bf16[2,64,1536]{2,1,0:T(8,128)(2,1)S(1)}, bf16[2,64,1536]{2,1,0:T(8,128)(2,1)S(1)}, u32[]{:S(2)}, u32[]{:S(2)}) collective-permute-start(bf16[2,64,1536]{2,1,0:T(8,128)(2,1)S(1)} %gelu.6.refs_8_.refs_4_), channel_id=1, source_target_pairs={{0,4},{4,0},{8,12},{12,8},{1,5},{5,1},{9,13},{13,9},{2,6},{6,2},{1... | collective-permute-start | bytes 1179656 | tf_op jit(solution)/shard_map/ppermute | solution.py:153
  77.8 17.3 %collective-permute-start.18 = (bf16[2,64,1536]{2,1,0:T(8,128)(2,1)S(1)}, bf16[2,64,1536]{2,1,0:T(8,128)(2,1)S(1)}, u32[]{:S(2)}, u32[]{:S(2)}) collective-permute-start(bf16[2,64,1536]{2,1,0:T(8,128)(2,1)S(1)} %add_convert_fusion.own_ref), channel_id=1, source_target_pairs={{0,8},{4,12},{8,0},{12,4},{1,9},{5,13},{9,1},{13,5},{2,10},{6,14},... | collective-permute-start | bytes 1179656 | tf_op jit(solution)/shard_map/ppermute | solution.py:179
  87.6 13.8 %collective-permute-start.7 = (bf16[2,64,1536]{2,1,0:T(8,128)(2,1)S(1)}, bf16[2,64,1536]{2,1,0:T(8,128)(2,1)S(1)}, u32[]{:S(2)}, u32[]{:S(2)}) collective-permute-start(bf16[2,64,1536]{2,1,0:T(8,128)(2,1)S(1)} %gelu.5.refs_6_.refs_2_), channel_id=1, source_target_pairs={{0,4},{4,0},{8,12},{12,8},{1,5},{5,1},{9,13},{13,9},{2,6},{6,2},{1... | collective-permute-start | bytes 1179656 | tf_op jit(solution)/shard_map/ppermute | solution.py:153
  95.4 11.5 %collective-permute-start.19 = (bf16[2,64,1536]{2,1,0:T(8,128)(2,1)S(1)}, bf16[2,64,1536]{2,1,0:T(8,128)(2,1)S(1)}, u32[]{:S(2)}, u32[]{:S(2)}) collective-permute-start(bf16[2,64,1536]{2,1,0:T(8,128)(2,1)S(1)} %gelu.7.refs_10_.refs_6_), channel_id=1, source_target_pairs={{0,4},{4,0},{8,12},{12,8},{1,5},{5,1},{9,13},{13,9},{2,6},{6,2},{1... | collective-permute-start | bytes 1179656 | tf_op jit(solution)/shard_map/ppermute | solution.py:153
  98.5 29.5 %collective-permute-start.14 = (bf16[64,1536]{1,0:T(8,128)(2,1)S(1)}, bf16[64,1536]{1,0:T(8,128)(2,1)S(1)}, u32[]{:S(2)}, u32[]{:S(2)}) collective-permute-start(bf16[64,1536]{1,0:T(8,128)(2,1)S(1)} %input_product.6), channel_id=1, source_target_pairs={{0,2},{1,3},{2,0},{3,1},{4,6},{5,7},{6,4},{7,5},{8,10},{9,11},{10,... | collective-permute-start | bytes 589832 | tf_op jit(solution)/shard_map/ppermute | solution.py:189
  104.3 23.6 %collective-permute-start.8 = (bf16[64,1536]{1,0:T(8,128)(2,1)S(1)}, bf16[64,1536]{1,0:T(8,128)(2,1)S(1)}, u32[]{:S(2)}, u32[]{:S(2)}) collective-permute-start(bf16[64,1536]{1,0:T(8,128)(2,1)S(1)} %input_product.5), channel_id=1, source_target_pairs={{0,1},{1,0},{2,3},{3,2},{4,5},{5,4},{6,7},{7,6},{8,9},{9,8},{10,11... | collective-permute-start | bytes 589832 | tf_op jit(solution)/shard_map/ppermute | solution.py:189
  109.9 18.1 %collective-permute-start.20 = (bf16[64,1536]{1,0:T(8,128)(2,1)S(1)}, bf16[64,1536]{1,0:T(8,128)(2,1)S(1)}, u32[]{:S(2)}, u32[]{:S(2)}) collective-permute-start(bf16[64,1536]{1,0:T(8,128)(2,1)S(1)} %input_product.7), channel_id=1, source_target_pairs={{0,3},{1,2},{2,1},{3,0},{4,7},{5,6},{6,5},{7,4},{8,11},{9,10},{10,... | collective-permute-start | bytes 589832 | tf_op jit(solution)/shard_map/ppermute | solution.py:189

commit v2 on v1

v2 whole, which is shorter than its diff:
```python
import functools

import jax
import jax.numpy as jnp
from jax import lax
from jax.experimental import pallas as pl
from jax.experimental.pallas import tpu as pltpu
from jax.sharding import PartitionSpec as P

F32, BF16 = jnp.float32, jnp.bfloat16
MIB = 1 << 20
VMEM = pltpu.VMEM
NN = (((1,), (0,)), ((), ()))
NT = (((1,), (1,)), ((), ()))
TN = (((0,), (0,)), ((), ()))


def dot(a, b, dims):
    return lax.dot_general(a, b, dims, preferred_element_type=F32)


def in_vmem(x):
    return pltpu.with_memory_space_constraint(x, VMEM)


def in_hbm(x):
    return pltpu.with_memory_space_constraint(x, pltpu.HBM)


def whole(x):
    return pl.BlockSpec(memory_space=pltpu.SMEM if x.dtype == jnp.int32 else VMEM)


def params(limit_mib):
    return pltpu.CompilerParams(vmem_limit_bytes=limit_mib * MIB)


def cost(flops, bytes_accessed):
    return pl.CostEstimate(flops=flops, bytes_accessed=bytes_accessed, transcendentals=0)


def tile_of(extent):
    return next(t for t in (512, 384, 256, 128) if extent % t == 0)


def load_and_product(core, other, tokens, up_weight, down_weight, name):
    _, rows, features = tokens.shape
    half = up_weight.shape[1] // 2
    tile = tile_of(half)
    pieces = half // tile

    def body(core_ref, tokens_ref, up_hbm, down_hbm, up_ref, down_ref, out_ref, sems):
        side = 1 - core_ref[0] if other else core_ref[0]
        base = side * half
        copies = []
        for i in range(pieces):
            units = pl.ds(pl.multiple_of(base + i * tile, tile), tile)
            part = pl.ds(i * tile, tile)
            copies.append(
                (
                    pltpu.make_async_copy(up_hbm.at[:, units], up_ref.at[:, part], sems.at[2 * i]),
                    pltpu.make_async_copy(down_hbm.at[units, :], down_ref.at[part, :], sems.at[2 * i + 1]),
                )
            )
        for first, second in copies:
            first.start()
            second.start()
        for i, (first, second) in enumerate(copies):
            part = slice(i * tile, (i + 1) * tile)
            first.wait()
            out_ref[0, :, part] = dot(tokens_ref[0], up_ref[:, part], NN).astype(BF16)
            second.wait()
            out_ref[1, :, part] = dot(tokens_ref[1], down_ref[part, :], NT).astype(BF16)

    hbm = pl.BlockSpec(memory_space=pl.ANY)
    return pl.pallas_call(
        body,
        out_shape=(
            VMEM((features, half), BF16),
            VMEM((half, features), BF16),
            jax.ShapeDtypeStruct((2, rows, half), BF16),
        ),
        in_specs=[whole(core), whole(tokens), hbm, hbm],
        out_specs=(pl.BlockSpec(memory_space=VMEM),) * 3,
        scratch_shapes=[pltpu.SemaphoreType.DMA((2 * pieces,))],
        compiler_params=params(24),
        cost_estimate=cost(4 * rows * features * half, 4 * features * half),
        name=name,
    )(core, tokens, in_hbm(up_weight), in_hbm(down_weight))


def product(tokens, up_half, down_half, name):
    _, rows, features = tokens.shape
    half = up_half.shape[1]
    tile = tile_of(half)

    def body(tokens_ref, up_ref, down_ref, out_ref):
        for start in range(0, half, tile):
            part = slice(start, start + tile)
            out_ref[0, :, part] = dot(tokens_ref[0], up_ref[:, part], NN).astype(BF16)
            out_ref[1, :, part] = dot(tokens_ref[1], down_ref[part, :], NT).astype(BF16)

    args = (tokens, in_vmem(up_half), in_vmem(down_half))
    return pl.pallas_call(
        body,
        out_shape=jax.ShapeDtypeStruct((2, rows, half), BF16),
        in_specs=[whole(a) for a in args],
        out_specs=pl.BlockSpec(memory_space=VMEM),
        compiler_params=params(16),
        cost_estimate=cost(4 * rows * features * half, 4 * features * half),
        name=name,
    )(*args)


def input_product(mine, other, up_mine, up_other, so_far):
    _, rows, half = mine.shape
    features = up_mine.shape[0]
    tile = tile_of(features)

    def body(mine_ref, other_ref, up_mine_ref, up_other_ref, *refs):
        for start in range(0, features, tile):
            part = slice(start, start + tile)
            share = dot(mine_ref[0], up_mine_ref[part, :], NT) + dot(other_ref[0], up_other_ref[part, :], NT)
            if so_far is not None:
                share = share + refs[0][:, part].astype(F32)
            refs[-1][:, part] = share.astype(BF16)

    args = (mine, other, in_vmem(up_mine), in_vmem(up_other)) + (() if so_far is None else (so_far,))
    return pl.pallas_call(
        body,
        out_shape=jax.ShapeDtypeStruct((rows, features), BF16),
        in_specs=[whole(a) for a in args],
        out_specs=pl.BlockSpec(memory_space=VMEM),
        compiler_params=params(16),
        cost_estimate=cost(4 * rows * features * half, 4 * features * half),
        name="input_product",
    )(*args)


def gelu_kernel(own, peer):
    _, rows, half = own.shape

    def body(own_ref, peer_ref, out_ref):
        hidden = own_ref[0].astype(F32) + peer_ref[0].astype(F32)
        grad_hidden = own_ref[1].astype(F32) + peer_ref[1].astype(F32)
        cdf = 0.5 * (1.0 + lax.erf(hidden * 0.7071067811865476))
        pdf = jnp.exp(-0.5 * hidden * hidden) * 0.3989422804014327
        out_ref[0] = (grad_hidden * (cdf + hidden * pdf)).astype(BF16)
        out_ref[1] = (hidden * cdf).astype(BF16)

    return pl.pallas_call(
        body,
        out_shape=jax.ShapeDtypeStruct((2, rows, half), BF16),
        in_specs=[whole(own), whole(peer)],
        out_specs=pl.BlockSpec(memory_space=VMEM),
        compiler_params=params(16),
        cost_estimate=cost(40 * rows * half, 12 * rows * half),
        name="gelu",
    )(own, peer)


def weight_grad(core, left_chunks, right_chunks, which, left_split, right_split, tile, scale, name):
    def flat(chunks, split):
        return [a for pair in chunks for a in pair] if split else list(chunks)

    left, right = flat(left_chunks, left_split), flat(right_chunks, right_split)
    count = len(left_chunks)
    rows = left[0].shape[1]
    wide_left = left[0].shape[2] * (2 if left_split else 1)
    wide_right = right[0].shape[2] * (2 if right_split else 1)
    tokens = rows * count
    tile = next(t for t in (tile, 256, 128) if wide_left % t == 0)

    def fill(me, refs, split, scratch, index):
        for chunk in range(count):
            at = slice(chunk * rows, (chunk + 1) * rows)
            if split:
                half = scratch.shape[1] // 2
                scratch[at, pl.ds(pl.multiple_of(me * half, half), half)] = refs[2 * chunk][index]
                scratch[at, pl.ds(pl.multiple_of((1 - me) * half, half), half)] = refs[2 * chunk + 1][index]
            else:
                scratch[at, :] = refs[chunk][index]

    def body(core_ref, *refs):
        left_refs, right_refs = refs[: len(left)], refs[len(left) : len(left) + len(right)]
        out_ref, left_all, right_all = refs[len(left) + len(right) :]

        @pl.when(pl.program_id(0) == 0)
        def _():
            fill(core_ref[0], left_refs, left_split, left_all, which[0])
            fill(core_ref[0], right_refs, right_split, right_all, which[1])

        part = pl.ds(pl.multiple_of(pl.program_id(0) * tile, tile), tile)
        out_ref[...] = dot(left_all[:, part], right_all[...], TN) * scale

    return pl.pallas_call(
        body,
        grid=(wide_left // tile,),
        out_shape=jax.ShapeDtypeStruct((wide_left, wide_right), F32),
        in_specs=[whole(core)] + [pl.BlockSpec(memory_space=VMEM)] * (len(left) + len(right)),
        out_specs=pl.BlockSpec((tile, wide_right), lambda i: (i, 0)),
        scratch_shapes=[VMEM((tokens, wide_left), BF16), VMEM((tokens, wide_right), BF16)],
        compiler_params=params(24),
        cost_estimate=cost(2 * tokens * wide_left * wide_right, 4 * wide_left * wide_right),
        name=name,
    )(core, *left, *right)


def per_device(wide, narrow, inputs, up_weight, down_weight, out_grad):
    rows = inputs.shape[0]
    chips = wide // 2
    core = (lax.axis_index("wide") & 1).astype(jnp.int32).reshape(1)

    def swap_cores(x):
        return lax.ppermute(x, "wide", [(i, i ^ 1) for i in range(wide)])

    def pass_on(x):
        return lax.ppermute(x, "narrow", [(i, (i + 1) % narrow) for i in range(narrow)])

    chunks = [jnp.stack([inputs, out_grad])]
    for _ in range(1, narrow):
        chunks.append(pass_on(chunks[-1]))

    acts = []
    share = kept = None
    for step, chunk in enumerate(chunks):
        if step == 0:
            up_other, down_other, give = load_and_product(core, True, chunk, up_weight, down_weight, "give_first")
            got = swap_cores(give)
            up_mine, down_mine, keep = load_and_product(core, False, chunk, up_weight, down_weight, "keep_first")
        else:
            give = product(chunk, up_other, down_other, "give")
            got = swap_cores(give)
            keep = product(chunk, up_mine, down_mine, "keep")
        partial = (keep.astype(F32) + got.astype(F32)).astype(BF16)
        hop = 1
        while hop < chips:
            peer = lax.ppermute(partial, "wide", [(i, i ^ (2 * hop)) for i in range(wide)])
            if 2 * hop < chips:
                partial = (partial.astype(F32) + peer.astype(F32)).astype(BF16)
            hop *= 2
        mine = gelu_kernel(partial, peer)
        other = swap_cores(mine)
        acts.append((mine, other))
        if step == 0:
            kept = input_product(mine, other, up_mine, up_other, None)
        else:
            share = pass_on(input_product(mine, other, up_mine, up_other, share))
    input_grad = kept if share is None else (kept.astype(F32) + share.astype(F32)).astype(BF16)
    scale = (rows * narrow) ** -0.5
    up_grad = weight_grad(core, chunks, acts, (0, 0), False, True, 256, scale, "up_grad")
    down_grad = weight_grad(core, acts, chunks, (1, 1), True, False, 512, scale, "down_grad")
    return input_grad, up_grad, down_grad


def solution(mesh):
    placed = (
        P(("groups", "narrow"), "wide"),
        P("wide", "narrow"),
        P("narrow", "wide"),
        P(("groups", "narrow"), "wide"),
    )
    return jax.shard_map(
        functools.partial(per_device, mesh.shape["wide"], mesh.shape["narrow"]),
        mesh=mesh,
        in_specs=placed,
        out_specs=(
            P(("groups", "narrow"), "wide"),
            P(("groups", "wide"), "narrow"),
            P(("groups", "narrow"), "wide"),
        ),
        check_vma=False,
    )
```

time: 129 us -> 106 us (0.82)
  local copies, waits for them, and re-layouts: 14.8 us -> 0 us
  starting transfers between devices: 23.5 us -> 10.1 us
  waiting for transfers between devices: 37.6 us -> 40.6 us
  Pallas kernels: 49.4 us -> 52.1 us
    unnamed x14 -> x0, local copies, waits for them, and re-layouts: 14.7 us -> none
    ppermute x9 -> x6, starting transfers between devices: 16.6 us -> 3.57 us  [pass_on(): lax.ppermute(x, 'narrow', [(i, (i + 1) % narrow) for i in range(narrow)])]
    ppermute x9 -> x6, waiting for transfers between devices: 20.7 us -> 29.9 us  [pass_on(): lax.ppermute(x, 'narrow', [(i, (i + 1) % narrow) for i in range(narrow)])]
    ppermute x4, waiting for transfers between devices: 16.8 us -> 10.6 us  [per_device(): lax.ppermute(partial, 'wide', [(i, i ^ 2 * hop) for i in range(wide)])]
    pallas_call x12 -> x16, Pallas kernels: 31.4 us -> 36 us  [the longest x6 14.1 us: product(): pl.pallas_call(body, out_shape=jax.ShapeDtypeStruct((2, rows, half), BF16...]
    pallas_call x2, Pallas kernels: 18 us -> 16 us  [weight_grad(): pl.pallas_call(body, grid=(wide_left // tile,), out_shape=jax.ShapeDtypeS...]
  transfers between devices with their start and end apart: 21 -> 18, of which waited for: 5 -> 7; matrix products, arithmetic and copies ran while one was open for 1% -> 0% of each run, Pallas kernels for 38% -> 46%
where the time goes in v2:
time: 106 us
  Pallas kernels  52.1 us (49%)
  waiting for transfers between devices  40.6 us (38%)
  starting transfers between devices  10.1 us (10%)
  other arithmetic  2.16 us (2%)
    ppermute x6, waiting for transfers between devices, pass_on(): lax.ppermute(x, 'narrow', [(i, (i + 1) % narrow) for i in range(narrow)])  29.9 us
    pallas_call x2, Pallas kernels, weight_grad(): pl.pallas_call(body, grid=(wide_left // tile,), out_shape=jax.ShapeDtypeS...  16 us
    pallas_call x6, Pallas kernels, product(): pl.pallas_call(body, out_shape=jax.ShapeDtypeStruct((2, rows, half), BF16...  14.1 us
    pallas_call x4, Pallas kernels, input_product(): pl.pallas_call(body, out_shape=jax.ShapeDtypeStruct((rows, features), BF1...  11.8 us
    ppermute x4, waiting for transfers between devices, per_device(): lax.ppermute(partial, 'wide', [(i, i ^ 2 * hop) for i in range(wide)])  10.6 us
    pallas_call x2, Pallas kernels, load_and_product(): pl.pallas_call(body, out_shape=(VMEM((features, half), BF16), VMEM((half,...  9.06 us
    ppermute x4, starting transfers between devices, per_device(): lax.ppermute(partial, 'wide', [(i, i ^ 2 * hop) for i in range(wide)])  5.28 us
    ppermute x6, starting transfers between devices, pass_on(): lax.ppermute(x, 'narrow', [(i, (i + 1) % narrow) for i in range(narrow)])  3.57 us
  transfers between devices with their start and end apart: 18, of which 7 were waited for; matrix products, arithmetic and copies ran while one was open for 0% of the time, Pallas kernels for 46%

profile of v2, /device:TPU:0, one launch (start us, length us, event | category | flops | bytes accessed | tf_op | source)
XLA Modules:
  0.0 105.8 jit_solution(9295744366791712618)
XLA Ops:
  0.6 1.1 %pad_maximum_fusion.tokens_ref.refs_0_.refs_8_ = bf16[2,64,1536]{2,1,0:T(8,128)(2,1)S(1)} fusion(bf16[1,64,1536]{2,1,0:T(8,128)(2,1)} %bitcast.3, bf16[1,64,1536]{2,1,0:T(8,128)(2,1)} %bitcast.4), kind=kLoop, calls=%fused_computation.4 | loop fusion | flops 196608 | bytes 786432 | tf_op jit(solution)/shard_map/stack | solution.py:220
  1.7 3.1 %collective-permute-start.3 = (bf16[2,64,1536]{2,1,0:T(8,128)(2,1)S(1)}, bf16[2,64,1536]{2,1,0:T(8,128)(2,1)S(1)}, u32[]{:S(2)}, u32[]{:S(2)}) collective-permute-start(bf16[2,64,1536]{2,1,0:T(8,128)(2,1)S(1)} %pad_maximum_fusion.tokens_ref.refs_0_.refs_8_), channel_id=1, source_target_pairs={{0,1},{1,2},{2,3},{3,0},{4,5},{5,6},{6,7},{7,4},{8,9},{9,10},{10,1... | collective-permute-start | bytes 1179656 | tf_op jit(solution)/shard_map/ppermute | solution.py:218
  4.8 4.5 %give_first.1 = (bf16[1536,1536]{1,0:T(8,128)(2,1)S(1)}, bf16[1536,1536]{1,0:T(8,128)(2,1)S(1)}, bf16[2,64,1536]{2,1,0:T(8,128)(2,1)S(1)}) custom-call(s32[1]{0:T(128)} %bitcast.core_ref, bf16[2,64,1536]{2,1,0:T(8,128)(2,1)S(1)} %pad_maximum_fusion.tokens_ref.refs_0_.refs_8_, bf16[1536,3072]{1,0:T(8,128)(2,1)} %up_hbm.3, bf16[3072,1536]{1,0:T(8,128)(2,1)} %down_hbm.3), custom_call_target="tpu_custom_call" | custom-call | flops 603979776 | bytes 9437184 | tf_op jit(solution)/shard_map/give_first/pallas_call | solution.py:76
  9.4 4.5 %keep_first.1 = (bf16[1536,1536]{1,0:T(8,128)(2,1)S(1)}, bf16[1536,1536]{1,0:T(8,128)(2,1)S(1)}, bf16[2,64,1536]{2,1,0:T(8,128)(2,1)S(1)}) custom-call(s32[1]{0:T(128)} %bitcast.core_ref, bf16[2,64,1536]{2,1,0:T(8,128)(2,1)S(1)} %pad_maximum_fusion.tokens_ref.refs_0_.refs_8_, bf16[1536,3072]{1,0:T(8,128)(2,1)} %up_hbm.3, bf16[3072,1536]{1,0:T(8,128)(2,1)} %down_hbm.3), custom_call_target="tpu_custom_call" | custom-call | flops 603979776 | bytes 9437184 | tf_op jit(solution)/shard_map/keep_first/pallas_call | solution.py:76
  13.9 2.0 %collective-permute-done.3.tokens_ref.refs_1_.refs_9_ = bf16[2,64,1536]{2,1,0:T(8,128)(2,1)S(1)} collective-permute-done((bf16[2,64,1536]{2,1,0:T(8,128)(2,1)S(1)}, bf16[2,64,1536]{2,1,0:T(8,128)(2,1)S(1)}, u32[]{:S(2)}, u32[]{:S(2)}) %collective-permute-start.3) | collective-permute-done | bytes 393248 | tf_op jit(solution)/shard_map/ppermute | solution.py:218
  15.9 2.4 %give.5 = bf16[2,64,1536]{2,1,0:T(8,128)(2,1)S(1)} custom-call(bf16[2,64,1536]{2,1,0:T(8,128)(2,1)S(1)} %collective-permute-done.3.tokens_ref.refs_1_.refs_9_, bf16[1536,1536]{1,0:T(8,128)(2,1)S(1)} %get-tuple-element.12.up_other_ref.up_ref, bf16[1536,1536]{1,0:T(8,128)(2,1)S(1)} %get-tuple-element.14.down_ref), custom_call_target="tpu_custom_call" | custom-call | flops 603979776 | bytes 9437184 | tf_op jit(solution)/shard_map/give/pallas_call | solution.py:104
  18.5 1.6 %collective-permute-start.1 = (bf16[2,64,1536]{2,1,0:T(8,128)(2,1)S(1)}, bf16[2,64,1536]{2,1,0:T(8,128)(2,1)S(1)}, u32[]{:S(2)}, u32[]{:S(2)}) collective-permute-start(bf16[2,64,1536]{2,1,0:T(8,128)(2,1)S(1)} %add_convert_fusion.3.own_ref), channel_id=1, source_target_pairs={{0,8},{4,12},{8,0},{12,4},{1,9},{5,13},{9,1},{13,5},{2,10},{6,14},... | collective-permute-start | bytes 1179656 | tf_op jit(solution)/shard_map/ppermute | solution.py:238
  20.1 2.3 %keep.5 = bf16[2,64,1536]{2,1,0:T(8,128)(2,1)S(1)} custom-call(bf16[2,64,1536]{2,1,0:T(8,128)(2,1)S(1)} %collective-permute-done.3.tokens_ref.refs_1_.refs_9_, bf16[1536,1536]{1,0:T(8,128)(2,1)S(1)} %get-tuple-element.11.up_mine_ref.up_ref, bf16[1536,1536]{1,0:T(8,128)(2,1)S(1)} %get-tuple-element.13.down_ref), custom_call_target="tpu_custom_call" | custom-call | flops 603979776 | bytes 9437184 | tf_op jit(solution)/shard_map/keep/pallas_call | solution.py:104
  22.4 9.2 %collective-permute-done.4.tokens_ref.refs_2_.refs_10_ = bf16[2,64,1536]{2,1,0:T(8,128)(2,1)S(1)} collective-permute-done((bf16[2,64,1536]{2,1,0:T(8,128)(2,1)S(1)}, bf16[2,64,1536]{2,1,0:T(8,128)(2,1)S(1)}, u32[]{:S(2)}, u32[]{:S(2)}) %collective-permute-start.4) | collective-permute-done | bytes 393248 | tf_op jit(solution)/shard_map/ppermute | solution.py:218
  31.7 2.3 %give.4 = bf16[2,64,1536]{2,1,0:T(8,128)(2,1)S(1)} custom-call(bf16[2,64,1536]{2,1,0:T(8,128)(2,1)S(1)} %collective-permute-done.4.tokens_ref.refs_2_.refs_10_, bf16[1536,1536]{1,0:T(8,128)(2,1)S(1)} %get-tuple-element.12.up_other_ref.up_ref, bf16[1536,1536]{1,0:T(8,128)(2,1)S(1)} %get-tuple-element.14.down_ref), custom_call_target="tpu_custom_call" | custom-call | flops 603979776 | bytes 9437184 | tf_op jit(solution)/shard_map/give/pallas_call | solution.py:104
  34.5 1.6 %collective-permute-start.13 = (bf16[2,64,1536]{2,1,0:T(8,128)(2,1)S(1)}, bf16[2,64,1536]{2,1,0:T(8,128)(2,1)S(1)}, u32[]{:S(2)}, u32[]{:S(2)}) collective-permute-start(bf16[2,64,1536]{2,1,0:T(8,128)(2,1)S(1)} %add_convert_fusion.own_ref), channel_id=1, source_target_pairs={{0,8},{4,12},{8,0},{12,4},{1,9},{5,13},{9,1},{13,5},{2,10},{6,14},... | collective-permute-start | bytes 1179656 | tf_op jit(solution)/shard_map/ppermute | solution.py:238
  36.0 2.4 %keep.4 = bf16[2,64,1536]{2,1,0:T(8,128)(2,1)S(1)} custom-call(bf16[2,64,1536]{2,1,0:T(8,128)(2,1)S(1)} %collective-permute-done.4.tokens_ref.refs_2_.refs_10_, bf16[1536,1536]{1,0:T(8,128)(2,1)S(1)} %get-tuple-element.11.up_mine_ref.up_ref, bf16[1536,1536]{1,0:T(8,128)(2,1)S(1)} %get-tuple-element.13.down_ref), custom_call_target="tpu_custom_call" | custom-call | flops 603979776 | bytes 9437184 | tf_op jit(solution)/shard_map/keep/pallas_call | solution.py:104
  38.4 9.0 %collective-permute-done.5.tokens_ref.refs_3_.refs_11_ = bf16[2,64,1536]{2,1,0:T(8,128)(2,1)S(1)} collective-permute-done((bf16[2,64,1536]{2,1,0:T(8,128)(2,1)S(1)}, bf16[2,64,1536]{2,1,0:T(8,128)(2,1)S(1)}, u32[]{:S(2)}, u32[]{:S(2)}) %collective-permute-start.5) | collective-permute-done | bytes 393248 | tf_op jit(solution)/shard_map/ppermute | solution.py:218
  47.4 2.4 %give.3 = bf16[2,64,1536]{2,1,0:T(8,128)(2,1)S(1)} custom-call(bf16[2,64,1536]{2,1,0:T(8,128)(2,1)S(1)} %collective-permute-done.5.tokens_ref.refs_3_.refs_11_, bf16[1536,1536]{1,0:T(8,128)(2,1)S(1)} %get-tuple-element.12.up_other_ref.up_ref, bf16[1536,1536]{1,0:T(8,128)(2,1)S(1)} %get-tuple-element.14.down_ref), custom_call_target="tpu_custom_call" | custom-call | flops 603979776 | bytes 9437184 | tf_op jit(solution)/shard_map/give/pallas_call | solution.py:104
  50.0 1.6 %collective-permute-start.10 = (bf16[2,64,1536]{2,1,0:T(8,128)(2,1)S(1)}, bf16[2,64,1536]{2,1,0:T(8,128)(2,1)S(1)}, u32[]{:S(2)}, u32[]{:S(2)}) collective-permute-start(bf16[2,64,1536]{2,1,0:T(8,128)(2,1)S(1)} %add_convert_fusion.1.own_ref), channel_id=1, source_target_pairs={{0,8},{4,12},{8,0},{12,4},{1,9},{5,13},{9,1},{13,5},{2,10},{6,14},... | collective-permute-start | bytes 1179656 | tf_op jit(solution)/shard_map/ppermute | solution.py:238
  51.5 0.3 gelu.7.mine_ref.refs_6_.refs_2_
  51.8 0.3 collective-permute-start.14
  52.1 2.3 %keep.3 = bf16[2,64,1536]{2,1,0:T(8,128)(2,1)S(1)} custom-call(bf16[2,64,1536]{2,1,0:T(8,128)(2,1)S(1)} %collective-permute-done.5.tokens_ref.refs_3_.refs_11_, bf16[1536,1536]{1,0:T(8,128)(2,1)S(1)} %get-tuple-element.11.up_mine_ref.up_ref, bf16[1536,1536]{1,0:T(8,128)(2,1)S(1)} %get-tuple-element.13.down_ref), custom_call_target="tpu_custom_call" | custom-call | flops 603979776 | bytes 9437184 | tf_op jit(solution)/shard_map/keep/pallas_call | solution.py:104
  54.5 0.6 collective-permute-start.7
  55.1 6.8 %collective-permute-done.10.peer_ref = bf16[2,64,1536]{2,1,0:T(8,128)(2,1)S(1)} collective-permute-done((bf16[2,64,1536]{2,1,0:T(8,128)(2,1)S(1)}, bf16[2,64,1536]{2,1,0:T(8,128)(2,1)S(1)}, u32[]{:S(2)}, u32[]{:S(2)}) %collective-permute-start.10) | collective-permute-done | bytes 393248 | tf_op jit(solution)/shard_map/ppermute | solution.py:238
  62.3 0.3 gelu.4.mine_ref.refs_4_.refs_0_
  62.6 2.9 %input_product.5 = bf16[64,1536]{1,0:T(8,128)(2,1)S(1)} custom-call(bf16[2,64,1536]{2,1,0:T(8,128)(2,1)S(1)} %gelu.7.mine_ref.refs_6_.refs_2_, bf16[2,64,1536]{2,1,0:T(8,128)(2,1)S(1)} %collective-permute-done.14.other_ref.refs_7_.refs_3_, bf16[1536,1536]{1,0:T(8,128)(2,1)S(1)} %get-tuple-element.11.up_mine_ref.up_ref, ...), custom_call_target="tpu_custom_call" | custom-call | flops 603979776 | bytes 9437184 | tf_op jit(solution)/shard_map/input_product/pallas_call | solution.py:129
  65.6 0.6 collective-permute-start.2
  66.1 3.8 %collective-permute-done.7.peer_ref = bf16[2,64,1536]{2,1,0:T(8,128)(2,1)S(1)} collective-permute-done((bf16[2,64,1536]{2,1,0:T(8,128)(2,1)S(1)}, bf16[2,64,1536]{2,1,0:T(8,128)(2,1)S(1)}, u32[]{:S(2)}, u32[]{:S(2)}) %collective-permute-start.7) | collective-permute-done | bytes 393248 | tf_op jit(solution)/shard_map/ppermute | solution.py:238
  70.3 4.4 %collective-permute-done.15.refs_0_ = bf16[64,1536]{1,0:T(8,128)(2,1)S(1)} collective-permute-done((bf16[64,1536]{1,0:T(8,128)(2,1)S(1)}, bf16[64,1536]{1,0:T(8,128)(2,1)S(1)}, u32[]{:S(2)}, u32[]{:S(2)}) %collective-permute-start.15) | collective-permute-done | bytes 196640 | tf_op jit(solution)/shard_map/ppermute | solution.py:218
  74.7 2.9 %input_product.6 = bf16[64,1536]{1,0:T(8,128)(2,1)S(1)} custom-call(bf16[2,64,1536]{2,1,0:T(8,128)(2,1)S(1)} %gelu.6.mine_ref.refs_8_.refs_4_, bf16[2,64,1536]{2,1,0:T(8,128)(2,1)S(1)} %collective-permute-done.11.other_ref.refs_9_.refs_5_, bf16[1536,1536]{1,0:T(8,128)(2,1)S(1)} %get-tuple-element.11.up_mine_ref.up_ref, ...), custom_call_target="tpu_custom_call" | custom-call | flops 603979776 | bytes 9437184 | tf_op jit(solution)/shard_map/input_product/pallas_call | solution.py:129
  77.7 3.0 %input_product.4 = bf16[64,1536]{1,0:T(8,128)(2,1)S(1)} custom-call(bf16[2,64,1536]{2,1,0:T(8,128)(2,1)S(1)} %gelu.4.mine_ref.refs_4_.refs_0_, bf16[2,64,1536]{2,1,0:T(8,128)(2,1)S(1)} %collective-permute-done.2.other_ref.refs_5_.refs_1_, bf16[1536,1536]{1,0:T(8,128)(2,1)S(1)} %get-tuple-element.11.up_mine_ref.up_ref, ...), custom_call_target="tpu_custom_call" | custom-call | flops 603979776 | bytes 9437184 | tf_op jit(solution)/shard_map/input_product/pallas_call | solution.py:129
  80.7 5.3 %collective-permute-done.16.refs_0_ = bf16[64,1536]{1,0:T(8,128)(2,1)S(1)} collective-permute-done((bf16[64,1536]{1,0:T(8,128)(2,1)S(1)}, bf16[64,1536]{1,0:T(8,128)(2,1)S(1)}, u32[]{:S(2)}, u32[]{:S(2)}) %collective-permute-start.16) | collective-permute-done | bytes 196640 | tf_op jit(solution)/shard_map/ppermute | solution.py:218
  86.0 3.0 %input_product.7 = bf16[64,1536]{1,0:T(8,128)(2,1)S(1)} custom-call(bf16[2,64,1536]{2,1,0:T(8,128)(2,1)S(1)} %gelu.5.mine_ref.refs_10_.refs_6_, bf16[2,64,1536]{2,1,0:T(8,128)(2,1)S(1)} %collective-permute-done.8.other_ref.refs_11_.refs_7_, bf16[1536,1536]{1,0:T(8,128)(2,1)S(1)} %get-tuple-element.11.up_mine_ref.up_ref, ...), custom_call_target="tpu_custom_call" | custom-call | flops 603979776 | bytes 9437184 | tf_op jit(solution)/shard_map/input_product/pallas_call | solution.py:129
  89.0 8.0 %down_grad.1 = f32[3072,1536]{1,0:T(8,128)} custom-call(s32[1]{0:T(128)} %bitcast.core_ref, bf16[2,64,1536]{2,1,0:T(8,128)(2,1)S(1)} %gelu.4.mine_ref.refs_4_.refs_0_, bf16[2,64,1536]{2,1,0:T(8,128)(2,1)S(1)} %collective-permute-done.2.other_ref.refs_5_.refs_1_, bf16[2,64,1536]{2,1,0:T(8,128)(2,1)S(1)} %gelu.7.mine_ref.refs_6_.refs_2_, ...), custom_call_target="tpu_custom_call" | custom-call | flops 2415919104 | bytes 18874368 | tf_op jit(solution)/shard_map/down_grad/pallas_call | solution.py:196
  97.0 8.0 %up_grad.1 = f32[1536,3072]{1,0:T(8,128)} custom-call(s32[1]{0:T(128)} %bitcast.core_ref, bf16[2,64,1536]{2,1,0:T(8,128)(2,1)S(1)} %pad_maximum_fusion.tokens_ref.refs_0_.refs_8_, bf16[2,64,1536]{2,1,0:T(8,128)(2,1)S(1)} %collective-permute-done.3.tokens_ref.refs_1_.refs_9_, bf16[2,64,1536]{2,1,0:T(8,128)(2,1)S(1)} %collective-permute-done.4.tokens_ref.refs_2_.refs_10_, ...), custom_call_target="tpu_custom_call" | custom-call | flops 2415919104 | bytes 18874368 | tf_op jit(solution)/shard_map/up_grad/pallas_call | solution.py:196
  105.0 0.7 add_convert_fusion.4
  (28 shorter events, 1.8 us)
Async XLA Ops:
  1.7 14.2 %collective-permute-start.3 = (bf16[2,64,1536]{2,1,0:T(8,128)(2,1)S(1)}, bf16[2,64,1536]{2,1,0:T(8,128)(2,1)S(1)}, u32[]{:S(2)}, u32[]{:S(2)}) collective-permute-start(bf16[2,64,1536]{2,1,0:T(8,128)(2,1)S(1)} %pad_maximum_fusion.tokens_ref.refs_0_.refs_8_), channel_id=1, source_target_pairs={{0,1},{1,2},{2,3},{3,0},{4,5},{5,6},{6,7},{7,4},{8,9},{9,10},{10,1... | collective-permute-start | bytes 1179656 | tf_op jit(solution)/shard_map/ppermute | solution.py:218
  9.3 9.1 %collective-permute-start = (bf16[2,64,1536]{2,1,0:T(8,128)(2,1)S(1)}, bf16[2,64,1536]{2,1,0:T(8,128)(2,1)S(1)}, u32[]{:S(2)}, u32[]{:S(2)}) collective-permute-start(bf16[2,64,1536]{2,1,0:T(8,128)(2,1)S(1)} %get-tuple-element.10), channel_id=1, source_target_pairs={{0,4},{4,0},{8,12},{12,8},{1,5},{5,1},{9,13},{13,9},{2,6},{6,2},{1... | collective-permute-start | bytes 1179656 | tf_op jit(solution)/shard_map/ppermute | solution.py:215
  18.3 16.1 %collective-permute-start.12 = (bf16[2,64,1536]{2,1,0:T(8,128)(2,1)S(1)}, bf16[2,64,1536]{2,1,0:T(8,128)(2,1)S(1)}, u32[]{:S(2)}, u32[]{:S(2)}) collective-permute-start(bf16[2,64,1536]{2,1,0:T(8,128)(2,1)S(1)} %give.5), channel_id=1, source_target_pairs={{0,4},{4,0},{8,12},{12,8},{1,5},{5,1},{9,13},{13,9},{2,6},{6,2},{1... | collective-permute-start | bytes 1179656 | tf_op jit(solution)/shard_map/ppermute | solution.py:215
  18.4 13.3 %collective-permute-start.4 = (bf16[2,64,1536]{2,1,0:T(8,128)(2,1)S(1)}, bf16[2,64,1536]{2,1,0:T(8,128)(2,1)S(1)}, u32[]{:S(2)}, u32[]{:S(2)}) collective-permute-start(bf16[2,64,1536]{2,1,0:T(8,128)(2,1)S(1)} %collective-permute-done.3.tokens_ref.refs_1_.refs_9_), channel_id=1, source_target_pairs={{0,1},{1,2},{2,3},{3,0},{4,5},{5,6},{6,7},{7,4},{8,9},{9,10},{10,1... | collective-permute-start | bytes 1179656 | tf_op jit(solution)/shard_map/ppermute | solution.py:218
  18.5 43.8 %collective-permute-start.1 = (bf16[2,64,1536]{2,1,0:T(8,128)(2,1)S(1)}, bf16[2,64,1536]{2,1,0:T(8,128)(2,1)S(1)}, u32[]{:S(2)}, u32[]{:S(2)}) collective-permute-start(bf16[2,64,1536]{2,1,0:T(8,128)(2,1)S(1)} %add_convert_fusion.3.own_ref), channel_id=1, source_target_pairs={{0,8},{4,12},{8,0},{12,4},{1,9},{5,13},{9,1},{13,5},{2,10},{6,14},... | collective-permute-start | bytes 1179656 | tf_op jit(solution)/shard_map/ppermute | solution.py:238
  34.0 15.8 %collective-permute-start.9 = (bf16[2,64,1536]{2,1,0:T(8,128)(2,1)S(1)}, bf16[2,64,1536]{2,1,0:T(8,128)(2,1)S(1)}, u32[]{:S(2)}, u32[]{:S(2)}) collective-permute-start(bf16[2,64,1536]{2,1,0:T(8,128)(2,1)S(1)} %give.4), channel_id=1, source_target_pairs={{0,4},{4,0},{8,12},{12,8},{1,5},{5,1},{9,13},{13,9},{2,6},{6,2},{1... | collective-permute-start | bytes 1179656 | tf_op jit(solution)/shard_map/ppermute | solution.py:215
  34.1 13.3 %collective-permute-start.5 = (bf16[2,64,1536]{2,1,0:T(8,128)(2,1)S(1)}, bf16[2,64,1536]{2,1,0:T(8,128)(2,1)S(1)}, u32[]{:S(2)}, u32[]{:S(2)}) collective-permute-start(bf16[2,64,1536]{2,1,0:T(8,128)(2,1)S(1)} %collective-permute-done.4.tokens_ref.refs_2_.refs_10_), channel_id=1, source_target_pairs={{0,1},{1,2},{2,3},{3,0},{4,5},{5,6},{6,7},{7,4},{8,9},{9,10},{10,1... | collective-permute-start | bytes 1179656 | tf_op jit(solution)/shard_map/ppermute | solution.py:218
  34.5 17.1 %collective-permute-start.13 = (bf16[2,64,1536]{2,1,0:T(8,128)(2,1)S(1)}, bf16[2,64,1536]{2,1,0:T(8,128)(2,1)S(1)}, u32[]{:S(2)}, u32[]{:S(2)}) collective-permute-start(bf16[2,64,1536]{2,1,0:T(8,128)(2,1)S(1)} %add_convert_fusion.own_ref), channel_id=1, source_target_pairs={{0,8},{4,12},{8,0},{12,4},{1,9},{5,13},{9,1},{13,5},{2,10},{6,14},... | collective-permute-start | bytes 1179656 | tf_op jit(solution)/shard_map/ppermute | solution.py:238
  49.8 4.7 %collective-permute-start.6 = (bf16[2,64,1536]{2,1,0:T(8,128)(2,1)S(1)}, bf16[2,64,1536]{2,1,0:T(8,128)(2,1)S(1)}, u32[]{:S(2)}, u32[]{:S(2)}) collective-permute-start(bf16[2,64,1536]{2,1,0:T(8,128)(2,1)S(1)} %give.3), channel_id=1, source_target_pairs={{0,4},{4,0},{8,12},{12,8},{1,5},{5,1},{9,13},{13,9},{2,6},{6,2},{1... | collective-permute-start | bytes 1179656 | tf_op jit(solution)/shard_map/ppermute | solution.py:215
  50.0 12.0 %collective-permute-start.10 = (bf16[2,64,1536]{2,1,0:T(8,128)(2,1)S(1)}, bf16[2,64,1536]{2,1,0:T(8,128)(2,1)S(1)}, u32[]{:S(2)}, u32[]{:S(2)}) collective-permute-start(bf16[2,64,1536]{2,1,0:T(8,128)(2,1)S(1)} %add_convert_fusion.1.own_ref), channel_id=1, source_target_pairs={{0,8},{4,12},{8,0},{12,4},{1,9},{5,13},{9,1},{13,5},{2,10},{6,14},... | collective-permute-start | bytes 1179656 | tf_op jit(solution)/shard_map/ppermute | solution.py:238
  51.8 10.8 %collective-permute-start.14 = (bf16[2,64,1536]{2,1,0:T(8,128)(2,1)S(1)}, bf16[2,64,1536]{2,1,0:T(8,128)(2,1)S(1)}, u32[]{:S(2)}, u32[]{:S(2)}) collective-permute-start(bf16[2,64,1536]{2,1,0:T(8,128)(2,1)S(1)} %gelu.7.mine_ref.refs_6_.refs_2_), channel_id=1, source_target_pairs={{0,4},{4,0},{8,12},{12,8},{1,5},{5,1},{9,13},{13,9},{2,6},{6,2},{1... | collective-permute-start | bytes 1179656 | tf_op jit(solution)/shard_map/ppermute | solution.py:215
  54.5 15.4 %collective-permute-start.7 = (bf16[2,64,1536]{2,1,0:T(8,128)(2,1)S(1)}, bf16[2,64,1536]{2,1,0:T(8,128)(2,1)S(1)}, u32[]{:S(2)}, u32[]{:S(2)}) collective-permute-start(bf16[2,64,1536]{2,1,0:T(8,128)(2,1)S(1)} %add_convert_fusion.2.own_ref), channel_id=1, source_target_pairs={{0,8},{4,12},{8,0},{12,4},{1,9},{5,13},{9,1},{13,5},{2,10},{6,14},... | collective-permute-start | bytes 1179656 | tf_op jit(solution)/shard_map/ppermute | solution.py:238
  62.2 12.5 %collective-permute-start.11 = (bf16[2,64,1536]{2,1,0:T(8,128)(2,1)S(1)}, bf16[2,64,1536]{2,1,0:T(8,128)(2,1)S(1)}, u32[]{:S(2)}, u32[]{:S(2)}) collective-permute-start(bf16[2,64,1536]{2,1,0:T(8,128)(2,1)S(1)} %gelu.6.mine_ref.refs_8_.refs_4_), channel_id=1, source_target_pairs={{0,4},{4,0},{8,12},{12,8},{1,5},{5,1},{9,13},{13,9},{2,6},{6,2},{1... | collective-permute-start | bytes 1179656 | tf_op jit(solution)/shard_map/ppermute | solution.py:215
  65.5 9.1 %collective-permute-start.15 = (bf16[64,1536]{1,0:T(8,128)(2,1)S(1)}, bf16[64,1536]{1,0:T(8,128)(2,1)S(1)}, u32[]{:S(2)}, u32[]{:S(2)}) collective-permute-start(bf16[64,1536]{1,0:T(8,128)(2,1)S(1)} %input_product.5), channel_id=1, source_target_pairs={{0,1},{1,2},{2,3},{3,0},{4,5},{5,6},{6,7},{7,4},{8,9},{9,10},{10,1... | collective-permute-start | bytes 589832 | tf_op jit(solution)/shard_map/ppermute | solution.py:218
  65.6 12.1 %collective-permute-start.2 = (bf16[2,64,1536]{2,1,0:T(8,128)(2,1)S(1)}, bf16[2,64,1536]{2,1,0:T(8,128)(2,1)S(1)}, u32[]{:S(2)}, u32[]{:S(2)}) collective-permute-start(bf16[2,64,1536]{2,1,0:T(8,128)(2,1)S(1)} %gelu.4.mine_ref.refs_4_.refs_0_), channel_id=1, source_target_pairs={{0,4},{4,0},{8,12},{12,8},{1,5},{5,1},{9,13},{13,9},{2,6},{6,2},{1... | collective-permute-start | bytes 1179656 | tf_op jit(solution)/shard_map/ppermute | solution.py:215
  70.2 15.7 %collective-permute-start.8 = (bf16[2,64,1536]{2,1,0:T(8,128)(2,1)S(1)}, bf16[2,64,1536]{2,1,0:T(8,128)(2,1)S(1)}, u32[]{:S(2)}, u32[]{:S(2)}) collective-permute-start(bf16[2,64,1536]{2,1,0:T(8,128)(2,1)S(1)} %gelu.5.mine_ref.refs_10_.refs_6_), channel_id=1, source_target_pairs={{0,4},{4,0},{8,12},{12,8},{1,5},{5,1},{9,13},{13,9},{2,6},{6,2},{1... | collective-permute-start | bytes 1179656 | tf_op jit(solution)/shard_map/ppermute | solution.py:215
  77.6 8.4 %collective-permute-start.16 = (bf16[64,1536]{1,0:T(8,128)(2,1)S(1)}, bf16[64,1536]{1,0:T(8,128)(2,1)S(1)}, u32[]{:S(2)}, u32[]{:S(2)}) collective-permute-start(bf16[64,1536]{1,0:T(8,128)(2,1)S(1)} %input_product.6), channel_id=1, source_target_pairs={{0,1},{1,2},{2,3},{3,0},{4,5},{5,6},{6,7},{7,4},{8,9},{9,10},{10,1... | collective-permute-start | bytes 589832 | tf_op jit(solution)/shard_map/ppermute | solution.py:218
  88.9 16.1 %collective-permute-start.17 = (bf16[64,1536]{1,0:T(8,128)(2,1)S(1)}, bf16[64,1536]{1,0:T(8,128)(2,1)S(1)}, u32[]{:S(2)}, u32[]{:S(2)}) collective-permute-start(bf16[64,1536]{1,0:T(8,128)(2,1)S(1)} %input_product.7), channel_id=1, source_target_pairs={{0,1},{1,2},{2,3},{3,0},{4,5},{5,6},{6,7},{7,4},{8,9},{9,10},{10,1... | collective-permute-start | bytes 589832 | tf_op jit(solution)/shard_map/ppermute | solution.py:218

commit v3 on v0

v3 whole, which is shorter than its diff:
```python
import functools

import jax
import jax.numpy as jnp
from jax import lax
from jax.experimental import pallas as pl
from jax.experimental.pallas import tpu as pltpu
from jax.sharding import PartitionSpec as P

F32, BF16 = jnp.float32, jnp.bfloat16
MIB = 1 << 20
WEIGHT = 262144
VMEM = pltpu.VMEM
NN = (((1,), (0,)), ((), ()))
NT = (((1,), (1,)), ((), ()))
TN = (((0,), (0,)), ((), ()))


def dot(a, b, dims):
    return lax.dot_general(a, b, dims, preferred_element_type=F32)


def in_vmem(x):
    return pltpu.with_memory_space_constraint(x, VMEM)


def in_hbm(x):
    return pltpu.with_memory_space_constraint(x, pltpu.HBM)


def tile_of(extent, largest=512):
    return next(t for t in (768, 512, 384, 256, 128) if t <= largest and extent % t == 0)


class Ordered:
    def __init__(self):
        self.last = None

    def __call__(self, body, args, outs, name, micros, limit=16, spaces=None, out_spaces=None, scratch=(), aliases=None):
        args = list(args)
        spaces = spaces or [None] * len(args)
        specs = [
            pl.BlockSpec(memory_space=pltpu.SMEM if a.dtype == jnp.int32 else space or VMEM) for a, space in zip(args, spaces)
        ]
        count = len(args)
        if self.last is not None:
            args.append(self.last)
            specs.append(pl.BlockSpec(memory_space=pl.ANY))
        extra = len(args) - count

        def kernel(*refs):
            body(*refs[:count], *refs[count + extra :])

        result = pl.pallas_call(
            kernel,
            out_shape=outs,
            in_specs=specs,
            out_specs=[pl.BlockSpec(memory_space=s) for s in out_spaces or [VMEM] * len(outs)],
            scratch_shapes=scratch,
            input_output_aliases=aliases or {},
            compiler_params=pltpu.CompilerParams(vmem_limit_bytes=limit * MIB),
            cost_estimate=pl.CostEstimate(flops=0, bytes_accessed=int(micros * WEIGHT), transcendentals=0),
            name=name,
        )(*args)
        self.last = result[-1]
        return result


def first_product(ordered, core, other, tokens, weight, units_dim, name):
    rows, features = tokens.shape
    half = weight.shape[units_dim] // 2
    tile = tile_of(half, 256)
    pieces = half // tile

    def body(core_ref, tokens_ref, weight_hbm, weight_ref, out_ref, sems):
        side = 1 - core_ref[0] if other else core_ref[0]
        copies = []
        for i in range(pieces):
            units = pl.ds(pl.multiple_of(side * half + i * tile, tile), tile)
            part = pl.ds(i * tile, tile)
            at = (lambda u: (slice(None), u)) if units_dim else (lambda u: (u, slice(None)))
            copies.append(pltpu.make_async_copy(weight_hbm.at[at(units)], weight_ref.at[at(part)], sems.at[i]))
        for copy in copies:
            copy.start()
        for i, copy in enumerate(copies):
            part = slice(i * tile, (i + 1) * tile)
            copy.wait()
            if units_dim:
                out_ref[:, part] = dot(tokens_ref[...], weight_ref[:, part], NN).astype(BF16)
            else:
                out_ref[:, part] = dot(tokens_ref[...], weight_ref[part, :], NT).astype(BF16)

    shape = (features, half) if units_dim else (half, features)
    return ordered(
        body,
        (core, tokens, in_hbm(weight)),
        [VMEM(shape, BF16), jax.ShapeDtypeStruct((rows, half), BF16)],
        name,
        2.5,
        spaces=[None, None, pl.ANY],
        scratch=[pltpu.SemaphoreType.DMA((pieces,))],
    )


def product(ordered, tokens, grads, up_half, down_half, name):
    rows, features = tokens.shape
    half = up_half.shape[1]
    tile = tile_of(half)

    def body(tokens_ref, grads_ref, up_ref, down_ref, out_ref):
        for start in range(0, half, tile):
            part = slice(start, start + tile)
            out_ref[0, :, part] = dot(tokens_ref[...], up_ref[:, part], NN).astype(BF16)
            out_ref[1, :, part] = dot(grads_ref[...], down_ref[part, :], NT).astype(BF16)

    args = (tokens, grads, in_vmem(up_half), in_vmem(down_half))
    return ordered(body, args, [jax.ShapeDtypeStruct((2, rows, half), BF16)], name, 2.4)[0]


def input_product(ordered, chunks, up_mine, up_other, so_far):
    rows = chunks[0][0][0].shape[1]
    features = up_mine.shape[0]
    tile = tile_of(features)
    flat = [a for chunk in chunks for pair in chunk for a in pair]
    widths = [pair[0].shape[2] for pair in chunks[0]]

    def body(up_mine_ref, up_other_ref, *refs):
        act_refs, out_refs = refs[: len(flat)], refs[len(refs) - len(chunks) :]
        for start in range(0, features, tile):
            part = slice(start, start + tile)
            share = None
            low = 0
            for i, width in enumerate(widths):
                for side, up_ref in enumerate((up_mine_ref, up_other_ref)):
                    acts = [act_refs[(c * len(widths) + i) * 2 + side][0] for c in range(len(chunks))]
                    acts = acts[0] if len(acts) == 1 else jnp.concatenate(acts, axis=0)
                    term = dot(acts, up_ref[part, low : low + width], NT)
                    share = term if share is None else share + term
                low += width
            for c, out_ref in enumerate(out_refs):
                own = share[c * rows : (c + 1) * rows]
                if so_far is not None and c == len(chunks) - 1:
                    own = own + refs[len(flat)][:, part].astype(F32)
                out_ref[:, part] = own.astype(BF16)

    args = (in_vmem(up_mine), in_vmem(up_other), *flat) + (() if so_far is None else (so_far,))
    return ordered(body, args, [jax.ShapeDtypeStruct((rows, features), BF16)] * len(chunks), "input_product", 3.0)


def gelu(ordered, own, peer):
    rows, units = own[0].shape[-2:]
    args = (own, peer) if not isinstance(own, tuple) else (*own, *peer)

    def body(*refs):
        parts = [r[i] for r in refs[:-1] for i in (0, 1)] if len(refs) == 3 else [r[...] for r in refs[:-1]]
        own_hidden, own_grad, peer_hidden, peer_grad = [p.astype(F32) for p in parts]
        hidden, grad_hidden = own_hidden + peer_hidden, own_grad + peer_grad
        cdf = 0.5 * (1.0 + lax.erf(hidden * 0.7071067811865476))
        pdf = jnp.exp(-0.5 * hidden * hidden) * 0.3989422804014327
        refs[-1][0] = (grad_hidden * (cdf + hidden * pdf)).astype(BF16)
        refs[-1][1] = (hidden * cdf).astype(BF16)

    return ordered(body, args, [jax.ShapeDtypeStruct((2, rows, units), BF16)], "gelu", 0.3)[0]


def collect(ordered, tokens, grads):
    count = len(tokens)
    rows, features = tokens[0].shape
    tile = tile_of(features, 256)

    def body(*refs):
        turned_ref, grads_ref, scratch = refs[2 * count :]
        for i in range(count):
            scratch[i * rows : (i + 1) * rows, :] = refs[i][...]
            grads_ref[i * rows : (i + 1) * rows, :] = refs[count + i][...]
        for start in range(0, features, tile):
            turned_ref[start : start + tile, :] = scratch[:, start : start + tile].T

    outs = [VMEM((features, rows * count), BF16), VMEM((rows * count, features), BF16)]
    return ordered(body, (*tokens, *grads), outs, "collect", 1.5, scratch=[VMEM((rows * count, features), BF16)])


def weight_grads(ordered, core, blocks, turned, all_grads, half, scale, before, name):
    features, tokens = turned.shape
    rows = tokens // len(blocks[0][2])
    width = min(a.shape[2] for a, _ in blocks[0][2])
    up_tile, down_tile = tile_of(features), tile_of(width, 256)
    up_steps, down_steps = features // up_tile, width // down_tile
    slots = 3
    flat = [a for block in blocks for a, _ in block[2]]

    def body(core_ref, turned_ref, grads_ref, *refs):
        up_hbm, down_hbm, done_ref, act_g, act_v, up_stage, down_stage, sems = refs[-8:]
        done_ref[...] = jnp.zeros_like(done_ref)
        busy = {}

        def send(kind, index, value, stage, target):
            slot = index % slots
            if (kind, slot) in busy:
                busy[kind, slot].wait()
            stage[slot] = value * scale
            copy = pltpu.make_async_copy(stage.at[slot], target, sems.at[kind, slot])
            copy.start()
            busy[kind, slot] = copy

        for b, (other, first, acts) in enumerate(blocks):
            side = 1 - core_ref[0] if other else core_ref[0]
            base = side * half + first
            for i, (_, column) in enumerate(acts):
                ref = refs[b * len(acts) + i]
                act_g[i * rows : (i + 1) * rows, :] = ref[0, :, column : column + width]
                act_v[i * rows : (i + 1) * rows, :] = ref[1, :, column : column + width]
            for step in range(max(up_steps, down_steps)):
                if step < up_steps:
                    part = slice(step * up_tile, (step + 1) * up_tile)
                    value = dot(turned_ref[part, :], act_g[...], NN)
                    target = up_hbm.at[pl.ds(step * up_tile, up_tile), pl.ds(pl.multiple_of(base, 128), width)]
                    send(0, b * up_steps + step, value, up_stage, target)
                if step < down_steps:
                    part = slice(step * down_tile, (step + 1) * down_tile)
                    value = dot(act_v[:, part], grads_ref[...], TN)
                    target = down_hbm.at[pl.ds(pl.multiple_of(base + step * down_tile, 128), down_tile), :]
                    send(1, b * down_steps + step, value, down_stage, target)
        for copy in busy.values():
            copy.wait()

    args = [core, turned, all_grads, *flat]
    spaces = [None] * len(args)
    aliases = {}
    if before is not None:
        aliases = {len(args): 0, len(args) + 1: 1}
        args += [in_hbm(a) for a in before]
        spaces += [pl.ANY, pl.ANY]
    return ordered(
        body,
        args,
        [pltpu.HBM((features, 2 * half), F32), pltpu.HBM((2 * half, features), F32), jax.ShapeDtypeStruct((8, 128), F32)],
        name,
        4.0 * len(blocks),
        spaces=spaces,
        out_spaces=[pl.ANY, pl.ANY, VMEM],
        scratch=[
            VMEM((tokens, width), BF16),
            VMEM((tokens, width), BF16),
            VMEM((slots, up_tile, width), F32),
            VMEM((slots, down_tile, features), F32),
            pltpu.SemaphoreType.DMA((2, slots)),
        ],
        aliases=aliases,
    )


def per_device(wide, narrow, inputs, up_weight, down_weight, out_grad):
    rows = inputs.shape[0]
    half = up_weight.shape[1] // 2
    chips = wide // 2
    core = (lax.axis_index("wide") & 1).astype(jnp.int32).reshape(1)
    ordered = Ordered()

    def swap_cores(x):
        return lax.ppermute(x, "wide", [(i, i ^ 1) for i in range(wide)])

    def pass_on(x):
        return lax.ppermute(x, "narrow", [(i, (i + 1) % narrow) for i in range(narrow)])

    def across_chips(partial):
        hop = 1
        while True:
            peer = lax.ppermute(partial, "wide", [(i, i ^ (2 * hop)) for i in range(wide)])
            hop *= 2
            if hop >= chips:
                return partial, peer
            partial = (partial.astype(F32) + peer.astype(F32)).astype(BF16)

    def added(keep, got):
        return (keep.astype(F32) + got.astype(F32)).astype(BF16)

    tokens, grads = [inputs], [out_grad]
    for _ in range(1, narrow):
        tokens.append(pass_on(tokens[-1]))
        grads.append(pass_on(grads[-1]))

    slices = 2 if half % 256 == 0 else 1
    width = half // slices

    def send_acts(own_peer):
        mine = gelu(ordered, *own_peer)
        return mine, swap_cores(mine)

    up_other, give_h = first_product(ordered, core, True, inputs, up_weight, 1, "give_hidden")
    got_h = swap_cores(give_h)
    up_mine, keep_h = first_product(ordered, core, False, inputs, up_weight, 1, "keep_hidden")
    own_h, peer_h = across_chips(added(keep_h, got_h))
    down_other, give_g = first_product(ordered, core, True, out_grad, down_weight, 0, "give_grad")
    got_g = swap_cores(give_g)
    down_mine, keep_g = first_product(ordered, core, False, out_grad, down_weight, 0, "keep_grad")
    own_g, peer_g = across_chips(added(keep_g, got_g))
    pending = ((own_h, own_g), (peer_h, peer_g))

    acts = []
    kept = share = None
    for step in range(1, narrow):
        give = product(ordered, tokens[step], grads[step], up_other, down_other, "give")
        got = swap_cores(give)
        if step > 1:
            acts.append([send_acts(pending)])
        keep = product(ordered, tokens[step], grads[step], up_mine, down_mine, "keep")
        if step < narrow - 1:
            sent = across_chips(added(keep, got))
        else:
            sent = [
                across_chips(added(keep[:, :, i * width : (i + 1) * width], got[:, :, i * width : (i + 1) * width]))
                for i in range(slices)
            ]
        if step == 1:
            acts.append([send_acts(pending)])
        elif step == 2:
            pass
        pending = sent
        if step == 3:
            kept, share = input_product(ordered, acts[:2], up_mine, up_other, None)
            share = pass_on(share)
        elif step > 3:
            share = pass_on(input_product(ordered, [acts[step - 2]], up_mine, up_other, share)[0])
    turned, all_grads = collect(ordered, tokens, grads)
    if narrow > 2:
        share = pass_on(input_product(ordered, [acts[narrow - 2]], up_mine, up_other, share)[0])

    scale = (rows * narrow) ** -0.5

    def block(other, i):
        earlier = [(chunk[0][other], i * width) for chunk in acts]
        return (other, i * width, earlier + [(last[i][other], 0)])

    last = []
    result = None
    for i in range(slices):
        last.append(send_acts(pending[i]))
        blocks = [block(0, i)] if i == 0 else [block(1, i - 1), block(0, i)]
        result = weight_grads(ordered, core, blocks, turned, all_grads, half, scale, result, "weight_grads")[:2]
    share = pass_on(input_product(ordered, [last], up_mine, up_other, share)[0])
    result = weight_grads(ordered, core, [block(1, slices - 1)], turned, all_grads, half, scale, result, "weight_grads")[:2]
    return (kept.astype(F32) + share.astype(F32)).astype(BF16), *result


def solution(mesh):
    placed = (
        P(("groups", "narrow"), "wide"),
        P("wide", "narrow"),
        P("narrow", "wide"),
        P(("groups", "narrow"), "wide"),
    )
    return jax.shard_map(
        functools.partial(per_device, mesh.shape["wide"], mesh.shape["narrow"]),
        mesh=mesh,
        in_specs=placed,
        out_specs=(
            P(("groups", "narrow"), "wide"),
            P(("groups", "wide"), "narrow"),
            P(("groups", "narrow"), "wide"),
        ),
        check_vma=False,
    )
```

time: 175 us -> 102 us (0.58)
  Pallas kernels: 0 us -> 58.5 us
  matrix products: 44 us -> 0 us
  blocking collectives: 39.4 us -> 0 us
  waiting for transfers between devices: 56.4 us -> 22.8 us
  local copies, waits for them, and re-layouts: 18.7 us -> 0.01 us
  starting transfers between devices: 0.2 us -> 18.3 us
  between operations: 13.8 us -> 0.99 us
    pallas_call x0 -> x22, Pallas kernels: none -> 58.5 us  [__call__(): pl.pallas_call(kernel, out_shape=outs, in_specs=specs, out_specs=[pl.Bloc...]
    dot_general x5 -> x0, matrix products: 44 us -> none  [the longest x1 10.9 us: per_device(): lax.dot_general(row_block, down_weight, (((1,), (1,)), ((), ())), preferr...]
    all_gather x2 -> x0, blocking collectives: 39.4 us -> none  [the longest x1 21.6 us: per_device(): lax.all_gather(out_grad, 'narrow', axis=0, tiled=True)]
    reduce_scatter x3 -> x0, waiting for transfers between devices: 36.6 us -> none  [the longest x1 31.5 us: per_device(): lax.psum_scatter(jnp.dot(row_block, up_weight, preferred_element_type=jnp...]
    ppermute x0 -> x25, waiting for transfers between devices: none -> 22.8 us  [the longest x9 17.9 us: pass_on(): lax.ppermute(x, 'narrow', [(i, (i + 1) % narrow) for i in range(narrow)])]
    all_gather x2 -> x0, waiting for transfers between devices: 19.2 us -> none  [the longest x1 19.2 us: per_device(): lax.all_gather(grad_rows, 'wide', axis=0, tiled=True)]
    unnamed x5 -> x2, local copies, waits for them, and re-layouts: 18.7 us -> 0.01 us
    ppermute x0 -> x25, starting transfers between devices: none -> 18.3 us  [the longest x9 8.19 us: pass_on(): lax.ppermute(x, 'narrow', [(i, (i + 1) % narrow) for i in range(narrow)])]
  transfers between devices with their start and end apart: 5 -> 25, of which waited for: 4 -> 8; matrix products, arithmetic and copies ran while one was open for 30% -> 0% of each run, Pallas kernels for 0% -> 50%
where the time goes in v3:
time: 102 us
  Pallas kernels  58.5 us (57%)
  waiting for transfers between devices  22.8 us (22%)
  starting transfers between devices  18.3 us (18%)
  other arithmetic  1.11 us (1%)
    pallas_call x22, Pallas kernels, __call__(): pl.pallas_call(kernel, out_shape=outs, in_specs=specs, out_specs=[pl.Bloc...  58.5 us
    ppermute x9, waiting for transfers between devices, pass_on(): lax.ppermute(x, 'narrow', [(i, (i + 1) % narrow) for i in range(narrow)])  17.9 us
    ppermute x9, starting transfers between devices, pass_on(): lax.ppermute(x, 'narrow', [(i, (i + 1) % narrow) for i in range(narrow)])  8.19 us
    ppermute x6, starting transfers between devices, across_chips(): lax.ppermute(partial, 'wide', [(i, i ^ 2 * hop) for i in range(wide)])  7.41 us
    ppermute x6, waiting for transfers between devices, across_chips(): lax.ppermute(partial, 'wide', [(i, i ^ 2 * hop) for i in range(wide)])  4.9 us
    ppermute x10, starting transfers between devices, swap_cores(): return lax.ppermute(x, 'wide', [(i, i ^ 1) for i in range(wide)])  2.69 us
  transfers between devices with their start and end apart: 25, of which 8 were waited for; matrix products, arithmetic and copies ran while one was open for 0% of the time, Pallas kernels for 50%

profile of v3, /device:TPU:0, one launch (start us, length us, event | category | flops | bytes accessed | tf_op | source)
XLA Modules:
  0.0 101.7 jit_solution(4367704136620210516)
XLA Ops:
  0.6 4.3 %give_hidden.1 = (bf16[1536,1536]{1,0:T(8,128)(2,1)S(1)}, bf16[64,1536]{1,0:T(8,128)(2,1)S(1)}) custom-call(s32[1]{0:T(128)} %bitcast.refs_0_, bf16[64,1536]{1,0:T(8,128)(2,1)} %refs_0_.1, bf16[1536,3072]{1,0:T(8,128)(2,1)} %refs_2_.5), custom_call_target="tpu_custom_call" | custom-call | bytes 655360 | tf_op jit(solution)/shard_map/give_hidden/pallas_call | solution.py:54
  5.4 2.6 %collective-permute-start.4 = (bf16[64,1536]{1,0:T(8,128)(2,1)}, bf16[64,1536]{1,0:T(8,128)(2,1)S(1)}, u32[]{:S(2)}, u32[]{:S(2)}) collective-permute-start(bf16[64,1536]{1,0:T(8,128)(2,1)} %refs_0_.1), channel_id=1, source_target_pairs={{0,1},{1,2},{2,3},{3,0},{4,5},{5,6},{6,7},{7,4},{8,9},{9,10},{10,1... | collective-permute-start | bytes 589832 | tf_op jit(solution)/shard_map/ppermute | solution.py:264
  8.1 1.6 %collective-permute-start.5 = (bf16[64,1536]{1,0:T(8,128)(2,1)}, bf16[64,1536]{1,0:T(8,128)(2,1)S(1)}, u32[]{:S(2)}, u32[]{:S(2)}) collective-permute-start(bf16[64,1536]{1,0:T(8,128)(2,1)} %refs_4_.1), channel_id=1, source_target_pairs={{0,1},{1,2},{2,3},{3,0},{4,5},{5,6},{6,7},{7,4},{8,9},{9,10},{10,1... | collective-permute-start | bytes 589832 | tf_op jit(solution)/shard_map/ppermute | solution.py:264
  9.6 4.2 %keep_hidden.1 = (bf16[1536,1536]{1,0:T(8,128)(2,1)S(1)}, bf16[64,1536]{1,0:T(8,128)(2,1)S(1)}) custom-call(s32[1]{0:T(128)} %bitcast.refs_0_, bf16[64,1536]{1,0:T(8,128)(2,1)} %refs_0_.1, bf16[1536,3072]{1,0:T(8,128)(2,1)} %refs_2_.5, bf16[64,1536]{1,0:T(8,128)(2,1)S(1)} %get-tuple-element.23.refs_3_), custom_call_target="tpu_custom_call" | custom-call | bytes 655360 | tf_op jit(solution)/shard_map/keep_hidden/pallas_call | solution.py:54
  13.9 4.4 %give_grad.1 = (bf16[1536,1536]{1,0:T(8,128)(2,1)S(1)}, bf16[64,1536]{1,0:T(8,128)(2,1)S(1)}) custom-call(s32[1]{0:T(128)} %bitcast.refs_0_, bf16[64,1536]{1,0:T(8,128)(2,1)S(1)} %copy-done, bf16[3072,1536]{1,0:T(8,128)(2,1)} %refs_2_.7, bf16[64,1536]{1,0:T(8,128)(2,1)S(1)} %get-tuple-element.26.refs_3_), custom_call_target="tpu_custom_call" | custom-call | bytes 655360 | tf_op jit(solution)/shard_map/give_grad/pallas_call | solution.py:54
  18.4 4.4 %keep_grad.1 = (bf16[1536,1536]{1,0:T(8,128)(2,1)S(1)}, bf16[64,1536]{1,0:T(8,128)(2,1)S(1)}) custom-call(s32[1]{0:T(128)} %bitcast.refs_0_, bf16[64,1536]{1,0:T(8,128)(2,1)S(1)} %copy-done, bf16[3072,1536]{1,0:T(8,128)(2,1)} %refs_2_.7, bf16[64,1536]{1,0:T(8,128)(2,1)S(1)} %get-tuple-element.27.refs_3_), custom_call_target="tpu_custom_call" | custom-call | bytes 655360 | tf_op jit(solution)/shard_map/keep_grad/pallas_call | solution.py:54
  22.9 1.6 %collective-permute-start.2 = (bf16[64,1536]{1,0:T(8,128)(2,1)S(1)}, bf16[64,1536]{1,0:T(8,128)(2,1)S(1)}, u32[]{:S(2)}, u32[]{:S(2)}) collective-permute-start(bf16[64,1536]{1,0:T(8,128)(2,1)S(1)} %add_convert_fusion.6.refs_0_), channel_id=1, source_target_pairs={{0,8},{4,12},{8,0},{12,4},{1,9},{5,13},{9,1},{13,5},{2,10},{6,14},... | collective-permute-start | bytes 589832 | tf_op jit(solution)/shard_map/ppermute | solution.py:269
  24.4 2.4 %give.3.refs_4_ = bf16[2,64,1536]{2,1,0:T(8,128)(2,1)S(1)} custom-call(bf16[64,1536]{1,0:T(8,128)(2,1)S(1)} %collective-permute-done.4.refs_0_.refs_1_, bf16[64,1536]{1,0:T(8,128)(2,1)S(1)} %collective-permute-done.5.refs_1_.refs_5_, bf16[1536,1536]{1,0:T(8,128)(2,1)S(1)} %get-tuple-element.25.refs_2_.refs_1_, ...), custom_call_target="tpu_custom_call" | custom-call | bytes 629145 | tf_op jit(solution)/shard_map/give/pallas_call | solution.py:54
  27.7 1.6 %collective-permute-start.9 = (bf16[64,1536]{1,0:T(8,128)(2,1)S(1)}, bf16[64,1536]{1,0:T(8,128)(2,1)S(1)}, u32[]{:S(2)}, u32[]{:S(2)}) collective-permute-start(bf16[64,1536]{1,0:T(8,128)(2,1)S(1)} %collective-permute-done.4.refs_0_.refs_1_), channel_id=1, source_target_pairs={{0,1},{1,2},{2,3},{3,0},{4,5},{5,6},{6,7},{7,4},{8,9},{9,10},{10,1... | collective-permute-start | bytes 589832 | tf_op jit(solution)/shard_map/ppermute | solution.py:264
  29.4 2.3 %keep.3.refs_4_ = bf16[2,64,1536]{2,1,0:T(8,128)(2,1)S(1)} custom-call(bf16[64,1536]{1,0:T(8,128)(2,1)S(1)} %collective-permute-done.4.refs_0_.refs_1_, bf16[64,1536]{1,0:T(8,128)(2,1)S(1)} %collective-permute-done.5.refs_1_.refs_5_, bf16[1536,1536]{1,0:T(8,128)(2,1)S(1)} %get-tuple-element.24.refs_2_.refs_0_, ...), custom_call_target="tpu_custom_call" | custom-call | bytes 629145 | tf_op jit(solution)/shard_map/keep/pallas_call | solution.py:54
  31.8 2.6 %collective-permute-done.3.refs_3_ = bf16[64,1536]{1,0:T(8,128)(2,1)S(1)} collective-permute-done((bf16[64,1536]{1,0:T(8,128)(2,1)S(1)}, bf16[64,1536]{1,0:T(8,128)(2,1)S(1)}, u32[]{:S(2)}, u32[]{:S(2)}) %collective-permute-start.3) | collective-permute-done | bytes 196640 | tf_op jit(solution)/shard_map/ppermute | solution.py:269
  34.8 1.6 %collective-permute-start.8 = (bf16[2,64,1536]{2,1,0:T(8,128)(2,1)S(1)}, bf16[2,64,1536]{2,1,0:T(8,128)(2,1)S(1)}, u32[]{:S(2)}, u32[]{:S(2)}) collective-permute-start(bf16[2,64,1536]{2,1,0:T(8,128)(2,1)S(1)} %add_convert_fusion.1.refs_0_), channel_id=1, source_target_pairs={{0,8},{4,12},{8,0},{12,4},{1,9},{5,13},{9,1},{13,5},{2,10},{6,14},... | collective-permute-start | bytes 1179656 | tf_op jit(solution)/shard_map/ppermute | solution.py:269
  37.3 3.3 %collective-permute-done.10.refs_1_.refs_6_ = bf16[64,1536]{1,0:T(8,128)(2,1)S(1)} collective-permute-done((bf16[64,1536]{1,0:T(8,128)(2,1)S(1)}, bf16[64,1536]{1,0:T(8,128)(2,1)S(1)}, u32[]{:S(2)}, u32[]{:S(2)}) %collective-permute-start.10) | collective-permute-done | bytes 196640 | tf_op jit(solution)/shard_map/ppermute | solution.py:264
  40.6 2.3 %give.4.refs_2_ = bf16[2,64,1536]{2,1,0:T(8,128)(2,1)S(1)} custom-call(bf16[64,1536]{1,0:T(8,128)(2,1)S(1)} %collective-permute-done.9.refs_0_.refs_2_, bf16[64,1536]{1,0:T(8,128)(2,1)S(1)} %collective-permute-done.10.refs_1_.refs_6_, bf16[1536,1536]{1,0:T(8,128)(2,1)S(1)} %get-tuple-element.25.refs_2_.refs_1_, ...), custom_call_target="tpu_custom_call" | custom-call | bytes 629145 | tf_op jit(solution)/shard_map/give/pallas_call | solution.py:54
  43.3 2.2 %collective-permute-done.8.refs_1_ = bf16[2,64,1536]{2,1,0:T(8,128)(2,1)S(1)} collective-permute-done((bf16[2,64,1536]{2,1,0:T(8,128)(2,1)S(1)}, bf16[2,64,1536]{2,1,0:T(8,128)(2,1)S(1)}, u32[]{:S(2)}, u32[]{:S(2)}) %collective-permute-start.8) | collective-permute-done | bytes 393248 | tf_op jit(solution)/shard_map/ppermute | solution.py:269
  45.8 2.3 %keep.4.refs_4_ = bf16[2,64,1536]{2,1,0:T(8,128)(2,1)S(1)} custom-call(bf16[64,1536]{1,0:T(8,128)(2,1)S(1)} %collective-permute-done.9.refs_0_.refs_2_, bf16[64,1536]{1,0:T(8,128)(2,1)S(1)} %collective-permute-done.10.refs_1_.refs_6_, bf16[1536,1536]{1,0:T(8,128)(2,1)S(1)} %get-tuple-element.24.refs_2_.refs_0_, ...), custom_call_target="tpu_custom_call" | custom-call | bytes 629145 | tf_op jit(solution)/shard_map/keep/pallas_call | solution.py:54
  48.3 1.6 %collective-permute-start.15 = (bf16[2,64,1536]{2,1,0:T(8,128)(2,1)S(1)}, bf16[2,64,1536]{2,1,0:T(8,128)(2,1)S(1)}, u32[]{:S(2)}, u32[]{:S(2)}) collective-permute-start(bf16[2,64,1536]{2,1,0:T(8,128)(2,1)S(1)} %add_convert_fusion.refs_0_), channel_id=1, source_target_pairs={{0,8},{4,12},{8,0},{12,4},{1,9},{5,13},{9,1},{13,5},{2,10},{6,14},... | collective-permute-start | bytes 1179656 | tf_op jit(solution)/shard_map/ppermute | solution.py:269
  50.4 2.1 %collective-permute-done.12.refs_0_.refs_3_ = bf16[64,1536]{1,0:T(8,128)(2,1)S(1)} collective-permute-done((bf16[64,1536]{1,0:T(8,128)(2,1)S(1)}, bf16[64,1536]{1,0:T(8,128)(2,1)S(1)}, u32[]{:S(2)}, u32[]{:S(2)}) %collective-permute-start.12) | collective-permute-done | bytes 196640 | tf_op jit(solution)/shard_map/ppermute | solution.py:264
  52.6 3.8 %collective-permute-done.13.refs_1_.refs_7_ = bf16[64,1536]{1,0:T(8,128)(2,1)S(1)} collective-permute-done((bf16[64,1536]{1,0:T(8,128)(2,1)S(1)}, bf16[64,1536]{1,0:T(8,128)(2,1)S(1)}, u32[]{:S(2)}, u32[]{:S(2)}) %collective-permute-start.13) | collective-permute-done | bytes 196640 | tf_op jit(solution)/shard_map/ppermute | solution.py:264
  56.3 2.3 %give.5.refs_2_ = bf16[2,64,1536]{2,1,0:T(8,128)(2,1)S(1)} custom-call(bf16[64,1536]{1,0:T(8,128)(2,1)S(1)} %collective-permute-done.12.refs_0_.refs_3_, bf16[64,1536]{1,0:T(8,128)(2,1)S(1)} %collective-permute-done.13.refs_1_.refs_7_, bf16[1536,1536]{1,0:T(8,128)(2,1)S(1)} %get-tuple-element.25.refs_2_.refs_1_, ...), custom_call_target="tpu_custom_call" | custom-call | bytes 629145 | tf_op jit(solution)/shard_map/give/pallas_call | solution.py:54
  59.6 2.3 %keep.5.refs_6_ = bf16[2,64,1536]{2,1,0:T(8,128)(2,1)S(1)} custom-call(bf16[64,1536]{1,0:T(8,128)(2,1)S(1)} %collective-permute-done.12.refs_0_.refs_3_, bf16[64,1536]{1,0:T(8,128)(2,1)S(1)} %collective-permute-done.13.refs_1_.refs_7_, bf16[1536,1536]{1,0:T(8,128)(2,1)S(1)} %get-tuple-element.24.refs_2_.refs_0_, ...), custom_call_target="tpu_custom_call" | custom-call | bytes 629145 | tf_op jit(solution)/shard_map/keep/pallas_call | solution.py:54
  61.9 3.1 %input_product.3 = (bf16[64,1536]{1,0:T(8,128)(2,1)S(1)}, bf16[64,1536]{1,0:T(8,128)(2,1)S(1)}) custom-call(bf16[1536,1536]{1,0:T(8,128)(2,1)S(1)} %get-tuple-element.24.refs_2_.refs_0_, bf16[1536,1536]{1,0:T(8,128)(2,1)S(1)} %get-tuple-element.25.refs_2_.refs_1_, bf16[2,64,1536]{2,1,0:T(8,128)(2,1)S(1)} %gelu.5.refs_4_.refs_2_.refs_3_.refs_7_, ...), custom_call_target="tpu_custom_call" | custom-call | bytes 786432 | tf_op jit(solution)/shard_map/input_product/pallas_call | solution.py:54
  65.7 1.7 %collective-permute-start.17 = (bf16[2,64,768]{2,1,0:T(8,128)(2,1)S(1)}, bf16[2,64,768]{2,1,0:T(8,128)(2,1)S(1)}, u32[]{:S(2)}, u32[]{:S(2)}) collective-permute-start(bf16[2,64,768]{2,1,0:T(8,128)(2,1)S(1)} %get-tuple-element.44.refs_0_), channel_id=1, source_target_pairs={{0,8},{4,12},{8,0},{12,4},{1,9},{5,13},{9,1},{13,5},{2,10},{6,14},... | collective-permute-start | bytes 589832 | tf_op jit(solution)/shard_map/ppermute | solution.py:269
  67.8 1.2 %collect.1 = (bf16[1536,256]{1,0:T(8,128)(2,1)S(1)}, bf16[256,1536]{1,0:T(8,128)(2,1)S(1)}) custom-call(bf16[64,1536]{1,0:T(8,128)(2,1)} %refs_0_.1, bf16[64,1536]{1,0:T(8,128)(2,1)S(1)} %collective-permute-done.4.refs_0_.refs_1_, bf16[64,1536]{1,0:T(8,128)(2,1)S(1)} %collective-permute-done.9.refs_0_.refs_2_, ...), custom_call_target="tpu_custom_call" | custom-call | bytes 393216 | tf_op jit(solution)/shard_map/collect/pallas_call | solution.py:54
  69.0 4.7 %collective-permute-done.19.refs_4_ = bf16[64,1536]{1,0:T(8,128)(2,1)S(1)} collective-permute-done((bf16[64,1536]{1,0:T(8,128)(2,1)S(1)}, bf16[64,1536]{1,0:T(8,128)(2,1)S(1)}, u32[]{:S(2)}, u32[]{:S(2)}) %collective-permute-start.19) | collective-permute-done | bytes 196640 | tf_op jit(solution)/shard_map/ppermute | solution.py:264
  73.8 2.9 %input_product.4.refs_2_ = bf16[64,1536]{1,0:T(8,128)(2,1)S(1)} custom-call(bf16[1536,1536]{1,0:T(8,128)(2,1)S(1)} %get-tuple-element.24.refs_2_.refs_0_, bf16[1536,1536]{1,0:T(8,128)(2,1)S(1)} %get-tuple-element.25.refs_2_.refs_1_, bf16[2,64,1536]{2,1,0:T(8,128)(2,1)S(1)} %gelu.7.refs_4_.refs_2_.refs_5_.refs_9_, ...), custom_call_target="tpu_custom_call" | custom-call | bytes 786432 | tf_op jit(solution)/shard_map/input_product/pallas_call | solution.py:54
  77.2 4.1 %weight_grads.3 = (f32[1536,3072]{1,0:T(8,128)}, f32[3072,1536]{1,0:T(8,128)}, f32[8,128]{1,0:T(8,128)S(1)}) custom-call(s32[1]{0:T(128)} %bitcast.refs_0_, bf16[1536,256]{1,0:T(8,128)(2,1)S(1)} %get-tuple-element.34.refs_1_, bf16[256,1536]{1,0:T(8,128)(2,1)S(1)} %get-tuple-element.33.refs_5_.refs_2_, ...), custom_call_target="tpu_custom_call" | custom-call | bytes 1048576 | tf_op jit(solution)/shard_map/weight_grads/pallas_call | solution.py:54
  82.1 7.0 %weight_grads.4 = (f32[1536,3072]{1,0:T(8,128)}, f32[3072,1536]{1,0:T(8,128)}, f32[8,128]{1,0:T(8,128)S(1)}) custom-call(s32[1]{0:T(128)} %bitcast.refs_0_, bf16[1536,256]{1,0:T(8,128)(2,1)S(1)} %get-tuple-element.34.refs_1_, bf16[256,1536]{1,0:T(8,128)(2,1)S(1)} %get-tuple-element.33.refs_5_.refs_2_, ...), custom_call_target="tpu_custom_call", output_to_operand_aliasing={{0}: (11, {}), {1}: (12, {})} | custom-call | bytes 2097152 | tf_op jit(solution)/shard_map/weight_grads/pallas_call | solution.py:54
  89.1 2.9 %input_product.5.refs_9_ = bf16[64,1536]{1,0:T(8,128)(2,1)S(1)} custom-call(bf16[1536,1536]{1,0:T(8,128)(2,1)S(1)} %get-tuple-element.24.refs_2_.refs_0_, bf16[1536,1536]{1,0:T(8,128)(2,1)S(1)} %get-tuple-element.25.refs_2_.refs_1_, bf16[2,64,768]{2,1,0:T(8,128)(2,1)S(1)} %gelu.8.refs_6_.refs_7_.refs_2_, ...), custom_call_target="tpu_custom_call" | custom-call | bytes 786432 | tf_op jit(solution)/shard_map/input_product/pallas_call | solution.py:54
  92.0 1.2 %collective-permute-start.24 = (bf16[64,1536]{1,0:T(8,128)(2,1)S(1)}, bf16[64,1536]{1,0:T(8,128)(2,1)S(1)}, u32[]{:S(2)}, u32[]{:S(2)}) collective-permute-start(bf16[64,1536]{1,0:T(8,128)(2,1)S(1)} %input_product.5.refs_9_), channel_id=1, source_target_pairs={{0,1},{1,2},{2,3},{3,0},{4,5},{5,6},{6,7},{7,4},{8,9},{9,10},{10,1... | collective-permute-start | bytes 589832 | tf_op jit(solution)/shard_map/ppermute | solution.py:264
  93.2 4.7 %weight_grads.5 = (f32[1536,3072]{1,0:T(8,128)}, f32[3072,1536]{1,0:T(8,128)}, f32[8,128]{1,0:T(8,128)}) custom-call(s32[1]{0:T(128)} %bitcast.refs_0_, bf16[1536,256]{1,0:T(8,128)(2,1)S(1)} %get-tuple-element.34.refs_1_, bf16[256,1536]{1,0:T(8,128)(2,1)S(1)} %get-tuple-element.33.refs_5_.refs_2_, ...), custom_call_target="tpu_custom_call", output_to_operand_aliasing={{0}: (7, {}), {1}: (8, {})} | custom-call | bytes 1048576 | tf_op jit(solution)/shard_map/weight_grads/pallas_call | solution.py:54
  97.9 3.0 %collective-permute-done.24 = bf16[64,1536]{1,0:T(8,128)(2,1)S(1)} collective-permute-done((bf16[64,1536]{1,0:T(8,128)(2,1)S(1)}, bf16[64,1536]{1,0:T(8,128)(2,1)S(1)}, u32[]{:S(2)}, u32[]{:S(2)}) %collective-permute-start.24) | collective-permute-done | bytes 196640 | tf_op jit(solution)/shard_map/ppermute | solution.py:264
  (48 shorter events, 8.0 us)
Async XLA Ops:
  0.6 13.2 %copy-start = (bf16[64,1536]{1,0:T(8,128)(2,1)S(1)}, bf16[64,1536]{1,0:T(8,128)(2,1)}, u32[]{:S(2)}) copy-start(bf16[64,1536]{1,0:T(8,128)(2,1)} %refs_4_.1) | copy-start | bytes 589828
  4.9 17.9 %collective-permute-start = (bf16[64,1536]{1,0:T(8,128)(2,1)S(1)}, bf16[64,1536]{1,0:T(8,128)(2,1)S(1)}, u32[]{:S(2)}, u32[]{:S(2)}) collective-permute-start(bf16[64,1536]{1,0:T(8,128)(2,1)S(1)} %get-tuple-element.23.refs_3_), channel_id=1, source_target_pairs={{0,4},{4,0},{8,12},{12,8},{1,5},{5,1},{9,13},{13,9},{2,6},{6,2},{1... | collective-permute-start | bytes 589832 | tf_op jit(solution)/shard_map/ppermute | solution.py:261
  5.4 19.0 %collective-permute-start.4 = (bf16[64,1536]{1,0:T(8,128)(2,1)}, bf16[64,1536]{1,0:T(8,128)(2,1)S(1)}, u32[]{:S(2)}, u32[]{:S(2)}) collective-permute-start(bf16[64,1536]{1,0:T(8,128)(2,1)} %refs_0_.1), channel_id=1, source_target_pairs={{0,1},{1,2},{2,3},{3,0},{4,5},{5,6},{6,7},{7,4},{8,9},{9,10},{10,1... | collective-permute-start | bytes 589832 | tf_op jit(solution)/shard_map/ppermute | solution.py:264
  8.1 16.4 %collective-permute-start.5 = (bf16[64,1536]{1,0:T(8,128)(2,1)}, bf16[64,1536]{1,0:T(8,128)(2,1)S(1)}, u32[]{:S(2)}, u32[]{:S(2)}) collective-permute-start(bf16[64,1536]{1,0:T(8,128)(2,1)} %refs_4_.1), channel_id=1, source_target_pairs={{0,1},{1,2},{2,3},{3,0},{4,5},{5,6},{6,7},{7,4},{8,9},{9,10},{10,1... | collective-permute-start | bytes 589832 | tf_op jit(solution)/shard_map/ppermute | solution.py:264
  18.3 8.8 %collective-permute-start.1 = (bf16[64,1536]{1,0:T(8,128)(2,1)S(1)}, bf16[64,1536]{1,0:T(8,128)(2,1)S(1)}, u32[]{:S(2)}, u32[]{:S(2)}) collective-permute-start(bf16[64,1536]{1,0:T(8,128)(2,1)S(1)} %get-tuple-element.27.refs_3_), channel_id=1, source_target_pairs={{0,4},{4,0},{8,12},{12,8},{1,5},{5,1},{9,13},{13,9},{2,6},{6,2},{1... | collective-permute-start | bytes 589832 | tf_op jit(solution)/shard_map/ppermute | solution.py:261
  22.9 8.9 %collective-permute-start.2 = (bf16[64,1536]{1,0:T(8,128)(2,1)S(1)}, bf16[64,1536]{1,0:T(8,128)(2,1)S(1)}, u32[]{:S(2)}, u32[]{:S(2)}) collective-permute-start(bf16[64,1536]{1,0:T(8,128)(2,1)S(1)} %add_convert_fusion.6.refs_0_), channel_id=1, source_target_pairs={{0,8},{4,12},{8,0},{12,4},{1,9},{5,13},{9,1},{13,5},{2,10},{6,14},... | collective-permute-start | bytes 589832 | tf_op jit(solution)/shard_map/ppermute | solution.py:269
  26.8 7.9 %collective-permute-start.7 = (bf16[2,64,1536]{2,1,0:T(8,128)(2,1)S(1)}, bf16[2,64,1536]{2,1,0:T(8,128)(2,1)S(1)}, u32[]{:S(2)}, u32[]{:S(2)}) collective-permute-start(bf16[2,64,1536]{2,1,0:T(8,128)(2,1)S(1)} %give.3.refs_4_), channel_id=1, source_target_pairs={{0,4},{4,0},{8,12},{12,8},{1,5},{5,1},{9,13},{13,9},{2,6},{6,2},{1... | collective-permute-start | bytes 1179656 | tf_op jit(solution)/shard_map/ppermute | solution.py:261
  27.1 7.3 %collective-permute-start.3 = (bf16[64,1536]{1,0:T(8,128)(2,1)S(1)}, bf16[64,1536]{1,0:T(8,128)(2,1)S(1)}, u32[]{:S(2)}, u32[]{:S(2)}) collective-permute-start(bf16[64,1536]{1,0:T(8,128)(2,1)S(1)} %add_convert_fusion.5.refs_1_), channel_id=1, source_target_pairs={{0,8},{4,12},{8,0},{12,4},{1,9},{5,13},{9,1},{13,5},{2,10},{6,14},... | collective-permute-start | bytes 589832 | tf_op jit(solution)/shard_map/ppermute | solution.py:269
  27.7 9.6 %collective-permute-start.9 = (bf16[64,1536]{1,0:T(8,128)(2,1)S(1)}, bf16[64,1536]{1,0:T(8,128)(2,1)S(1)}, u32[]{:S(2)}, u32[]{:S(2)}) collective-permute-start(bf16[64,1536]{1,0:T(8,128)(2,1)S(1)} %collective-permute-done.4.refs_0_.refs_1_), channel_id=1, source_target_pairs={{0,1},{1,2},{2,3},{3,0},{4,5},{5,6},{6,7},{7,4},{8,9},{9,10},{10,1... | collective-permute-start | bytes 589832 | tf_op jit(solution)/shard_map/ppermute | solution.py:264
  29.3 11.3 %collective-permute-start.10 = (bf16[64,1536]{1,0:T(8,128)(2,1)S(1)}, bf16[64,1536]{1,0:T(8,128)(2,1)S(1)}, u32[]{:S(2)}, u32[]{:S(2)}) collective-permute-start(bf16[64,1536]{1,0:T(8,128)(2,1)S(1)} %collective-permute-done.5.refs_1_.refs_5_), channel_id=1, source_target_pairs={{0,1},{1,2},{2,3},{3,0},{4,5},{5,6},{6,7},{7,4},{8,9},{9,10},{10,1... | collective-permute-start | bytes 589832 | tf_op jit(solution)/shard_map/ppermute | solution.py:264
  34.8 10.7 %collective-permute-start.8 = (bf16[2,64,1536]{2,1,0:T(8,128)(2,1)S(1)}, bf16[2,64,1536]{2,1,0:T(8,128)(2,1)S(1)}, u32[]{:S(2)}, u32[]{:S(2)}) collective-permute-start(bf16[2,64,1536]{2,1,0:T(8,128)(2,1)S(1)} %add_convert_fusion.1.refs_0_), channel_id=1, source_target_pairs={{0,8},{4,12},{8,0},{12,4},{1,9},{5,13},{9,1},{13,5},{2,10},{6,14},... | collective-permute-start | bytes 1179656 | tf_op jit(solution)/shard_map/ppermute | solution.py:269
  42.9 5.3 %collective-permute-start.14 = (bf16[2,64,1536]{2,1,0:T(8,128)(2,1)S(1)}, bf16[2,64,1536]{2,1,0:T(8,128)(2,1)S(1)}, u32[]{:S(2)}, u32[]{:S(2)}) collective-permute-start(bf16[2,64,1536]{2,1,0:T(8,128)(2,1)S(1)} %give.4.refs_2_), channel_id=1, source_target_pairs={{0,4},{4,0},{8,12},{12,8},{1,5},{5,1},{9,13},{13,9},{2,6},{6,2},{1... | collective-permute-start | bytes 1179656 | tf_op jit(solution)/shard_map/ppermute | solution.py:261
  43.0 9.6 %collective-permute-start.12 = (bf16[64,1536]{1,0:T(8,128)(2,1)S(1)}, bf16[64,1536]{1,0:T(8,128)(2,1)S(1)}, u32[]{:S(2)}, u32[]{:S(2)}) collective-permute-start(bf16[64,1536]{1,0:T(8,128)(2,1)S(1)} %collective-permute-done.9.refs_0_.refs_2_), channel_id=1, source_target_pairs={{0,1},{1,2},{2,3},{3,0},{4,5},{5,6},{6,7},{7,4},{8,9},{9,10},{10,1... | collective-permute-start | bytes 589832 | tf_op jit(solution)/shard_map/ppermute | solution.py:264
  43.1 13.2 %collective-permute-start.13 = (bf16[64,1536]{1,0:T(8,128)(2,1)S(1)}, bf16[64,1536]{1,0:T(8,128)(2,1)S(1)}, u32[]{:S(2)}, u32[]{:S(2)}) collective-permute-start(bf16[64,1536]{1,0:T(8,128)(2,1)S(1)} %collective-permute-done.10.refs_1_.refs_6_), channel_id=1, source_target_pairs={{0,1},{1,2},{2,3},{3,0},{4,5},{5,6},{6,7},{7,4},{8,9},{9,10},{10,1... | collective-permute-start | bytes 589832 | tf_op jit(solution)/shard_map/ppermute | solution.py:264
  48.3 10.5 %collective-permute-start.15 = (bf16[2,64,1536]{2,1,0:T(8,128)(2,1)S(1)}, bf16[2,64,1536]{2,1,0:T(8,128)(2,1)S(1)}, u32[]{:S(2)}, u32[]{:S(2)}) collective-permute-start(bf16[2,64,1536]{2,1,0:T(8,128)(2,1)S(1)} %add_convert_fusion.refs_0_), channel_id=1, source_target_pairs={{0,8},{4,12},{8,0},{12,4},{1,9},{5,13},{9,1},{13,5},{2,10},{6,14},... | collective-permute-start | bytes 1179656 | tf_op jit(solution)/shard_map/ppermute | solution.py:269
  49.9 12.0 %collective-permute-start.6 = (bf16[2,64,1536]{2,1,0:T(8,128)(2,1)S(1)}, bf16[2,64,1536]{2,1,0:T(8,128)(2,1)S(1)}, u32[]{:S(2)}, u32[]{:S(2)}) collective-permute-start(bf16[2,64,1536]{2,1,0:T(8,128)(2,1)S(1)} %gelu.5.refs_4_.refs_2_.refs_3_.refs_7_), channel_id=1, source_target_pairs={{0,4},{4,0},{8,12},{12,8},{1,5},{5,1},{9,13},{13,9},{2,6},{6,2},{1... | collective-permute-start | bytes 1179656 | tf_op jit(solution)/shard_map/ppermute | solution.py:261
  49.9 12.0 %collective-permute-start.11 = (bf16[2,64,1536]{2,1,0:T(8,128)(2,1)S(1)}, bf16[2,64,1536]{2,1,0:T(8,128)(2,1)S(1)}, u32[]{:S(2)}, u32[]{:S(2)}) collective-permute-start(bf16[2,64,1536]{2,1,0:T(8,128)(2,1)S(1)} %gelu.6.refs_4_.refs_8_), channel_id=1, source_target_pairs={{0,4},{4,0},{8,12},{12,8},{1,5},{5,1},{9,13},{13,9},{2,6},{6,2},{1... | collective-permute-start | bytes 1179656 | tf_op jit(solution)/shard_map/ppermute | solution.py:261
  58.7 6.9 %collective-permute-start.16 = (bf16[2,64,1536]{2,1,0:T(8,128)(2,1)S(1)}, bf16[2,64,1536]{2,1,0:T(8,128)(2,1)S(1)}, u32[]{:S(2)}, u32[]{:S(2)}) collective-permute-start(bf16[2,64,1536]{2,1,0:T(8,128)(2,1)S(1)} %give.5.refs_2_), channel_id=1, source_target_pairs={{0,4},{4,0},{8,12},{12,8},{1,5},{5,1},{9,13},{13,9},{2,6},{6,2},{1... | collective-permute-start | bytes 1179656 | tf_op jit(solution)/shard_map/ppermute | solution.py:261
  59.0 14.7 %collective-permute-start.18 = (bf16[2,64,1536]{2,1,0:T(8,128)(2,1)S(1)}, bf16[2,64,1536]{2,1,0:T(8,128)(2,1)S(1)}, u32[]{:S(2)}, u32[]{:S(2)}) collective-permute-start(bf16[2,64,1536]{2,1,0:T(8,128)(2,1)S(1)} %gelu.7.refs_4_.refs_2_.refs_5_.refs_9_), channel_id=1, source_target_pairs={{0,4},{4,0},{8,12},{12,8},{1,5},{5,1},{9,13},{13,9},{2,6},{6,2},{1... | collective-permute-start | bytes 1179656 | tf_op jit(solution)/shard_map/ppermute | solution.py:261
  65.1 8.7 %collective-permute-start.19 = (bf16[64,1536]{1,0:T(8,128)(2,1)S(1)}, bf16[64,1536]{1,0:T(8,128)(2,1)S(1)}, u32[]{:S(2)}, u32[]{:S(2)}) collective-permute-start(bf16[64,1536]{1,0:T(8,128)(2,1)S(1)} %get-tuple-element.32.refs_8_), channel_id=1, source_target_pairs={{0,1},{1,2},{2,3},{3,0},{4,5},{5,6},{6,7},{7,4},{8,9},{9,10},{10,1... | collective-permute-start | bytes 589832 | tf_op jit(solution)/shard_map/ppermute | solution.py:264
  65.7 11.3 %collective-permute-start.17 = (bf16[2,64,768]{2,1,0:T(8,128)(2,1)S(1)}, bf16[2,64,768]{2,1,0:T(8,128)(2,1)S(1)}, u32[]{:S(2)}, u32[]{:S(2)}) collective-permute-start(bf16[2,64,768]{2,1,0:T(8,128)(2,1)S(1)} %get-tuple-element.44.refs_0_), channel_id=1, source_target_pairs={{0,8},{4,12},{8,0},{12,4},{1,9},{5,13},{9,1},{13,5},{2,10},{6,14},... | collective-permute-start | bytes 589832 | tf_op jit(solution)/shard_map/ppermute | solution.py:269
  67.4 14.0 %collective-permute-start.21 = (bf16[2,64,768]{2,1,0:T(8,128)(2,1)S(1)}, bf16[2,64,768]{2,1,0:T(8,128)(2,1)S(1)}, u32[]{:S(2)}, u32[]{:S(2)}) collective-permute-start(bf16[2,64,768]{2,1,0:T(8,128)(2,1)S(1)} %get-tuple-element.43.refs_0_), channel_id=1, source_target_pairs={{0,8},{4,12},{8,0},{12,4},{1,9},{5,13},{9,1},{13,5},{2,10},{6,14},... | collective-permute-start | bytes 589832 | tf_op jit(solution)/shard_map/ppermute | solution.py:269
  76.7 12.4 %collective-permute-start.23 = (bf16[64,1536]{1,0:T(8,128)(2,1)S(1)}, bf16[64,1536]{1,0:T(8,128)(2,1)S(1)}, u32[]{:S(2)}, u32[]{:S(2)}) collective-permute-start(bf16[64,1536]{1,0:T(8,128)(2,1)S(1)} %input_product.4.refs_2_), channel_id=1, source_target_pairs={{0,1},{1,2},{2,3},{3,0},{4,5},{5,6},{6,7},{7,4},{8,9},{9,10},{10,1... | collective-permute-start | bytes 589832 | tf_op jit(solution)/shard_map/ppermute | solution.py:264
  77.1 4.9 %collective-permute-start.20 = (bf16[2,64,768]{2,1,0:T(8,128)(2,1)S(1)}, bf16[2,64,768]{2,1,0:T(8,128)(2,1)S(1)}, u32[]{:S(2)}, u32[]{:S(2)}) collective-permute-start(bf16[2,64,768]{2,1,0:T(8,128)(2,1)S(1)} %gelu.8.refs_6_.refs_7_.refs_2_), channel_id=1, source_target_pairs={{0,4},{4,0},{8,12},{12,8},{1,5},{5,1},{9,13},{13,9},{2,6},{6,2},{1... | collective-permute-start | bytes 589832 | tf_op jit(solution)/shard_map/ppermute | solution.py:261
  81.5 7.6 %collective-permute-start.22 = (bf16[2,64,768]{2,1,0:T(8,128)(2,1)S(1)}, bf16[2,64,768]{2,1,0:T(8,128)(2,1)S(1)}, u32[]{:S(2)}, u32[]{:S(2)}) collective-permute-start(bf16[2,64,768]{2,1,0:T(8,128)(2,1)S(1)} %gelu.9.refs_10_.refs_13_.refs_4_), channel_id=1, source_target_pairs={{0,4},{4,0},{8,12},{12,8},{1,5},{5,1},{9,13},{13,9},{2,6},{6,2},{1... | collective-permute-start | bytes 589832 | tf_op jit(solution)/shard_map/ppermute | solution.py:261
  92.0 8.9 %collective-permute-start.24 = (bf16[64,1536]{1,0:T(8,128)(2,1)S(1)}, bf16[64,1536]{1,0:T(8,128)(2,1)S(1)}, u32[]{:S(2)}, u32[]{:S(2)}) collective-permute-start(bf16[64,1536]{1,0:T(8,128)(2,1)S(1)} %input_product.5.refs_9_), channel_id=1, source_target_pairs={{0,1},{1,2},{2,3},{3,0},{4,5},{5,6},{6,7},{7,4},{8,9},{9,10},{10,1... | collective-permute-start | bytes 589832 | tf_op jit(solution)/shard_map/ppermute | solution.py:264

commit v4 on v3

v4 whole, which is shorter than its diff:
```python
import functools

import jax
import jax.numpy as jnp
from jax import lax
from jax.experimental import pallas as pl
from jax.experimental.pallas import tpu as pltpu
from jax.sharding import PartitionSpec as P

F32, BF16 = jnp.float32, jnp.bfloat16
MIB = 1 << 20
VMEM = pltpu.VMEM
NN = (((1,), (0,)), ((), ()))
NT = (((1,), (1,)), ((), ()))
TN = (((0,), (0,)), ((), ()))


def dot(a, b, dims):
    return lax.dot_general(a, b, dims, preferred_element_type=F32)


def in_vmem(x):
    return pltpu.with_memory_space_constraint(x, VMEM)


def in_hbm(x):
    return pltpu.with_memory_space_constraint(x, pltpu.HBM)


def tile_of(extent, largest=512):
    return next(t for t in (768, 512, 384, 256, 128) if t <= largest and extent % t == 0)


class Ordered:
    def __init__(self):
        self.last = None

    def __call__(self, body, args, outs, name, micros, limit=16, spaces=None, out_spaces=None, scratch=(), aliases=None, after=()):
        args = list(args)
        spaces = spaces or [None] * len(args)
        specs = [
            pl.BlockSpec(memory_space=pltpu.SMEM if a.dtype == jnp.int32 else space or VMEM) for a, space in zip(args, spaces)
        ]
        count = len(args)
        for waited in (*after, *([] if self.last is None else [self.last])):
            args.append(waited)
            specs.append(pl.BlockSpec(memory_space=pl.ANY))
        extra = len(args) - count

        def kernel(*refs):
            body(*refs[:count], *refs[count + extra :])

        result = pl.pallas_call(
            kernel,
            out_shape=outs,
            in_specs=specs,
            out_specs=[pl.BlockSpec(memory_space=s) for s in out_spaces or [VMEM] * len(outs)],
            scratch_shapes=scratch,
            input_output_aliases=aliases or {},
            compiler_params=pltpu.CompilerParams(vmem_limit_bytes=limit * MIB),
            cost_estimate=pl.CostEstimate(flops=int(micros * 4e9), bytes_accessed=0, transcendentals=0),
            name=name,
        )(*args)
        self.last = result[-1]
        return result


def first_product(ordered, core, other, chunk, weight, units_dim, name, after=()):
    _, rows, features = chunk.shape
    half = weight.shape[units_dim] // 2
    tile = tile_of(half)
    pieces = half // tile

    def body(core_ref, chunk_ref, weight_hbm, weight_ref, out_ref, sems):
        side = 1 - core_ref[0] if other else core_ref[0]
        copies = []
        for i in range(pieces):
            units = pl.ds(pl.multiple_of(side * half + i * tile, tile), tile)
            part = pl.ds(i * tile, tile)
            at = (lambda u: (slice(None), u)) if units_dim else (lambda u: (u, slice(None)))
            copies.append(pltpu.make_async_copy(weight_hbm.at[at(units)], weight_ref.at[at(part)], sems.at[i]))
        for copy in copies:
            copy.start()
        for i, copy in enumerate(copies):
            part = slice(i * tile, (i + 1) * tile)
            copy.wait()
            if units_dim:
                out_ref[:, part] = dot(chunk_ref[0], weight_ref[:, part], NN).astype(BF16)
            else:
                out_ref[:, part] = dot(chunk_ref[1], weight_ref[part, :], NT).astype(BF16)

    shape = (features, half) if units_dim else (half, features)
    return ordered(
        body,
        (core, chunk, in_hbm(weight)),
        [VMEM(shape, BF16), jax.ShapeDtypeStruct((rows, half), BF16)],
        name,
        2.5,
        spaces=[None, None, pl.ANY],
        scratch=[pltpu.SemaphoreType.DMA((pieces,))],
        after=after,
    )


def product(ordered, chunk, up_half, down_half, name, after=()):
    _, rows, features = chunk.shape
    half = up_half.shape[1]
    tile = tile_of(half)

    def body(chunk_ref, up_ref, down_ref, out_ref):
        for start in range(0, half, tile):
            part = slice(start, start + tile)
            out_ref[0, :, part] = dot(chunk_ref[0], up_ref[:, part], NN).astype(BF16)
            out_ref[1, :, part] = dot(chunk_ref[1], down_ref[part, :], NT).astype(BF16)

    args = (chunk, in_vmem(up_half), in_vmem(down_half))
    return ordered(body, args, [jax.ShapeDtypeStruct((2, rows, half), BF16)], name, 2.4, after=after)[0]


def input_product(ordered, mine, other, up_mine, up_other, chunks, micros, returned=()):
    rows = mine[0].shape[1] // chunks
    features = up_mine.shape[0]
    tile = tile_of(features)
    widths = [a.shape[2] for a in mine]

    def body(up_mine_ref, up_other_ref, *refs):
        returned_refs, out_refs = refs[2 * len(widths) :][: len(returned)], refs[-chunks:]
        if returned:
            total = returned_refs[0][...].astype(F32)
            for ref in returned_refs[1:]:
                total = total + ref[...].astype(F32)
            refs[-chunks - 1][...] = total
        for start in range(0, features, tile):
            part = slice(start, start + tile)
            share = None
            for side, up_ref in enumerate((up_mine_ref, up_other_ref)):
                low = 0
                for i, width in enumerate(widths):
                    term = dot(refs[side * len(widths) + i][0], up_ref[part, low : low + width], NT)
                    share = term if share is None else share + term
                    low += width
            for c, out_ref in enumerate(out_refs):
                out_ref[:, part] = share[c * rows : (c + 1) * rows].astype(BF16)

    args = (in_vmem(up_mine), in_vmem(up_other), *mine, *other, *returned)
    outs = [jax.ShapeDtypeStruct((rows, features), F32)] if returned else []
    return ordered(body, args, outs + [jax.ShapeDtypeStruct((rows, features), BF16)] * chunks, "input_product", micros)


def gelu(ordered, sums, after=()):
    flat, places = [], []
    for own, peer in sums:
        where = []
        for side in (own, peer):
            where += [(len(flat) + i, None) for i in (0, 1)] if len(side) == 2 else [(len(flat), i) for i in (0, 1)]
            flat += side
        places.append(where)
    rows, units = flat[0].shape[-2:]

    def body(*refs):
        out_ref = refs[-1]
        for chunk, where in enumerate(places):
            at = slice(chunk * rows, (chunk + 1) * rows)
            own_h, own_g, peer_h, peer_g = [(refs[r][...] if i is None else refs[r][i]).astype(F32) for r, i in where]
            hidden, grad_hidden = own_h + peer_h, own_g + peer_g
            cdf = 0.5 * (1.0 + lax.erf(hidden * 0.7071067811865476))
            pdf = jnp.exp(-0.5 * hidden * hidden) * 0.3989422804014327
            out_ref[0, at] = (grad_hidden * (cdf + hidden * pdf)).astype(BF16)
            out_ref[1, at] = (hidden * cdf).astype(BF16)

    out = jax.ShapeDtypeStruct((2, rows * len(sums), units), BF16)
    return ordered(body, flat, [out], "gelu", 0.1, after=after)[0]


def collect(ordered, chunks, after):
    count = len(chunks)
    _, rows, features = chunks[0].shape
    tile = tile_of(features, 256)

    def body(*refs):
        turned_ref, grads_ref, scratch = refs[count:]
        for i in range(count):
            scratch[i * rows : (i + 1) * rows, :] = refs[i][0]
            grads_ref[i * rows : (i + 1) * rows, :] = refs[i][1]
        for start in range(0, features, tile):
            turned_ref[start : start + tile, :] = scratch[:, start : start + tile].T

    outs = [VMEM((features, rows * count), BF16), VMEM((rows * count, features), BF16)]
    return ordered(body, chunks, outs, "collect", 0.1, scratch=[VMEM((rows * count, features), BF16)], after=after)


def weight_grads(ordered, core, blocks, turned, all_grads, half, scale, before, name):
    features, tokens = turned.shape
    width = min(a.shape[2] for a, _ in blocks[0][2])
    up_tile, down_tile = tile_of(features), tile_of(width, 256)
    up_steps, down_steps = features // up_tile, width // down_tile
    slots = 3
    flat = [a for block in blocks for a, _ in block[2]]

    def body(core_ref, turned_ref, grads_ref, *refs):
        up_hbm, down_hbm, done_ref, act_g, act_v, up_stage, down_stage, sems = refs[-8:]
        done_ref[...] = jnp.zeros_like(done_ref)
        busy = {}

        def send(kind, index, value, stage, target):
            slot = index % slots
            if (kind, slot) in busy:
                busy[kind, slot].wait()
            stage[slot] = value * scale
            copy = pltpu.make_async_copy(stage.at[slot], target, sems.at[kind, slot])
            copy.start()
            busy[kind, slot] = copy

        for b, (other, first, acts) in enumerate(blocks):
            side = 1 - core_ref[0] if other else core_ref[0]
            base = side * half + first
            row = 0
            for i, (array, column) in enumerate(acts):
                ref, rows = refs[b * len(acts) + i], slice(row, row + array.shape[1])
                act_g[rows, :] = ref[0, :, column : column + width]
                act_v[rows, :] = ref[1, :, column : column + width]
                row += array.shape[1]
            for step in range(max(up_steps, down_steps)):
                if step < up_steps:
                    part = slice(step * up_tile, (step + 1) * up_tile)
                    value = dot(turned_ref[part, :], act_g[...], NN)
                    target = up_hbm.at[pl.ds(step * up_tile, up_tile), pl.ds(pl.multiple_of(base, 128), width)]
                    send(0, b * up_steps + step, value, up_stage, target)
                if step < down_steps:
                    part = slice(step * down_tile, (step + 1) * down_tile)
                    value = dot(act_v[:, part], grads_ref[...], TN)
                    target = down_hbm.at[pl.ds(pl.multiple_of(base + step * down_tile, 128), down_tile), :]
                    send(1, b * down_steps + step, value, down_stage, target)
        for copy in busy.values():
            copy.wait()

    args = [core, turned, all_grads, *flat]
    spaces = [None] * len(args)
    aliases = {}
    if before is not None:
        aliases = {len(args): 0, len(args) + 1: 1}
        args += [in_hbm(a) for a in before]
        spaces += [pl.ANY, pl.ANY]
    return ordered(
        body,
        args,
        [pltpu.HBM((features, 2 * half), F32), pltpu.HBM((2 * half, features), F32), jax.ShapeDtypeStruct((8, 128), F32)],
        name,
        4.0 * len(blocks),
        spaces=spaces,
        out_spaces=[pl.ANY, pl.ANY, VMEM],
        scratch=[
            VMEM((tokens, width), BF16),
            VMEM((tokens, width), BF16),
            VMEM((slots, up_tile, width), F32),
            VMEM((slots, down_tile, features), F32),
            pltpu.SemaphoreType.DMA((2, slots)),
        ],
        aliases=aliases,
    )


def per_device(wide, narrow, inputs, up_weight, down_weight, out_grad):
    rows = inputs.shape[0]
    half = up_weight.shape[1] // 2
    chips = wide // 2
    core = (lax.axis_index("wide") & 1).astype(jnp.int32).reshape(1)
    ordered = Ordered()

    def swap_cores(x):
        return lax.ppermute(x, "wide", [(i, i ^ 1) for i in range(wide)])

    def shift(x, places):
        return lax.ppermute(x, "narrow", [(i, (i + places) % narrow) for i in range(narrow)])

    def across_chips(keep, got):
        partial = (keep.astype(F32) + got.astype(F32)).astype(BF16)
        hop = 1
        while True:
            peer = lax.ppermute(partial, "wide", [(i, i ^ (2 * hop)) for i in range(wide)])
            hop *= 2
            if hop >= chips:
                return partial, peer
            partial = (partial.astype(F32) + peer.astype(F32)).astype(BF16)

    offsets = sorted(range(narrow // 2 - narrow + 1, narrow // 2 + 1), key=lambda places: (abs(places), -places))
    chunks = {0: jnp.stack([inputs, out_grad])}

    up_other, give_h = first_product(ordered, core, True, chunks[0], up_weight, 1, "give_hidden")
    got_h = swap_cores(give_h)
    up_mine, keep_h = first_product(ordered, core, False, chunks[0], up_weight, 1, "keep_hidden")
    own_h, peer_h = across_chips(keep_h, got_h)
    down_other, give_g = first_product(ordered, core, True, chunks[0], down_weight, 0, "give_grad", after=[own_h])
    got_g = swap_cores(give_g)
    down_mine, keep_g = first_product(ordered, core, False, chunks[0], down_weight, 0, "keep_grad")
    own_g, peer_g = across_chips(keep_g, got_g)

    slices = 2 if half % 256 == 0 else 1
    width = half // slices
    early = [((own_h, own_g), (peer_h, peer_g))]
    late = None
    waiting = [peer_h, peer_g]
    for offset in offsets[1:]:
        places = 1 if offset > 0 else -1
        chunk = chunks[offset] = shift(chunks[offset - places], places)
        give = product(ordered, chunk, up_other, down_other, "give", after=[waiting[0], early[-1][0][-1]])
        waiting = waiting[1:]
        got = swap_cores(give)
        keep = product(ordered, chunk, up_mine, down_mine, "keep")
        if offset != offsets[-1]:
            own, peer = across_chips(keep, got)
            early.append(((own,), (peer,)))
            waiting.append(peer)
        else:
            parts = [slice(i * width, (i + 1) * width) for i in range(slices)]
            late = [[(x,) for x in across_chips(keep[:, :, part], got[:, :, part])] for part in parts]

    turned, all_grads = collect(ordered, [chunks[offset] for offset in offsets], [own for (own,), _ in late])
    mine = gelu(ordered, early)
    other = swap_cores(mine)
    shares = input_product(ordered, [mine], [other], up_mine, up_other, narrow - 1, 0.1)
    shares = [share if offset == 0 else shift(share, -offset) for offset, share in zip(offsets, shares)]

    scale = (rows * narrow) ** -0.5
    late_acts = ([], [])

    def block(side, i):
        return (side, i * width, [((mine, other)[side], i * width), (late_acts[side][i], 0)])

    def grads(blocks, before):
        return weight_grads(ordered, core, blocks, turned, all_grads, half, scale, before, "weight_grads")[:2]

    result = None
    for i in range(slices):
        late_acts[0].append(gelu(ordered, [late[i]]))
        late_acts[1].append(swap_cores(late_acts[0][i]))
        if i < slices - 1:
            result = grads([block(0, i)], result)
    for i in range(slices - 1):
        result = grads([block(1, i)], result)
    so_far, share = input_product(ordered, *late_acts, up_mine, up_other, 1, 3.0, shares)
    share = shift(share, -offsets[-1])
    result = grads([block(0, slices - 1), block(1, slices - 1)], result)
    return (so_far + share.astype(F32)).astype(BF16), *result


def solution(mesh):
    placed = (
        P(("groups", "narrow"), "wide"),
        P("wide", "narrow"),
        P("narrow", "wide"),
        P(("groups", "narrow"), "wide"),
    )
    return jax.shard_map(
        functools.partial(per_device, mesh.shape["wide"], mesh.shape["narrow"]),
        mesh=mesh,
        in_specs=placed,
        out_specs=(
            P(("groups", "narrow"), "wide"),
            P(("groups", "wide"), "narrow"),
            P(("groups", "narrow"), "wide"),
        ),
        check_vma=False,
    )
```

time: 102 us -> 85 us (0.83)
  Pallas kernels: 58.5 us -> 49.4 us
  waiting for transfers between devices: 22.8 us -> 14.4 us
  other arithmetic: 1.11 us -> 2.15 us
    ppermute x9 -> x6, waiting for transfers between devices: 17.9 us -> 8.32 us  [shift(): lax.ppermute(x, 'narrow', [(i, (i + places) % narrow) for i in range(narr...]
    pallas_call x22 -> x19, Pallas kernels: 58.5 us -> 49.4 us  [__call__(): pl.pallas_call(kernel, out_shape=outs, in_specs=specs, out_specs=[pl.Bloc...]
    ppermute x9 -> x6, starting transfers between devices: 8.19 us -> 10.3 us  [shift(): lax.ppermute(x, 'narrow', [(i, (i + places) % narrow) for i in range(narr...]
    ppermute x10 -> x8, starting transfers between devices: 2.69 us -> 1.26 us  [swap_cores(): return lax.ppermute(x, 'wide', [(i, i ^ 1) for i in range(wide)])]
    another operation x0 -> x1, other arithmetic: none -> 1.06 us  [per_device(): chunks = {0: jnp.stack([inputs, out_grad])}]
  transfers between devices with their start and end apart: 25 -> 20, of which waited for: 8 -> 7; matrix products, arithmetic and copies ran while one was open for 0% -> 0% of each run, Pallas kernels for 50% -> 54%
where the time goes in v4:
time: 85 us; the launch traced here: 84.9 us
  Pallas kernels  49.4 us (58%)
  starting transfers between devices  18 us (21%)
  waiting for transfers between devices  14.4 us (17%)
  other arithmetic  2.15 us (3%)
  between operations  0.93 us (1%)
    pallas_call x19, Pallas kernels, __call__(): pl.pallas_call(kernel, out_shape=outs, in_specs=specs, out_specs=[pl.Bloc...  49.4 us
    ppermute x6, starting transfers between devices, shift(): lax.ppermute(x, 'narrow', [(i, (i + places) % narrow) for i in range(narr...  10.3 us
    ppermute x6, waiting for transfers between devices, shift(): lax.ppermute(x, 'narrow', [(i, (i + places) % narrow) for i in range(narr...  8.32 us
    ppermute x6, starting transfers between devices, across_chips(): lax.ppermute(partial, 'wide', [(i, i ^ 2 * hop) for i in range(wide)])  6.41 us
    ppermute x6, waiting for transfers between devices, across_chips(): lax.ppermute(partial, 'wide', [(i, i ^ 2 * hop) for i in range(wide)])  5.35 us
  transfers between devices with their start and end apart: 20, of which 7 were waited for; matrix products, arithmetic and copies ran while one was open for 0% of the time, Pallas kernels for 54%

profile of v4, /device:TPU:0, one launch (start us, length us, event | category | flops | bytes accessed | tf_op | source)
XLA Modules:
  0.0 84.9 jit_solution(12296510131647668695)
XLA Ops:
  0.6 1.1 %pad_maximum_fusion.refs_1_.refs_0_ = bf16[2,64,1536]{2,1,0:T(8,128)(2,1)S(1)} fusion(bf16[1,64,1536]{2,1,0:T(8,128)(2,1)} %bitcast.3, bf16[1,64,1536]{2,1,0:T(8,128)(2,1)} %bitcast.4), kind=kLoop, calls=%fused_computation.2 | loop fusion | flops 196608 | bytes 786432 | tf_op jit(solution)/shard_map/stack | solution.py:287
  1.7 5.1 %collective-permute-start.7 = (bf16[2,64,1536]{2,1,0:T(8,128)(2,1)S(1)}, bf16[2,64,1536]{2,1,0:T(8,128)(2,1)S(1)}, u32[]{:S(2)}, u32[]{:S(2)}) collective-permute-start(bf16[2,64,1536]{2,1,0:T(8,128)(2,1)S(1)} %pad_maximum_fusion.refs_1_.refs_0_), channel_id=1, source_target_pairs={{0,3},{1,0},{2,1},{3,2},{4,7},{5,4},{6,5},{7,6},{8,11},{9,8},{10,9... | collective-permute-start | bytes 1179656 | tf_op jit(solution)/shard_map/ppermute | solution.py:274
  6.8 2.8 %give_hidden.1 = (bf16[1536,1536]{1,0:T(8,128)(2,1)S(1)}, bf16[64,1536]{1,0:T(8,128)(2,1)S(1)}) custom-call(s32[1]{0:T(128)} %bitcast.refs_0_, bf16[2,64,1536]{2,1,0:T(8,128)(2,1)S(1)} %pad_maximum_fusion.refs_1_.refs_0_, bf16[1536,3072]{1,0:T(8,128)(2,1)} %refs_2_.5), custom_call_target="tpu_custom_call" | custom-call | flops 10000000000 | tf_op jit(solution)/shard_map/give_hidden/pallas_call | solution.py:53
  9.7 2.8 %keep_hidden.1 = (bf16[1536,1536]{1,0:T(8,128)(2,1)S(1)}, bf16[64,1536]{1,0:T(8,128)(2,1)S(1)}) custom-call(s32[1]{0:T(128)} %bitcast.refs_0_, bf16[2,64,1536]{2,1,0:T(8,128)(2,1)S(1)} %pad_maximum_fusion.refs_1_.refs_0_, bf16[1536,3072]{1,0:T(8,128)(2,1)} %refs_2_.5, bf16[64,1536]{1,0:T(8,128)(2,1)S(1)} %get-tuple-element.26.refs_3_), custom_call_target="tpu_custom_call" | custom-call | flops 10000000000 | tf_op jit(solution)/shard_map/keep_hidden/pallas_call | solution.py:53
  12.6 1.6 %collective-permute-start.3 = (bf16[64,1536]{1,0:T(8,128)(2,1)S(1)}, bf16[64,1536]{1,0:T(8,128)(2,1)S(1)}, u32[]{:S(2)}, u32[]{:S(2)}) collective-permute-start(bf16[64,1536]{1,0:T(8,128)(2,1)S(1)} %add_convert_fusion.6.refs_3_.refs_0_), channel_id=1, source_target_pairs={{0,8},{4,12},{8,0},{12,4},{1,9},{5,13},{9,1},{13,5},{2,10},{6,14},... | collective-permute-start | bytes 589832 | tf_op jit(solution)/shard_map/ppermute | solution.py:280
  14.1 3.2 %give_grad.1 = (bf16[1536,1536]{1,0:T(8,128)(2,1)S(1)}, bf16[64,1536]{1,0:T(8,128)(2,1)S(1)}) custom-call(s32[1]{0:T(128)} %bitcast.refs_0_, bf16[2,64,1536]{2,1,0:T(8,128)(2,1)S(1)} %pad_maximum_fusion.refs_1_.refs_0_, bf16[3072,1536]{1,0:T(8,128)(2,1)} %refs_2_.7, bf16[64,1536]{1,0:T(8,128)(2,1)S(1)} %add_convert_fusion.6.refs_3_.refs_0_, ...), custom_call_target="tpu_custom_call" | custom-call | flops 10000000000 | tf_op jit(solution)/shard_map/give_grad/pallas_call | solution.py:53
  17.6 3.2 %keep_grad.1 = (bf16[1536,1536]{1,0:T(8,128)(2,1)S(1)}, bf16[64,1536]{1,0:T(8,128)(2,1)S(1)}) custom-call(s32[1]{0:T(128)} %bitcast.refs_0_, bf16[2,64,1536]{2,1,0:T(8,128)(2,1)S(1)} %pad_maximum_fusion.refs_1_.refs_0_, bf16[3072,1536]{1,0:T(8,128)(2,1)} %refs_2_.7, bf16[64,1536]{1,0:T(8,128)(2,1)S(1)} %get-tuple-element.30.refs_3_), custom_call_target="tpu_custom_call" | custom-call | flops 10000000000 | tf_op jit(solution)/shard_map/keep_grad/pallas_call | solution.py:53
  20.9 0.6 collective-permute-start.8
  21.5 3.0 %collective-permute-done.refs_0_.refs_1_ = bf16[2,64,1536]{2,1,0:T(8,128)(2,1)S(1)} collective-permute-done((bf16[2,64,1536]{2,1,0:T(8,128)(2,1)S(1)}, bf16[2,64,1536]{2,1,0:T(8,128)(2,1)S(1)}, u32[]{:S(2)}, u32[]{:S(2)}) %collective-permute-start) | collective-permute-done | bytes 393248 | tf_op jit(solution)/shard_map/ppermute | solution.py:274
  24.5 2.3 %give.3.refs_3_ = bf16[2,64,1536]{2,1,0:T(8,128)(2,1)S(1)} custom-call(bf16[2,64,1536]{2,1,0:T(8,128)(2,1)S(1)} %collective-permute-done.refs_0_.refs_1_, bf16[1536,1536]{1,0:T(8,128)(2,1)S(1)} %get-tuple-element.28.refs_1_, bf16[1536,1536]{1,0:T(8,128)(2,1)S(1)} %get-tuple-element.32.refs_2_, bf16[64,1536]{1,0:T(8,128)(2,1)S(1)} %collective-permute-done.3.refs_3_.refs_2_, ...), custom_call_target="tpu_custom_call" | custom-call | flops 9600000000 | tf_op jit(solution)/shard_map/give/pallas_call | solution.py:53
  26.9 1.9 %collective-permute-start.1 = (bf16[2,64,1536]{2,1,0:T(8,128)(2,1)S(1)}, bf16[2,64,1536]{2,1,0:T(8,128)(2,1)S(1)}, u32[]{:S(2)}, u32[]{:S(2)}) collective-permute-start(bf16[2,64,1536]{2,1,0:T(8,128)(2,1)S(1)} %collective-permute-done.refs_0_.refs_1_), channel_id=1, source_target_pairs={{0,1},{1,2},{2,3},{3,0},{4,5},{5,6},{6,7},{7,4},{8,9},{9,10},{10,1... | collective-permute-start | bytes 1179656 | tf_op jit(solution)/shard_map/ppermute | solution.py:274
  28.8 2.3 %keep.3.refs_5_ = bf16[2,64,1536]{2,1,0:T(8,128)(2,1)S(1)} custom-call(bf16[2,64,1536]{2,1,0:T(8,128)(2,1)S(1)} %collective-permute-done.refs_0_.refs_1_, bf16[1536,1536]{1,0:T(8,128)(2,1)S(1)} %get-tuple-element.27.refs_1_.refs_0_, bf16[1536,1536]{1,0:T(8,128)(2,1)S(1)} %get-tuple-element.31.refs_2_, bf16[2,64,1536]{2,1,0:T(8,128)(2,1)S(1)} %give.3.refs_3_), custom_call_target="tpu_custom_call" | custom-call | flops 9600000000 | tf_op jit(solution)/shard_map/keep/pallas_call | solution.py:53
  31.2 1.6 %collective-permute-start.6 = (bf16[2,64,1536]{2,1,0:T(8,128)(2,1)S(1)}, bf16[2,64,1536]{2,1,0:T(8,128)(2,1)S(1)}, u32[]{:S(2)}, u32[]{:S(2)}) collective-permute-start(bf16[2,64,1536]{2,1,0:T(8,128)(2,1)S(1)} %add_convert_fusion.1.refs_4_), channel_id=1, source_target_pairs={{0,8},{4,12},{8,0},{12,4},{1,9},{5,13},{9,1},{13,5},{2,10},{6,14},... | collective-permute-start | bytes 1179656 | tf_op jit(solution)/shard_map/ppermute | solution.py:280
  32.8 2.3 %give.4.refs_3_ = bf16[2,64,1536]{2,1,0:T(8,128)(2,1)S(1)} custom-call(bf16[2,64,1536]{2,1,0:T(8,128)(2,1)S(1)} %collective-permute-done.7.refs_0_.refs_2_, bf16[1536,1536]{1,0:T(8,128)(2,1)S(1)} %get-tuple-element.28.refs_1_, bf16[1536,1536]{1,0:T(8,128)(2,1)S(1)} %get-tuple-element.32.refs_2_, bf16[64,1536]{1,0:T(8,128)(2,1)S(1)} %collective-permute-done.8.refs_3_, ...), custom_call_target="tpu_custom_call" | custom-call | flops 9600000000 | tf_op jit(solution)/shard_map/give/pallas_call | solution.py:53
  35.2 2.3 %keep.4.refs_5_ = bf16[2,64,1536]{2,1,0:T(8,128)(2,1)S(1)} custom-call(bf16[2,64,1536]{2,1,0:T(8,128)(2,1)S(1)} %collective-permute-done.7.refs_0_.refs_2_, bf16[1536,1536]{1,0:T(8,128)(2,1)S(1)} %get-tuple-element.27.refs_1_.refs_0_, bf16[1536,1536]{1,0:T(8,128)(2,1)S(1)} %get-tuple-element.31.refs_2_, bf16[2,64,1536]{2,1,0:T(8,128)(2,1)S(1)} %give.4.refs_3_), custom_call_target="tpu_custom_call" | custom-call | flops 9600000000 | tf_op jit(solution)/shard_map/keep/pallas_call | solution.py:53
  38.3 1.9 %collective-permute-done.1.refs_0_.refs_3_ = bf16[2,64,1536]{2,1,0:T(8,128)(2,1)S(1)} collective-permute-done((bf16[2,64,1536]{2,1,0:T(8,128)(2,1)S(1)}, bf16[2,64,1536]{2,1,0:T(8,128)(2,1)S(1)}, u32[]{:S(2)}, u32[]{:S(2)}) %collective-permute-start.1) | collective-permute-done | bytes 393248 | tf_op jit(solution)/shard_map/ppermute | solution.py:274
  40.2 3.0 %collective-permute-done.6.refs_3_.refs_5_ = bf16[2,64,1536]{2,1,0:T(8,128)(2,1)S(1)} collective-permute-done((bf16[2,64,1536]{2,1,0:T(8,128)(2,1)S(1)}, bf16[2,64,1536]{2,1,0:T(8,128)(2,1)S(1)}, u32[]{:S(2)}, u32[]{:S(2)}) %collective-permute-start.6) | collective-permute-done | bytes 393248 | tf_op jit(solution)/shard_map/ppermute | solution.py:280
  43.3 2.3 %give.5.refs_3_ = bf16[2,64,1536]{2,1,0:T(8,128)(2,1)S(1)} custom-call(bf16[2,64,1536]{2,1,0:T(8,128)(2,1)S(1)} %collective-permute-done.1.refs_0_.refs_3_, bf16[1536,1536]{1,0:T(8,128)(2,1)S(1)} %get-tuple-element.28.refs_1_, bf16[1536,1536]{1,0:T(8,128)(2,1)S(1)} %get-tuple-element.32.refs_2_, ...), custom_call_target="tpu_custom_call" | custom-call | flops 9600000000 | tf_op jit(solution)/shard_map/give/pallas_call | solution.py:53
  45.7 2.3 %keep.5.refs_6_ = bf16[2,64,1536]{2,1,0:T(8,128)(2,1)S(1)} custom-call(bf16[2,64,1536]{2,1,0:T(8,128)(2,1)S(1)} %collective-permute-done.1.refs_0_.refs_3_, bf16[1536,1536]{1,0:T(8,128)(2,1)S(1)} %get-tuple-element.27.refs_1_.refs_0_, bf16[1536,1536]{1,0:T(8,128)(2,1)S(1)} %get-tuple-element.31.refs_2_, bf16[2,64,1536]{2,1,0:T(8,128)(2,1)S(1)} %give.5.refs_3_), custom_call_target="tpu_custom_call" | custom-call | flops 9600000000 | tf_op jit(solution)/shard_map/keep/pallas_call | solution.py:53
  48.5 2.3 %collective-permute-done.12.refs_7_ = bf16[2,64,1536]{2,1,0:T(8,128)(2,1)S(1)} collective-permute-done((bf16[2,64,1536]{2,1,0:T(8,128)(2,1)S(1)}, bf16[2,64,1536]{2,1,0:T(8,128)(2,1)S(1)}, u32[]{:S(2)}, u32[]{:S(2)}) %collective-permute-start.12) | collective-permute-done | bytes 393248 | tf_op jit(solution)/shard_map/ppermute | solution.py:280
  50.7 0.8 gelu.3.refs_2_.refs_4_.refs_3_
  51.6 1.6 %collective-permute-start.11 = (bf16[2,64,768]{2,1,0:T(8,128)(2,1)S(1)}, bf16[2,64,768]{2,1,0:T(8,128)(2,1)S(1)}, u32[]{:S(2)}, u32[]{:S(2)}) collective-permute-start(bf16[2,64,768]{2,1,0:T(8,128)(2,1)S(1)} %get-tuple-element.50.refs_4_.refs_0_), channel_id=1, source_target_pairs={{0,8},{4,12},{8,0},{12,4},{1,9},{5,13},{9,1},{13,5},{2,10},{6,14},... | collective-permute-start | bytes 589832 | tf_op jit(solution)/shard_map/ppermute | solution.py:280
  53.7 0.7 collective-permute-done.13.refs_3_.refs_5_
  54.4 3.2 %input_product.2 = (bf16[64,1536]{1,0:T(8,128)(2,1)S(1)}, bf16[64,1536]{1,0:T(8,128)(2,1)S(1)}, bf16[64,1536]{1,0:T(8,128)(2,1)S(1)}) custom-call(bf16[1536,1536]{1,0:T(8,128)(2,1)S(1)} %get-tuple-element.27.refs_1_.refs_0_, bf16[1536,1536]{1,0:T(8,128)(2,1)S(1)} %get-tuple-element.28.refs_1_, bf16[2,192,1536]{2,1,0:T(8,128)(2,1)S(1)} %gelu.3.refs_2_.refs_4_.refs_3_, ...), custom_call_target="tpu_custom_call" | custom-call | flops 400000000 | tf_op jit(solution)/shard_map/input_product/pallas_call | solution.py:53
  57.6 2.3 %collective-permute-start.17 = (bf16[64,1536]{1,0:T(8,128)(2,1)S(1)}, bf16[64,1536]{1,0:T(8,128)(2,1)S(1)}, u32[]{:S(2)}, u32[]{:S(2)}) collective-permute-start(bf16[64,1536]{1,0:T(8,128)(2,1)S(1)} %get-tuple-element.39), channel_id=1, source_target_pairs={{0,3},{1,0},{2,1},{3,2},{4,7},{5,4},{6,5},{7,6},{8,11},{9,8},{10,9... | collective-permute-start | bytes 589832 | tf_op jit(solution)/shard_map/ppermute | solution.py:274
  60.1 4.1 %weight_grads.3 = (f32[1536,3072]{1,0:T(8,128)}, f32[3072,1536]{1,0:T(8,128)}, f32[8,128]{1,0:T(8,128)S(1)}) custom-call(s32[1]{0:T(128)} %bitcast.refs_0_, bf16[1536,256]{1,0:T(8,128)(2,1)S(1)} %get-tuple-element.36.refs_1_, bf16[256,1536]{1,0:T(8,128)(2,1)S(1)} %get-tuple-element.34.refs_8_.refs_2_, bf16[2,192,1536]{2,1,0:T(8,128)(2,1)S(1)} %gelu.3.refs_2_.refs_4_.refs_3_, ...), custom_call_target="tpu_custom_call" | custom-call | flops 16000000000 | tf_op jit(solution)/shard_map/weight_grads/pallas_call | solution.py:53
  65.0 4.1 %weight_grads.4 = (f32[1536,3072]{1,0:T(8,128)}, f32[3072,1536]{1,0:T(8,128)}, f32[8,128]{1,0:T(8,128)S(1)}) custom-call(s32[1]{0:T(128)} %bitcast.refs_0_, bf16[1536,256]{1,0:T(8,128)(2,1)S(1)} %get-tuple-element.36.refs_1_, bf16[256,1536]{1,0:T(8,128)(2,1)S(1)} %get-tuple-element.34.refs_8_.refs_2_, ...), custom_call_target="tpu_custom_call", output_to_operand_aliasing={{0}: (5, {}), {1}: (6, {})} | custom-call | flops 16000000000 | tf_op jit(solution)/shard_map/weight_grads/pallas_call | solution.py:53
  69.3 3.0 %input_product.3 = (f32[64,1536]{1,0:T(8,128)S(1)}, bf16[64,1536]{1,0:T(8,128)(2,1)S(1)}) custom-call(bf16[1536,1536]{1,0:T(8,128)(2,1)S(1)} %get-tuple-element.27.refs_1_.refs_0_, bf16[1536,1536]{1,0:T(8,128)(2,1)S(1)} %get-tuple-element.28.refs_1_, bf16[2,64,768]{2,1,0:T(8,128)(2,1)S(1)} %gelu.4.refs_4_.refs_5_.refs_2_, ...), custom_call_target="tpu_custom_call" | custom-call | flops 12000000000 | tf_op jit(solution)/shard_map/input_product/pallas_call | solution.py:53
  72.3 1.1 %collective-permute-start.19 = (bf16[64,1536]{1,0:T(8,128)(2,1)S(1)}, bf16[64,1536]{1,0:T(8,128)(2,1)S(1)}, u32[]{:S(2)}, u32[]{:S(2)}) collective-permute-start(bf16[64,1536]{1,0:T(8,128)(2,1)S(1)} %get-tuple-element.44.refs_9_), channel_id=1, source_target_pairs={{0,2},{1,3},{2,0},{3,1},{4,6},{5,7},{6,4},{7,5},{8,10},{9,11},{10,... | collective-permute-start | bytes 589832 | tf_op jit(solution)/shard_map/ppermute | solution.py:274
  73.4 7.6 %weight_grads.5 = (f32[1536,3072]{1,0:T(8,128)}, f32[3072,1536]{1,0:T(8,128)}, f32[8,128]{1,0:T(8,128)}) custom-call(s32[1]{0:T(128)} %bitcast.refs_0_, bf16[1536,256]{1,0:T(8,128)(2,1)S(1)} %get-tuple-element.36.refs_1_, bf16[256,1536]{1,0:T(8,128)(2,1)S(1)} %get-tuple-element.34.refs_8_.refs_2_, ...), custom_call_target="tpu_custom_call", output_to_operand_aliasing={{0}: (7, {}), {1}: (8, {})} | custom-call | flops 32000000000 | tf_op jit(solution)/shard_map/weight_grads/pallas_call | solution.py:53
  80.9 3.2 %collective-permute-done.19 = bf16[64,1536]{1,0:T(8,128)(2,1)S(1)} collective-permute-done((bf16[64,1536]{1,0:T(8,128)(2,1)S(1)}, bf16[64,1536]{1,0:T(8,128)(2,1)S(1)}, u32[]{:S(2)}, u32[]{:S(2)}) %collective-permute-start.19) | collective-permute-done | bytes 196640 | tf_op jit(solution)/shard_map/ppermute | solution.py:274
  84.1 0.7 add_convert_fusion.2
  (34 shorter events, 3.5 us)
Async XLA Ops:
  1.7 31.1 %collective-permute-start.7 = (bf16[2,64,1536]{2,1,0:T(8,128)(2,1)S(1)}, bf16[2,64,1536]{2,1,0:T(8,128)(2,1)S(1)}, u32[]{:S(2)}, u32[]{:S(2)}) collective-permute-start(bf16[2,64,1536]{2,1,0:T(8,128)(2,1)S(1)} %pad_maximum_fusion.refs_1_.refs_0_), channel_id=1, source_target_pairs={{0,3},{1,0},{2,1},{3,2},{4,7},{5,4},{6,5},{7,6},{8,11},{9,8},{10,9... | collective-permute-start | bytes 1179656 | tf_op jit(solution)/shard_map/ppermute | solution.py:274
  6.8 17.7 %collective-permute-start = (bf16[2,64,1536]{2,1,0:T(8,128)(2,1)S(1)}, bf16[2,64,1536]{2,1,0:T(8,128)(2,1)S(1)}, u32[]{:S(2)}, u32[]{:S(2)}) collective-permute-start(bf16[2,64,1536]{2,1,0:T(8,128)(2,1)S(1)} %pad_maximum_fusion.refs_1_.refs_0_), channel_id=1, source_target_pairs={{0,1},{1,2},{2,3},{3,0},{4,5},{5,6},{6,7},{7,4},{8,9},{9,10},{10,1... | collective-permute-start | bytes 1179656 | tf_op jit(solution)/shard_map/ppermute | solution.py:274
  9.6 2.9 %collective-permute-start.2 = (bf16[64,1536]{1,0:T(8,128)(2,1)S(1)}, bf16[64,1536]{1,0:T(8,128)(2,1)S(1)}, u32[]{:S(2)}, u32[]{:S(2)}) collective-permute-start(bf16[64,1536]{1,0:T(8,128)(2,1)S(1)} %get-tuple-element.26.refs_3_), channel_id=1, source_target_pairs={{0,4},{4,0},{8,12},{12,8},{1,5},{5,1},{9,13},{13,9},{2,6},{6,2},{1... | collective-permute-start | bytes 589832 | tf_op jit(solution)/shard_map/ppermute | solution.py:271
  12.6 11.9 %collective-permute-start.3 = (bf16[64,1536]{1,0:T(8,128)(2,1)S(1)}, bf16[64,1536]{1,0:T(8,128)(2,1)S(1)}, u32[]{:S(2)}, u32[]{:S(2)}) collective-permute-start(bf16[64,1536]{1,0:T(8,128)(2,1)S(1)} %add_convert_fusion.6.refs_3_.refs_0_), channel_id=1, source_target_pairs={{0,8},{4,12},{8,0},{12,4},{1,9},{5,13},{9,1},{13,5},{2,10},{6,14},... | collective-permute-start | bytes 589832 | tf_op jit(solution)/shard_map/ppermute | solution.py:280
  17.3 3.5 %collective-permute-start.4 = (bf16[64,1536]{1,0:T(8,128)(2,1)S(1)}, bf16[64,1536]{1,0:T(8,128)(2,1)S(1)}, u32[]{:S(2)}, u32[]{:S(2)}) collective-permute-start(bf16[64,1536]{1,0:T(8,128)(2,1)S(1)} %get-tuple-element.30.refs_3_), channel_id=1, source_target_pairs={{0,4},{4,0},{8,12},{12,8},{1,5},{5,1},{9,13},{13,9},{2,6},{6,2},{1... | collective-permute-start | bytes 589832 | tf_op jit(solution)/shard_map/ppermute | solution.py:271
  20.9 11.9 %collective-permute-start.8 = (bf16[64,1536]{1,0:T(8,128)(2,1)S(1)}, bf16[64,1536]{1,0:T(8,128)(2,1)S(1)}, u32[]{:S(2)}, u32[]{:S(2)}) collective-permute-start(bf16[64,1536]{1,0:T(8,128)(2,1)S(1)} %add_convert_fusion.5.refs_4_.refs_1_), channel_id=1, source_target_pairs={{0,8},{4,12},{8,0},{12,4},{1,9},{5,13},{9,1},{13,5},{2,10},{6,14},... | collective-permute-start | bytes 589832 | tf_op jit(solution)/shard_map/ppermute | solution.py:280
  26.9 4.3 %collective-permute-start.5 = (bf16[2,64,1536]{2,1,0:T(8,128)(2,1)S(1)}, bf16[2,64,1536]{2,1,0:T(8,128)(2,1)S(1)}, u32[]{:S(2)}, u32[]{:S(2)}) collective-permute-start(bf16[2,64,1536]{2,1,0:T(8,128)(2,1)S(1)} %give.3.refs_3_), channel_id=1, source_target_pairs={{0,4},{4,0},{8,12},{12,8},{1,5},{5,1},{9,13},{13,9},{2,6},{6,2},{1... | collective-permute-start | bytes 1179656 | tf_op jit(solution)/shard_map/ppermute | solution.py:271
  26.9 13.3 %collective-permute-start.1 = (bf16[2,64,1536]{2,1,0:T(8,128)(2,1)S(1)}, bf16[2,64,1536]{2,1,0:T(8,128)(2,1)S(1)}, u32[]{:S(2)}, u32[]{:S(2)}) collective-permute-start(bf16[2,64,1536]{2,1,0:T(8,128)(2,1)S(1)} %collective-permute-done.refs_0_.refs_1_), channel_id=1, source_target_pairs={{0,1},{1,2},{2,3},{3,0},{4,5},{5,6},{6,7},{7,4},{8,9},{9,10},{10,1... | collective-permute-start | bytes 1179656 | tf_op jit(solution)/shard_map/ppermute | solution.py:274
  31.2 12.0 %collective-permute-start.6 = (bf16[2,64,1536]{2,1,0:T(8,128)(2,1)S(1)}, bf16[2,64,1536]{2,1,0:T(8,128)(2,1)S(1)}, u32[]{:S(2)}, u32[]{:S(2)}) collective-permute-start(bf16[2,64,1536]{2,1,0:T(8,128)(2,1)S(1)} %add_convert_fusion.1.refs_4_), channel_id=1, source_target_pairs={{0,8},{4,12},{8,0},{12,4},{1,9},{5,13},{9,1},{13,5},{2,10},{6,14},... | collective-permute-start | bytes 1179656 | tf_op jit(solution)/shard_map/ppermute | solution.py:280
  35.2 2.4 %collective-permute-start.9 = (bf16[2,64,1536]{2,1,0:T(8,128)(2,1)S(1)}, bf16[2,64,1536]{2,1,0:T(8,128)(2,1)S(1)}, u32[]{:S(2)}, u32[]{:S(2)}) collective-permute-start(bf16[2,64,1536]{2,1,0:T(8,128)(2,1)S(1)} %give.4.refs_3_), channel_id=1, source_target_pairs={{0,4},{4,0},{8,12},{12,8},{1,5},{5,1},{9,13},{13,9},{2,6},{6,2},{1... | collective-permute-start | bytes 1179656 | tf_op jit(solution)/shard_map/ppermute | solution.py:271
  37.7 13.0 %collective-permute-start.12 = (bf16[2,64,1536]{2,1,0:T(8,128)(2,1)S(1)}, bf16[2,64,1536]{2,1,0:T(8,128)(2,1)S(1)}, u32[]{:S(2)}, u32[]{:S(2)}) collective-permute-start(bf16[2,64,1536]{2,1,0:T(8,128)(2,1)S(1)} %add_convert_fusion.refs_4_.refs_6_), channel_id=1, source_target_pairs={{0,8},{4,12},{8,0},{12,4},{1,9},{5,13},{9,1},{13,5},{2,10},{6,14},... | collective-permute-start | bytes 1179656 | tf_op jit(solution)/shard_map/ppermute | solution.py:280
  45.6 2.4 %collective-permute-start.10 = (bf16[2,64,1536]{2,1,0:T(8,128)(2,1)S(1)}, bf16[2,64,1536]{2,1,0:T(8,128)(2,1)S(1)}, u32[]{:S(2)}, u32[]{:S(2)}) collective-permute-start(bf16[2,64,1536]{2,1,0:T(8,128)(2,1)S(1)} %give.5.refs_3_), channel_id=1, source_target_pairs={{0,4},{4,0},{8,12},{12,8},{1,5},{5,1},{9,13},{13,9},{2,6},{6,2},{1... | collective-permute-start | bytes 1179656 | tf_op jit(solution)/shard_map/ppermute | solution.py:271
  51.5 2.9 %collective-permute-start.13 = (bf16[2,192,1536]{2,1,0:T(8,128)(2,1)S(1)}, bf16[2,192,1536]{2,1,0:T(8,128)(2,1)S(1)}, u32[]{:S(2)}, u32[]{:S(2)}) collective-permute-start(bf16[2,192,1536]{2,1,0:T(8,128)(2,1)S(1)} %gelu.3.refs_2_.refs_4_.refs_3_), channel_id=1, source_target_pairs={{0,4},{4,0},{8,12},{12,8},{1,5},{5,1},{9,13},{13,9},{2,6},{6,2},{1... | collective-permute-start | bytes 3538952 | tf_op jit(solution)/shard_map/ppermute | solution.py:271
  51.6 8.3 %collective-permute-start.11 = (bf16[2,64,768]{2,1,0:T(8,128)(2,1)S(1)}, bf16[2,64,768]{2,1,0:T(8,128)(2,1)S(1)}, u32[]{:S(2)}, u32[]{:S(2)}) collective-permute-start(bf16[2,64,768]{2,1,0:T(8,128)(2,1)S(1)} %get-tuple-element.50.refs_4_.refs_0_), channel_id=1, source_target_pairs={{0,8},{4,12},{8,0},{12,4},{1,9},{5,13},{9,1},{13,5},{2,10},{6,14},... | collective-permute-start | bytes 589832 | tf_op jit(solution)/shard_map/ppermute | solution.py:280
  53.2 11.1 %collective-permute-start.14 = (bf16[2,64,768]{2,1,0:T(8,128)(2,1)S(1)}, bf16[2,64,768]{2,1,0:T(8,128)(2,1)S(1)}, u32[]{:S(2)}, u32[]{:S(2)}) collective-permute-start(bf16[2,64,768]{2,1,0:T(8,128)(2,1)S(1)} %get-tuple-element.49.refs_5_.refs_0_), channel_id=1, source_target_pairs={{0,8},{4,12},{8,0},{12,4},{1,9},{5,13},{9,1},{13,5},{2,10},{6,14},... | collective-permute-start | bytes 589832 | tf_op jit(solution)/shard_map/ppermute | solution.py:280
  57.6 11.5 %collective-permute-start.17 = (bf16[64,1536]{1,0:T(8,128)(2,1)S(1)}, bf16[64,1536]{1,0:T(8,128)(2,1)S(1)}, u32[]{:S(2)}, u32[]{:S(2)}) collective-permute-start(bf16[64,1536]{1,0:T(8,128)(2,1)S(1)} %get-tuple-element.39), channel_id=1, source_target_pairs={{0,3},{1,0},{2,1},{3,2},{4,7},{5,4},{6,5},{7,6},{8,11},{9,8},{10,9... | collective-permute-start | bytes 589832 | tf_op jit(solution)/shard_map/ppermute | solution.py:274
  59.9 9.4 %collective-permute-start.18 = (bf16[64,1536]{1,0:T(8,128)(2,1)S(1)}, bf16[64,1536]{1,0:T(8,128)(2,1)S(1)}, u32[]{:S(2)}, u32[]{:S(2)}) collective-permute-start(bf16[64,1536]{1,0:T(8,128)(2,1)S(1)} %get-tuple-element.35.refs_2_), channel_id=1, source_target_pairs={{0,1},{1,2},{2,3},{3,0},{4,5},{5,6},{6,7},{7,4},{8,9},{9,10},{10,1... | collective-permute-start | bytes 589832 | tf_op jit(solution)/shard_map/ppermute | solution.py:274
  60.0 4.9 %collective-permute-start.15 = (bf16[2,64,768]{2,1,0:T(8,128)(2,1)S(1)}, bf16[2,64,768]{2,1,0:T(8,128)(2,1)S(1)}, u32[]{:S(2)}, u32[]{:S(2)}) collective-permute-start(bf16[2,64,768]{2,1,0:T(8,128)(2,1)S(1)} %gelu.4.refs_4_.refs_5_.refs_2_), channel_id=1, source_target_pairs={{0,4},{4,0},{8,12},{12,8},{1,5},{5,1},{9,13},{13,9},{2,6},{6,2},{1... | collective-permute-start | bytes 589832 | tf_op jit(solution)/shard_map/ppermute | solution.py:271
  64.4 4.9 %collective-permute-start.16 = (bf16[2,64,768]{2,1,0:T(8,128)(2,1)S(1)}, bf16[2,64,768]{2,1,0:T(8,128)(2,1)S(1)}, u32[]{:S(2)}, u32[]{:S(2)}) collective-permute-start(bf16[2,64,768]{2,1,0:T(8,128)(2,1)S(1)} %gelu.5.refs_7_.refs_3_.refs_4_), channel_id=1, source_target_pairs={{0,4},{4,0},{8,12},{12,8},{1,5},{5,1},{9,13},{13,9},{2,6},{6,2},{1... | collective-permute-start | bytes 589832 | tf_op jit(solution)/shard_map/ppermute | solution.py:271
  72.3 11.8 %collective-permute-start.19 = (bf16[64,1536]{1,0:T(8,128)(2,1)S(1)}, bf16[64,1536]{1,0:T(8,128)(2,1)S(1)}, u32[]{:S(2)}, u32[]{:S(2)}) collective-permute-start(bf16[64,1536]{1,0:T(8,128)(2,1)S(1)} %get-tuple-element.44.refs_9_), channel_id=1, source_target_pairs={{0,2},{1,3},{2,0},{3,1},{4,6},{5,7},{6,4},{7,5},{8,10},{9,11},{10,... | collective-permute-start | bytes 589832 | tf_op jit(solution)/shard_map/ppermute | solution.py:274

commit v5 on v4

--- a/solution.py
+++ b/solution.py
@@ -65,40 +65,42 @@
         return result
 
 
-def first_product(ordered, core, other, chunk, weight, units_dim, name, after=()):
+def first_product(ordered, core, other, chunk, up_weight, down_weight, name):
     _, rows, features = chunk.shape
-    half = weight.shape[units_dim] // 2
+    half = up_weight.shape[1] // 2
     tile = tile_of(half)
     pieces = half // tile
 
-    def body(core_ref, chunk_ref, weight_hbm, weight_ref, out_ref, sems):
+    def body(core_ref, chunk_ref, up_hbm, down_hbm, up_ref, down_ref, *refs):
+        out_ref, sems = refs[-2:]
         side = 1 - core_ref[0] if other else core_ref[0]
         copies = []
         for i in range(pieces):
             units = pl.ds(pl.multiple_of(side * half + i * tile, tile), tile)
             part = pl.ds(i * tile, tile)
-            at = (lambda u: (slice(None), u)) if units_dim else (lambda u: (u, slice(None)))
-            copies.append(pltpu.make_async_copy(weight_hbm.at[at(units)], weight_ref.at[at(part)], sems.at[i]))
+            copies.append(pltpu.make_async_copy(up_hbm.at[:, units], up_ref.at[:, part], sems.at[0, i]))
+            copies.append(pltpu.make_async_copy(down_hbm.at[units, :], down_ref.at[part, :], sems.at[1, i]))
         for copy in copies:
             copy.start()
-        for i, copy in enumerate(copies):
+        if other:
+            refs[0][...] = chunk_ref[...]
+        for i in range(pieces):
             part = slice(i * tile, (i + 1) * tile)
-            copy.wait()
-            if units_dim:
-                out_ref[:, part] = dot(chunk_ref[0], weight_ref[:, part], NN).astype(BF16)
-            else:
-                out_ref[:, part] = dot(chunk_ref[1], weight_ref[part, :], NT).astype(BF16)
-
-    shape = (features, half) if units_dim else (half, features)
+            copies[2 * i].wait()
+            out_ref[0, :, part] = dot(chunk_ref[0], up_ref[:, part], NN).astype(BF16)
+            copies[2 * i + 1].wait()
+            out_ref[1, :, part] = dot(chunk_ref[1], down_ref[part, :], NT).astype(BF16)
+
+    outs = [VMEM((features, half), BF16), VMEM((half, features), BF16)]
+    outs += [jax.ShapeDtypeStruct(chunk.shape, BF16)] if other else []
     return ordered(
         body,
-        (core, chunk, in_hbm(weight)),
-        [VMEM(shape, BF16), jax.ShapeDtypeStruct((rows, half), BF16)],
+        (core, chunk, in_hbm(up_weight), in_hbm(down_weight)),
+        outs + [jax.ShapeDtypeStruct((2, rows, half), BF16)],
         name,
-        2.5,
-        spaces=[None, None, pl.ANY],
-        scratch=[pltpu.SemaphoreType.DMA((pieces,))],
-        after=after,
+        4.5,
+        spaces=[None, None, pl.ANY, pl.ANY],
+        scratch=[pltpu.SemaphoreType.DMA((2, pieces))],
     )
 
 
@@ -117,14 +119,18 @@
     return ordered(body, args, [jax.ShapeDtypeStruct((2, rows, half), BF16)], name, 2.4, after=after)[0]
 
 
-def input_product(ordered, mine, other, up_mine, up_other, chunks, micros, returned=()):
-    rows = mine[0].shape[1] // chunks
+def product_terms(acts, up_refs, part, low):
+    terms = [dot(act, up_ref[part, low : low + act.shape[1]], NT) for act, up_ref in zip(acts, up_refs)]
+    return terms[0] + terms[1]
+
+
+def input_product(ordered, mine, other, up_mine, up_other, low, chunks, micros, partial=None, returned=()):
+    rows = mine.shape[1] // chunks
     features = up_mine.shape[0]
     tile = tile_of(features)
-    widths = [a.shape[2] for a in mine]
-
-    def body(up_mine_ref, up_other_ref, *refs):
-        returned_refs, out_refs = refs[2 * len(widths) :][: len(returned)], refs[-chunks:]
+
+    def body(up_mine_ref, up_other_ref, mine_ref, other_ref, *refs):
+        returned_refs, out_refs = refs[: len(returned)], refs[-chunks:]
         if returned:
             total = returned_refs[0][...].astype(F32)
             for ref in returned_refs[1:]:
@@ -132,36 +138,26 @@
             refs[-chunks - 1][...] = total
         for start in range(0, features, tile):
             part = slice(start, start + tile)
-            share = None
-            for side, up_ref in enumerate((up_mine_ref, up_other_ref)):
-                low = 0
-                for i, width in enumerate(widths):
-                    term = dot(refs[side * len(widths) + i][0], up_ref[part, low : low + width], NT)
-                    share = term if share is None else share + term
-                    low += width
+            share = product_terms((mine_ref[0], other_ref[0]), (up_mine_ref, up_other_ref), part, low)
+            if partial is not None:
+                share = share + refs[len(returned)][:, part]
             for c, out_ref in enumerate(out_refs):
                 out_ref[:, part] = share[c * rows : (c + 1) * rows].astype(BF16)
 
-    args = (in_vmem(up_mine), in_vmem(up_other), *mine, *other, *returned)
+    args = (in_vmem(up_mine), in_vmem(up_other), mine, other, *returned, *([] if partial is None else [partial]))
     outs = [jax.ShapeDtypeStruct((rows, features), F32)] if returned else []
     return ordered(body, args, outs + [jax.ShapeDtypeStruct((rows, features), BF16)] * chunks, "input_product", micros)
 
 
 def gelu(ordered, sums, after=()):
-    flat, places = [], []
-    for own, peer in sums:
-        where = []
-        for side in (own, peer):
-            where += [(len(flat) + i, None) for i in (0, 1)] if len(side) == 2 else [(len(flat), i) for i in (0, 1)]
-            flat += side
-        places.append(where)
-    rows, units = flat[0].shape[-2:]
+    flat = [a for pair in sums for a in pair]
+    _, rows, units = flat[0].shape
 
     def body(*refs):
         out_ref = refs[-1]
-        for chunk, where in enumerate(places):
+        for chunk in range(len(sums)):
             at = slice(chunk * rows, (chunk + 1) * rows)
-            own_h, own_g, peer_h, peer_g = [(refs[r][...] if i is None else refs[r][i]).astype(F32) for r, i in where]
+            own_h, own_g, peer_h, peer_g = [refs[2 * chunk + side][i].astype(F32) for side in (0, 1) for i in (0, 1)]
             hidden, grad_hidden = own_h + peer_h, own_g + peer_g
             cdf = 0.5 * (1.0 + lax.erf(hidden * 0.7071067811865476))
             pdf = jnp.exp(-0.5 * hidden * hidden) * 0.3989422804014327
@@ -189,7 +185,7 @@
     return ordered(body, chunks, outs, "collect", 0.1, scratch=[VMEM((rows * count, features), BF16)], after=after)
 
 
-def weight_grads(ordered, core, blocks, turned, all_grads, half, scale, before, name):
+def weight_grads(ordered, core, blocks, turned, all_grads, half, scale, before, name, share=None):
     features, tokens = turned.shape
     width = min(a.shape[2] for a, _ in blocks[0][2])
     up_tile, down_tile = tile_of(features), tile_of(width, 256)
@@ -198,7 +194,8 @@
     flat = [a for block in blocks for a, _ in block[2]]
 
     def body(core_ref, turned_ref, grads_ref, *refs):
-        up_hbm, down_hbm, done_ref, act_g, act_v, up_stage, down_stage, sems = refs[-8:]
+        up_hbm, down_hbm = refs[outs_at : outs_at + 2]
+        done_ref, act_g, act_v, up_stage, down_stage, sems = refs[-6:]
         done_ref[...] = jnp.zeros_like(done_ref)
         busy = {}
 
@@ -231,11 +228,21 @@
                     value = dot(act_v[:, part], grads_ref[...], TN)
                     target = down_hbm.at[pl.ds(pl.multiple_of(base + step * down_tile, 128), down_tile), :]
                     send(1, b * down_steps + step, value, down_stage, target)
+                if share is not None and b == 0 and step < up_steps:
+                    part = slice(step * up_tile, (step + 1) * up_tile)
+                    mine_ref, other_ref, up_mine_ref, up_other_ref = refs[len(flat) : len(flat) + 4]
+                    value = product_terms((mine_ref[0], other_ref[0]), (up_mine_ref, up_other_ref), part, 0)
+                    refs[outs_at + 2][:, part] = value.astype(share[4])
         for copy in busy.values():
             copy.wait()
 
     args = [core, turned, all_grads, *flat]
+    outs = [pltpu.HBM((features, 2 * half), F32), pltpu.HBM((2 * half, features), F32)]
+    if share is not None:
+        args += [*share[:2], in_vmem(share[2]), in_vmem(share[3])]
+        outs.append(jax.ShapeDtypeStruct((share[0].shape[1], features), share[4]))
     spaces = [None] * len(args)
+    outs_at = len(args) - 3 + (0 if before is None else 2)
     aliases = {}
     if before is not None:
         aliases = {len(args): 0, len(args) + 1: 1}
@@ -244,11 +251,11 @@
     return ordered(
         body,
         args,
-        [pltpu.HBM((features, 2 * half), F32), pltpu.HBM((2 * half, features), F32), jax.ShapeDtypeStruct((8, 128), F32)],
+        [*outs, jax.ShapeDtypeStruct((8, 128), F32)],
         name,
         4.0 * len(blocks),
         spaces=spaces,
-        out_spaces=[pl.ANY, pl.ANY, VMEM],
+        out_spaces=[pl.ANY, pl.ANY] + [VMEM] * (len(outs) - 1),
         scratch=[
             VMEM((tokens, width), BF16),
             VMEM((tokens, width), BF16),
@@ -286,62 +293,59 @@
     offsets = sorted(range(narrow // 2 - narrow + 1, narrow // 2 + 1), key=lambda places: (abs(places), -places))
     chunks = {0: jnp.stack([inputs, out_grad])}
 
-    up_other, give_h = first_product(ordered, core, True, chunks[0], up_weight, 1, "give_hidden")
-    got_h = swap_cores(give_h)
-    up_mine, keep_h = first_product(ordered, core, False, chunks[0], up_weight, 1, "keep_hidden")
-    own_h, peer_h = across_chips(keep_h, got_h)
-    down_other, give_g = first_product(ordered, core, True, chunks[0], down_weight, 0, "give_grad", after=[own_h])
-    got_g = swap_cores(give_g)
-    down_mine, keep_g = first_product(ordered, core, False, chunks[0], down_weight, 0, "keep_grad")
-    own_g, peer_g = across_chips(keep_g, got_g)
+    up_other, down_other, sent_back, give = first_product(ordered, core, True, chunks[0], up_weight, down_weight, "give_first")
+    got = swap_cores(give)
+    up_mine, down_mine, keep = first_product(ordered, core, False, chunks[0], up_weight, down_weight, "keep_first")
+    sums = [across_chips(keep, got)]
+
+    def acts_of(sums):
+        mine = gelu(ordered, sums)
+        return mine, swap_cores(mine)
 
     slices = 2 if half % 256 == 0 else 1
     width = half // slices
-    early = [((own_h, own_g), (peer_h, peer_g))]
-    late = None
-    waiting = [peer_h, peer_g]
     for offset in offsets[1:]:
         places = 1 if offset > 0 else -1
-        chunk = chunks[offset] = shift(chunks[offset - places], places)
-        give = product(ordered, chunk, up_other, down_other, "give", after=[waiting[0], early[-1][0][-1]])
-        waiting = waiting[1:]
+        chunk = chunks[offset] = shift(sent_back if offset == -1 else chunks[offset - places], places)
+        give = product(ordered, chunk, up_other, down_other, "give", after=[sums[-1][0]] + [peer for _, peer in sums[-2:-1]])
         got = swap_cores(give)
+        if offset == offsets[-1]:
+            early = acts_of(sums[:-1])
         keep = product(ordered, chunk, up_mine, down_mine, "keep")
         if offset != offsets[-1]:
-            own, peer = across_chips(keep, got)
-            early.append(((own,), (peer,)))
-            waiting.append(peer)
+            sums.append(across_chips(keep, got))
         else:
             parts = [slice(i * width, (i + 1) * width) for i in range(slices)]
-            late = [[(x,) for x in across_chips(keep[:, :, part], got[:, :, part])] for part in parts]
-
-    turned, all_grads = collect(ordered, [chunks[offset] for offset in offsets], [own for (own,), _ in late])
-    mine = gelu(ordered, early)
-    other = swap_cores(mine)
-    shares = input_product(ordered, [mine], [other], up_mine, up_other, narrow - 1, 0.1)
+            late = [across_chips(keep[:, :, part], got[:, :, part]) for part in parts]
+
+    turned, all_grads = collect(ordered, [chunks[offset] for offset in offsets], [own for own, _ in late])
+    shares = input_product(ordered, *early, up_mine, up_other, 0, narrow - 2, 0.1)
     shares = [share if offset == 0 else shift(share, -offset) for offset, share in zip(offsets, shares)]
+    middle = acts_of(sums[-1:])
 
     scale = (rows * narrow) ** -0.5
-    late_acts = ([], [])
-
-    def block(side, i):
-        return (side, i * width, [((mine, other)[side], i * width), (late_acts[side][i], 0)])
-
-    def grads(blocks, before):
-        return weight_grads(ordered, core, blocks, turned, all_grads, half, scale, before, "weight_grads")[:2]
-
-    result = None
-    for i in range(slices):
-        late_acts[0].append(gelu(ordered, [late[i]]))
-        late_acts[1].append(swap_cores(late_acts[0][i]))
-        if i < slices - 1:
-            result = grads([block(0, i)], result)
-    for i in range(slices - 1):
-        result = grads([block(1, i)], result)
-    so_far, share = input_product(ordered, *late_acts, up_mine, up_other, 1, 3.0, shares)
+    late_acts = []
+
+    def grads(places, before, share):
+        blocks = [
+            (side, i * width, [(early[side], i * width), (middle[side], i * width), (late_acts[i][side], 0)])
+            for side, i in places
+        ]
+        return weight_grads(ordered, core, blocks, turned, all_grads, half, scale, before, "weight_grads", share)
+
+    late_acts.append(acts_of(late[:1]))
+    up_grad, down_grad, share, _ = grads([(0, 0)], None, (*middle, up_mine, up_other, BF16))
+    shares.append(shift(share, -offsets[-2]))
+    partial = None
+    if slices > 1:
+        late_acts.append(acts_of(late[1:]))
+        up_grad, down_grad, partial, _ = grads([(1, 0)], (up_grad, down_grad), (*late_acts[0], up_mine, up_other, F32))
+    low = width * (slices - 1)
+    so_far, share = input_product(ordered, *late_acts[-1], up_mine, up_other, low, 1, 3.0, partial, shares)
     share = shift(share, -offsets[-1])
-    result = grads([block(0, slices - 1), block(1, slices - 1)], result)
-    return (so_far + share.astype(F32)).astype(BF16), *result
+    last = [(0, 1), (1, 1)] if slices > 1 else [(1, 0)]
+    up_grad, down_grad, _ = grads(last, (up_grad, down_grad), None)
+    return (so_far + share.astype(F32)).astype(BF16), up_grad, down_grad
 
 
 def solution(mesh):

time: 85 us -> 85.9 us (1.011)
  starting transfers between devices: 18 us -> 24.9 us
  Pallas kernels: 49.4 us -> 45.7 us
  waiting for transfers between devices: 14.4 us -> 12 us
    ppermute x6, starting transfers between devices: 10.3 us -> 16.9 us  [shift(): lax.ppermute(x, 'narrow', [(i, (i + places) % narrow) for i in range(narr...]
    pallas_call x19 -> x18, Pallas kernels: 49.4 us -> 45.7 us  [__call__(): pl.pallas_call(kernel, out_shape=outs, in_specs=specs, out_specs=[pl.Bloc...]
    ppermute x6 -> x5, waiting for transfers between devices: 5.35 us -> 4.45 us  [across_chips(): lax.ppermute(partial, 'wide', [(i, i ^ 2 * hop) for i in range(wide)])]
    ppermute x6 -> x5, starting transfers between devices: 6.41 us -> 6.39 us  [across_chips(): lax.ppermute(partial, 'wide', [(i, i ^ 2 * hop) for i in range(wide)])]
  transfers between devices with their start and end apart: 20 -> 19, of which waited for: 7 -> 6; matrix products, arithmetic and copies ran while one was open for 0% -> 0% of each run, Pallas kernels for 54% -> 51%
where the time goes in v5:
time: 85.9 us; the launch traced here: 85.7 us
  Pallas kernels  45.7 us (53%)
  starting transfers between devices  24.9 us (29%)
  waiting for transfers between devices  12 us (14%)
  other arithmetic  2.15 us (3%)
  between operations  0.93 us (1%)
    pallas_call x18, Pallas kernels, __call__(): pl.pallas_call(kernel, out_shape=outs, in_specs=specs, out_specs=[pl.Bloc...  45.7 us
    ppermute x6, starting transfers between devices, shift(): lax.ppermute(x, 'narrow', [(i, (i + places) % narrow) for i in range(narr...  16.9 us
    ppermute x6, waiting for transfers between devices, shift(): lax.ppermute(x, 'narrow', [(i, (i + places) % narrow) for i in range(narr...  7.53 us
    ppermute x5, starting transfers between devices, across_chips(): lax.ppermute(partial, 'wide', [(i, i ^ 2 * hop) for i in range(wide)])  6.39 us
    ppermute x5, waiting for transfers between devices, across_chips(): lax.ppermute(partial, 'wide', [(i, i ^ 2 * hop) for i in range(wide)])  4.45 us
  transfers between devices with their start and end apart: 19, of which 6 were waited for; matrix products, arithmetic and copies ran while one was open for 0% of the time, Pallas kernels for 51%

profile of v5, /device:TPU:0, one launch (start us, length us, event | category | flops | bytes accessed | tf_op | source)
XLA Modules:
  0.0 85.7 jit_solution(10103122439640481891)
XLA Ops:
  0.6 1.1 %pad_maximum_fusion.refs_1_.refs_0_ = bf16[2,64,1536]{2,1,0:T(8,128)(2,1)S(1)} fusion(bf16[1,64,1536]{2,1,0:T(8,128)(2,1)} %bitcast.3, bf16[1,64,1536]{2,1,0:T(8,128)(2,1)} %bitcast.4), kind=kLoop, calls=%fused_computation.3 | loop fusion | flops 196608 | bytes 786432 | tf_op jit(solution)/shard_map/stack | solution.py:294
  1.7 3.1 %collective-permute-start = (bf16[2,64,1536]{2,1,0:T(8,128)(2,1)S(1)}, bf16[2,64,1536]{2,1,0:T(8,128)(2,1)S(1)}, u32[]{:S(2)}, u32[]{:S(2)}) collective-permute-start(bf16[2,64,1536]{2,1,0:T(8,128)(2,1)S(1)} %pad_maximum_fusion.refs_1_.refs_0_), channel_id=1, source_target_pairs={{0,1},{1,2},{2,3},{3,0},{4,5},{5,6},{6,7},{7,4},{8,9},{9,10},{10,1... | collective-permute-start | bytes 1179656 | tf_op jit(solution)/shard_map/ppermute | solution.py:281
  4.8 4.5 %give_first.1 = (bf16[1536,1536]{1,0:T(8,128)(2,1)S(1)}, bf16[1536,1536]{1,0:T(8,128)(2,1)S(1)}, bf16[2,64,1536]{2,1,0:T(8,128)(2,1)S(1)}, bf16[2,64,1536]{2,1,0:T(8,128)(2,1)S(1)}) custom-call(s32[1]{0:T(128)} %bitcast.refs_0_, bf16[2,64,1536]{2,1,0:T(8,128)(2,1)S(1)} %pad_maximum_fusion.refs_1_.refs_0_, bf16[1536,3072]{1,0:T(8,128)(2,1)} %refs_2_.3, ...), custom_call_target="tpu_custom_call" | custom-call | flops 17999998976 | tf_op jit(solution)/shard_map/give_first/pallas_call | solution.py:53
  9.3 2.1 %collective-permute-start.6 = (bf16[2,64,1536]{2,1,0:T(8,128)(2,1)S(1)}, bf16[2,64,1536]{2,1,0:T(8,128)(2,1)S(1)}, u32[]{:S(2)}, u32[]{:S(2)}) collective-permute-start(bf16[2,64,1536]{2,1,0:T(8,128)(2,1)S(1)} %get-tuple-element.32), channel_id=1, source_target_pairs={{0,3},{1,0},{2,1},{3,2},{4,7},{5,4},{6,5},{7,6},{8,11},{9,8},{10,9... | collective-permute-start | bytes 1179656 | tf_op jit(solution)/shard_map/ppermute | solution.py:281
  11.4 4.5 %keep_first.1 = (bf16[1536,1536]{1,0:T(8,128)(2,1)S(1)}, bf16[1536,1536]{1,0:T(8,128)(2,1)S(1)}, bf16[2,64,1536]{2,1,0:T(8,128)(2,1)S(1)}) custom-call(s32[1]{0:T(128)} %bitcast.refs_0_, bf16[2,64,1536]{2,1,0:T(8,128)(2,1)S(1)} %pad_maximum_fusion.refs_1_.refs_0_, bf16[1536,3072]{1,0:T(8,128)(2,1)} %refs_2_.3, bf16[3072,1536]{1,0:T(8,128)(2,1)} %refs_3_.3, ...), custom_call_target="tpu_custom_call" | custom-call | flops 17999998976 | tf_op jit(solution)/shard_map/keep_first/pallas_call | solution.py:53
  16.0 1.8 %collective-permute-start.3 = (bf16[2,64,1536]{2,1,0:T(8,128)(2,1)S(1)}, bf16[2,64,1536]{2,1,0:T(8,128)(2,1)S(1)}, u32[]{:S(2)}, u32[]{:S(2)}) collective-permute-start(bf16[2,64,1536]{2,1,0:T(8,128)(2,1)S(1)} %add_convert_fusion.2.refs_3_.refs_0_), channel_id=1, source_target_pairs={{0,8},{4,12},{8,0},{12,4},{1,9},{5,13},{9,1},{13,5},{2,10},{6,14},... | collective-permute-start | bytes 1179656 | tf_op jit(solution)/shard_map/ppermute | solution.py:287
  17.8 2.3 %give.3.refs_3_ = bf16[2,64,1536]{2,1,0:T(8,128)(2,1)S(1)} custom-call(bf16[2,64,1536]{2,1,0:T(8,128)(2,1)S(1)} %collective-permute-done.refs_0_.refs_1_, bf16[1536,1536]{1,0:T(8,128)(2,1)S(1)} %get-tuple-element.28.refs_1_.refs_9_, bf16[1536,1536]{1,0:T(8,128)(2,1)S(1)} %get-tuple-element.31.refs_2_, ...), custom_call_target="tpu_custom_call" | custom-call | flops 9600000000 | tf_op jit(solution)/shard_map/give/pallas_call | solution.py:53
  20.5 2.3 %keep.3.refs_5_ = bf16[2,64,1536]{2,1,0:T(8,128)(2,1)S(1)} custom-call(bf16[2,64,1536]{2,1,0:T(8,128)(2,1)S(1)} %collective-permute-done.refs_0_.refs_1_, bf16[1536,1536]{1,0:T(8,128)(2,1)S(1)} %get-tuple-element.27.refs_1_.refs_0_.refs_8_, bf16[1536,1536]{1,0:T(8,128)(2,1)S(1)} %get-tuple-element.29.refs_2_, bf16[2,64,1536]{2,1,0:T(8,128)(2,1)S(1)} %give.3.refs_3_), custom_call_target="tpu_custom_call" | custom-call | flops 9600000000 | tf_op jit(solution)/shard_map/keep/pallas_call | solution.py:53
  22.9 0.8 collective-permute-start.5
  23.7 0.6 collective-permute-done.6.refs_0_.refs_2_
  24.3 3.7 %collective-permute-done.3.refs_4_.refs_1_ = bf16[2,64,1536]{2,1,0:T(8,128)(2,1)S(1)} collective-permute-done((bf16[2,64,1536]{2,1,0:T(8,128)(2,1)S(1)}, bf16[2,64,1536]{2,1,0:T(8,128)(2,1)S(1)}, u32[]{:S(2)}, u32[]{:S(2)}) %collective-permute-start.3) | collective-permute-done | bytes 393248 | tf_op jit(solution)/shard_map/ppermute | solution.py:287
  28.0 2.3 %give.4.refs_3_ = bf16[2,64,1536]{2,1,0:T(8,128)(2,1)S(1)} custom-call(bf16[2,64,1536]{2,1,0:T(8,128)(2,1)S(1)} %collective-permute-done.6.refs_0_.refs_2_, bf16[1536,1536]{1,0:T(8,128)(2,1)S(1)} %get-tuple-element.28.refs_1_.refs_9_, bf16[1536,1536]{1,0:T(8,128)(2,1)S(1)} %get-tuple-element.31.refs_2_, ...), custom_call_target="tpu_custom_call" | custom-call | flops 9600000000 | tf_op jit(solution)/shard_map/give/pallas_call | solution.py:53
  30.4 2.3 %keep.4.refs_5_ = bf16[2,64,1536]{2,1,0:T(8,128)(2,1)S(1)} custom-call(bf16[2,64,1536]{2,1,0:T(8,128)(2,1)S(1)} %collective-permute-done.6.refs_0_.refs_2_, bf16[1536,1536]{1,0:T(8,128)(2,1)S(1)} %get-tuple-element.27.refs_1_.refs_0_.refs_8_, bf16[1536,1536]{1,0:T(8,128)(2,1)S(1)} %get-tuple-element.29.refs_2_, bf16[2,64,1536]{2,1,0:T(8,128)(2,1)S(1)} %give.4.refs_3_), custom_call_target="tpu_custom_call" | custom-call | flops 9600000000 | tf_op jit(solution)/shard_map/keep/pallas_call | solution.py:53
  32.9 1.8 %collective-permute-start.10 = (bf16[2,64,1536]{2,1,0:T(8,128)(2,1)S(1)}, bf16[2,64,1536]{2,1,0:T(8,128)(2,1)S(1)}, u32[]{:S(2)}, u32[]{:S(2)}) collective-permute-start(bf16[2,64,1536]{2,1,0:T(8,128)(2,1)S(1)} %add_convert_fusion.refs_3_.refs_0_), channel_id=1, source_target_pairs={{0,8},{4,12},{8,0},{12,4},{1,9},{5,13},{9,1},{13,5},{2,10},{6,14},... | collective-permute-start | bytes 1179656 | tf_op jit(solution)/shard_map/ppermute | solution.py:287
  34.7 3.4 %collective-permute-done.1.refs_0_.refs_3_ = bf16[2,64,1536]{2,1,0:T(8,128)(2,1)S(1)} collective-permute-done((bf16[2,64,1536]{2,1,0:T(8,128)(2,1)S(1)}, bf16[2,64,1536]{2,1,0:T(8,128)(2,1)S(1)}, u32[]{:S(2)}, u32[]{:S(2)}) %collective-permute-start.1) | collective-permute-done | bytes 393248 | tf_op jit(solution)/shard_map/ppermute | solution.py:281
  38.0 2.3 %give.5.refs_4_ = bf16[2,64,1536]{2,1,0:T(8,128)(2,1)S(1)} custom-call(bf16[2,64,1536]{2,1,0:T(8,128)(2,1)S(1)} %collective-permute-done.1.refs_0_.refs_3_, bf16[1536,1536]{1,0:T(8,128)(2,1)S(1)} %get-tuple-element.28.refs_1_.refs_9_, bf16[1536,1536]{1,0:T(8,128)(2,1)S(1)} %get-tuple-element.31.refs_2_, ...), custom_call_target="tpu_custom_call" | custom-call | flops 9600000000 | tf_op jit(solution)/shard_map/give/pallas_call | solution.py:53
  41.0 0.6 collective-permute-start.11
  41.5 2.3 %keep.5.refs_6_ = bf16[2,64,1536]{2,1,0:T(8,128)(2,1)S(1)} custom-call(bf16[2,64,1536]{2,1,0:T(8,128)(2,1)S(1)} %collective-permute-done.1.refs_0_.refs_3_, bf16[1536,1536]{1,0:T(8,128)(2,1)S(1)} %get-tuple-element.27.refs_1_.refs_0_.refs_8_, bf16[1536,1536]{1,0:T(8,128)(2,1)S(1)} %get-tuple-element.29.refs_2_, bf16[2,128,1536]{2,1,0:T(8,128)(2,1)S(1)} %gelu.4.refs_3_.refs_2_), custom_call_target="tpu_custom_call" | custom-call | flops 9600000000 | tf_op jit(solution)/shard_map/keep/pallas_call | solution.py:53
  44.3 3.1 %input_product.2 = (bf16[64,1536]{1,0:T(8,128)(2,1)S(1)}, bf16[64,1536]{1,0:T(8,128)(2,1)S(1)}) custom-call(bf16[1536,1536]{1,0:T(8,128)(2,1)S(1)} %get-tuple-element.27.refs_1_.refs_0_.refs_8_, bf16[1536,1536]{1,0:T(8,128)(2,1)S(1)} %get-tuple-element.28.refs_1_.refs_9_, bf16[2,128,1536]{2,1,0:T(8,128)(2,1)S(1)} %gelu.4.refs_3_.refs_2_, ...), custom_call_target="tpu_custom_call" | custom-call | flops 400000000 | tf_op jit(solution)/shard_map/input_product/pallas_call | solution.py:53
  47.8 0.8 collective-permute-start.12
  48.6 1.3 %collective-permute-start.9 = (bf16[2,64,768]{2,1,0:T(8,128)(2,1)S(1)}, bf16[2,64,768]{2,1,0:T(8,128)(2,1)S(1)}, u32[]{:S(2)}, u32[]{:S(2)}) collective-permute-start(bf16[2,64,768]{2,1,0:T(8,128)(2,1)S(1)} %get-tuple-element.50.refs_5_.refs_0_), channel_id=1, source_target_pairs={{0,8},{4,12},{8,0},{12,4},{1,9},{5,13},{9,1},{13,5},{2,10},{6,14},... | collective-permute-start | bytes 589832 | tf_op jit(solution)/shard_map/ppermute | solution.py:287
  49.9 4.9 %collective-permute-start.15 = (bf16[64,1536]{1,0:T(8,128)(2,1)S(1)}, bf16[64,1536]{1,0:T(8,128)(2,1)S(1)}, u32[]{:S(2)}, u32[]{:S(2)}) collective-permute-start(bf16[64,1536]{1,0:T(8,128)(2,1)S(1)} %get-tuple-element.35.refs_2_), channel_id=1, source_target_pairs={{0,3},{1,0},{2,1},{3,2},{4,7},{5,4},{6,5},{7,6},{8,11},{9,8},{10,9... | collective-permute-start | bytes 589832 | tf_op jit(solution)/shard_map/ppermute | solution.py:281
  54.8 0.8 collective-permute-done.12.refs_1_
  55.8 4.9 %weight_grads.3 = (f32[1536,3072]{1,0:T(8,128)}, f32[3072,1536]{1,0:T(8,128)}, bf16[64,1536]{1,0:T(8,128)(2,1)S(1)}, f32[8,128]{1,0:T(8,128)S(1)}) custom-call(s32[1]{0:T(128)} %bitcast.refs_0_, bf16[1536,256]{1,0:T(8,128)(2,1)S(1)} %get-tuple-element.33.refs_1_, bf16[256,1536]{1,0:T(8,128)(2,1)S(1)} %get-tuple-element.34.refs_4_.refs_2_, ...), custom_call_target="tpu_custom_call" | custom-call | flops 16000000000 | tf_op jit(solution)/shard_map/weight_grads/pallas_call | solution.py:53
  61.4 4.4 %collective-permute-start.16 = (bf16[64,1536]{1,0:T(8,128)(2,1)S(1)}, bf16[64,1536]{1,0:T(8,128)(2,1)S(1)}, u32[]{:S(2)}, u32[]{:S(2)}) collective-permute-start(bf16[64,1536]{1,0:T(8,128)(2,1)S(1)} %get-tuple-element.38), channel_id=1, source_target_pairs={{0,1},{1,2},{2,3},{3,0},{4,5},{5,6},{6,7},{7,4},{8,9},{9,10},{10,1... | collective-permute-start | bytes 589832 | tf_op jit(solution)/shard_map/ppermute | solution.py:281
  65.7 4.1 %weight_grads.4 = (f32[1536,3072]{1,0:T(8,128)}, f32[3072,1536]{1,0:T(8,128)}, f32[64,1536]{1,0:T(8,128)S(1)}, f32[8,128]{1,0:T(8,128)S(1)}) custom-call(s32[1]{0:T(128)} %bitcast.refs_0_, bf16[1536,256]{1,0:T(8,128)(2,1)S(1)} %get-tuple-element.33.refs_1_, ...), custom_call_target="tpu_custom_call", output_to_operand_aliasing={{0}: (10, {}), {1}: (11, {})} | custom-call | flops 16000000000 | tf_op jit(solution)/shard_map/weight_grads/pallas_call | solution.py:53
  69.9 1.7 %collective-permute-done.16.refs_6_ = bf16[64,1536]{1,0:T(8,128)(2,1)S(1)} collective-permute-done((bf16[64,1536]{1,0:T(8,128)(2,1)S(1)}, bf16[64,1536]{1,0:T(8,128)(2,1)S(1)}, u32[]{:S(2)}, u32[]{:S(2)}) %collective-permute-start.16) | collective-permute-done | bytes 196640 | tf_op jit(solution)/shard_map/ppermute | solution.py:281
  71.6 1.6 %input_product.3 = (f32[64,1536]{1,0:T(8,128)S(1)}, bf16[64,1536]{1,0:T(8,128)(2,1)S(1)}) custom-call(bf16[1536,1536]{1,0:T(8,128)(2,1)S(1)} %get-tuple-element.27.refs_1_.refs_0_.refs_8_, bf16[1536,1536]{1,0:T(8,128)(2,1)S(1)} %get-tuple-element.28.refs_1_.refs_9_, bf16[2,64,768]{2,1,0:T(8,128)(2,1)S(1)} %gelu.7.refs_12_.refs_2_.refs_5_, ...), custom_call_target="tpu_custom_call" | custom-call | flops 12000000000 | tf_op jit(solution)/shard_map/input_product/pallas_call | solution.py:53
  73.2 2.4 %collective-permute-start.18 = (bf16[64,1536]{1,0:T(8,128)(2,1)S(1)}, bf16[64,1536]{1,0:T(8,128)(2,1)S(1)}, u32[]{:S(2)}, u32[]{:S(2)}) collective-permute-start(bf16[64,1536]{1,0:T(8,128)(2,1)S(1)} %get-tuple-element.44.refs_11_), channel_id=1, source_target_pairs={{0,2},{1,3},{2,0},{3,1},{4,6},{5,7},{6,4},{7,5},{8,10},{9,11},{10,... | collective-permute-start | bytes 589832 | tf_op jit(solution)/shard_map/ppermute | solution.py:281
  75.6 7.6 %weight_grads.5 = (f32[1536,3072]{1,0:T(8,128)}, f32[3072,1536]{1,0:T(8,128)}, f32[8,128]{1,0:T(8,128)}) custom-call(s32[1]{0:T(128)} %bitcast.refs_0_, bf16[1536,256]{1,0:T(8,128)(2,1)S(1)} %get-tuple-element.33.refs_1_, bf16[256,1536]{1,0:T(8,128)(2,1)S(1)} %get-tuple-element.34.refs_4_.refs_2_, ...), custom_call_target="tpu_custom_call", output_to_operand_aliasing={{0}: (9, {}), {1}: (10, {})} | custom-call | flops 32000000000 | tf_op jit(solution)/shard_map/weight_grads/pallas_call | solution.py:53
  83.2 1.8 %collective-permute-done.18 = bf16[64,1536]{1,0:T(8,128)(2,1)S(1)} collective-permute-done((bf16[64,1536]{1,0:T(8,128)(2,1)S(1)}, bf16[64,1536]{1,0:T(8,128)(2,1)S(1)}, u32[]{:S(2)}, u32[]{:S(2)}) %collective-permute-start.18) | collective-permute-done | bytes 196640 | tf_op jit(solution)/shard_map/ppermute | solution.py:281
  85.0 0.7 add_convert_fusion.3
  (30 shorter events, 2.9 us)
Async XLA Ops:
  1.7 16.1 %collective-permute-start = (bf16[2,64,1536]{2,1,0:T(8,128)(2,1)S(1)}, bf16[2,64,1536]{2,1,0:T(8,128)(2,1)S(1)}, u32[]{:S(2)}, u32[]{:S(2)}) collective-permute-start(bf16[2,64,1536]{2,1,0:T(8,128)(2,1)S(1)} %pad_maximum_fusion.refs_1_.refs_0_), channel_id=1, source_target_pairs={{0,1},{1,2},{2,3},{3,0},{4,5},{5,6},{6,7},{7,4},{8,9},{9,10},{10,1... | collective-permute-start | bytes 1179656 | tf_op jit(solution)/shard_map/ppermute | solution.py:281
  9.3 15.0 %collective-permute-start.6 = (bf16[2,64,1536]{2,1,0:T(8,128)(2,1)S(1)}, bf16[2,64,1536]{2,1,0:T(8,128)(2,1)S(1)}, u32[]{:S(2)}, u32[]{:S(2)}) collective-permute-start(bf16[2,64,1536]{2,1,0:T(8,128)(2,1)S(1)} %get-tuple-element.32), channel_id=1, source_target_pairs={{0,3},{1,0},{2,1},{3,2},{4,7},{5,4},{6,5},{7,6},{8,11},{9,8},{10,9... | collective-permute-start | bytes 1179656 | tf_op jit(solution)/shard_map/ppermute | solution.py:281
  11.4 4.5 %collective-permute-start.2 = (bf16[2,64,1536]{2,1,0:T(8,128)(2,1)S(1)}, bf16[2,64,1536]{2,1,0:T(8,128)(2,1)S(1)}, u32[]{:S(2)}, u32[]{:S(2)}) collective-permute-start(bf16[2,64,1536]{2,1,0:T(8,128)(2,1)S(1)} %get-tuple-element.26.refs_4_), channel_id=1, source_target_pairs={{0,4},{4,0},{8,12},{12,8},{1,5},{5,1},{9,13},{13,9},{2,6},{6,2},{1... | collective-permute-start | bytes 1179656 | tf_op jit(solution)/shard_map/ppermute | solution.py:278
  16.0 12.0 %collective-permute-start.3 = (bf16[2,64,1536]{2,1,0:T(8,128)(2,1)S(1)}, bf16[2,64,1536]{2,1,0:T(8,128)(2,1)S(1)}, u32[]{:S(2)}, u32[]{:S(2)}) collective-permute-start(bf16[2,64,1536]{2,1,0:T(8,128)(2,1)S(1)} %add_convert_fusion.2.refs_3_.refs_0_), channel_id=1, source_target_pairs={{0,8},{4,12},{8,0},{12,4},{1,9},{5,13},{9,1},{13,5},{2,10},{6,14},... | collective-permute-start | bytes 1179656 | tf_op jit(solution)/shard_map/ppermute | solution.py:287
  20.1 2.7 %collective-permute-start.4 = (bf16[2,64,1536]{2,1,0:T(8,128)(2,1)S(1)}, bf16[2,64,1536]{2,1,0:T(8,128)(2,1)S(1)}, u32[]{:S(2)}, u32[]{:S(2)}) collective-permute-start(bf16[2,64,1536]{2,1,0:T(8,128)(2,1)S(1)} %give.3.refs_3_), channel_id=1, source_target_pairs={{0,4},{4,0},{8,12},{12,8},{1,5},{5,1},{9,13},{13,9},{2,6},{6,2},{1... | collective-permute-start | bytes 1179656 | tf_op jit(solution)/shard_map/ppermute | solution.py:278
  20.5 17.6 %collective-permute-start.1 = (bf16[2,64,1536]{2,1,0:T(8,128)(2,1)S(1)}, bf16[2,64,1536]{2,1,0:T(8,128)(2,1)S(1)}, u32[]{:S(2)}, u32[]{:S(2)}) collective-permute-start(bf16[2,64,1536]{2,1,0:T(8,128)(2,1)S(1)} %collective-permute-done.refs_0_.refs_1_), channel_id=1, source_target_pairs={{0,1},{1,2},{2,3},{3,0},{4,5},{5,6},{6,7},{7,4},{8,9},{9,10},{10,1... | collective-permute-start | bytes 1179656 | tf_op jit(solution)/shard_map/ppermute | solution.py:281
  22.9 15.1 %collective-permute-start.5 = (bf16[2,64,1536]{2,1,0:T(8,128)(2,1)S(1)}, bf16[2,64,1536]{2,1,0:T(8,128)(2,1)S(1)}, u32[]{:S(2)}, u32[]{:S(2)}) collective-permute-start(bf16[2,64,1536]{2,1,0:T(8,128)(2,1)S(1)} %add_convert_fusion.1.refs_3_.refs_2_), channel_id=1, source_target_pairs={{0,8},{4,12},{8,0},{12,4},{1,9},{5,13},{9,1},{13,5},{2,10},{6,14},... | collective-permute-start | bytes 1179656 | tf_op jit(solution)/shard_map/ppermute | solution.py:287
  30.4 2.4 %collective-permute-start.7 = (bf16[2,64,1536]{2,1,0:T(8,128)(2,1)S(1)}, bf16[2,64,1536]{2,1,0:T(8,128)(2,1)S(1)}, u32[]{:S(2)}, u32[]{:S(2)}) collective-permute-start(bf16[2,64,1536]{2,1,0:T(8,128)(2,1)S(1)} %give.4.refs_3_), channel_id=1, source_target_pairs={{0,4},{4,0},{8,12},{12,8},{1,5},{5,1},{9,13},{13,9},{2,6},{6,2},{1... | collective-permute-start | bytes 1179656 | tf_op jit(solution)/shard_map/ppermute | solution.py:278
  32.9 14.5 %collective-permute-start.10 = (bf16[2,64,1536]{2,1,0:T(8,128)(2,1)S(1)}, bf16[2,64,1536]{2,1,0:T(8,128)(2,1)S(1)}, u32[]{:S(2)}, u32[]{:S(2)}) collective-permute-start(bf16[2,64,1536]{2,1,0:T(8,128)(2,1)S(1)} %add_convert_fusion.refs_3_.refs_0_), channel_id=1, source_target_pairs={{0,8},{4,12},{8,0},{12,4},{1,9},{5,13},{9,1},{13,5},{2,10},{6,14},... | collective-permute-start | bytes 1179656 | tf_op jit(solution)/shard_map/ppermute | solution.py:287
  40.4 3.5 %collective-permute-start.8 = (bf16[2,64,1536]{2,1,0:T(8,128)(2,1)S(1)}, bf16[2,64,1536]{2,1,0:T(8,128)(2,1)S(1)}, u32[]{:S(2)}, u32[]{:S(2)}) collective-permute-start(bf16[2,64,1536]{2,1,0:T(8,128)(2,1)S(1)} %give.5.refs_4_), channel_id=1, source_target_pairs={{0,4},{4,0},{8,12},{12,8},{1,5},{5,1},{9,13},{13,9},{2,6},{6,2},{1... | collective-permute-start | bytes 1179656 | tf_op jit(solution)/shard_map/ppermute | solution.py:278
  41.0 3.3 %collective-permute-start.11 = (bf16[2,128,1536]{2,1,0:T(8,128)(2,1)S(1)}, bf16[2,128,1536]{2,1,0:T(8,128)(2,1)S(1)}, u32[]{:S(2)}, u32[]{:S(2)}) collective-permute-start(bf16[2,128,1536]{2,1,0:T(8,128)(2,1)S(1)} %gelu.4.refs_3_.refs_2_), channel_id=1, source_target_pairs={{0,4},{4,0},{8,12},{12,8},{1,5},{5,1},{9,13},{13,9},{2,6},{6,2},{1... | collective-permute-start | bytes 2359304 | tf_op jit(solution)/shard_map/ppermute | solution.py:278
  47.7 8.1 %collective-permute-start.13 = (bf16[2,64,1536]{2,1,0:T(8,128)(2,1)S(1)}, bf16[2,64,1536]{2,1,0:T(8,128)(2,1)S(1)}, u32[]{:S(2)}, u32[]{:S(2)}) collective-permute-start(bf16[2,64,1536]{2,1,0:T(8,128)(2,1)S(1)} %gelu.5.refs_2_.refs_4_.refs_6_), channel_id=1, source_target_pairs={{0,4},{4,0},{8,12},{12,8},{1,5},{5,1},{9,13},{13,9},{2,6},{6,2},{1... | collective-permute-start | bytes 1179656 | tf_op jit(solution)/shard_map/ppermute | solution.py:278
  47.8 7.8 %collective-permute-start.12 = (bf16[2,64,768]{2,1,0:T(8,128)(2,1)S(1)}, bf16[2,64,768]{2,1,0:T(8,128)(2,1)S(1)}, u32[]{:S(2)}, u32[]{:S(2)}) collective-permute-start(bf16[2,64,768]{2,1,0:T(8,128)(2,1)S(1)} %get-tuple-element.49.refs_4_.refs_0_), channel_id=1, source_target_pairs={{0,8},{4,12},{8,0},{12,4},{1,9},{5,13},{9,1},{13,5},{2,10},{6,14},... | collective-permute-start | bytes 589832 | tf_op jit(solution)/shard_map/ppermute | solution.py:287
  48.6 12.1 %collective-permute-start.9 = (bf16[2,64,768]{2,1,0:T(8,128)(2,1)S(1)}, bf16[2,64,768]{2,1,0:T(8,128)(2,1)S(1)}, u32[]{:S(2)}, u32[]{:S(2)}) collective-permute-start(bf16[2,64,768]{2,1,0:T(8,128)(2,1)S(1)} %get-tuple-element.50.refs_5_.refs_0_), channel_id=1, source_target_pairs={{0,8},{4,12},{8,0},{12,4},{1,9},{5,13},{9,1},{13,5},{2,10},{6,14},... | collective-permute-start | bytes 589832 | tf_op jit(solution)/shard_map/ppermute | solution.py:287
  49.9 20.0 %collective-permute-start.15 = (bf16[64,1536]{1,0:T(8,128)(2,1)S(1)}, bf16[64,1536]{1,0:T(8,128)(2,1)S(1)}, u32[]{:S(2)}, u32[]{:S(2)}) collective-permute-start(bf16[64,1536]{1,0:T(8,128)(2,1)S(1)} %get-tuple-element.35.refs_2_), channel_id=1, source_target_pairs={{0,3},{1,0},{2,1},{3,2},{4,7},{5,4},{6,5},{7,6},{8,11},{9,8},{10,9... | collective-permute-start | bytes 589832 | tf_op jit(solution)/shard_map/ppermute | solution.py:281
  55.7 10.1 %collective-permute-start.17 = (bf16[2,64,768]{2,1,0:T(8,128)(2,1)S(1)}, bf16[2,64,768]{2,1,0:T(8,128)(2,1)S(1)}, u32[]{:S(2)}, u32[]{:S(2)}) collective-permute-start(bf16[2,64,768]{2,1,0:T(8,128)(2,1)S(1)} %gelu.6.refs_5_.refs_10_.refs_6_), channel_id=1, source_target_pairs={{0,4},{4,0},{8,12},{12,8},{1,5},{5,1},{9,13},{13,9},{2,6},{6,2},{1... | collective-permute-start | bytes 589832 | tf_op jit(solution)/shard_map/ppermute | solution.py:278
  60.8 9.1 %collective-permute-start.14 = (bf16[2,64,768]{2,1,0:T(8,128)(2,1)S(1)}, bf16[2,64,768]{2,1,0:T(8,128)(2,1)S(1)}, u32[]{:S(2)}, u32[]{:S(2)}) collective-permute-start(bf16[2,64,768]{2,1,0:T(8,128)(2,1)S(1)} %gelu.7.refs_12_.refs_2_.refs_5_), channel_id=1, source_target_pairs={{0,4},{4,0},{8,12},{12,8},{1,5},{5,1},{9,13},{13,9},{2,6},{6,2},{1... | collective-permute-start | bytes 589832 | tf_op jit(solution)/shard_map/ppermute | solution.py:278
  61.4 10.3 %collective-permute-start.16 = (bf16[64,1536]{1,0:T(8,128)(2,1)S(1)}, bf16[64,1536]{1,0:T(8,128)(2,1)S(1)}, u32[]{:S(2)}, u32[]{:S(2)}) collective-permute-start(bf16[64,1536]{1,0:T(8,128)(2,1)S(1)} %get-tuple-element.38), channel_id=1, source_target_pairs={{0,1},{1,2},{2,3},{3,0},{4,5},{5,6},{6,7},{7,4},{8,9},{9,10},{10,1... | collective-permute-start | bytes 589832 | tf_op jit(solution)/shard_map/ppermute | solution.py:281
  73.2 11.8 %collective-permute-start.18 = (bf16[64,1536]{1,0:T(8,128)(2,1)S(1)}, bf16[64,1536]{1,0:T(8,128)(2,1)S(1)}, u32[]{:S(2)}, u32[]{:S(2)}) collective-permute-start(bf16[64,1536]{1,0:T(8,128)(2,1)S(1)} %get-tuple-element.44.refs_11_), channel_id=1, source_target_pairs={{0,2},{1,3},{2,0},{3,1},{4,6},{5,7},{6,4},{7,5},{8,10},{9,11},{10,... | collective-permute-start | bytes 589832 | tf_op jit(solution)/shard_map/ppermute | solution.py:281

commit v6 on v5

--- a/solution.py
+++ b/solution.py
@@ -82,7 +82,7 @@
             copies.append(pltpu.make_async_copy(down_hbm.at[units, :], down_ref.at[part, :], sems.at[1, i]))
         for copy in copies:
             copy.start()
-        if other:
+        if not other:
             refs[0][...] = chunk_ref[...]
         for i in range(pieces):
             part = slice(i * tile, (i + 1) * tile)
@@ -92,7 +92,7 @@
             out_ref[1, :, part] = dot(chunk_ref[1], down_ref[part, :], NT).astype(BF16)
 
     outs = [VMEM((features, half), BF16), VMEM((half, features), BF16)]
-    outs += [jax.ShapeDtypeStruct(chunk.shape, BF16)] if other else []
+    outs += [] if other else [jax.ShapeDtypeStruct(chunk.shape, BF16)]
     return ordered(
         body,
         (core, chunk, in_hbm(up_weight), in_hbm(down_weight)),
@@ -124,13 +124,16 @@
     return terms[0] + terms[1]
 
 
-def input_product(ordered, mine, other, up_mine, up_other, low, chunks, micros, partial=None, returned=()):
-    rows = mine.shape[1] // chunks
+def input_product(ordered, rows, mine, other, up_mine, up_other, low, micros, partial=None, returned=()):
     features = up_mine.shape[0]
     tile = tile_of(features)
-
-    def body(up_mine_ref, up_other_ref, mine_ref, other_ref, *refs):
-        returned_refs, out_refs = refs[: len(returned)], refs[-chunks:]
+    count = len(mine)
+    chunks = sum(a.shape[-2] for a in mine) // rows
+
+    def body(up_mine_ref, up_other_ref, *refs):
+        acts = [[r[...] if len(r.shape) == 2 else r[0] for r in part] for part in (refs[:count], refs[count : 2 * count])]
+        acts = [a[0] if count == 1 else jnp.concatenate(a, axis=0) for a in acts]
+        returned_refs, out_refs = refs[2 * count :][: len(returned)], refs[-chunks:]
         if returned:
             total = returned_refs[0][...].astype(F32)
             for ref in returned_refs[1:]:
@@ -138,34 +141,36 @@
             refs[-chunks - 1][...] = total
         for start in range(0, features, tile):
             part = slice(start, start + tile)
-            share = product_terms((mine_ref[0], other_ref[0]), (up_mine_ref, up_other_ref), part, low)
+            share = product_terms(acts, (up_mine_ref, up_other_ref), part, low)
             if partial is not None:
-                share = share + refs[len(returned)][:, part]
+                share = share + refs[2 * count + len(returned)][:, part]
             for c, out_ref in enumerate(out_refs):
                 out_ref[:, part] = share[c * rows : (c + 1) * rows].astype(BF16)
 
-    args = (in_vmem(up_mine), in_vmem(up_other), mine, other, *returned, *([] if partial is None else [partial]))
+    args = (in_vmem(up_mine), in_vmem(up_other), *mine, *other, *returned, *([] if partial is None else [partial]))
     outs = [jax.ShapeDtypeStruct((rows, features), F32)] if returned else []
     return ordered(body, args, outs + [jax.ShapeDtypeStruct((rows, features), BF16)] * chunks, "input_product", micros)
 
 
-def gelu(ordered, sums, after=()):
+def gelu(ordered, sums, apart=False):
     flat = [a for pair in sums for a in pair]
     _, rows, units = flat[0].shape
 
     def body(*refs):
-        out_ref = refs[-1]
+        grad_ref, value_ref = refs[-2:] if apart else (refs[-1].at[0], refs[-1].at[1])
         for chunk in range(len(sums)):
             at = slice(chunk * rows, (chunk + 1) * rows)
             own_h, own_g, peer_h, peer_g = [refs[2 * chunk + side][i].astype(F32) for side in (0, 1) for i in (0, 1)]
             hidden, grad_hidden = own_h + peer_h, own_g + peer_g
             cdf = 0.5 * (1.0 + lax.erf(hidden * 0.7071067811865476))
             pdf = jnp.exp(-0.5 * hidden * hidden) * 0.3989422804014327
-            out_ref[0, at] = (grad_hidden * (cdf + hidden * pdf)).astype(BF16)
-            out_ref[1, at] = (hidden * cdf).astype(BF16)
-
-    out = jax.ShapeDtypeStruct((2, rows * len(sums), units), BF16)
-    return ordered(body, flat, [out], "gelu", 0.1, after=after)[0]
+            grad_ref[at] = (grad_hidden * (cdf + hidden * pdf)).astype(BF16)
+            value_ref[at] = (hidden * cdf).astype(BF16)
+
+    outs = [jax.ShapeDtypeStruct((rows * len(sums), units), BF16)] * 2
+    if not apart:
+        outs = [jax.ShapeDtypeStruct((2, rows * len(sums), units), BF16)]
+    return ordered(body, flat, outs, "gelu", 0.1)
 
 
 def collect(ordered, chunks, after):
@@ -187,11 +192,11 @@
 
 def weight_grads(ordered, core, blocks, turned, all_grads, half, scale, before, name, share=None):
     features, tokens = turned.shape
-    width = min(a.shape[2] for a, _ in blocks[0][2])
+    width = min(a[0].shape[-1] for a, _ in blocks[0][2])
     up_tile, down_tile = tile_of(features), tile_of(width, 256)
     up_steps, down_steps = features // up_tile, width // down_tile
     slots = 3
-    flat = [a for block in blocks for a, _ in block[2]]
+    flat = [a for block in blocks for acts, _ in block[2] for a in acts]
 
     def body(core_ref, turned_ref, grads_ref, *refs):
         up_hbm, down_hbm = refs[outs_at : outs_at + 2]
@@ -208,15 +213,18 @@
             copy.start()
             busy[kind, slot] = copy
 
+        left = refs[: len(flat)]
         for b, (other, first, acts) in enumerate(blocks):
             side = 1 - core_ref[0] if other else core_ref[0]
             base = side * half + first
             row = 0
-            for i, (array, column) in enumerate(acts):
-                ref, rows = refs[b * len(acts) + i], slice(row, row + array.shape[1])
-                act_g[rows, :] = ref[0, :, column : column + width]
-                act_v[rows, :] = ref[1, :, column : column + width]
-                row += array.shape[1]
+            for arrays, column in acts:
+                rows = slice(row, row + arrays[0].shape[-2])
+                columns = slice(column, column + width)
+                taken, left = left[: len(arrays)], left[len(arrays) :]
+                act_g[rows, :] = taken[0][:, columns] if len(taken) == 2 else taken[0][0, :, columns]
+                act_v[rows, :] = taken[1][:, columns] if len(taken) == 2 else taken[0][1, :, columns]
+                row += arrays[0].shape[-2]
             for step in range(max(up_steps, down_steps)):
                 if step < up_steps:
                     part = slice(step * up_tile, (step + 1) * up_tile)
@@ -231,7 +239,8 @@
                 if share is not None and b == 0 and step < up_steps:
                     part = slice(step * up_tile, (step + 1) * up_tile)
                     mine_ref, other_ref, up_mine_ref, up_other_ref = refs[len(flat) : len(flat) + 4]
-                    value = product_terms((mine_ref[0], other_ref[0]), (up_mine_ref, up_other_ref), part, 0)
+                    pair = [r[...] if len(r.shape) == 2 else r[0] for r in (mine_ref, other_ref)]
+                    value = product_terms(pair, (up_mine_ref, up_other_ref), part, 0)
                     refs[outs_at + 2][:, part] = value.astype(share[4])
         for copy in busy.values():
             copy.wait()
@@ -240,7 +249,7 @@
     outs = [pltpu.HBM((features, 2 * half), F32), pltpu.HBM((2 * half, features), F32)]
     if share is not None:
         args += [*share[:2], in_vmem(share[2]), in_vmem(share[3])]
-        outs.append(jax.ShapeDtypeStruct((share[0].shape[1], features), share[4]))
+        outs.append(jax.ShapeDtypeStruct((share[0].shape[-2], features), share[4]))
     spaces = [None] * len(args)
     outs_at = len(args) - 3 + (0 if before is None else 2)
     aliases = {}
@@ -293,21 +302,21 @@
     offsets = sorted(range(narrow // 2 - narrow + 1, narrow // 2 + 1), key=lambda places: (abs(places), -places))
     chunks = {0: jnp.stack([inputs, out_grad])}
 
-    up_other, down_other, sent_back, give = first_product(ordered, core, True, chunks[0], up_weight, down_weight, "give_first")
+    up_other, down_other, give = first_product(ordered, core, True, chunks[0], up_weight, down_weight, "give_first")
     got = swap_cores(give)
-    up_mine, down_mine, keep = first_product(ordered, core, False, chunks[0], up_weight, down_weight, "keep_first")
+    up_mine, down_mine, sent_back, keep = first_product(ordered, core, False, chunks[0], up_weight, down_weight, "keep_first")
     sums = [across_chips(keep, got)]
 
-    def acts_of(sums):
-        mine = gelu(ordered, sums)
-        return mine, swap_cores(mine)
+    def acts_of(sums, apart=False):
+        mine = gelu(ordered, sums, apart)
+        return mine, [swap_cores(a) for a in mine]
 
     slices = 2 if half % 256 == 0 else 1
     width = half // slices
     for offset in offsets[1:]:
         places = 1 if offset > 0 else -1
         chunk = chunks[offset] = shift(sent_back if offset == -1 else chunks[offset - places], places)
-        give = product(ordered, chunk, up_other, down_other, "give", after=[sums[-1][0]] + [peer for _, peer in sums[-2:-1]])
+        give = product(ordered, chunk, up_other, down_other, "give", after=[sums[-1][0]] + [sums[0][1]] * (len(sums) == 2))
         got = swap_cores(give)
         if offset == offsets[-1]:
             early = acts_of(sums[:-1])
@@ -319,9 +328,9 @@
             late = [across_chips(keep[:, :, part], got[:, :, part]) for part in parts]
 
     turned, all_grads = collect(ordered, [chunks[offset] for offset in offsets], [own for own, _ in late])
-    shares = input_product(ordered, *early, up_mine, up_other, 0, narrow - 2, 0.1)
+    shares = input_product(ordered, rows, *early, up_mine, up_other, 0, 0.1)
     shares = [share if offset == 0 else shift(share, -offset) for offset, share in zip(offsets, shares)]
-    middle = acts_of(sums[-1:])
+    middle = acts_of(sums[-1:], True)
 
     scale = (rows * narrow) ** -0.5
     late_acts = []
@@ -334,14 +343,16 @@
         return weight_grads(ordered, core, blocks, turned, all_grads, half, scale, before, "weight_grads", share)
 
     late_acts.append(acts_of(late[:1]))
-    up_grad, down_grad, share, _ = grads([(0, 0)], None, (*middle, up_mine, up_other, BF16))
+    share = (middle[0][0], middle[1][0], up_mine, up_other, BF16)
+    up_grad, down_grad, share, _ = grads([(0, 0)], None, share)
     shares.append(shift(share, -offsets[-2]))
     partial = None
     if slices > 1:
         late_acts.append(acts_of(late[1:]))
-        up_grad, down_grad, partial, _ = grads([(1, 0)], (up_grad, down_grad), (*late_acts[0], up_mine, up_other, F32))
+        share = (late_acts[0][0][0], late_acts[0][1][0], up_mine, up_other, F32)
+        up_grad, down_grad, partial, _ = grads([(1, 0)], (up_grad, down_grad), share)
     low = width * (slices - 1)
-    so_far, share = input_product(ordered, *late_acts[-1], up_mine, up_other, low, 1, 3.0, partial, shares)
+    so_far, share = input_product(ordered, rows, *late_acts[-1], up_mine, up_other, low, 3.0, partial, shares)
     share = shift(share, -offsets[-1])
     last = [(0, 1), (1, 1)] if slices > 1 else [(1, 0)]
     up_grad, down_grad, _ = grads(last, (up_grad, down_grad), None)

time: 85.9 us -> 76.4 us (0.89)
  starting transfers between devices: 24.9 us -> 15.4 us
    ppermute x6, starting transfers between devices: 16.9 us -> 7.77 us  [shift(): lax.ppermute(x, 'narrow', [(i, (i + places) % narrow) for i in range(narr...]
    ppermute x6, waiting for transfers between devices: 7.53 us -> 9.43 us  [shift(): lax.ppermute(x, 'narrow', [(i, (i + places) % narrow) for i in range(narr...]
    ppermute x5, waiting for transfers between devices: 4.45 us -> 2.64 us  [across_chips(): lax.ppermute(partial, 'wide', [(i, i ^ 2 * hop) for i in range(wide)])]
  transfers between devices with their start and end apart: 19 -> 20, of which waited for: 6 -> 5; matrix products, arithmetic and copies ran while one was open for 0% -> 0% of each run, Pallas kernels for 51% -> 58%
where the time goes in v6:
time: 76.4 us; the launch traced here: 76.2 us
  Pallas kernels  45.7 us (60%)
  starting transfers between devices  15.4 us (20%)
  waiting for transfers between devices  12.1 us (16%)
  other arithmetic  2.14 us (3%)
  between operations  0.94 us (1%)
    pallas_call x18, Pallas kernels, __call__(): pl.pallas_call(kernel, out_shape=outs, in_specs=specs, out_specs=[pl.Bloc...  45.7 us
    ppermute x6, waiting for transfers between devices, shift(): lax.ppermute(x, 'narrow', [(i, (i + places) % narrow) for i in range(narr...  9.43 us
    ppermute x6, starting transfers between devices, shift(): lax.ppermute(x, 'narrow', [(i, (i + places) % narrow) for i in range(narr...  7.77 us
    ppermute x5, starting transfers between devices, across_chips(): lax.ppermute(partial, 'wide', [(i, i ^ 2 * hop) for i in range(wide)])  6.08 us
    ppermute x5, waiting for transfers between devices, across_chips(): lax.ppermute(partial, 'wide', [(i, i ^ 2 * hop) for i in range(wide)])  2.64 us
    ppermute x9, starting transfers between devices, swap_cores(): return lax.ppermute(x, 'wide', [(i, i ^ 1) for i in range(wide)])  1.57 us
  transfers between devices with their start and end apart: 20, of which 5 were waited for; matrix products, arithmetic and copies ran while one was open for 0% of the time, Pallas kernels for 58%

profile of v6, /device:TPU:0, one launch (start us, length us, event | category | flops | bytes accessed | tf_op | source)
XLA Modules:
  0.0 76.2 jit_solution(11766092888002755825)
XLA Ops:
  0.6 1.1 %pad_maximum_fusion.refs_1_.refs_0_ = bf16[2,64,1536]{2,1,0:T(8,128)(2,1)S(1)} fusion(bf16[1,64,1536]{2,1,0:T(8,128)(2,1)} %bitcast.3, bf16[1,64,1536]{2,1,0:T(8,128)(2,1)} %bitcast.4), kind=kLoop, calls=%fused_computation.3 | loop fusion | flops 196608 | bytes 786432 | tf_op jit(solution)/shard_map/stack | solution.py:303
  1.7 3.1 %collective-permute-start = (bf16[2,64,1536]{2,1,0:T(8,128)(2,1)S(1)}, bf16[2,64,1536]{2,1,0:T(8,128)(2,1)S(1)}, u32[]{:S(2)}, u32[]{:S(2)}) collective-permute-start(bf16[2,64,1536]{2,1,0:T(8,128)(2,1)S(1)} %pad_maximum_fusion.refs_1_.refs_0_), channel_id=1, source_target_pairs={{0,1},{1,2},{2,3},{3,0},{4,5},{5,6},{6,7},{7,4},{8,9},{9,10},{10,1... | collective-permute-start | bytes 1179656 | tf_op jit(solution)/shard_map/ppermute | solution.py:290
  4.8 4.5 %give_first.1 = (bf16[1536,1536]{1,0:T(8,128)(2,1)S(1)}, bf16[1536,1536]{1,0:T(8,128)(2,1)S(1)}, bf16[2,64,1536]{2,1,0:T(8,128)(2,1)S(1)}) custom-call(s32[1]{0:T(128)} %bitcast.refs_0_, bf16[2,64,1536]{2,1,0:T(8,128)(2,1)S(1)} %pad_maximum_fusion.refs_1_.refs_0_, bf16[1536,3072]{1,0:T(8,128)(2,1)} %refs_2_.3, bf16[3072,1536]{1,0:T(8,128)(2,1)} %refs_3_.3), custom_call_target="tpu_custom_call" | custom-call | flops 17999998976 | tf_op jit(solution)/shard_map/give_first/pallas_call | solution.py:53
  9.4 4.5 %keep_first.1 = (bf16[1536,1536]{1,0:T(8,128)(2,1)S(1)}, bf16[1536,1536]{1,0:T(8,128)(2,1)S(1)}, bf16[2,64,1536]{2,1,0:T(8,128)(2,1)S(1)}, bf16[2,64,1536]{2,1,0:T(8,128)(2,1)S(1)}) custom-call(s32[1]{0:T(128)} %bitcast.refs_0_, bf16[2,64,1536]{2,1,0:T(8,128)(2,1)S(1)} %pad_maximum_fusion.refs_1_.refs_0_, bf16[1536,3072]{1,0:T(8,128)(2,1)} %refs_2_.3, ...), custom_call_target="tpu_custom_call" | custom-call | flops 17999998976 | tf_op jit(solution)/shard_map/keep_first/pallas_call | solution.py:53
  13.9 2.1 %collective-permute-start.6 = (bf16[2,64,1536]{2,1,0:T(8,128)(2,1)S(1)}, bf16[2,64,1536]{2,1,0:T(8,128)(2,1)S(1)}, u32[]{:S(2)}, u32[]{:S(2)}) collective-permute-start(bf16[2,64,1536]{2,1,0:T(8,128)(2,1)S(1)} %get-tuple-element.34), channel_id=1, source_target_pairs={{0,3},{1,0},{2,1},{3,2},{4,7},{5,4},{6,5},{7,6},{8,11},{9,8},{10,9... | collective-permute-start | bytes 1179656 | tf_op jit(solution)/shard_map/ppermute | solution.py:290
  16.1 1.8 %collective-permute-start.3 = (bf16[2,64,1536]{2,1,0:T(8,128)(2,1)S(1)}, bf16[2,64,1536]{2,1,0:T(8,128)(2,1)S(1)}, u32[]{:S(2)}, u32[]{:S(2)}) collective-permute-start(bf16[2,64,1536]{2,1,0:T(8,128)(2,1)S(1)} %add_convert_fusion.2.refs_3_.refs_0_), channel_id=1, source_target_pairs={{0,8},{4,12},{8,0},{12,4},{1,9},{5,13},{9,1},{13,5},{2,10},{6,14},... | collective-permute-start | bytes 1179656 | tf_op jit(solution)/shard_map/ppermute | solution.py:296
  17.9 2.3 %give.3.refs_3_ = bf16[2,64,1536]{2,1,0:T(8,128)(2,1)S(1)} custom-call(bf16[2,64,1536]{2,1,0:T(8,128)(2,1)S(1)} %collective-permute-done.refs_0_.refs_1_, bf16[1536,1536]{1,0:T(8,128)(2,1)S(1)} %get-tuple-element.30.refs_1_.refs_10_, bf16[1536,1536]{1,0:T(8,128)(2,1)S(1)} %get-tuple-element.33.refs_2_, ...), custom_call_target="tpu_custom_call" | custom-call | flops 9600000000 | tf_op jit(solution)/shard_map/give/pallas_call | solution.py:53
  20.5 2.3 %keep.3.refs_5_ = bf16[2,64,1536]{2,1,0:T(8,128)(2,1)S(1)} custom-call(bf16[2,64,1536]{2,1,0:T(8,128)(2,1)S(1)} %collective-permute-done.refs_0_.refs_1_, bf16[1536,1536]{1,0:T(8,128)(2,1)S(1)} %get-tuple-element.29.refs_1_.refs_0_.refs_9_, bf16[1536,1536]{1,0:T(8,128)(2,1)S(1)} %get-tuple-element.31.refs_2_, bf16[2,64,1536]{2,1,0:T(8,128)(2,1)S(1)} %give.3.refs_3_), custom_call_target="tpu_custom_call" | custom-call | flops 9600000000 | tf_op jit(solution)/shard_map/keep/pallas_call | solution.py:53
  23.0 0.4 collective-permute-start.5
  23.4 2.1 %collective-permute-done.6.refs_0_.refs_2_ = bf16[2,64,1536]{2,1,0:T(8,128)(2,1)S(1)} collective-permute-done((bf16[2,64,1536]{2,1,0:T(8,128)(2,1)S(1)}, bf16[2,64,1536]{2,1,0:T(8,128)(2,1)S(1)}, u32[]{:S(2)}, u32[]{:S(2)}) %collective-permute-start.6) | collective-permute-done | bytes 393248 | tf_op jit(solution)/shard_map/ppermute | solution.py:290
  25.5 2.6 %collective-permute-done.3.refs_4_.refs_1_ = bf16[2,64,1536]{2,1,0:T(8,128)(2,1)S(1)} collective-permute-done((bf16[2,64,1536]{2,1,0:T(8,128)(2,1)S(1)}, bf16[2,64,1536]{2,1,0:T(8,128)(2,1)S(1)}, u32[]{:S(2)}, u32[]{:S(2)}) %collective-permute-start.3) | collective-permute-done | bytes 393248 | tf_op jit(solution)/shard_map/ppermute | solution.py:296
  28.1 2.3 %give.4.refs_3_ = bf16[2,64,1536]{2,1,0:T(8,128)(2,1)S(1)} custom-call(bf16[2,64,1536]{2,1,0:T(8,128)(2,1)S(1)} %collective-permute-done.6.refs_0_.refs_2_, bf16[1536,1536]{1,0:T(8,128)(2,1)S(1)} %get-tuple-element.30.refs_1_.refs_10_, bf16[1536,1536]{1,0:T(8,128)(2,1)S(1)} %get-tuple-element.33.refs_2_, ...), custom_call_target="tpu_custom_call" | custom-call | flops 9600000000 | tf_op jit(solution)/shard_map/give/pallas_call | solution.py:53
  30.5 2.3 %keep.4.refs_4_ = bf16[2,64,1536]{2,1,0:T(8,128)(2,1)S(1)} custom-call(bf16[2,64,1536]{2,1,0:T(8,128)(2,1)S(1)} %collective-permute-done.6.refs_0_.refs_2_, bf16[1536,1536]{1,0:T(8,128)(2,1)S(1)} %get-tuple-element.29.refs_1_.refs_0_.refs_9_, bf16[1536,1536]{1,0:T(8,128)(2,1)S(1)} %get-tuple-element.31.refs_2_, bf16[2,64,1536]{2,1,0:T(8,128)(2,1)S(1)} %give.4.refs_3_), custom_call_target="tpu_custom_call" | custom-call | flops 9600000000 | tf_op jit(solution)/shard_map/keep/pallas_call | solution.py:53
  33.0 1.8 %collective-permute-start.10 = (bf16[2,64,1536]{2,1,0:T(8,128)(2,1)S(1)}, bf16[2,64,1536]{2,1,0:T(8,128)(2,1)S(1)}, u32[]{:S(2)}, u32[]{:S(2)}) collective-permute-start(bf16[2,64,1536]{2,1,0:T(8,128)(2,1)S(1)} %add_convert_fusion.refs_3_.refs_0_), channel_id=1, source_target_pairs={{0,8},{4,12},{8,0},{12,4},{1,9},{5,13},{9,1},{13,5},{2,10},{6,14},... | collective-permute-start | bytes 1179656 | tf_op jit(solution)/shard_map/ppermute | solution.py:296
  34.8 1.2 %collective-permute-done.1.refs_0_.refs_3_ = bf16[2,64,1536]{2,1,0:T(8,128)(2,1)S(1)} collective-permute-done((bf16[2,64,1536]{2,1,0:T(8,128)(2,1)S(1)}, bf16[2,64,1536]{2,1,0:T(8,128)(2,1)S(1)}, u32[]{:S(2)}, u32[]{:S(2)}) %collective-permute-start.1) | collective-permute-done | bytes 393248 | tf_op jit(solution)/shard_map/ppermute | solution.py:290
  35.9 2.3 %give.5.refs_4_ = bf16[2,64,1536]{2,1,0:T(8,128)(2,1)S(1)} custom-call(bf16[2,64,1536]{2,1,0:T(8,128)(2,1)S(1)} %collective-permute-done.1.refs_0_.refs_3_, bf16[1536,1536]{1,0:T(8,128)(2,1)S(1)} %get-tuple-element.30.refs_1_.refs_10_, bf16[1536,1536]{1,0:T(8,128)(2,1)S(1)} %get-tuple-element.33.refs_2_, ...), custom_call_target="tpu_custom_call" | custom-call | flops 9600000000 | tf_op jit(solution)/shard_map/give/pallas_call | solution.py:53
  38.4 0.5 gelu.4.refs_3_.refs_2_
  38.9 0.5 collective-permute-start.11
  39.5 2.3 %keep.5.refs_6_ = bf16[2,64,1536]{2,1,0:T(8,128)(2,1)S(1)} custom-call(bf16[2,64,1536]{2,1,0:T(8,128)(2,1)S(1)} %collective-permute-done.1.refs_0_.refs_3_, bf16[1536,1536]{1,0:T(8,128)(2,1)S(1)} %get-tuple-element.29.refs_1_.refs_0_.refs_9_, bf16[1536,1536]{1,0:T(8,128)(2,1)S(1)} %get-tuple-element.31.refs_2_, bf16[2,128,1536]{2,1,0:T(8,128)(2,1)S(1)} %gelu.4.refs_3_.refs_2_), custom_call_target="tpu_custom_call" | custom-call | flops 9600000000 | tf_op jit(solution)/shard_map/keep/pallas_call | solution.py:53
  41.9 1.6 %collective-permute-start.12 = (bf16[2,64,768]{2,1,0:T(8,128)(2,1)S(1)}, bf16[2,64,768]{2,1,0:T(8,128)(2,1)S(1)}, u32[]{:S(2)}, u32[]{:S(2)}) collective-permute-start(bf16[2,64,768]{2,1,0:T(8,128)(2,1)S(1)} %get-tuple-element.53.refs_4_.refs_0_), channel_id=1, source_target_pairs={{0,8},{4,12},{8,0},{12,4},{1,9},{5,13},{9,1},{13,5},{2,10},{6,14},... | collective-permute-start | bytes 589832 | tf_op jit(solution)/shard_map/ppermute | solution.py:296
  43.7 3.1 %input_product.2 = (bf16[64,1536]{1,0:T(8,128)(2,1)S(1)}, bf16[64,1536]{1,0:T(8,128)(2,1)S(1)}) custom-call(bf16[1536,1536]{1,0:T(8,128)(2,1)S(1)} %get-tuple-element.29.refs_1_.refs_0_.refs_9_, bf16[1536,1536]{1,0:T(8,128)(2,1)S(1)} %get-tuple-element.30.refs_1_.refs_10_, bf16[2,128,1536]{2,1,0:T(8,128)(2,1)S(1)} %gelu.4.refs_3_.refs_2_, ...), custom_call_target="tpu_custom_call" | custom-call | flops 400000000 | tf_op jit(solution)/shard_map/input_product/pallas_call | solution.py:53
  47.2 0.6 collective-permute-start.9
  47.8 1.8 %collective-permute-start.15 = (bf16[64,1536]{1,0:T(8,128)(2,1)S(1)}, bf16[64,1536]{1,0:T(8,128)(2,1)S(1)}, u32[]{:S(2)}, u32[]{:S(2)}) collective-permute-start(bf16[64,1536]{1,0:T(8,128)(2,1)S(1)} %get-tuple-element.37.refs_2_), channel_id=1, source_target_pairs={{0,3},{1,0},{2,1},{3,2},{4,7},{5,4},{6,5},{7,6},{8,11},{9,8},{10,9... | collective-permute-start | bytes 589832 | tf_op jit(solution)/shard_map/ppermute | solution.py:290
  49.8 0.6 collective-permute-start.18
  50.3 4.9 %weight_grads.3 = (f32[1536,3072]{1,0:T(8,128)}, f32[3072,1536]{1,0:T(8,128)}, bf16[64,1536]{1,0:T(8,128)(2,1)S(1)}, f32[8,128]{1,0:T(8,128)S(1)}) custom-call(s32[1]{0:T(128)} %bitcast.refs_0_, bf16[1536,256]{1,0:T(8,128)(2,1)S(1)} %get-tuple-element.35.refs_1_, bf16[256,1536]{1,0:T(8,128)(2,1)S(1)} %get-tuple-element.36.refs_4_.refs_2_, ...), custom_call_target="tpu_custom_call" | custom-call | flops 16000000000 | tf_op jit(solution)/shard_map/weight_grads/pallas_call | solution.py:53
  55.5 0.5 collective-permute-start.16
  56.0 4.1 %weight_grads.4 = (f32[1536,3072]{1,0:T(8,128)}, f32[3072,1536]{1,0:T(8,128)}, f32[64,1536]{1,0:T(8,128)S(1)}, f32[8,128]{1,0:T(8,128)S(1)}) custom-call(s32[1]{0:T(128)} %bitcast.refs_0_, bf16[1536,256]{1,0:T(8,128)(2,1)S(1)} %get-tuple-element.35.refs_1_, ...), custom_call_target="tpu_custom_call", output_to_operand_aliasing={{0}: (11, {}), {1}: (12, {})} | custom-call | flops 16000000000 | tf_op jit(solution)/shard_map/weight_grads/pallas_call | solution.py:53
  60.1 4.4 %collective-permute-done.16.refs_6_ = bf16[64,1536]{1,0:T(8,128)(2,1)S(1)} collective-permute-done((bf16[64,1536]{1,0:T(8,128)(2,1)S(1)}, bf16[64,1536]{1,0:T(8,128)(2,1)S(1)}, u32[]{:S(2)}, u32[]{:S(2)}) %collective-permute-start.16) | collective-permute-done | bytes 196640 | tf_op jit(solution)/shard_map/ppermute | solution.py:290
  64.6 1.6 %input_product.3 = (f32[64,1536]{1,0:T(8,128)S(1)}, bf16[64,1536]{1,0:T(8,128)(2,1)S(1)}) custom-call(bf16[1536,1536]{1,0:T(8,128)(2,1)S(1)} %get-tuple-element.29.refs_1_.refs_0_.refs_9_, bf16[1536,1536]{1,0:T(8,128)(2,1)S(1)} %get-tuple-element.30.refs_1_.refs_10_, bf16[2,64,768]{2,1,0:T(8,128)(2,1)S(1)} %gelu.7.refs_13_.refs_2_.refs_6_, ...), custom_call_target="tpu_custom_call" | custom-call | flops 12000000000 | tf_op jit(solution)/shard_map/input_product/pallas_call | solution.py:53
  66.2 7.6 %weight_grads.5 = (f32[1536,3072]{1,0:T(8,128)}, f32[3072,1536]{1,0:T(8,128)}, f32[8,128]{1,0:T(8,128)}) custom-call(s32[1]{0:T(128)} %bitcast.refs_0_, bf16[1536,256]{1,0:T(8,128)(2,1)S(1)} %get-tuple-element.35.refs_1_, bf16[256,1536]{1,0:T(8,128)(2,1)S(1)} %get-tuple-element.36.refs_4_.refs_2_, ...), custom_call_target="tpu_custom_call", output_to_operand_aliasing={{0}: (11, {}), {1}: (12, {})} | custom-call | flops 32000000000 | tf_op jit(solution)/shard_map/weight_grads/pallas_call | solution.py:53
  73.8 1.7 %collective-permute-done.19 = bf16[64,1536]{1,0:T(8,128)(2,1)S(1)} collective-permute-done((bf16[64,1536]{1,0:T(8,128)(2,1)S(1)}, bf16[64,1536]{1,0:T(8,128)(2,1)S(1)}, u32[]{:S(2)}, u32[]{:S(2)}) %collective-permute-start.19) | collective-permute-done | bytes 196640 | tf_op jit(solution)/shard_map/ppermute | solution.py:290
  75.5 0.7 add_convert_fusion.3
  (32 shorter events, 2.0 us)
Async XLA Ops:
  1.7 16.2 %collective-permute-start = (bf16[2,64,1536]{2,1,0:T(8,128)(2,1)S(1)}, bf16[2,64,1536]{2,1,0:T(8,128)(2,1)S(1)}, u32[]{:S(2)}, u32[]{:S(2)}) collective-permute-start(bf16[2,64,1536]{2,1,0:T(8,128)(2,1)S(1)} %pad_maximum_fusion.refs_1_.refs_0_), channel_id=1, source_target_pairs={{0,1},{1,2},{2,3},{3,0},{4,5},{5,6},{6,7},{7,4},{8,9},{9,10},{10,1... | collective-permute-start | bytes 1179656 | tf_op jit(solution)/shard_map/ppermute | solution.py:290
  9.3 6.7 %collective-permute-start.2 = (bf16[2,64,1536]{2,1,0:T(8,128)(2,1)S(1)}, bf16[2,64,1536]{2,1,0:T(8,128)(2,1)S(1)}, u32[]{:S(2)}, u32[]{:S(2)}) collective-permute-start(bf16[2,64,1536]{2,1,0:T(8,128)(2,1)S(1)} %get-tuple-element.28.refs_4_), channel_id=1, source_target_pairs={{0,4},{4,0},{8,12},{12,8},{1,5},{5,1},{9,13},{13,9},{2,6},{6,2},{1... | collective-permute-start | bytes 1179656 | tf_op jit(solution)/shard_map/ppermute | solution.py:287
  13.9 11.6 %collective-permute-start.6 = (bf16[2,64,1536]{2,1,0:T(8,128)(2,1)S(1)}, bf16[2,64,1536]{2,1,0:T(8,128)(2,1)S(1)}, u32[]{:S(2)}, u32[]{:S(2)}) collective-permute-start(bf16[2,64,1536]{2,1,0:T(8,128)(2,1)S(1)} %get-tuple-element.34), channel_id=1, source_target_pairs={{0,3},{1,0},{2,1},{3,2},{4,7},{5,4},{6,5},{7,6},{8,11},{9,8},{10,9... | collective-permute-start | bytes 1179656 | tf_op jit(solution)/shard_map/ppermute | solution.py:290
  16.1 12.0 %collective-permute-start.3 = (bf16[2,64,1536]{2,1,0:T(8,128)(2,1)S(1)}, bf16[2,64,1536]{2,1,0:T(8,128)(2,1)S(1)}, u32[]{:S(2)}, u32[]{:S(2)}) collective-permute-start(bf16[2,64,1536]{2,1,0:T(8,128)(2,1)S(1)} %add_convert_fusion.2.refs_3_.refs_0_), channel_id=1, source_target_pairs={{0,8},{4,12},{8,0},{12,4},{1,9},{5,13},{9,1},{13,5},{2,10},{6,14},... | collective-permute-start | bytes 1179656 | tf_op jit(solution)/shard_map/ppermute | solution.py:296
  20.2 2.7 %collective-permute-start.4 = (bf16[2,64,1536]{2,1,0:T(8,128)(2,1)S(1)}, bf16[2,64,1536]{2,1,0:T(8,128)(2,1)S(1)}, u32[]{:S(2)}, u32[]{:S(2)}) collective-permute-start(bf16[2,64,1536]{2,1,0:T(8,128)(2,1)S(1)} %give.3.refs_3_), channel_id=1, source_target_pairs={{0,4},{4,0},{8,12},{12,8},{1,5},{5,1},{9,13},{13,9},{2,6},{6,2},{1... | collective-permute-start | bytes 1179656 | tf_op jit(solution)/shard_map/ppermute | solution.py:287
  20.3 15.6 %collective-permute-start.1 = (bf16[2,64,1536]{2,1,0:T(8,128)(2,1)S(1)}, bf16[2,64,1536]{2,1,0:T(8,128)(2,1)S(1)}, u32[]{:S(2)}, u32[]{:S(2)}) collective-permute-start(bf16[2,64,1536]{2,1,0:T(8,128)(2,1)S(1)} %collective-permute-done.refs_0_.refs_1_), channel_id=1, source_target_pairs={{0,1},{1,2},{2,3},{3,0},{4,5},{5,6},{6,7},{7,4},{8,9},{9,10},{10,1... | collective-permute-start | bytes 1179656 | tf_op jit(solution)/shard_map/ppermute | solution.py:290
  23.0 15.4 %collective-permute-start.5 = (bf16[2,64,1536]{2,1,0:T(8,128)(2,1)S(1)}, bf16[2,64,1536]{2,1,0:T(8,128)(2,1)S(1)}, u32[]{:S(2)}, u32[]{:S(2)}) collective-permute-start(bf16[2,64,1536]{2,1,0:T(8,128)(2,1)S(1)} %add_convert_fusion.1.refs_3_.refs_2_), channel_id=1, source_target_pairs={{0,8},{4,12},{8,0},{12,4},{1,9},{5,13},{9,1},{13,5},{2,10},{6,14},... | collective-permute-start | bytes 1179656 | tf_op jit(solution)/shard_map/ppermute | solution.py:296
  30.5 2.4 %collective-permute-start.7 = (bf16[2,64,1536]{2,1,0:T(8,128)(2,1)S(1)}, bf16[2,64,1536]{2,1,0:T(8,128)(2,1)S(1)}, u32[]{:S(2)}, u32[]{:S(2)}) collective-permute-start(bf16[2,64,1536]{2,1,0:T(8,128)(2,1)S(1)} %give.4.refs_3_), channel_id=1, source_target_pairs={{0,4},{4,0},{8,12},{12,8},{1,5},{5,1},{9,13},{13,9},{2,6},{6,2},{1... | collective-permute-start | bytes 1179656 | tf_op jit(solution)/shard_map/ppermute | solution.py:287
  33.0 13.8 %collective-permute-start.10 = (bf16[2,64,1536]{2,1,0:T(8,128)(2,1)S(1)}, bf16[2,64,1536]{2,1,0:T(8,128)(2,1)S(1)}, u32[]{:S(2)}, u32[]{:S(2)}) collective-permute-start(bf16[2,64,1536]{2,1,0:T(8,128)(2,1)S(1)} %add_convert_fusion.refs_3_.refs_0_), channel_id=1, source_target_pairs={{0,8},{4,12},{8,0},{12,4},{1,9},{5,13},{9,1},{13,5},{2,10},{6,14},... | collective-permute-start | bytes 1179656 | tf_op jit(solution)/shard_map/ppermute | solution.py:296
  38.3 3.5 %collective-permute-start.8 = (bf16[2,64,1536]{2,1,0:T(8,128)(2,1)S(1)}, bf16[2,64,1536]{2,1,0:T(8,128)(2,1)S(1)}, u32[]{:S(2)}, u32[]{:S(2)}) collective-permute-start(bf16[2,64,1536]{2,1,0:T(8,128)(2,1)S(1)} %give.5.refs_4_), channel_id=1, source_target_pairs={{0,4},{4,0},{8,12},{12,8},{1,5},{5,1},{9,13},{13,9},{2,6},{6,2},{1... | collective-permute-start | bytes 1179656 | tf_op jit(solution)/shard_map/ppermute | solution.py:287
  38.9 4.8 %collective-permute-start.11 = (bf16[2,128,1536]{2,1,0:T(8,128)(2,1)S(1)}, bf16[2,128,1536]{2,1,0:T(8,128)(2,1)S(1)}, u32[]{:S(2)}, u32[]{:S(2)}) collective-permute-start(bf16[2,128,1536]{2,1,0:T(8,128)(2,1)S(1)} %gelu.4.refs_3_.refs_2_), channel_id=1, source_target_pairs={{0,4},{4,0},{8,12},{12,8},{1,5},{5,1},{9,13},{13,9},{2,6},{6,2},{1... | collective-permute-start | bytes 2359304 | tf_op jit(solution)/shard_map/ppermute | solution.py:287
  41.9 7.7 %collective-permute-start.12 = (bf16[2,64,768]{2,1,0:T(8,128)(2,1)S(1)}, bf16[2,64,768]{2,1,0:T(8,128)(2,1)S(1)}, u32[]{:S(2)}, u32[]{:S(2)}) collective-permute-start(bf16[2,64,768]{2,1,0:T(8,128)(2,1)S(1)} %get-tuple-element.53.refs_4_.refs_0_), channel_id=1, source_target_pairs={{0,8},{4,12},{8,0},{12,4},{1,9},{5,13},{9,1},{13,5},{2,10},{6,14},... | collective-permute-start | bytes 589832 | tf_op jit(solution)/shard_map/ppermute | solution.py:296
  47.1 3.2 %collective-permute-start.13 = (bf16[64,1536]{1,0:T(8,128)(2,1)S(1)}, bf16[64,1536]{1,0:T(8,128)(2,1)S(1)}, u32[]{:S(2)}, u32[]{:S(2)}) collective-permute-start(bf16[64,1536]{1,0:T(8,128)(2,1)S(1)} %get-tuple-element.38.refs_4_.refs_7_), channel_id=1, source_target_pairs={{0,4},{4,0},{8,12},{12,8},{1,5},{5,1},{9,13},{13,9},{2,6},{6,2},{1... | collective-permute-start | bytes 589832 | tf_op jit(solution)/shard_map/ppermute | solution.py:287
  47.2 8.0 %collective-permute-start.9 = (bf16[2,64,768]{2,1,0:T(8,128)(2,1)S(1)}, bf16[2,64,768]{2,1,0:T(8,128)(2,1)S(1)}, u32[]{:S(2)}, u32[]{:S(2)}) collective-permute-start(bf16[2,64,768]{2,1,0:T(8,128)(2,1)S(1)} %get-tuple-element.54.refs_5_.refs_0_), channel_id=1, source_target_pairs={{0,8},{4,12},{8,0},{12,4},{1,9},{5,13},{9,1},{13,5},{2,10},{6,14},... | collective-permute-start | bytes 589832 | tf_op jit(solution)/shard_map/ppermute | solution.py:296
  47.8 12.3 %collective-permute-start.15 = (bf16[64,1536]{1,0:T(8,128)(2,1)S(1)}, bf16[64,1536]{1,0:T(8,128)(2,1)S(1)}, u32[]{:S(2)}, u32[]{:S(2)}) collective-permute-start(bf16[64,1536]{1,0:T(8,128)(2,1)S(1)} %get-tuple-element.37.refs_2_), channel_id=1, source_target_pairs={{0,3},{1,0},{2,1},{3,2},{4,7},{5,4},{6,5},{7,6},{8,11},{9,8},{10,9... | collective-permute-start | bytes 589832 | tf_op jit(solution)/shard_map/ppermute | solution.py:290
  49.6 6.3 %collective-permute-start.17 = (bf16[64,1536]{1,0:T(8,128)(2,1)S(1)}, bf16[64,1536]{1,0:T(8,128)(2,1)S(1)}, u32[]{:S(2)}, u32[]{:S(2)}) collective-permute-start(bf16[64,1536]{1,0:T(8,128)(2,1)S(1)} %get-tuple-element.39.refs_2_.refs_5_), channel_id=1, source_target_pairs={{0,4},{4,0},{8,12},{12,8},{1,5},{5,1},{9,13},{13,9},{2,6},{6,2},{1... | collective-permute-start | bytes 589832 | tf_op jit(solution)/shard_map/ppermute | solution.py:287
  49.8 6.2 %collective-permute-start.18 = (bf16[2,64,768]{2,1,0:T(8,128)(2,1)S(1)}, bf16[2,64,768]{2,1,0:T(8,128)(2,1)S(1)}, u32[]{:S(2)}, u32[]{:S(2)}) collective-permute-start(bf16[2,64,768]{2,1,0:T(8,128)(2,1)S(1)} %gelu.6.refs_6_.refs_11_.refs_7_), channel_id=1, source_target_pairs={{0,4},{4,0},{8,12},{12,8},{1,5},{5,1},{9,13},{13,9},{2,6},{6,2},{1... | collective-permute-start | bytes 589832 | tf_op jit(solution)/shard_map/ppermute | solution.py:287
  55.4 4.7 %collective-permute-start.14 = (bf16[2,64,768]{2,1,0:T(8,128)(2,1)S(1)}, bf16[2,64,768]{2,1,0:T(8,128)(2,1)S(1)}, u32[]{:S(2)}, u32[]{:S(2)}) collective-permute-start(bf16[2,64,768]{2,1,0:T(8,128)(2,1)S(1)} %gelu.7.refs_13_.refs_2_.refs_6_), channel_id=1, source_target_pairs={{0,4},{4,0},{8,12},{12,8},{1,5},{5,1},{9,13},{13,9},{2,6},{6,2},{1... | collective-permute-start | bytes 589832 | tf_op jit(solution)/shard_map/ppermute | solution.py:287
  55.5 9.1 %collective-permute-start.16 = (bf16[64,1536]{1,0:T(8,128)(2,1)S(1)}, bf16[64,1536]{1,0:T(8,128)(2,1)S(1)}, u32[]{:S(2)}, u32[]{:S(2)}) collective-permute-start(bf16[64,1536]{1,0:T(8,128)(2,1)S(1)} %get-tuple-element.42), channel_id=1, source_target_pairs={{0,1},{1,2},{2,3},{3,0},{4,5},{5,6},{6,7},{7,4},{8,9},{9,10},{10,1... | collective-permute-start | bytes 589832 | tf_op jit(solution)/shard_map/ppermute | solution.py:290
  66.1 9.4 %collective-permute-start.19 = (bf16[64,1536]{1,0:T(8,128)(2,1)S(1)}, bf16[64,1536]{1,0:T(8,128)(2,1)S(1)}, u32[]{:S(2)}, u32[]{:S(2)}) collective-permute-start(bf16[64,1536]{1,0:T(8,128)(2,1)S(1)} %get-tuple-element.48.refs_13_), channel_id=1, source_target_pairs={{0,2},{1,3},{2,0},{3,1},{4,6},{5,7},{6,4},{7,5},{8,10},{9,11},{10,... | collective-permute-start | bytes 589832 | tf_op jit(solution)/shard_map/ppermute | solution.py:290

commit v7 on v6

--- a/solution.py
+++ b/solution.py
@@ -63,6 +63,27 @@
         )(*args)
         self.last = result[-1]
         return result
+
+
+def stacked(ordered, inputs, out_grad):
+    def body(inputs_hbm, grads_hbm, out_ref, sems):
+        copies = [
+            pltpu.make_async_copy(source, out_ref.at[i], sems.at[i]) for i, source in enumerate((inputs_hbm, grads_hbm))
+        ]
+        for copy in copies:
+            copy.start()
+        for copy in copies:
+            copy.wait()
+
+    return ordered(
+        body,
+        (in_hbm(inputs), in_hbm(out_grad)),
+        [VMEM((2, *inputs.shape), BF16)],
+        "stacked",
+        0.5,
+        spaces=[pl.ANY, pl.ANY],
+        scratch=[pltpu.SemaphoreType.DMA((2,))],
+    )[0]
 
 
 def first_product(ordered, core, other, chunk, up_weight, down_weight, name):
@@ -119,20 +140,26 @@
     return ordered(body, args, [jax.ShapeDtypeStruct((2, rows, half), BF16)], name, 2.4, after=after)[0]
 
 
-def product_terms(acts, up_refs, part, low):
-    terms = [dot(act, up_ref[part, low : low + act.shape[1]], NT) for act, up_ref in zip(acts, up_refs)]
-    return terms[0] + terms[1]
-
-
-def input_product(ordered, rows, mine, other, up_mine, up_other, low, micros, partial=None, returned=()):
-    features = up_mine.shape[0]
+def product_terms(terms, part):
+    share = None
+    for act, up_ref, low in terms:
+        term = dot(act, up_ref[part, low : low + act.shape[1]], NT)
+        share = term if share is None else share + term
+    return share
+
+
+def grad_of(ref):
+    return ref[...] if len(ref.shape) == 2 else ref[0]
+
+
+def input_product(ordered, rows, terms, micros, partial=None, returned=()):
+    features = terms[0][1].shape[0]
     tile = tile_of(features)
-    count = len(mine)
-    chunks = sum(a.shape[-2] for a in mine) // rows
-
-    def body(up_mine_ref, up_other_ref, *refs):
-        acts = [[r[...] if len(r.shape) == 2 else r[0] for r in part] for part in (refs[:count], refs[count : 2 * count])]
-        acts = [a[0] if count == 1 else jnp.concatenate(a, axis=0) for a in acts]
+    count = len(terms)
+    chunks = terms[0][0].shape[-2] // rows
+
+    def body(*refs):
+        filled = [(grad_of(refs[i]), refs[count + i], low) for i, (_, _, low) in enumerate(terms)]
         returned_refs, out_refs = refs[2 * count :][: len(returned)], refs[-chunks:]
         if returned:
             total = returned_refs[0][...].astype(F32)
@@ -141,13 +168,14 @@
             refs[-chunks - 1][...] = total
         for start in range(0, features, tile):
             part = slice(start, start + tile)
-            share = product_terms(acts, (up_mine_ref, up_other_ref), part, low)
+            share = product_terms(filled, part)
             if partial is not None:
                 share = share + refs[2 * count + len(returned)][:, part]
             for c, out_ref in enumerate(out_refs):
                 out_ref[:, part] = share[c * rows : (c + 1) * rows].astype(BF16)
 
-    args = (in_vmem(up_mine), in_vmem(up_other), *mine, *other, *returned, *([] if partial is None else [partial]))
+    args = [act for act, _, _ in terms] + [in_vmem(weight) for _, weight, _ in terms]
+    args += [*returned, *([] if partial is None else [partial])]
     outs = [jax.ShapeDtypeStruct((rows, features), F32)] if returned else []
     return ordered(body, args, outs + [jax.ShapeDtypeStruct((rows, features), BF16)] * chunks, "input_product", micros)
 
@@ -238,18 +266,20 @@
                     send(1, b * down_steps + step, value, down_stage, target)
                 if share is not None and b == 0 and step < up_steps:
                     part = slice(step * up_tile, (step + 1) * up_tile)
-                    mine_ref, other_ref, up_mine_ref, up_other_ref = refs[len(flat) : len(flat) + 4]
-                    pair = [r[...] if len(r.shape) == 2 else r[0] for r in (mine_ref, other_ref)]
-                    value = product_terms(pair, (up_mine_ref, up_other_ref), part, 0)
-                    refs[outs_at + 2][:, part] = value.astype(share[4])
+                    terms = [
+                        (grad_of(refs[len(flat) + i]), refs[len(flat) + len(share[0]) + i], low)
+                        for i, (_, _, low) in enumerate(share[0])
+                    ]
+                    refs[outs_at + 2][:, part] = product_terms(terms, part).astype(share[1])
         for copy in busy.values():
             copy.wait()
 
     args = [core, turned, all_grads, *flat]
     outs = [pltpu.HBM((features, 2 * half), F32), pltpu.HBM((2 * half, features), F32)]
     if share is not None:
-        args += [*share[:2], in_vmem(share[2]), in_vmem(share[3])]
-        outs.append(jax.ShapeDtypeStruct((share[0].shape[-2], features), share[4]))
+        terms, kind = share
+        args += [act for act, _, _ in terms] + [in_vmem(weight) for _, weight, _ in terms]
+        outs.append(jax.ShapeDtypeStruct((terms[0][0].shape[-2], features), kind))
     spaces = [None] * len(args)
     outs_at = len(args) - 3 + (0 if before is None else 2)
     aliases = {}
@@ -300,7 +330,7 @@
             partial = (partial.astype(F32) + peer.astype(F32)).astype(BF16)
 
     offsets = sorted(range(narrow // 2 - narrow + 1, narrow // 2 + 1), key=lambda places: (abs(places), -places))
-    chunks = {0: jnp.stack([inputs, out_grad])}
+    chunks = {0: stacked(ordered, inputs, out_grad)}
 
     up_other, down_other, give = first_product(ordered, core, True, chunks[0], up_weight, down_weight, "give_first")
     got = swap_cores(give)
@@ -328,7 +358,8 @@
             late = [across_chips(keep[:, :, part], got[:, :, part]) for part in parts]
 
     turned, all_grads = collect(ordered, [chunks[offset] for offset in offsets], [own for own, _ in late])
-    shares = input_product(ordered, rows, *early, up_mine, up_other, 0, 0.1)
+    both = (up_mine, up_other)
+    shares = input_product(ordered, rows, [(early[side][0], both[side], 0) for side in (0, 1)], 0.1)
     shares = [share if offset == 0 else shift(share, -offset) for offset, share in zip(offsets, shares)]
     middle = acts_of(sums[-1:], True)
 
@@ -343,20 +374,20 @@
         return weight_grads(ordered, core, blocks, turned, all_grads, half, scale, before, "weight_grads", share)
 
     late_acts.append(acts_of(late[:1]))
-    share = (middle[0][0], middle[1][0], up_mine, up_other, BF16)
-    up_grad, down_grad, share, _ = grads([(0, 0)], None, share)
-    shares.append(shift(share, -offsets[-2]))
+    up_grad, down_grad, share, _ = grads([(0, 0)], None, ([(middle[side][0], both[side], 0) for side in (0, 1)], BF16))
+    middle_share = shift(share, -offsets[-2])
     partial = None
+    terms = [(late_acts[0][side][0], both[side], 0) for side in (0, 1)]
     if slices > 1:
         late_acts.append(acts_of(late[1:]))
-        share = (late_acts[0][0][0], late_acts[0][1][0], up_mine, up_other, F32)
-        up_grad, down_grad, partial, _ = grads([(1, 0)], (up_grad, down_grad), share)
-    low = width * (slices - 1)
-    so_far, share = input_product(ordered, rows, *late_acts[-1], up_mine, up_other, low, 3.0, partial, shares)
+        terms.append((late_acts[1][0][0], up_mine, width))
+        up_grad, down_grad, partial, _ = grads([(1, 0)], (up_grad, down_grad), (terms, F32))
+        terms = [(late_acts[1][1][0], up_other, width)]
+    so_far, share = input_product(ordered, rows, terms, 3.0, partial, shares)
     share = shift(share, -offsets[-1])
     last = [(0, 1), (1, 1)] if slices > 1 else [(1, 0)]
     up_grad, down_grad, _ = grads(last, (up_grad, down_grad), None)
-    return (so_far + share.astype(F32)).astype(BF16), up_grad, down_grad
+    return (so_far + middle_share.astype(F32) + share.astype(F32)).astype(BF16), up_grad, down_grad
 
 
 def solution(mesh):

time: 76.4 us -> 74.2 us (0.971)
  waiting for transfers between devices: 12.1 us -> 8.67 us
  starting transfers between devices: 15.4 us -> 17.1 us
  other arithmetic: 2.14 us -> 1.11 us
    ppermute x6, waiting for transfers between devices: 9.43 us -> 5.99 us  [shift(): lax.ppermute(x, 'narrow', [(i, (i + places) % narrow) for i in range(narr...]
    ppermute x6, starting transfers between devices: 7.77 us -> 9.42 us  [shift(): lax.ppermute(x, 'narrow', [(i, (i + places) % narrow) for i in range(narr...]
    another operation x1 -> x0, other arithmetic: 1.06 us -> none  [per_device(): chunks = {0: jnp.stack([inputs, out_grad])}]
    pallas_call x18 -> x19, Pallas kernels: 45.7 us -> 46.3 us  [__call__(): pl.pallas_call(kernel, out_shape=outs, in_specs=specs, out_specs=[pl.Bloc...]
  transfers between devices with their start and end apart: 20 -> 20, of which waited for: 5 -> 4; matrix products, arithmetic and copies ran while one was open for 0% -> 1% of each run, Pallas kernels for 58% -> 61%
where the time goes in v7:
time: 74.2 us; the launch traced here: 74 us
  Pallas kernels  46.3 us (62%)
  starting transfers between devices  17.1 us (23%)
  waiting for transfers between devices  8.67 us (12%)
  other arithmetic  1.11 us (1%)
  between operations  0.94 us (1%)
    pallas_call x19, Pallas kernels, __call__(): pl.pallas_call(kernel, out_shape=outs, in_specs=specs, out_specs=[pl.Bloc...  46.3 us
    ppermute x6, starting transfers between devices, shift(): lax.ppermute(x, 'narrow', [(i, (i + places) % narrow) for i in range(narr...  9.42 us
    ppermute x5, starting transfers between devices, across_chips(): lax.ppermute(partial, 'wide', [(i, i ^ 2 * hop) for i in range(wide)])  6.07 us
    ppermute x6, waiting for transfers between devices, shift(): lax.ppermute(x, 'narrow', [(i, (i + places) % narrow) for i in range(narr...  5.99 us
    ppermute x5, waiting for transfers between devices, across_chips(): lax.ppermute(partial, 'wide', [(i, i ^ 2 * hop) for i in range(wide)])  2.65 us
    ppermute x9, starting transfers between devices, swap_cores(): return lax.ppermute(x, 'wide', [(i, i ^ 1) for i in range(wide)])  1.57 us
  transfers between devices with their start and end apart: 20, of which 4 were waited for; matrix products, arithmetic and copies ran while one was open for 1% of the time, Pallas kernels for 61%

profile of v7, /device:TPU:0, one launch (start us, length us, event | category | flops | bytes accessed | tf_op | source)
XLA Modules:
  0.0 74.0 jit_solution(673348246974100918)
XLA Ops:
  0.6 1.0 %stacked.1.refs_1_.refs_4_.refs_0_ = bf16[2,64,1536]{2,1,0:T(8,128)(2,1)S(1)} custom-call(bf16[64,1536]{1,0:T(8,128)(2,1)} %refs_0_.1, bf16[64,1536]{1,0:T(8,128)(2,1)} %refs_1_.1), custom_call_target="tpu_custom_call" | custom-call | flops 2000000000 | tf_op jit(solution)/shard_map/stacked/pallas_call | solution.py:53
  1.7 3.1 %collective-permute-start = (bf16[2,64,1536]{2,1,0:T(8,128)(2,1)S(1)}, bf16[2,64,1536]{2,1,0:T(8,128)(2,1)S(1)}, u32[]{:S(2)}, u32[]{:S(2)}) collective-permute-start(bf16[2,64,1536]{2,1,0:T(8,128)(2,1)S(1)} %stacked.1.refs_1_.refs_4_.refs_0_), channel_id=1, source_target_pairs={{0,1},{1,2},{2,3},{3,0},{4,5},{5,6},{6,7},{7,4},{8,9},{9,10},{10,1... | collective-permute-start | bytes 1179656 | tf_op jit(solution)/shard_map/ppermute | solution.py:320
  4.8 4.5 %give_first.1 = (bf16[1536,1536]{1,0:T(8,128)(2,1)S(1)}, bf16[1536,1536]{1,0:T(8,128)(2,1)S(1)}, bf16[2,64,1536]{2,1,0:T(8,128)(2,1)S(1)}) custom-call(s32[1]{0:T(128)} %bitcast.refs_0_, bf16[2,64,1536]{2,1,0:T(8,128)(2,1)S(1)} %stacked.1.refs_1_.refs_4_.refs_0_, bf16[1536,3072]{1,0:T(8,128)(2,1)} %refs_2_.3, bf16[3072,1536]{1,0:T(8,128)(2,1)} %refs_3_.3, ...), custom_call_target="tpu_custom_call" | custom-call | flops 17999998976 | tf_op jit(solution)/shard_map/give_first/pallas_call | solution.py:53
  9.4 4.5 %keep_first.1 = (bf16[1536,1536]{1,0:T(8,128)(2,1)S(1)}, bf16[1536,1536]{1,0:T(8,128)(2,1)S(1)}, bf16[2,64,1536]{2,1,0:T(8,128)(2,1)S(1)}, bf16[2,64,1536]{2,1,0:T(8,128)(2,1)S(1)}) custom-call(s32[1]{0:T(128)} %bitcast.refs_0_, bf16[2,64,1536]{2,1,0:T(8,128)(2,1)S(1)} %stacked.1.refs_1_.refs_4_.refs_0_, bf16[1536,3072]{1,0:T(8,128)(2,1)} %refs_2_.3, ...), custom_call_target="tpu_custom_call" | custom-call | flops 17999998976 | tf_op jit(solution)/shard_map/keep_first/pallas_call | solution.py:53
  13.9 2.1 %collective-permute-start.6 = (bf16[2,64,1536]{2,1,0:T(8,128)(2,1)S(1)}, bf16[2,64,1536]{2,1,0:T(8,128)(2,1)S(1)}, u32[]{:S(2)}, u32[]{:S(2)}) collective-permute-start(bf16[2,64,1536]{2,1,0:T(8,128)(2,1)S(1)} %get-tuple-element.34), channel_id=1, source_target_pairs={{0,3},{1,0},{2,1},{3,2},{4,7},{5,4},{6,5},{7,6},{8,11},{9,8},{10,9... | collective-permute-start | bytes 1179656 | tf_op jit(solution)/shard_map/ppermute | solution.py:320
  16.1 1.8 %collective-permute-start.3 = (bf16[2,64,1536]{2,1,0:T(8,128)(2,1)S(1)}, bf16[2,64,1536]{2,1,0:T(8,128)(2,1)S(1)}, u32[]{:S(2)}, u32[]{:S(2)}) collective-permute-start(bf16[2,64,1536]{2,1,0:T(8,128)(2,1)S(1)} %add_convert_fusion.2.refs_3_.refs_0_), channel_id=1, source_target_pairs={{0,8},{4,12},{8,0},{12,4},{1,9},{5,13},{9,1},{13,5},{2,10},{6,14},... | collective-permute-start | bytes 1179656 | tf_op jit(solution)/shard_map/ppermute | solution.py:326
  17.9 2.3 %give.3.refs_3_ = bf16[2,64,1536]{2,1,0:T(8,128)(2,1)S(1)} custom-call(bf16[2,64,1536]{2,1,0:T(8,128)(2,1)S(1)} %collective-permute-done.refs_0_.refs_1_, bf16[1536,1536]{1,0:T(8,128)(2,1)S(1)} %get-tuple-element.32.refs_1_.refs_3_.refs_10_.refs_11_, bf16[1536,1536]{1,0:T(8,128)(2,1)S(1)} %get-tuple-element.33.refs_2_, ...), custom_call_target="tpu_custom_call" | custom-call | flops 9600000000 | tf_op jit(solution)/shard_map/give/pallas_call | solution.py:53
  20.5 2.3 %keep.3.refs_5_ = bf16[2,64,1536]{2,1,0:T(8,128)(2,1)S(1)} custom-call(bf16[2,64,1536]{2,1,0:T(8,128)(2,1)S(1)} %collective-permute-done.refs_0_.refs_1_, bf16[1536,1536]{1,0:T(8,128)(2,1)S(1)} %get-tuple-element.29.refs_1_.refs_2_.refs_9_.refs_10_.refs_12_, bf16[1536,1536]{1,0:T(8,128)(2,1)S(1)} %get-tuple-element.30.refs_2_, ...), custom_call_target="tpu_custom_call" | custom-call | flops 9600000000 | tf_op jit(solution)/shard_map/keep/pallas_call | solution.py:53
  23.0 0.4 collective-permute-start.5
  23.4 2.1 %collective-permute-done.6.refs_0_.refs_2_ = bf16[2,64,1536]{2,1,0:T(8,128)(2,1)S(1)} collective-permute-done((bf16[2,64,1536]{2,1,0:T(8,128)(2,1)S(1)}, bf16[2,64,1536]{2,1,0:T(8,128)(2,1)S(1)}, u32[]{:S(2)}, u32[]{:S(2)}) %collective-permute-start.6) | collective-permute-done | bytes 393248 | tf_op jit(solution)/shard_map/ppermute | solution.py:320
  25.5 2.6 %collective-permute-done.3.refs_4_.refs_1_ = bf16[2,64,1536]{2,1,0:T(8,128)(2,1)S(1)} collective-permute-done((bf16[2,64,1536]{2,1,0:T(8,128)(2,1)S(1)}, bf16[2,64,1536]{2,1,0:T(8,128)(2,1)S(1)}, u32[]{:S(2)}, u32[]{:S(2)}) %collective-permute-start.3) | collective-permute-done | bytes 393248 | tf_op jit(solution)/shard_map/ppermute | solution.py:326
  28.1 2.3 %give.4.refs_3_ = bf16[2,64,1536]{2,1,0:T(8,128)(2,1)S(1)} custom-call(bf16[2,64,1536]{2,1,0:T(8,128)(2,1)S(1)} %collective-permute-done.6.refs_0_.refs_2_, bf16[1536,1536]{1,0:T(8,128)(2,1)S(1)} %get-tuple-element.32.refs_1_.refs_3_.refs_10_.refs_11_, bf16[1536,1536]{1,0:T(8,128)(2,1)S(1)} %get-tuple-element.33.refs_2_, ...), custom_call_target="tpu_custom_call" | custom-call | flops 9600000000 | tf_op jit(solution)/shard_map/give/pallas_call | solution.py:53
  30.5 2.3 %keep.4.refs_4_ = bf16[2,64,1536]{2,1,0:T(8,128)(2,1)S(1)} custom-call(bf16[2,64,1536]{2,1,0:T(8,128)(2,1)S(1)} %collective-permute-done.6.refs_0_.refs_2_, bf16[1536,1536]{1,0:T(8,128)(2,1)S(1)} %get-tuple-element.29.refs_1_.refs_2_.refs_9_.refs_10_.refs_12_, bf16[1536,1536]{1,0:T(8,128)(2,1)S(1)} %get-tuple-element.30.refs_2_, ...), custom_call_target="tpu_custom_call" | custom-call | flops 9600000000 | tf_op jit(solution)/shard_map/keep/pallas_call | solution.py:53
  33.0 1.7 %collective-permute-start.10 = (bf16[2,64,1536]{2,1,0:T(8,128)(2,1)S(1)}, bf16[2,64,1536]{2,1,0:T(8,128)(2,1)S(1)}, u32[]{:S(2)}, u32[]{:S(2)}) collective-permute-start(bf16[2,64,1536]{2,1,0:T(8,128)(2,1)S(1)} %add_convert_fusion.refs_3_.refs_0_), channel_id=1, source_target_pairs={{0,8},{4,12},{8,0},{12,4},{1,9},{5,13},{9,1},{13,5},{2,10},{6,14},... | collective-permute-start | bytes 1179656 | tf_op jit(solution)/shard_map/ppermute | solution.py:326
  34.8 1.2 %collective-permute-done.1.refs_0_.refs_3_ = bf16[2,64,1536]{2,1,0:T(8,128)(2,1)S(1)} collective-permute-done((bf16[2,64,1536]{2,1,0:T(8,128)(2,1)S(1)}, bf16[2,64,1536]{2,1,0:T(8,128)(2,1)S(1)}, u32[]{:S(2)}, u32[]{:S(2)}) %collective-permute-start.1) | collective-permute-done | bytes 393248 | tf_op jit(solution)/shard_map/ppermute | solution.py:320
  35.9 2.3 %give.5.refs_4_ = bf16[2,64,1536]{2,1,0:T(8,128)(2,1)S(1)} custom-call(bf16[2,64,1536]{2,1,0:T(8,128)(2,1)S(1)} %collective-permute-done.1.refs_0_.refs_3_, bf16[1536,1536]{1,0:T(8,128)(2,1)S(1)} %get-tuple-element.32.refs_1_.refs_3_.refs_10_.refs_11_, bf16[1536,1536]{1,0:T(8,128)(2,1)S(1)} %get-tuple-element.33.refs_2_, ...), custom_call_target="tpu_custom_call" | custom-call | flops 9600000000 | tf_op jit(solution)/shard_map/give/pallas_call | solution.py:53
  38.3 0.5 gelu.4.refs_3_.refs_0_
  38.9 0.5 collective-permute-start.11
  39.4 2.3 %keep.5.refs_6_ = bf16[2,64,1536]{2,1,0:T(8,128)(2,1)S(1)} custom-call(bf16[2,64,1536]{2,1,0:T(8,128)(2,1)S(1)} %collective-permute-done.1.refs_0_.refs_3_, bf16[1536,1536]{1,0:T(8,128)(2,1)S(1)} %get-tuple-element.29.refs_1_.refs_2_.refs_9_.refs_10_.refs_12_, bf16[1536,1536]{1,0:T(8,128)(2,1)S(1)} %get-tuple-element.30.refs_2_, ...), custom_call_target="tpu_custom_call" | custom-call | flops 9600000000 | tf_op jit(solution)/shard_map/keep/pallas_call | solution.py:53
  41.9 1.6 %collective-permute-start.12 = (bf16[2,64,768]{2,1,0:T(8,128)(2,1)S(1)}, bf16[2,64,768]{2,1,0:T(8,128)(2,1)S(1)}, u32[]{:S(2)}, u32[]{:S(2)}) collective-permute-start(bf16[2,64,768]{2,1,0:T(8,128)(2,1)S(1)} %get-tuple-element.53.refs_4_.refs_0_), channel_id=1, source_target_pairs={{0,8},{4,12},{8,0},{12,4},{1,9},{5,13},{9,1},{13,5},{2,10},{6,14},... | collective-permute-start | bytes 589832 | tf_op jit(solution)/shard_map/ppermute | solution.py:326
  43.7 3.1 %input_product.2 = (bf16[64,1536]{1,0:T(8,128)(2,1)S(1)}, bf16[64,1536]{1,0:T(8,128)(2,1)S(1)}) custom-call(bf16[2,128,1536]{2,1,0:T(8,128)(2,1)S(1)} %gelu.4.refs_3_.refs_0_, bf16[2,128,1536]{2,1,0:T(8,128)(2,1)S(1)} %collective-permute-done.11.refs_1_.refs_3_.refs_7_, bf16[1536,1536]{1,0:T(8,128)(2,1)S(1)} %get-tuple-element.29.refs_1_.refs_2_.refs_9_.refs_10_.refs_12_, ...), custom_call_target="tpu_custom_call" | custom-call | flops 400000000 | tf_op jit(solution)/shard_map/input_product/pallas_call | solution.py:53
  47.2 0.6 collective-permute-start.9
  47.8 1.8 %collective-permute-start.15 = (bf16[64,1536]{1,0:T(8,128)(2,1)S(1)}, bf16[64,1536]{1,0:T(8,128)(2,1)S(1)}, u32[]{:S(2)}, u32[]{:S(2)}) collective-permute-start(bf16[64,1536]{1,0:T(8,128)(2,1)S(1)} %get-tuple-element.37.refs_2_), channel_id=1, source_target_pairs={{0,3},{1,0},{2,1},{3,2},{4,7},{5,4},{6,5},{7,6},{8,11},{9,8},{10,9... | collective-permute-start | bytes 589832 | tf_op jit(solution)/shard_map/ppermute | solution.py:320
  49.8 0.6 collective-permute-start.17
  50.4 4.9 %weight_grads.3 = (f32[1536,3072]{1,0:T(8,128)}, f32[3072,1536]{1,0:T(8,128)}, bf16[64,1536]{1,0:T(8,128)(2,1)S(1)}, f32[8,128]{1,0:T(8,128)S(1)}) custom-call(s32[1]{0:T(128)} %bitcast.refs_0_, bf16[1536,256]{1,0:T(8,128)(2,1)S(1)} %get-tuple-element.35.refs_1_, bf16[256,1536]{1,0:T(8,128)(2,1)S(1)} %get-tuple-element.36.refs_4_.refs_2_, ...), custom_call_target="tpu_custom_call" | custom-call | flops 16000000000 | tf_op jit(solution)/shard_map/weight_grads/pallas_call | solution.py:53
  55.5 0.4 collective-permute-start.18
  55.9 4.4 %weight_grads.4 = (f32[1536,3072]{1,0:T(8,128)}, f32[3072,1536]{1,0:T(8,128)}, f32[64,1536]{1,0:T(8,128)S(1)}, f32[8,128]{1,0:T(8,128)S(1)}) custom-call(s32[1]{0:T(128)} %bitcast.refs_0_, bf16[1536,256]{1,0:T(8,128)(2,1)S(1)} %get-tuple-element.35.refs_1_, ...), custom_call_target="tpu_custom_call", output_to_operand_aliasing={{0}: (13, {}), {1}: (14, {})} | custom-call | flops 16000000000 | tf_op jit(solution)/shard_map/weight_grads/pallas_call | solution.py:53
  60.4 0.9 %input_product.3 = (f32[64,1536]{1,0:T(8,128)S(1)}, bf16[64,1536]{1,0:T(8,128)(2,1)S(1)}) custom-call(bf16[2,64,768]{2,1,0:T(8,128)(2,1)S(1)} %collective-permute-done.14.refs_0_.refs_10_, bf16[1536,1536]{1,0:T(8,128)(2,1)S(1)} %get-tuple-element.32.refs_1_.refs_3_.refs_10_.refs_11_, bf16[64,1536]{1,0:T(8,128)(2,1)S(1)} %get-tuple-element.41.refs_2_, ...), custom_call_target="tpu_custom_call" | custom-call | flops 12000000000 | tf_op jit(solution)/shard_map/input_product/pallas_call | solution.py:53
  61.2 1.7 %collective-permute-start.19 = (bf16[64,1536]{1,0:T(8,128)(2,1)S(1)}, bf16[64,1536]{1,0:T(8,128)(2,1)S(1)}, u32[]{:S(2)}, u32[]{:S(2)}) collective-permute-start(bf16[64,1536]{1,0:T(8,128)(2,1)S(1)} %get-tuple-element.48.refs_13_), channel_id=1, source_target_pairs={{0,2},{1,3},{2,0},{3,1},{4,6},{5,7},{6,4},{7,5},{8,10},{9,11},{10,... | collective-permute-start | bytes 589832 | tf_op jit(solution)/shard_map/ppermute | solution.py:320
  63.0 7.6 %weight_grads.5 = (f32[1536,3072]{1,0:T(8,128)}, f32[3072,1536]{1,0:T(8,128)}, f32[8,128]{1,0:T(8,128)}) custom-call(s32[1]{0:T(128)} %bitcast.refs_0_, bf16[1536,256]{1,0:T(8,128)(2,1)S(1)} %get-tuple-element.35.refs_1_, bf16[256,1536]{1,0:T(8,128)(2,1)S(1)} %get-tuple-element.36.refs_4_.refs_2_, ...), custom_call_target="tpu_custom_call", output_to_operand_aliasing={{0}: (11, {}), {1}: (12, {})} | custom-call | flops 32000000000 | tf_op jit(solution)/shard_map/weight_grads/pallas_call | solution.py:53
  70.5 2.7 %collective-permute-done.19 = bf16[64,1536]{1,0:T(8,128)(2,1)S(1)} collective-permute-done((bf16[64,1536]{1,0:T(8,128)(2,1)S(1)}, bf16[64,1536]{1,0:T(8,128)(2,1)S(1)}, u32[]{:S(2)}, u32[]{:S(2)}) %collective-permute-start.19) | collective-permute-done | bytes 196640 | tf_op jit(solution)/shard_map/ppermute | solution.py:320
  73.3 0.7 add_convert_fusion.3
  (32 shorter events, 1.9 us)
Async XLA Ops:
  1.7 16.2 %collective-permute-start = (bf16[2,64,1536]{2,1,0:T(8,128)(2,1)S(1)}, bf16[2,64,1536]{2,1,0:T(8,128)(2,1)S(1)}, u32[]{:S(2)}, u32[]{:S(2)}) collective-permute-start(bf16[2,64,1536]{2,1,0:T(8,128)(2,1)S(1)} %stacked.1.refs_1_.refs_4_.refs_0_), channel_id=1, source_target_pairs={{0,1},{1,2},{2,3},{3,0},{4,5},{5,6},{6,7},{7,4},{8,9},{9,10},{10,1... | collective-permute-start | bytes 1179656 | tf_op jit(solution)/shard_map/ppermute | solution.py:320
  9.3 6.7 %collective-permute-start.2 = (bf16[2,64,1536]{2,1,0:T(8,128)(2,1)S(1)}, bf16[2,64,1536]{2,1,0:T(8,128)(2,1)S(1)}, u32[]{:S(2)}, u32[]{:S(2)}) collective-permute-start(bf16[2,64,1536]{2,1,0:T(8,128)(2,1)S(1)} %get-tuple-element.28.refs_4_), channel_id=1, source_target_pairs={{0,4},{4,0},{8,12},{12,8},{1,5},{5,1},{9,13},{13,9},{2,6},{6,2},{1... | collective-permute-start | bytes 1179656 | tf_op jit(solution)/shard_map/ppermute | solution.py:317
  13.9 11.6 %collective-permute-start.6 = (bf16[2,64,1536]{2,1,0:T(8,128)(2,1)S(1)}, bf16[2,64,1536]{2,1,0:T(8,128)(2,1)S(1)}, u32[]{:S(2)}, u32[]{:S(2)}) collective-permute-start(bf16[2,64,1536]{2,1,0:T(8,128)(2,1)S(1)} %get-tuple-element.34), channel_id=1, source_target_pairs={{0,3},{1,0},{2,1},{3,2},{4,7},{5,4},{6,5},{7,6},{8,11},{9,8},{10,9... | collective-permute-start | bytes 1179656 | tf_op jit(solution)/shard_map/ppermute | solution.py:320
  16.1 12.0 %collective-permute-start.3 = (bf16[2,64,1536]{2,1,0:T(8,128)(2,1)S(1)}, bf16[2,64,1536]{2,1,0:T(8,128)(2,1)S(1)}, u32[]{:S(2)}, u32[]{:S(2)}) collective-permute-start(bf16[2,64,1536]{2,1,0:T(8,128)(2,1)S(1)} %add_convert_fusion.2.refs_3_.refs_0_), channel_id=1, source_target_pairs={{0,8},{4,12},{8,0},{12,4},{1,9},{5,13},{9,1},{13,5},{2,10},{6,14},... | collective-permute-start | bytes 1179656 | tf_op jit(solution)/shard_map/ppermute | solution.py:326
  20.2 2.7 %collective-permute-start.4 = (bf16[2,64,1536]{2,1,0:T(8,128)(2,1)S(1)}, bf16[2,64,1536]{2,1,0:T(8,128)(2,1)S(1)}, u32[]{:S(2)}, u32[]{:S(2)}) collective-permute-start(bf16[2,64,1536]{2,1,0:T(8,128)(2,1)S(1)} %give.3.refs_3_), channel_id=1, source_target_pairs={{0,4},{4,0},{8,12},{12,8},{1,5},{5,1},{9,13},{13,9},{2,6},{6,2},{1... | collective-permute-start | bytes 1179656 | tf_op jit(solution)/shard_map/ppermute | solution.py:317
  20.3 15.6 %collective-permute-start.1 = (bf16[2,64,1536]{2,1,0:T(8,128)(2,1)S(1)}, bf16[2,64,1536]{2,1,0:T(8,128)(2,1)S(1)}, u32[]{:S(2)}, u32[]{:S(2)}) collective-permute-start(bf16[2,64,1536]{2,1,0:T(8,128)(2,1)S(1)} %collective-permute-done.refs_0_.refs_1_), channel_id=1, source_target_pairs={{0,1},{1,2},{2,3},{3,0},{4,5},{5,6},{6,7},{7,4},{8,9},{9,10},{10,1... | collective-permute-start | bytes 1179656 | tf_op jit(solution)/shard_map/ppermute | solution.py:320
  23.0 15.3 %collective-permute-start.5 = (bf16[2,64,1536]{2,1,0:T(8,128)(2,1)S(1)}, bf16[2,64,1536]{2,1,0:T(8,128)(2,1)S(1)}, u32[]{:S(2)}, u32[]{:S(2)}) collective-permute-start(bf16[2,64,1536]{2,1,0:T(8,128)(2,1)S(1)} %add_convert_fusion.1.refs_3_.refs_2_), channel_id=1, source_target_pairs={{0,8},{4,12},{8,0},{12,4},{1,9},{5,13},{9,1},{13,5},{2,10},{6,14},... | collective-permute-start | bytes 1179656 | tf_op jit(solution)/shard_map/ppermute | solution.py:326
  30.5 2.4 %collective-permute-start.7 = (bf16[2,64,1536]{2,1,0:T(8,128)(2,1)S(1)}, bf16[2,64,1536]{2,1,0:T(8,128)(2,1)S(1)}, u32[]{:S(2)}, u32[]{:S(2)}) collective-permute-start(bf16[2,64,1536]{2,1,0:T(8,128)(2,1)S(1)} %give.4.refs_3_), channel_id=1, source_target_pairs={{0,4},{4,0},{8,12},{12,8},{1,5},{5,1},{9,13},{13,9},{2,6},{6,2},{1... | collective-permute-start | bytes 1179656 | tf_op jit(solution)/shard_map/ppermute | solution.py:317
  33.0 13.8 %collective-permute-start.10 = (bf16[2,64,1536]{2,1,0:T(8,128)(2,1)S(1)}, bf16[2,64,1536]{2,1,0:T(8,128)(2,1)S(1)}, u32[]{:S(2)}, u32[]{:S(2)}) collective-permute-start(bf16[2,64,1536]{2,1,0:T(8,128)(2,1)S(1)} %add_convert_fusion.refs_3_.refs_0_), channel_id=1, source_target_pairs={{0,8},{4,12},{8,0},{12,4},{1,9},{5,13},{9,1},{13,5},{2,10},{6,14},... | collective-permute-start | bytes 1179656 | tf_op jit(solution)/shard_map/ppermute | solution.py:326
  38.3 3.5 %collective-permute-start.8 = (bf16[2,64,1536]{2,1,0:T(8,128)(2,1)S(1)}, bf16[2,64,1536]{2,1,0:T(8,128)(2,1)S(1)}, u32[]{:S(2)}, u32[]{:S(2)}) collective-permute-start(bf16[2,64,1536]{2,1,0:T(8,128)(2,1)S(1)} %give.5.refs_4_), channel_id=1, source_target_pairs={{0,4},{4,0},{8,12},{12,8},{1,5},{5,1},{9,13},{13,9},{2,6},{6,2},{1... | collective-permute-start | bytes 1179656 | tf_op jit(solution)/shard_map/ppermute | solution.py:317
  38.9 4.8 %collective-permute-start.11 = (bf16[2,128,1536]{2,1,0:T(8,128)(2,1)S(1)}, bf16[2,128,1536]{2,1,0:T(8,128)(2,1)S(1)}, u32[]{:S(2)}, u32[]{:S(2)}) collective-permute-start(bf16[2,128,1536]{2,1,0:T(8,128)(2,1)S(1)} %gelu.4.refs_3_.refs_0_), channel_id=1, source_target_pairs={{0,4},{4,0},{8,12},{12,8},{1,5},{5,1},{9,13},{13,9},{2,6},{6,2},{1... | collective-permute-start | bytes 2359304 | tf_op jit(solution)/shard_map/ppermute | solution.py:317
  41.9 7.8 %collective-permute-start.12 = (bf16[2,64,768]{2,1,0:T(8,128)(2,1)S(1)}, bf16[2,64,768]{2,1,0:T(8,128)(2,1)S(1)}, u32[]{:S(2)}, u32[]{:S(2)}) collective-permute-start(bf16[2,64,768]{2,1,0:T(8,128)(2,1)S(1)} %get-tuple-element.53.refs_4_.refs_0_), channel_id=1, source_target_pairs={{0,8},{4,12},{8,0},{12,4},{1,9},{5,13},{9,1},{13,5},{2,10},{6,14},... | collective-permute-start | bytes 589832 | tf_op jit(solution)/shard_map/ppermute | solution.py:326
  47.1 3.2 %collective-permute-start.13 = (bf16[64,1536]{1,0:T(8,128)(2,1)S(1)}, bf16[64,1536]{1,0:T(8,128)(2,1)S(1)}, u32[]{:S(2)}, u32[]{:S(2)}) collective-permute-start(bf16[64,1536]{1,0:T(8,128)(2,1)S(1)} %get-tuple-element.38.refs_4_.refs_7_), channel_id=1, source_target_pairs={{0,4},{4,0},{8,12},{12,8},{1,5},{5,1},{9,13},{13,9},{2,6},{6,2},{1... | collective-permute-start | bytes 589832 | tf_op jit(solution)/shard_map/ppermute | solution.py:317
  47.2 8.1 %collective-permute-start.9 = (bf16[2,64,768]{2,1,0:T(8,128)(2,1)S(1)}, bf16[2,64,768]{2,1,0:T(8,128)(2,1)S(1)}, u32[]{:S(2)}, u32[]{:S(2)}) collective-permute-start(bf16[2,64,768]{2,1,0:T(8,128)(2,1)S(1)} %get-tuple-element.54.refs_5_.refs_0_), channel_id=1, source_target_pairs={{0,8},{4,12},{8,0},{12,4},{1,9},{5,13},{9,1},{13,5},{2,10},{6,14},... | collective-permute-start | bytes 589832 | tf_op jit(solution)/shard_map/ppermute | solution.py:326
  47.8 12.6 %collective-permute-start.15 = (bf16[64,1536]{1,0:T(8,128)(2,1)S(1)}, bf16[64,1536]{1,0:T(8,128)(2,1)S(1)}, u32[]{:S(2)}, u32[]{:S(2)}) collective-permute-start(bf16[64,1536]{1,0:T(8,128)(2,1)S(1)} %get-tuple-element.37.refs_2_), channel_id=1, source_target_pairs={{0,3},{1,0},{2,1},{3,2},{4,7},{5,4},{6,5},{7,6},{8,11},{9,8},{10,9... | collective-permute-start | bytes 589832 | tf_op jit(solution)/shard_map/ppermute | solution.py:320
  49.6 6.3 %collective-permute-start.16 = (bf16[64,1536]{1,0:T(8,128)(2,1)S(1)}, bf16[64,1536]{1,0:T(8,128)(2,1)S(1)}, u32[]{:S(2)}, u32[]{:S(2)}) collective-permute-start(bf16[64,1536]{1,0:T(8,128)(2,1)S(1)} %get-tuple-element.39.refs_2_.refs_5_), channel_id=1, source_target_pairs={{0,4},{4,0},{8,12},{12,8},{1,5},{5,1},{9,13},{13,9},{2,6},{6,2},{1... | collective-permute-start | bytes 589832 | tf_op jit(solution)/shard_map/ppermute | solution.py:317
  49.8 6.2 %collective-permute-start.17 = (bf16[2,64,768]{2,1,0:T(8,128)(2,1)S(1)}, bf16[2,64,768]{2,1,0:T(8,128)(2,1)S(1)}, u32[]{:S(2)}, u32[]{:S(2)}) collective-permute-start(bf16[2,64,768]{2,1,0:T(8,128)(2,1)S(1)} %gelu.6.refs_6_.refs_11_.refs_7_), channel_id=1, source_target_pairs={{0,4},{4,0},{8,12},{12,8},{1,5},{5,1},{9,13},{13,9},{2,6},{6,2},{1... | collective-permute-start | bytes 589832 | tf_op jit(solution)/shard_map/ppermute | solution.py:317
  55.4 5.0 %collective-permute-start.14 = (bf16[2,64,768]{2,1,0:T(8,128)(2,1)S(1)}, bf16[2,64,768]{2,1,0:T(8,128)(2,1)S(1)}, u32[]{:S(2)}, u32[]{:S(2)}) collective-permute-start(bf16[2,64,768]{2,1,0:T(8,128)(2,1)S(1)} %gelu.7.refs_9_.refs_15_.refs_6_), channel_id=1, source_target_pairs={{0,4},{4,0},{8,12},{12,8},{1,5},{5,1},{9,13},{13,9},{2,6},{6,2},{1... | collective-permute-start | bytes 589832 | tf_op jit(solution)/shard_map/ppermute | solution.py:317
  55.5 15.1 %collective-permute-start.18 = (bf16[64,1536]{1,0:T(8,128)(2,1)S(1)}, bf16[64,1536]{1,0:T(8,128)(2,1)S(1)}, u32[]{:S(2)}, u32[]{:S(2)}) collective-permute-start(bf16[64,1536]{1,0:T(8,128)(2,1)S(1)} %get-tuple-element.47), channel_id=1, source_target_pairs={{0,1},{1,2},{2,3},{3,0},{4,5},{5,6},{6,7},{7,4},{8,9},{9,10},{10,1... | collective-permute-start | bytes 589832 | tf_op jit(solution)/shard_map/ppermute | solution.py:320
  61.2 12.0 %collective-permute-start.19 = (bf16[64,1536]{1,0:T(8,128)(2,1)S(1)}, bf16[64,1536]{1,0:T(8,128)(2,1)S(1)}, u32[]{:S(2)}, u32[]{:S(2)}) collective-permute-start(bf16[64,1536]{1,0:T(8,128)(2,1)S(1)} %get-tuple-element.48.refs_13_), channel_id=1, source_target_pairs={{0,2},{1,3},{2,0},{3,1},{4,6},{5,7},{6,4},{7,5},{8,10},{9,11},{10,... | collective-permute-start | bytes 589832 | tf_op jit(solution)/shard_map/ppermute | solution.py:320

commit v8 on v7

--- a/solution.py
+++ b/solution.py
@@ -86,14 +86,20 @@
     )[0]
 
 
+def copied(ordered, chunk, after):
+    def body(chunk_ref, out_ref):
+        out_ref[...] = chunk_ref[...]
+
+    return ordered(body, (chunk,), [jax.ShapeDtypeStruct(chunk.shape, BF16)], "copied", 0.1, after=after)[0]
+
+
 def first_product(ordered, core, other, chunk, up_weight, down_weight, name):
     _, rows, features = chunk.shape
     half = up_weight.shape[1] // 2
     tile = tile_of(half)
     pieces = half // tile
 
-    def body(core_ref, chunk_ref, up_hbm, down_hbm, up_ref, down_ref, *refs):
-        out_ref, sems = refs[-2:]
+    def body(core_ref, chunk_ref, up_hbm, down_hbm, up_ref, down_ref, out_ref, sems):
         side = 1 - core_ref[0] if other else core_ref[0]
         copies = []
         for i in range(pieces):
@@ -103,8 +109,6 @@
             copies.append(pltpu.make_async_copy(down_hbm.at[units, :], down_ref.at[part, :], sems.at[1, i]))
         for copy in copies:
             copy.start()
-        if not other:
-            refs[0][...] = chunk_ref[...]
         for i in range(pieces):
             part = slice(i * tile, (i + 1) * tile)
             copies[2 * i].wait()
@@ -113,7 +117,6 @@
             out_ref[1, :, part] = dot(chunk_ref[1], down_ref[part, :], NT).astype(BF16)
 
     outs = [VMEM((features, half), BF16), VMEM((half, features), BF16)]
-    outs += [] if other else [jax.ShapeDtypeStruct(chunk.shape, BF16)]
     return ordered(
         body,
         (core, chunk, in_hbm(up_weight), in_hbm(down_weight)),
@@ -242,7 +245,8 @@
             busy[kind, slot] = copy
 
         left = refs[: len(flat)]
-        for b, (other, first, acts) in enumerate(blocks):
+        sent = [0, 0]
+        for b, (other, first, acts, parts) in enumerate(blocks):
             side = 1 - core_ref[0] if other else core_ref[0]
             base = side * half + first
             row = 0
@@ -254,16 +258,18 @@
                 act_v[rows, :] = taken[1][:, columns] if len(taken) == 2 else taken[0][1, :, columns]
                 row += arrays[0].shape[-2]
             for step in range(max(up_steps, down_steps)):
-                if step < up_steps:
+                if step < up_steps and 0 in parts:
                     part = slice(step * up_tile, (step + 1) * up_tile)
                     value = dot(turned_ref[part, :], act_g[...], NN)
                     target = up_hbm.at[pl.ds(step * up_tile, up_tile), pl.ds(pl.multiple_of(base, 128), width)]
-                    send(0, b * up_steps + step, value, up_stage, target)
-                if step < down_steps:
+                    send(0, sent[0], value, up_stage, target)
+                    sent[0] += 1
+                if step < down_steps and 1 in parts:
                     part = slice(step * down_tile, (step + 1) * down_tile)
                     value = dot(act_v[:, part], grads_ref[...], TN)
                     target = down_hbm.at[pl.ds(pl.multiple_of(base + step * down_tile, 128), down_tile), :]
-                    send(1, b * down_steps + step, value, down_stage, target)
+                    send(1, sent[1], value, down_stage, target)
+                    sent[1] += 1
                 if share is not None and b == 0 and step < up_steps:
                     part = slice(step * up_tile, (step + 1) * up_tile)
                     terms = [
@@ -292,7 +298,7 @@
         args,
         [*outs, jax.ShapeDtypeStruct((8, 128), F32)],
         name,
-        4.0 * len(blocks),
+        2.0 * sum(len(block[3]) for block in blocks),
         spaces=spaces,
         out_spaces=[pl.ANY, pl.ANY] + [VMEM] * (len(outs) - 1),
         scratch=[
@@ -334,8 +340,9 @@
 
     up_other, down_other, give = first_product(ordered, core, True, chunks[0], up_weight, down_weight, "give_first")
     got = swap_cores(give)
-    up_mine, down_mine, sent_back, keep = first_product(ordered, core, False, chunks[0], up_weight, down_weight, "keep_first")
+    up_mine, down_mine, keep = first_product(ordered, core, False, chunks[0], up_weight, down_weight, "keep_first")
     sums = [across_chips(keep, got)]
+    sent_back = copied(ordered, chunks[0], [sums[0][0]])
 
     def acts_of(sums, apart=False):
         mine = gelu(ordered, sums, apart)
@@ -368,24 +375,24 @@
 
     def grads(places, before, share):
         blocks = [
-            (side, i * width, [(early[side], i * width), (middle[side], i * width), (late_acts[i][side], 0)])
-            for side, i in places
+            (side, i * width, [(early[side], i * width), (middle[side], i * width), (late_acts[i][side], 0)], parts)
+            for side, i, parts in places
         ]
         return weight_grads(ordered, core, blocks, turned, all_grads, half, scale, before, "weight_grads", share)
 
     late_acts.append(acts_of(late[:1]))
-    up_grad, down_grad, share, _ = grads([(0, 0)], None, ([(middle[side][0], both[side], 0) for side in (0, 1)], BF16))
+    up_grad, down_grad, share, _ = grads([(0, 0, (0, 1))], None, ([(middle[side][0], both[side], 0) for side in (0, 1)], BF16))
     middle_share = shift(share, -offsets[-2])
     partial = None
     terms = [(late_acts[0][side][0], both[side], 0) for side in (0, 1)]
     if slices > 1:
         late_acts.append(acts_of(late[1:]))
         terms.append((late_acts[1][0][0], up_mine, width))
-        up_grad, down_grad, partial, _ = grads([(1, 0)], (up_grad, down_grad), (terms, F32))
+        up_grad, down_grad, partial, _ = grads([(1, 0, (0,))], (up_grad, down_grad), (terms, F32))
         terms = [(late_acts[1][1][0], up_other, width)]
     so_far, share = input_product(ordered, rows, terms, 3.0, partial, shares)
     share = shift(share, -offsets[-1])
-    last = [(0, 1), (1, 1)] if slices > 1 else [(1, 0)]
+    last = [(1, 0, (1,)), (0, 1, (0, 1)), (1, 1, (0, 1))] if slices > 1 else [(1, 0, (0, 1))]
     up_grad, down_grad, _ = grads(last, (up_grad, down_grad), None)
     return (so_far + middle_share.astype(F32) + share.astype(F32)).astype(BF16), up_grad, down_grad
 

time: 74.2 us -> 75.5 us (1.018)
  waiting for transfers between devices: 8.67 us -> 11.2 us
  starting transfers between devices: 17.1 us -> 15.5 us
    ppermute x6, waiting for transfers between devices: 5.99 us -> 11.1 us  [shift(): lax.ppermute(x, 'narrow', [(i, (i + places) % narrow) for i in range(narr...]
    ppermute x5, waiting for transfers between devices: 2.65 us -> 0.01 us  [across_chips(): lax.ppermute(partial, 'wide', [(i, i ^ 2 * hop) for i in range(wide)])]
    ppermute x5, starting transfers between devices: 6.07 us -> 4.51 us  [across_chips(): lax.ppermute(partial, 'wide', [(i, i ^ 2 * hop) for i in range(wide)])]
    pallas_call x19 -> x20, Pallas kernels: 46.3 us -> 46.6 us  [__call__(): pl.pallas_call(kernel, out_shape=outs, in_specs=specs, out_specs=[pl.Bloc...]
  transfers between devices with their start and end apart: 20 -> 20, of which waited for: 4 -> 3; matrix products, arithmetic and copies ran while one was open for 1% -> 0% of each run, Pallas kernels for 61% -> 61%
where the time goes in v8:
time: 75.5 us; the launch traced here: 75.3 us
  Pallas kernels  46.6 us (62%)
  starting transfers between devices  15.5 us (21%)
  waiting for transfers between devices  11.2 us (15%)
  other arithmetic  1.12 us (1%)
  between operations  0.97 us (1%)
    pallas_call x20, Pallas kernels, __call__(): pl.pallas_call(kernel, out_shape=outs, in_specs=specs, out_specs=[pl.Bloc...  46.6 us
    ppermute x6, waiting for transfers between devices, shift(): lax.ppermute(x, 'narrow', [(i, (i + places) % narrow) for i in range(narr...  11.1 us
    ppermute x6, starting transfers between devices, shift(): lax.ppermute(x, 'narrow', [(i, (i + places) % narrow) for i in range(narr...  9.38 us
    ppermute x5, starting transfers between devices, across_chips(): lax.ppermute(partial, 'wide', [(i, i ^ 2 * hop) for i in range(wide)])  4.51 us
    ppermute x9, starting transfers between devices, swap_cores(): return lax.ppermute(x, 'wide', [(i, i ^ 1) for i in range(wide)])  1.57 us
  transfers between devices with their start and end apart: 20, of which 3 were waited for; matrix products, arithmetic and copies ran while one was open for 0% of the time, Pallas kernels for 61%

profile of v8, /device:TPU:0, one launch (start us, length us, event | category | flops | bytes accessed | tf_op | source)
XLA Modules:
  0.0 75.3 jit_solution(3246710987327664057)
XLA Ops:
  0.6 1.0 %stacked.1.refs_1_.refs_4_.refs_0_ = bf16[2,64,1536]{2,1,0:T(8,128)(2,1)S(1)} custom-call(bf16[64,1536]{1,0:T(8,128)(2,1)} %refs_0_.1, bf16[64,1536]{1,0:T(8,128)(2,1)} %refs_1_.1), custom_call_target="tpu_custom_call" | custom-call | flops 2000000000 | tf_op jit(solution)/shard_map/stacked/pallas_call | solution.py:53
  1.7 3.1 %collective-permute-start = (bf16[2,64,1536]{2,1,0:T(8,128)(2,1)S(1)}, bf16[2,64,1536]{2,1,0:T(8,128)(2,1)S(1)}, u32[]{:S(2)}, u32[]{:S(2)}) collective-permute-start(bf16[2,64,1536]{2,1,0:T(8,128)(2,1)S(1)} %stacked.1.refs_1_.refs_4_.refs_0_), channel_id=1, source_target_pairs={{0,1},{1,2},{2,3},{3,0},{4,5},{5,6},{6,7},{7,4},{8,9},{9,10},{10,1... | collective-permute-start | bytes 1179656 | tf_op jit(solution)/shard_map/ppermute | solution.py:326
  4.8 4.5 %give_first.1 = (bf16[1536,1536]{1,0:T(8,128)(2,1)S(1)}, bf16[1536,1536]{1,0:T(8,128)(2,1)S(1)}, bf16[2,64,1536]{2,1,0:T(8,128)(2,1)S(1)}) custom-call(s32[1]{0:T(128)} %bitcast.refs_0_, bf16[2,64,1536]{2,1,0:T(8,128)(2,1)S(1)} %stacked.1.refs_1_.refs_4_.refs_0_, bf16[1536,3072]{1,0:T(8,128)(2,1)} %refs_2_.3, bf16[3072,1536]{1,0:T(8,128)(2,1)} %refs_3_.3, ...), custom_call_target="tpu_custom_call" | custom-call | flops 17999998976 | tf_op jit(solution)/shard_map/give_first/pallas_call | solution.py:53
  9.4 4.5 %keep_first.1 = (bf16[1536,1536]{1,0:T(8,128)(2,1)S(1)}, bf16[1536,1536]{1,0:T(8,128)(2,1)S(1)}, bf16[2,64,1536]{2,1,0:T(8,128)(2,1)S(1)}) custom-call(s32[1]{0:T(128)} %bitcast.refs_0_, bf16[2,64,1536]{2,1,0:T(8,128)(2,1)S(1)} %stacked.1.refs_1_.refs_4_.refs_0_, bf16[1536,3072]{1,0:T(8,128)(2,1)} %refs_2_.3, bf16[3072,1536]{1,0:T(8,128)(2,1)} %refs_3_.3, ...), custom_call_target="tpu_custom_call" | custom-call | flops 17999998976 | tf_op jit(solution)/shard_map/keep_first/pallas_call | solution.py:53
  14.0 1.5 %collective-permute-start.3 = (bf16[2,64,1536]{2,1,0:T(8,128)(2,1)S(1)}, bf16[2,64,1536]{2,1,0:T(8,128)(2,1)S(1)}, u32[]{:S(2)}, u32[]{:S(2)}) collective-permute-start(bf16[2,64,1536]{2,1,0:T(8,128)(2,1)S(1)} %add_convert_fusion.2.refs_1_.refs_3_.refs_0_), channel_id=1, source_target_pairs={{0,8},{4,12},{8,0},{12,4},{1,9},{5,13},{9,1},{13,5},{2,10},{6,14},... | collective-permute-start | bytes 1179656 | tf_op jit(solution)/shard_map/ppermute | solution.py:332
  15.6 2.3 %collective-permute-start.6 = (bf16[2,64,1536]{2,1,0:T(8,128)(2,1)S(1)}, bf16[2,64,1536]{2,1,0:T(8,128)(2,1)S(1)}, u32[]{:S(2)}, u32[]{:S(2)}) collective-permute-start(bf16[2,64,1536]{2,1,0:T(8,128)(2,1)S(1)} %copied.1.refs_4_), channel_id=1, source_target_pairs={{0,3},{1,0},{2,1},{3,2},{4,7},{5,4},{6,5},{7,6},{8,11},{9,8},{10,9... | collective-permute-start | bytes 1179656 | tf_op jit(solution)/shard_map/ppermute | solution.py:326
  17.9 2.3 %give.3.refs_3_ = bf16[2,64,1536]{2,1,0:T(8,128)(2,1)S(1)} custom-call(bf16[2,64,1536]{2,1,0:T(8,128)(2,1)S(1)} %collective-permute-done.refs_0_.refs_1_, bf16[1536,1536]{1,0:T(8,128)(2,1)S(1)} %get-tuple-element.31.refs_1_.refs_3_.refs_10_.refs_11_, bf16[1536,1536]{1,0:T(8,128)(2,1)S(1)} %get-tuple-element.32.refs_2_, ...), custom_call_target="tpu_custom_call" | custom-call | flops 9600000000 | tf_op jit(solution)/shard_map/give/pallas_call | solution.py:53
  20.6 2.3 %keep.3.refs_5_ = bf16[2,64,1536]{2,1,0:T(8,128)(2,1)S(1)} custom-call(bf16[2,64,1536]{2,1,0:T(8,128)(2,1)S(1)} %collective-permute-done.refs_0_.refs_1_, bf16[1536,1536]{1,0:T(8,128)(2,1)S(1)} %get-tuple-element.28.refs_1_.refs_2_.refs_9_.refs_10_.refs_12_, bf16[1536,1536]{1,0:T(8,128)(2,1)S(1)} %get-tuple-element.29.refs_2_, ...), custom_call_target="tpu_custom_call" | custom-call | flops 9600000000 | tf_op jit(solution)/shard_map/keep/pallas_call | solution.py:53
  23.0 0.4 collective-permute-start.5
  23.4 4.0 %collective-permute-done.6.refs_0_.refs_2_ = bf16[2,64,1536]{2,1,0:T(8,128)(2,1)S(1)} collective-permute-done((bf16[2,64,1536]{2,1,0:T(8,128)(2,1)S(1)}, bf16[2,64,1536]{2,1,0:T(8,128)(2,1)S(1)}, u32[]{:S(2)}, u32[]{:S(2)}) %collective-permute-start.6) | collective-permute-done | bytes 393248 | tf_op jit(solution)/shard_map/ppermute | solution.py:326
  27.4 2.3 %give.4.refs_3_ = bf16[2,64,1536]{2,1,0:T(8,128)(2,1)S(1)} custom-call(bf16[2,64,1536]{2,1,0:T(8,128)(2,1)S(1)} %collective-permute-done.6.refs_0_.refs_2_, bf16[1536,1536]{1,0:T(8,128)(2,1)S(1)} %get-tuple-element.31.refs_1_.refs_3_.refs_10_.refs_11_, bf16[1536,1536]{1,0:T(8,128)(2,1)S(1)} %get-tuple-element.32.refs_2_, ...), custom_call_target="tpu_custom_call" | custom-call | flops 9600000000 | tf_op jit(solution)/shard_map/give/pallas_call | solution.py:53
  29.8 2.3 %keep.4.refs_4_ = bf16[2,64,1536]{2,1,0:T(8,128)(2,1)S(1)} custom-call(bf16[2,64,1536]{2,1,0:T(8,128)(2,1)S(1)} %collective-permute-done.6.refs_0_.refs_2_, bf16[1536,1536]{1,0:T(8,128)(2,1)S(1)} %get-tuple-element.28.refs_1_.refs_2_.refs_9_.refs_10_.refs_12_, bf16[1536,1536]{1,0:T(8,128)(2,1)S(1)} %get-tuple-element.29.refs_2_, ...), custom_call_target="tpu_custom_call" | custom-call | flops 9600000000 | tf_op jit(solution)/shard_map/keep/pallas_call | solution.py:53
  32.3 0.4 collective-permute-start.10
  32.7 4.6 %collective-permute-done.1.refs_0_.refs_3_ = bf16[2,64,1536]{2,1,0:T(8,128)(2,1)S(1)} collective-permute-done((bf16[2,64,1536]{2,1,0:T(8,128)(2,1)S(1)}, bf16[2,64,1536]{2,1,0:T(8,128)(2,1)S(1)}, u32[]{:S(2)}, u32[]{:S(2)}) %collective-permute-start.1) | collective-permute-done | bytes 393248 | tf_op jit(solution)/shard_map/ppermute | solution.py:326
  37.3 2.3 %give.5.refs_4_ = bf16[2,64,1536]{2,1,0:T(8,128)(2,1)S(1)} custom-call(bf16[2,64,1536]{2,1,0:T(8,128)(2,1)S(1)} %collective-permute-done.1.refs_0_.refs_3_, bf16[1536,1536]{1,0:T(8,128)(2,1)S(1)} %get-tuple-element.31.refs_1_.refs_3_.refs_10_.refs_11_, bf16[1536,1536]{1,0:T(8,128)(2,1)S(1)} %get-tuple-element.32.refs_2_, ...), custom_call_target="tpu_custom_call" | custom-call | flops 9600000000 | tf_op jit(solution)/shard_map/give/pallas_call | solution.py:53
  39.8 0.5 gelu.4.refs_3_.refs_0_.refs_7_
  40.3 0.5 collective-permute-start.11
  40.8 2.3 %keep.5.refs_6_ = bf16[2,64,1536]{2,1,0:T(8,128)(2,1)S(1)} custom-call(bf16[2,64,1536]{2,1,0:T(8,128)(2,1)S(1)} %collective-permute-done.1.refs_0_.refs_3_, bf16[1536,1536]{1,0:T(8,128)(2,1)S(1)} %get-tuple-element.28.refs_1_.refs_2_.refs_9_.refs_10_.refs_12_, bf16[1536,1536]{1,0:T(8,128)(2,1)S(1)} %get-tuple-element.29.refs_2_, ...), custom_call_target="tpu_custom_call" | custom-call | flops 9600000000 | tf_op jit(solution)/shard_map/keep/pallas_call | solution.py:53
  43.3 0.6 collective-permute-start.12
  44.2 3.1 %input_product.2 = (bf16[64,1536]{1,0:T(8,128)(2,1)S(1)}, bf16[64,1536]{1,0:T(8,128)(2,1)S(1)}) custom-call(bf16[2,128,1536]{2,1,0:T(8,128)(2,1)S(1)} %gelu.4.refs_3_.refs_0_.refs_7_, bf16[2,128,1536]{2,1,0:T(8,128)(2,1)S(1)} %collective-permute-done.11.refs_1_.refs_3_.refs_11_, ...), custom_call_target="tpu_custom_call" | custom-call | flops 400000000 | tf_op jit(solution)/shard_map/input_product/pallas_call | solution.py:53
  47.3 0.3 gelu.5
  47.6 1.6 %collective-permute-start.9 = (bf16[2,64,768]{2,1,0:T(8,128)(2,1)S(1)}, bf16[2,64,768]{2,1,0:T(8,128)(2,1)S(1)}, u32[]{:S(2)}, u32[]{:S(2)}) collective-permute-start(bf16[2,64,768]{2,1,0:T(8,128)(2,1)S(1)} %get-tuple-element.52.refs_5_.refs_0_), channel_id=1, source_target_pairs={{0,8},{4,12},{8,0},{12,4},{1,9},{5,13},{9,1},{13,5},{2,10},{6,14},... | collective-permute-start | bytes 589832 | tf_op jit(solution)/shard_map/ppermute | solution.py:332
  49.2 2.0 %collective-permute-start.15 = (bf16[64,1536]{1,0:T(8,128)(2,1)S(1)}, bf16[64,1536]{1,0:T(8,128)(2,1)S(1)}, u32[]{:S(2)}, u32[]{:S(2)}) collective-permute-start(bf16[64,1536]{1,0:T(8,128)(2,1)S(1)} %get-tuple-element.35.refs_2_), channel_id=1, source_target_pairs={{0,3},{1,0},{2,1},{3,2},{4,7},{5,4},{6,5},{7,6},{8,11},{9,8},{10,9... | collective-permute-start | bytes 589832 | tf_op jit(solution)/shard_map/ppermute | solution.py:326
  51.4 0.6 collective-permute-start.17
  52.0 4.9 %weight_grads.3 = (f32[1536,3072]{1,0:T(8,128)}, f32[3072,1536]{1,0:T(8,128)}, bf16[64,1536]{1,0:T(8,128)(2,1)S(1)}, f32[8,128]{1,0:T(8,128)S(1)}) custom-call(s32[1]{0:T(128)} %bitcast.refs_0_, bf16[1536,256]{1,0:T(8,128)(2,1)S(1)} %get-tuple-element.33.refs_1_, bf16[256,1536]{1,0:T(8,128)(2,1)S(1)} %get-tuple-element.34.refs_4_.refs_2_, ...), custom_call_target="tpu_custom_call" | custom-call | flops 16000000000 | tf_op jit(solution)/shard_map/weight_grads/pallas_call | solution.py:53
  57.1 0.3 collective-permute-start.18
  57.4 3.4 %weight_grads.4 = (f32[1536,3072]{1,0:T(8,128)}, f32[3072,1536]{1,0:T(8,128)}, f32[64,1536]{1,0:T(8,128)S(1)}, f32[8,128]{1,0:T(8,128)S(1)}) custom-call(s32[1]{0:T(128)} %bitcast.refs_0_, bf16[1536,256]{1,0:T(8,128)(2,1)S(1)} %get-tuple-element.33.refs_1_, ...), custom_call_target="tpu_custom_call", output_to_operand_aliasing={{0}: (13, {}), {1}: (14, {})} | custom-call | flops 8000000000 | tf_op jit(solution)/shard_map/weight_grads/pallas_call | solution.py:53
  60.8 0.9 %input_product.3 = (f32[64,1536]{1,0:T(8,128)S(1)}, bf16[64,1536]{1,0:T(8,128)(2,1)S(1)}) custom-call(bf16[2,64,768]{2,1,0:T(8,128)(2,1)S(1)} %collective-permute-done.14.refs_0_.refs_14_, bf16[1536,1536]{1,0:T(8,128)(2,1)S(1)} %get-tuple-element.31.refs_1_.refs_3_.refs_10_.refs_11_, bf16[64,1536]{1,0:T(8,128)(2,1)S(1)} %get-tuple-element.39.refs_2_, ...), custom_call_target="tpu_custom_call" | custom-call | flops 12000000000 | tf_op jit(solution)/shard_map/input_product/pallas_call | solution.py:53
  61.6 1.5 %collective-permute-start.19 = (bf16[64,1536]{1,0:T(8,128)(2,1)S(1)}, bf16[64,1536]{1,0:T(8,128)(2,1)S(1)}, u32[]{:S(2)}, u32[]{:S(2)}) collective-permute-start(bf16[64,1536]{1,0:T(8,128)(2,1)S(1)} %get-tuple-element.46.refs_17_), channel_id=1, source_target_pairs={{0,2},{1,3},{2,0},{3,1},{4,6},{5,7},{6,4},{7,5},{8,10},{9,11},{10,... | collective-permute-start | bytes 589832 | tf_op jit(solution)/shard_map/ppermute | solution.py:326
  63.1 8.9 %weight_grads.5 = (f32[1536,3072]{1,0:T(8,128)}, f32[3072,1536]{1,0:T(8,128)}, f32[8,128]{1,0:T(8,128)}) custom-call(s32[1]{0:T(128)} %bitcast.refs_0_, bf16[1536,256]{1,0:T(8,128)(2,1)S(1)} %get-tuple-element.33.refs_1_, bf16[256,1536]{1,0:T(8,128)(2,1)S(1)} %get-tuple-element.34.refs_4_.refs_2_, ...), custom_call_target="tpu_custom_call", output_to_operand_aliasing={{0}: (15, {}), {1}: (16, {})} | custom-call | flops 40000000000 | tf_op jit(solution)/shard_map/weight_grads/pallas_call | solution.py:53
  72.1 2.5 %collective-permute-done.19 = bf16[64,1536]{1,0:T(8,128)(2,1)S(1)} collective-permute-done((bf16[64,1536]{1,0:T(8,128)(2,1)S(1)}, bf16[64,1536]{1,0:T(8,128)(2,1)S(1)}, u32[]{:S(2)}, u32[]{:S(2)}) %collective-permute-start.19) | collective-permute-done | bytes 196640 | tf_op jit(solution)/shard_map/ppermute | solution.py:326
  74.6 0.7 add_convert_fusion.3
  (33 shorter events, 1.7 us)
Async XLA Ops:
  1.7 16.2 %collective-permute-start = (bf16[2,64,1536]{2,1,0:T(8,128)(2,1)S(1)}, bf16[2,64,1536]{2,1,0:T(8,128)(2,1)S(1)}, u32[]{:S(2)}, u32[]{:S(2)}) collective-permute-start(bf16[2,64,1536]{2,1,0:T(8,128)(2,1)S(1)} %stacked.1.refs_1_.refs_4_.refs_0_), channel_id=1, source_target_pairs={{0,1},{1,2},{2,3},{3,0},{4,5},{5,6},{6,7},{7,4},{8,9},{9,10},{10,1... | collective-permute-start | bytes 1179656 | tf_op jit(solution)/shard_map/ppermute | solution.py:326
  9.3 4.6 %collective-permute-start.2 = (bf16[2,64,1536]{2,1,0:T(8,128)(2,1)S(1)}, bf16[2,64,1536]{2,1,0:T(8,128)(2,1)S(1)}, u32[]{:S(2)}, u32[]{:S(2)}) collective-permute-start(bf16[2,64,1536]{2,1,0:T(8,128)(2,1)S(1)} %get-tuple-element.27.refs_4_), channel_id=1, source_target_pairs={{0,4},{4,0},{8,12},{12,8},{1,5},{5,1},{9,13},{13,9},{2,6},{6,2},{1... | collective-permute-start | bytes 1179656 | tf_op jit(solution)/shard_map/ppermute | solution.py:323
  14.0 13.4 %collective-permute-start.3 = (bf16[2,64,1536]{2,1,0:T(8,128)(2,1)S(1)}, bf16[2,64,1536]{2,1,0:T(8,128)(2,1)S(1)}, u32[]{:S(2)}, u32[]{:S(2)}) collective-permute-start(bf16[2,64,1536]{2,1,0:T(8,128)(2,1)S(1)} %add_convert_fusion.2.refs_1_.refs_3_.refs_0_), channel_id=1, source_target_pairs={{0,8},{4,12},{8,0},{12,4},{1,9},{5,13},{9,1},{13,5},{2,10},{6,14},... | collective-permute-start | bytes 1179656 | tf_op jit(solution)/shard_map/ppermute | solution.py:332
  15.6 11.8 %collective-permute-start.6 = (bf16[2,64,1536]{2,1,0:T(8,128)(2,1)S(1)}, bf16[2,64,1536]{2,1,0:T(8,128)(2,1)S(1)}, u32[]{:S(2)}, u32[]{:S(2)}) collective-permute-start(bf16[2,64,1536]{2,1,0:T(8,128)(2,1)S(1)} %copied.1.refs_4_), channel_id=1, source_target_pairs={{0,3},{1,0},{2,1},{3,2},{4,7},{5,4},{6,5},{7,6},{8,11},{9,8},{10,9... | collective-permute-start | bytes 1179656 | tf_op jit(solution)/shard_map/ppermute | solution.py:326
  20.3 2.7 %collective-permute-start.4 = (bf16[2,64,1536]{2,1,0:T(8,128)(2,1)S(1)}, bf16[2,64,1536]{2,1,0:T(8,128)(2,1)S(1)}, u32[]{:S(2)}, u32[]{:S(2)}) collective-permute-start(bf16[2,64,1536]{2,1,0:T(8,128)(2,1)S(1)} %give.3.refs_3_), channel_id=1, source_target_pairs={{0,4},{4,0},{8,12},{12,8},{1,5},{5,1},{9,13},{13,9},{2,6},{6,2},{1... | collective-permute-start | bytes 1179656 | tf_op jit(solution)/shard_map/ppermute | solution.py:323
  20.3 17.0 %collective-permute-start.1 = (bf16[2,64,1536]{2,1,0:T(8,128)(2,1)S(1)}, bf16[2,64,1536]{2,1,0:T(8,128)(2,1)S(1)}, u32[]{:S(2)}, u32[]{:S(2)}) collective-permute-start(bf16[2,64,1536]{2,1,0:T(8,128)(2,1)S(1)} %collective-permute-done.refs_0_.refs_1_), channel_id=1, source_target_pairs={{0,1},{1,2},{2,3},{3,0},{4,5},{5,6},{6,7},{7,4},{8,9},{9,10},{10,1... | collective-permute-start | bytes 1179656 | tf_op jit(solution)/shard_map/ppermute | solution.py:326
  23.0 16.7 %collective-permute-start.5 = (bf16[2,64,1536]{2,1,0:T(8,128)(2,1)S(1)}, bf16[2,64,1536]{2,1,0:T(8,128)(2,1)S(1)}, u32[]{:S(2)}, u32[]{:S(2)}) collective-permute-start(bf16[2,64,1536]{2,1,0:T(8,128)(2,1)S(1)} %add_convert_fusion.1.refs_3_.refs_2_), channel_id=1, source_target_pairs={{0,8},{4,12},{8,0},{12,4},{1,9},{5,13},{9,1},{13,5},{2,10},{6,14},... | collective-permute-start | bytes 1179656 | tf_op jit(solution)/shard_map/ppermute | solution.py:332
  29.8 2.4 %collective-permute-start.7 = (bf16[2,64,1536]{2,1,0:T(8,128)(2,1)S(1)}, bf16[2,64,1536]{2,1,0:T(8,128)(2,1)S(1)}, u32[]{:S(2)}, u32[]{:S(2)}) collective-permute-start(bf16[2,64,1536]{2,1,0:T(8,128)(2,1)S(1)} %give.4.refs_3_), channel_id=1, source_target_pairs={{0,4},{4,0},{8,12},{12,8},{1,5},{5,1},{9,13},{13,9},{2,6},{6,2},{1... | collective-permute-start | bytes 1179656 | tf_op jit(solution)/shard_map/ppermute | solution.py:323
  32.3 15.0 %collective-permute-start.10 = (bf16[2,64,1536]{2,1,0:T(8,128)(2,1)S(1)}, bf16[2,64,1536]{2,1,0:T(8,128)(2,1)S(1)}, u32[]{:S(2)}, u32[]{:S(2)}) collective-permute-start(bf16[2,64,1536]{2,1,0:T(8,128)(2,1)S(1)} %add_convert_fusion.refs_3_.refs_0_), channel_id=1, source_target_pairs={{0,8},{4,12},{8,0},{12,4},{1,9},{5,13},{9,1},{13,5},{2,10},{6,14},... | collective-permute-start | bytes 1179656 | tf_op jit(solution)/shard_map/ppermute | solution.py:332
  39.7 3.5 %collective-permute-start.8 = (bf16[2,64,1536]{2,1,0:T(8,128)(2,1)S(1)}, bf16[2,64,1536]{2,1,0:T(8,128)(2,1)S(1)}, u32[]{:S(2)}, u32[]{:S(2)}) collective-permute-start(bf16[2,64,1536]{2,1,0:T(8,128)(2,1)S(1)} %give.5.refs_4_), channel_id=1, source_target_pairs={{0,4},{4,0},{8,12},{12,8},{1,5},{5,1},{9,13},{13,9},{2,6},{6,2},{1... | collective-permute-start | bytes 1179656 | tf_op jit(solution)/shard_map/ppermute | solution.py:323
  40.3 3.9 %collective-permute-start.11 = (bf16[2,128,1536]{2,1,0:T(8,128)(2,1)S(1)}, bf16[2,128,1536]{2,1,0:T(8,128)(2,1)S(1)}, u32[]{:S(2)}, u32[]{:S(2)}) collective-permute-start(bf16[2,128,1536]{2,1,0:T(8,128)(2,1)S(1)} %gelu.4.refs_3_.refs_0_.refs_7_), channel_id=1, source_target_pairs={{0,4},{4,0},{8,12},{12,8},{1,5},{5,1},{9,13},{13,9},{2,6},{6,2},{1... | collective-permute-start | bytes 2359304 | tf_op jit(solution)/shard_map/ppermute | solution.py:323
  43.3 7.9 %collective-permute-start.12 = (bf16[2,64,768]{2,1,0:T(8,128)(2,1)S(1)}, bf16[2,64,768]{2,1,0:T(8,128)(2,1)S(1)}, u32[]{:S(2)}, u32[]{:S(2)}) collective-permute-start(bf16[2,64,768]{2,1,0:T(8,128)(2,1)S(1)} %get-tuple-element.51.refs_4_.refs_0_), channel_id=1, source_target_pairs={{0,8},{4,12},{8,0},{12,4},{1,9},{5,13},{9,1},{13,5},{2,10},{6,14},... | collective-permute-start | bytes 589832 | tf_op jit(solution)/shard_map/ppermute | solution.py:332
  47.6 4.4 %collective-permute-start.13 = (bf16[64,1536]{1,0:T(8,128)(2,1)S(1)}, bf16[64,1536]{1,0:T(8,128)(2,1)S(1)}, u32[]{:S(2)}, u32[]{:S(2)}) collective-permute-start(bf16[64,1536]{1,0:T(8,128)(2,1)S(1)} %get-tuple-element.36.refs_4_.refs_7_.refs_8_), channel_id=1, source_target_pairs={{0,4},{4,0},{8,12},{12,8},{1,5},{5,1},{9,13},{13,9},{2,6},{6,2},{1... | collective-permute-start | bytes 589832 | tf_op jit(solution)/shard_map/ppermute | solution.py:323
  47.6 9.2 %collective-permute-start.9 = (bf16[2,64,768]{2,1,0:T(8,128)(2,1)S(1)}, bf16[2,64,768]{2,1,0:T(8,128)(2,1)S(1)}, u32[]{:S(2)}, u32[]{:S(2)}) collective-permute-start(bf16[2,64,768]{2,1,0:T(8,128)(2,1)S(1)} %get-tuple-element.52.refs_5_.refs_0_), channel_id=1, source_target_pairs={{0,8},{4,12},{8,0},{12,4},{1,9},{5,13},{9,1},{13,5},{2,10},{6,14},... | collective-permute-start | bytes 589832 | tf_op jit(solution)/shard_map/ppermute | solution.py:332
  49.2 11.6 %collective-permute-start.15 = (bf16[64,1536]{1,0:T(8,128)(2,1)S(1)}, bf16[64,1536]{1,0:T(8,128)(2,1)S(1)}, u32[]{:S(2)}, u32[]{:S(2)}) collective-permute-start(bf16[64,1536]{1,0:T(8,128)(2,1)S(1)} %get-tuple-element.35.refs_2_), channel_id=1, source_target_pairs={{0,3},{1,0},{2,1},{3,2},{4,7},{5,4},{6,5},{7,6},{8,11},{9,8},{10,9... | collective-permute-start | bytes 589832 | tf_op jit(solution)/shard_map/ppermute | solution.py:326
  51.2 6.1 %collective-permute-start.16 = (bf16[64,1536]{1,0:T(8,128)(2,1)S(1)}, bf16[64,1536]{1,0:T(8,128)(2,1)S(1)}, u32[]{:S(2)}, u32[]{:S(2)}) collective-permute-start(bf16[64,1536]{1,0:T(8,128)(2,1)S(1)} %get-tuple-element.37.refs_2_.refs_5_.refs_9_), channel_id=1, source_target_pairs={{0,4},{4,0},{8,12},{12,8},{1,5},{5,1},{9,13},{13,9},{2,6},{6,2},{1... | collective-permute-start | bytes 589832 | tf_op jit(solution)/shard_map/ppermute | solution.py:323
  51.4 6.0 %collective-permute-start.17 = (bf16[2,64,768]{2,1,0:T(8,128)(2,1)S(1)}, bf16[2,64,768]{2,1,0:T(8,128)(2,1)S(1)}, u32[]{:S(2)}, u32[]{:S(2)}) collective-permute-start(bf16[2,64,768]{2,1,0:T(8,128)(2,1)S(1)} %gelu.6.refs_6_.refs_11_.refs_7_), channel_id=1, source_target_pairs={{0,4},{4,0},{8,12},{12,8},{1,5},{5,1},{9,13},{13,9},{2,6},{6,2},{1... | collective-permute-start | bytes 589832 | tf_op jit(solution)/shard_map/ppermute | solution.py:323
  57.0 3.8 %collective-permute-start.14 = (bf16[2,64,768]{2,1,0:T(8,128)(2,1)S(1)}, bf16[2,64,768]{2,1,0:T(8,128)(2,1)S(1)}, u32[]{:S(2)}, u32[]{:S(2)}) collective-permute-start(bf16[2,64,768]{2,1,0:T(8,128)(2,1)S(1)} %gelu.7.refs_9_.refs_15_.refs_10_), channel_id=1, source_target_pairs={{0,4},{4,0},{8,12},{12,8},{1,5},{5,1},{9,13},{13,9},{2,6},{6,2},{1... | collective-permute-start | bytes 589832 | tf_op jit(solution)/shard_map/ppermute | solution.py:323
  57.1 15.0 %collective-permute-start.18 = (bf16[64,1536]{1,0:T(8,128)(2,1)S(1)}, bf16[64,1536]{1,0:T(8,128)(2,1)S(1)}, u32[]{:S(2)}, u32[]{:S(2)}) collective-permute-start(bf16[64,1536]{1,0:T(8,128)(2,1)S(1)} %get-tuple-element.45), channel_id=1, source_target_pairs={{0,1},{1,2},{2,3},{3,0},{4,5},{5,6},{6,7},{7,4},{8,9},{9,10},{10,1... | collective-permute-start | bytes 589832 | tf_op jit(solution)/shard_map/ppermute | solution.py:326
  61.6 13.0 %collective-permute-start.19 = (bf16[64,1536]{1,0:T(8,128)(2,1)S(1)}, bf16[64,1536]{1,0:T(8,128)(2,1)S(1)}, u32[]{:S(2)}, u32[]{:S(2)}) collective-permute-start(bf16[64,1536]{1,0:T(8,128)(2,1)S(1)} %get-tuple-element.46.refs_17_), channel_id=1, source_target_pairs={{0,2},{1,3},{2,0},{3,1},{4,6},{5,7},{6,4},{7,5},{8,10},{9,11},{10,... | collective-permute-start | bytes 589832 | tf_op jit(solution)/shard_map/ppermute | solution.py:326

commit v9 on v8

--- a/solution.py
+++ b/solution.py
@@ -86,20 +86,14 @@
     )[0]
 
 
-def copied(ordered, chunk, after):
-    def body(chunk_ref, out_ref):
-        out_ref[...] = chunk_ref[...]
-
-    return ordered(body, (chunk,), [jax.ShapeDtypeStruct(chunk.shape, BF16)], "copied", 0.1, after=after)[0]
-
-
 def first_product(ordered, core, other, chunk, up_weight, down_weight, name):
     _, rows, features = chunk.shape
     half = up_weight.shape[1] // 2
     tile = tile_of(half)
     pieces = half // tile
 
-    def body(core_ref, chunk_ref, up_hbm, down_hbm, up_ref, down_ref, out_ref, sems):
+    def body(core_ref, chunk_ref, up_hbm, down_hbm, up_ref, down_ref, *refs):
+        out_ref, sems = refs[-2:]
         side = 1 - core_ref[0] if other else core_ref[0]
         copies = []
         for i in range(pieces):
@@ -109,6 +103,8 @@
             copies.append(pltpu.make_async_copy(down_hbm.at[units, :], down_ref.at[part, :], sems.at[1, i]))
         for copy in copies:
             copy.start()
+        if not other:
+            refs[0][...] = chunk_ref[...]
         for i in range(pieces):
             part = slice(i * tile, (i + 1) * tile)
             copies[2 * i].wait()
@@ -117,6 +113,7 @@
             out_ref[1, :, part] = dot(chunk_ref[1], down_ref[part, :], NT).astype(BF16)
 
     outs = [VMEM((features, half), BF16), VMEM((half, features), BF16)]
+    outs += [] if other else [jax.ShapeDtypeStruct(chunk.shape, BF16)]
     return ordered(
         body,
         (core, chunk, in_hbm(up_weight), in_hbm(down_weight)),
@@ -272,20 +269,26 @@
                     sent[1] += 1
                 if share is not None and b == 0 and step < up_steps:
                     part = slice(step * up_tile, (step + 1) * up_tile)
-                    terms = [
-                        (grad_of(refs[len(flat) + i]), refs[len(flat) + len(share[0]) + i], low)
-                        for i, (_, _, low) in enumerate(share[0])
-                    ]
-                    refs[outs_at + 2][:, part] = product_terms(terms, part).astype(share[1])
+                    given = list(refs[len(flat) :])
+                    filled = []
+                    for acts, _, low in share[0]:
+                        rows = [grad_of(given.pop(0)) for _ in acts]
+                        filled.append((rows[0] if len(rows) == 1 else jnp.concatenate(rows, axis=0), given.pop(0), low))
+                    value = product_terms(filled, part).astype(share[1])
+                    height = value.shape[0] // share[2]
+                    for i in range(share[2]):
+                        refs[outs_at + 2 + i][:, part] = value[i * height : (i + 1) * height]
         for copy in busy.values():
             copy.wait()
 
     args = [core, turned, all_grads, *flat]
     outs = [pltpu.HBM((features, 2 * half), F32), pltpu.HBM((2 * half, features), F32)]
     if share is not None:
-        terms, kind = share
-        args += [act for act, _, _ in terms] + [in_vmem(weight) for _, weight, _ in terms]
-        outs.append(jax.ShapeDtypeStruct((terms[0][0].shape[-2], features), kind))
+        terms, kind, count = share
+        for acts, weight, _ in terms:
+            args += [*acts, in_vmem(weight)]
+        height = sum(a.shape[-2] for a in terms[0][0]) // count
+        outs += [jax.ShapeDtypeStruct((height, features), kind)] * count
     spaces = [None] * len(args)
     outs_at = len(args) - 3 + (0 if before is None else 2)
     aliases = {}
@@ -340,9 +343,8 @@
 
     up_other, down_other, give = first_product(ordered, core, True, chunks[0], up_weight, down_weight, "give_first")
     got = swap_cores(give)
-    up_mine, down_mine, keep = first_product(ordered, core, False, chunks[0], up_weight, down_weight, "keep_first")
+    up_mine, down_mine, sent_back, keep = first_product(ordered, core, False, chunks[0], up_weight, down_weight, "keep_first")
     sums = [across_chips(keep, got)]
-    sent_back = copied(ordered, chunks[0], [sums[0][0]])
 
     def acts_of(sums, apart=False):
         mine = gelu(ordered, sums, apart)
@@ -366,10 +368,9 @@
 
     turned, all_grads = collect(ordered, [chunks[offset] for offset in offsets], [own for own, _ in late])
     both = (up_mine, up_other)
-    shares = input_product(ordered, rows, [(early[side][0], both[side], 0) for side in (0, 1)], 0.1)
-    shares = [share if offset == 0 else shift(share, -offset) for offset, share in zip(offsets, shares)]
     middle = acts_of(sums[-1:], True)
 
+    both = (up_mine, up_other)
     scale = (rows * narrow) ** -0.5
     late_acts = []
 
@@ -381,20 +382,21 @@
         return weight_grads(ordered, core, blocks, turned, all_grads, half, scale, before, "weight_grads", share)
 
     late_acts.append(acts_of(late[:1]))
-    up_grad, down_grad, share, _ = grads([(0, 0, (0, 1))], None, ([(middle[side][0], both[side], 0) for side in (0, 1)], BF16))
-    middle_share = shift(share, -offsets[-2])
+    terms = [((early[side][0], middle[side][0]), both[side], 0) for side in (0, 1)]
+    up_grad, down_grad, *shares, _ = grads([(0, 0, (0, 1))], None, (terms, BF16, narrow - 1))
+    kept, *shares = [share if offset == 0 else shift(share, -offset) for offset, share in zip(offsets, shares)]
     partial = None
     terms = [(late_acts[0][side][0], both[side], 0) for side in (0, 1)]
     if slices > 1:
         late_acts.append(acts_of(late[1:]))
-        terms.append((late_acts[1][0][0], up_mine, width))
-        up_grad, down_grad, partial, _ = grads([(1, 0, (0,))], (up_grad, down_grad), (terms, F32))
+        terms = [((act,), weight, low) for act, weight, low in [*terms, (late_acts[1][0][0], up_mine, width)]]
+        up_grad, down_grad, partial, _ = grads([(1, 0, (0,))], (up_grad, down_grad), (terms, F32, 1))
         terms = [(late_acts[1][1][0], up_other, width)]
-    so_far, share = input_product(ordered, rows, terms, 3.0, partial, shares)
+    (share,) = input_product(ordered, rows, terms, 3.0, partial)
     share = shift(share, -offsets[-1])
     last = [(1, 0, (1,)), (0, 1, (0, 1)), (1, 1, (0, 1))] if slices > 1 else [(1, 0, (0, 1))]
     up_grad, down_grad, _ = grads(last, (up_grad, down_grad), None)
-    return (so_far + middle_share.astype(F32) + share.astype(F32)).astype(BF16), up_grad, down_grad
+    return sum(share.astype(F32) for share in (kept, *shares, share)).astype(BF16), up_grad, down_grad
 
 
 def solution(mesh):

time: 75.5 us -> 76.9 us (1.019)
  Pallas kernels: 46.6 us -> 44.1 us
  starting transfers between devices: 15.5 us -> 17.7 us
  waiting for transfers between devices: 11.2 us -> 12.9 us
    ppermute x5, waiting for transfers between devices: 0.01 us -> 5.98 us  [across_chips(): lax.ppermute(partial, 'wide', [(i, i ^ 2 * hop) for i in range(wide)])]
    ppermute x6, waiting for transfers between devices: 11.1 us -> 6.91 us  [shift(): lax.ppermute(x, 'narrow', [(i, (i + places) % narrow) for i in range(narr...]
    ppermute x5, starting transfers between devices: 4.51 us -> 7.34 us  [across_chips(): lax.ppermute(partial, 'wide', [(i, i ^ 2 * hop) for i in range(wide)])]
    pallas_call x20 -> x18, Pallas kernels: 46.6 us -> 44.1 us  [__call__(): pl.pallas_call(kernel, out_shape=outs, in_specs=specs, out_specs=[pl.Bloc...]
  transfers between devices with their start and end apart: 20 -> 20, of which waited for: 3 -> 6; matrix products, arithmetic and copies ran while one was open for 0% -> 0% of each run, Pallas kernels for 61% -> 56%
where the time goes in v9:
time: 76.9 us; the launch traced here: 76.8 us
  Pallas kernels  44.1 us (57%)
  starting transfers between devices  17.7 us (23%)
  waiting for transfers between devices  12.9 us (17%)
  other arithmetic  1.15 us (1%)
  between operations  0.93 us (1%)
    pallas_call x18, Pallas kernels, __call__(): pl.pallas_call(kernel, out_shape=outs, in_specs=specs, out_specs=[pl.Bloc...  44.1 us
    ppermute x6, starting transfers between devices, shift(): lax.ppermute(x, 'narrow', [(i, (i + places) % narrow) for i in range(narr...  8.72 us
    ppermute x5, starting transfers between devices, across_chips(): lax.ppermute(partial, 'wide', [(i, i ^ 2 * hop) for i in range(wide)])  7.34 us
    ppermute x6, waiting for transfers between devices, shift(): lax.ppermute(x, 'narrow', [(i, (i + places) % narrow) for i in range(narr...  6.91 us
    ppermute x5, waiting for transfers between devices, across_chips(): lax.ppermute(partial, 'wide', [(i, i ^ 2 * hop) for i in range(wide)])  5.98 us
    ppermute x9, starting transfers between devices, swap_cores(): return lax.ppermute(x, 'wide', [(i, i ^ 1) for i in range(wide)])  1.68 us
  transfers between devices with their start and end apart: 20, of which 6 were waited for; matrix products, arithmetic and copies ran while one was open for 0% of the time, Pallas kernels for 56%

profile of v9, /device:TPU:0, one launch (start us, length us, event | category | flops | bytes accessed | tf_op | source)
XLA Modules:
  0.0 76.8 jit_solution(722637548661785943)
XLA Ops:
  0.6 1.0 %stacked.1.refs_1_.refs_4_.refs_0_ = bf16[2,64,1536]{2,1,0:T(8,128)(2,1)S(1)} custom-call(bf16[64,1536]{1,0:T(8,128)(2,1)} %refs_0_.1, bf16[64,1536]{1,0:T(8,128)(2,1)} %refs_1_.1), custom_call_target="tpu_custom_call" | custom-call | flops 2000000000 | tf_op jit(solution)/shard_map/stacked/pallas_call | solution.py:53
  1.7 3.1 %collective-permute-start = (bf16[2,64,1536]{2,1,0:T(8,128)(2,1)S(1)}, bf16[2,64,1536]{2,1,0:T(8,128)(2,1)S(1)}, u32[]{:S(2)}, u32[]{:S(2)}) collective-permute-start(bf16[2,64,1536]{2,1,0:T(8,128)(2,1)S(1)} %stacked.1.refs_1_.refs_4_.refs_0_), channel_id=1, source_target_pairs={{0,1},{1,2},{2,3},{3,0},{4,5},{5,6},{6,7},{7,4},{8,9},{9,10},{10,1... | collective-permute-start | bytes 1179656 | tf_op jit(solution)/shard_map/ppermute | solution.py:329
  4.8 4.5 %give_first.1 = (bf16[1536,1536]{1,0:T(8,128)(2,1)S(1)}, bf16[1536,1536]{1,0:T(8,128)(2,1)S(1)}, bf16[2,64,1536]{2,1,0:T(8,128)(2,1)S(1)}) custom-call(s32[1]{0:T(128)} %bitcast.refs_0_, bf16[2,64,1536]{2,1,0:T(8,128)(2,1)S(1)} %stacked.1.refs_1_.refs_4_.refs_0_, bf16[1536,3072]{1,0:T(8,128)(2,1)} %refs_2_.3, bf16[3072,1536]{1,0:T(8,128)(2,1)} %refs_3_.3, ...), custom_call_target="tpu_custom_call" | custom-call | flops 17999998976 | tf_op jit(solution)/shard_map/give_first/pallas_call | solution.py:53
  9.4 4.5 %keep_first.1 = (bf16[1536,1536]{1,0:T(8,128)(2,1)S(1)}, bf16[1536,1536]{1,0:T(8,128)(2,1)S(1)}, bf16[2,64,1536]{2,1,0:T(8,128)(2,1)S(1)}, bf16[2,64,1536]{2,1,0:T(8,128)(2,1)S(1)}) custom-call(s32[1]{0:T(128)} %bitcast.refs_0_, bf16[2,64,1536]{2,1,0:T(8,128)(2,1)S(1)} %stacked.1.refs_1_.refs_4_.refs_0_, bf16[1536,3072]{1,0:T(8,128)(2,1)} %refs_2_.3, ...), custom_call_target="tpu_custom_call" | custom-call | flops 17999998976 | tf_op jit(solution)/shard_map/keep_first/pallas_call | solution.py:53
  13.9 2.1 %collective-permute-start.1 = (bf16[2,64,1536]{2,1,0:T(8,128)(2,1)S(1)}, bf16[2,64,1536]{2,1,0:T(8,128)(2,1)S(1)}, u32[]{:S(2)}, u32[]{:S(2)}) collective-permute-start(bf16[2,64,1536]{2,1,0:T(8,128)(2,1)S(1)} %get-tuple-element.27), channel_id=1, source_target_pairs={{0,3},{1,0},{2,1},{3,2},{4,7},{5,4},{6,5},{7,6},{8,11},{9,8},{10,9... | collective-permute-start | bytes 1179656 | tf_op jit(solution)/shard_map/ppermute | solution.py:329
  16.1 1.8 %collective-permute-start.4 = (bf16[2,64,1536]{2,1,0:T(8,128)(2,1)S(1)}, bf16[2,64,1536]{2,1,0:T(8,128)(2,1)S(1)}, u32[]{:S(2)}, u32[]{:S(2)}) collective-permute-start(bf16[2,64,1536]{2,1,0:T(8,128)(2,1)S(1)} %add_convert_fusion.2.refs_3_.refs_0_), channel_id=1, source_target_pairs={{0,8},{4,12},{8,0},{12,4},{1,9},{5,13},{9,1},{13,5},{2,10},{6,14},... | collective-permute-start | bytes 1179656 | tf_op jit(solution)/shard_map/ppermute | solution.py:335
  17.9 2.3 %give.3.refs_3_ = bf16[2,64,1536]{2,1,0:T(8,128)(2,1)S(1)} custom-call(bf16[2,64,1536]{2,1,0:T(8,128)(2,1)S(1)} %collective-permute-done.refs_0_.refs_1_, bf16[1536,1536]{1,0:T(8,128)(2,1)S(1)} %get-tuple-element.31.refs_1_.refs_12_.refs_10_, bf16[1536,1536]{1,0:T(8,128)(2,1)S(1)} %get-tuple-element.32.refs_2_, ...), custom_call_target="tpu_custom_call" | custom-call | flops 9600000000 | tf_op jit(solution)/shard_map/give/pallas_call | solution.py:53
  20.5 2.3 %keep.3.refs_5_ = bf16[2,64,1536]{2,1,0:T(8,128)(2,1)S(1)} custom-call(bf16[2,64,1536]{2,1,0:T(8,128)(2,1)S(1)} %collective-permute-done.refs_0_.refs_1_, bf16[1536,1536]{1,0:T(8,128)(2,1)S(1)} %get-tuple-element.28.refs_1_.refs_9_.refs_8_.refs_12_, bf16[1536,1536]{1,0:T(8,128)(2,1)S(1)} %get-tuple-element.29.refs_2_, bf16[2,64,1536]{2,1,0:T(8,128)(2,1)S(1)} %give.3.refs_3_), custom_call_target="tpu_custom_call" | custom-call | flops 9600000000 | tf_op jit(solution)/shard_map/keep/pallas_call | solution.py:53
  23.0 0.4 collective-permute-start.6
  23.4 2.1 %collective-permute-done.1.refs_0_.refs_2_ = bf16[2,64,1536]{2,1,0:T(8,128)(2,1)S(1)} collective-permute-done((bf16[2,64,1536]{2,1,0:T(8,128)(2,1)S(1)}, bf16[2,64,1536]{2,1,0:T(8,128)(2,1)S(1)}, u32[]{:S(2)}, u32[]{:S(2)}) %collective-permute-start.1) | collective-permute-done | bytes 393248 | tf_op jit(solution)/shard_map/ppermute | solution.py:329
  25.5 2.6 %collective-permute-done.4.refs_4_.refs_1_ = bf16[2,64,1536]{2,1,0:T(8,128)(2,1)S(1)} collective-permute-done((bf16[2,64,1536]{2,1,0:T(8,128)(2,1)S(1)}, bf16[2,64,1536]{2,1,0:T(8,128)(2,1)S(1)}, u32[]{:S(2)}, u32[]{:S(2)}) %collective-permute-start.4) | collective-permute-done | bytes 393248 | tf_op jit(solution)/shard_map/ppermute | solution.py:335
  28.1 2.3 %give.4.refs_3_ = bf16[2,64,1536]{2,1,0:T(8,128)(2,1)S(1)} custom-call(bf16[2,64,1536]{2,1,0:T(8,128)(2,1)S(1)} %collective-permute-done.1.refs_0_.refs_2_, bf16[1536,1536]{1,0:T(8,128)(2,1)S(1)} %get-tuple-element.31.refs_1_.refs_12_.refs_10_, bf16[1536,1536]{1,0:T(8,128)(2,1)S(1)} %get-tuple-element.32.refs_2_, ...), custom_call_target="tpu_custom_call" | custom-call | flops 9600000000 | tf_op jit(solution)/shard_map/give/pallas_call | solution.py:53
  30.5 2.3 %keep.4.refs_4_ = bf16[2,64,1536]{2,1,0:T(8,128)(2,1)S(1)} custom-call(bf16[2,64,1536]{2,1,0:T(8,128)(2,1)S(1)} %collective-permute-done.1.refs_0_.refs_2_, bf16[1536,1536]{1,0:T(8,128)(2,1)S(1)} %get-tuple-element.28.refs_1_.refs_9_.refs_8_.refs_12_, bf16[1536,1536]{1,0:T(8,128)(2,1)S(1)} %get-tuple-element.29.refs_2_, bf16[2,64,1536]{2,1,0:T(8,128)(2,1)S(1)} %give.4.refs_3_), custom_call_target="tpu_custom_call" | custom-call | flops 9600000000 | tf_op jit(solution)/shard_map/keep/pallas_call | solution.py:53
  33.0 1.7 %collective-permute-start.9 = (bf16[2,64,1536]{2,1,0:T(8,128)(2,1)S(1)}, bf16[2,64,1536]{2,1,0:T(8,128)(2,1)S(1)}, u32[]{:S(2)}, u32[]{:S(2)}) collective-permute-start(bf16[2,64,1536]{2,1,0:T(8,128)(2,1)S(1)} %add_convert_fusion.refs_3_.refs_0_), channel_id=1, source_target_pairs={{0,8},{4,12},{8,0},{12,4},{1,9},{5,13},{9,1},{13,5},{2,10},{6,14},... | collective-permute-start | bytes 1179656 | tf_op jit(solution)/shard_map/ppermute | solution.py:335
  34.8 1.2 %collective-permute-done.2.refs_0_.refs_3_ = bf16[2,64,1536]{2,1,0:T(8,128)(2,1)S(1)} collective-permute-done((bf16[2,64,1536]{2,1,0:T(8,128)(2,1)S(1)}, bf16[2,64,1536]{2,1,0:T(8,128)(2,1)S(1)}, u32[]{:S(2)}, u32[]{:S(2)}) %collective-permute-start.2) | collective-permute-done | bytes 393248 | tf_op jit(solution)/shard_map/ppermute | solution.py:329
  35.9 2.3 %give.5.refs_4_ = bf16[2,64,1536]{2,1,0:T(8,128)(2,1)S(1)} custom-call(bf16[2,64,1536]{2,1,0:T(8,128)(2,1)S(1)} %collective-permute-done.2.refs_0_.refs_3_, bf16[1536,1536]{1,0:T(8,128)(2,1)S(1)} %get-tuple-element.31.refs_1_.refs_12_.refs_10_, bf16[1536,1536]{1,0:T(8,128)(2,1)S(1)} %get-tuple-element.32.refs_2_, ...), custom_call_target="tpu_custom_call" | custom-call | flops 9600000000 | tf_op jit(solution)/shard_map/give/pallas_call | solution.py:53
  38.3 0.5 gelu.4.refs_3_.refs_7_
  38.9 0.5 collective-permute-start.11
  39.4 2.3 %keep.5.refs_6_ = bf16[2,64,1536]{2,1,0:T(8,128)(2,1)S(1)} custom-call(bf16[2,64,1536]{2,1,0:T(8,128)(2,1)S(1)} %collective-permute-done.2.refs_0_.refs_3_, bf16[1536,1536]{1,0:T(8,128)(2,1)S(1)} %get-tuple-element.28.refs_1_.refs_9_.refs_8_.refs_12_, bf16[1536,1536]{1,0:T(8,128)(2,1)S(1)} %get-tuple-element.29.refs_2_, ...), custom_call_target="tpu_custom_call" | custom-call | flops 9600000000 | tf_op jit(solution)/shard_map/keep/pallas_call | solution.py:53
  41.9 1.6 %collective-permute-start.10 = (bf16[2,64,768]{2,1,0:T(8,128)(2,1)S(1)}, bf16[2,64,768]{2,1,0:T(8,128)(2,1)S(1)}, u32[]{:S(2)}, u32[]{:S(2)}) collective-permute-start(bf16[2,64,768]{2,1,0:T(8,128)(2,1)S(1)} %get-tuple-element.49.refs_4_.refs_0_), channel_id=1, source_target_pairs={{0,8},{4,12},{8,0},{12,4},{1,9},{5,13},{9,1},{13,5},{2,10},{6,14},... | collective-permute-start | bytes 589832 | tf_op jit(solution)/shard_map/ppermute | solution.py:335
  43.7 0.9 %collective-permute-done.9.refs_1_ = bf16[2,64,1536]{2,1,0:T(8,128)(2,1)S(1)} collective-permute-done((bf16[2,64,1536]{2,1,0:T(8,128)(2,1)S(1)}, bf16[2,64,1536]{2,1,0:T(8,128)(2,1)S(1)}, u32[]{:S(2)}, u32[]{:S(2)}) %collective-permute-start.9) | collective-permute-done | bytes 393248 | tf_op jit(solution)/shard_map/ppermute | solution.py:335
  44.9 1.9 %collective-permute-start.15 = (bf16[2,64,768]{2,1,0:T(8,128)(2,1)S(1)}, bf16[2,64,768]{2,1,0:T(8,128)(2,1)S(1)}, u32[]{:S(2)}, u32[]{:S(2)}) collective-permute-start(bf16[2,64,768]{2,1,0:T(8,128)(2,1)S(1)} %get-tuple-element.50.refs_5_.refs_0_), channel_id=1, source_target_pairs={{0,8},{4,12},{8,0},{12,4},{1,9},{5,13},{9,1},{13,5},{2,10},{6,14},... | collective-permute-start | bytes 589832 | tf_op jit(solution)/shard_map/ppermute | solution.py:335
  47.0 2.5 %collective-permute-done.10.refs_1_ = bf16[2,64,768]{2,1,0:T(8,128)(2,1)S(1)} collective-permute-done((bf16[2,64,768]{2,1,0:T(8,128)(2,1)S(1)}, bf16[2,64,768]{2,1,0:T(8,128)(2,1)S(1)}, u32[]{:S(2)}, u32[]{:S(2)}) %collective-permute-start.10) | collective-permute-done | bytes 196640 | tf_op jit(solution)/shard_map/ppermute | solution.py:335
  49.7 5.5 %weight_grads.3 = (f32[1536,3072]{1,0:T(8,128)}, f32[3072,1536]{1,0:T(8,128)}, bf16[64,1536]{1,0:T(8,128)(2,1)S(1)}, bf16[64,1536]{1,0:T(8,128)(2,1)S(1)}, bf16[...) custom-call(s32[1]{0:T(128)} %bitcast.refs_0_, bf16[1536,256]{1,0:T(8,128)(2,1)S(1)} %get-tuple-element.33.refs_1_, ...), custom_call_target="tpu_custom_call" | custom-call | flops 16000000000 | tf_op jit(solution)/shard_map/weight_grads/pallas_call | solution.py:53
  55.3 0.5 collective-permute-start.16
  55.9 2.0 %collective-permute-start.13 = (bf16[64,1536]{1,0:T(8,128)(2,1)S(1)}, bf16[64,1536]{1,0:T(8,128)(2,1)S(1)}, u32[]{:S(2)}, u32[]{:S(2)}) collective-permute-start(bf16[64,1536]{1,0:T(8,128)(2,1)S(1)} %get-tuple-element.38), channel_id=1, source_target_pairs={{0,3},{1,0},{2,1},{3,2},{4,7},{5,4},{6,5},{7,6},{8,11},{9,8},{10,9... | collective-permute-start | bytes 589832 | tf_op jit(solution)/shard_map/ppermute | solution.py:329
  57.9 3.4 %weight_grads.4 = (f32[1536,3072]{1,0:T(8,128)}, f32[3072,1536]{1,0:T(8,128)}, f32[64,1536]{1,0:T(8,128)S(1)}, f32[8,128]{1,0:T(8,128)S(1)}) custom-call(s32[1]{0:T(128)} %bitcast.refs_0_, bf16[1536,256]{1,0:T(8,128)(2,1)S(1)} %get-tuple-element.33.refs_1_, ...), custom_call_target="tpu_custom_call", output_to_operand_aliasing={{0}: (13, {}), {1}: (14, {})} | custom-call | flops 8000000000 | tf_op jit(solution)/shard_map/weight_grads/pallas_call | solution.py:53
  61.3 0.8 %input_product.1.refs_17_ = bf16[64,1536]{1,0:T(8,128)(2,1)S(1)} custom-call(bf16[2,64,768]{2,1,0:T(8,128)(2,1)S(1)} %collective-permute-done.16.refs_0_.refs_14_, bf16[1536,1536]{1,0:T(8,128)(2,1)S(1)} %get-tuple-element.31.refs_1_.refs_12_.refs_10_, f32[64,1536]{1,0:T(8,128)S(1)} %get-tuple-element.43.refs_2_, f32[8,128]{1,0:T(8,128)S(1)} %get-tuple-element.44.refs_3_), custom_call_target="tpu_custom_call" | custom-call | flops 12000000000 | tf_op jit(solution)/shard_map/input_product/pallas_call | solution.py:53
  62.1 1.3 %collective-permute-start.19 = (bf16[64,1536]{1,0:T(8,128)(2,1)S(1)}, bf16[64,1536]{1,0:T(8,128)(2,1)S(1)}, u32[]{:S(2)}, u32[]{:S(2)}) collective-permute-start(bf16[64,1536]{1,0:T(8,128)(2,1)S(1)} %input_product.1.refs_17_), channel_id=1, source_target_pairs={{0,2},{1,3},{2,0},{3,1},{4,6},{5,7},{6,4},{7,5},{8,10},{9,11},{10,... | collective-permute-start | bytes 589832 | tf_op jit(solution)/shard_map/ppermute | solution.py:329
  63.4 8.9 %weight_grads.5 = (f32[1536,3072]{1,0:T(8,128)}, f32[3072,1536]{1,0:T(8,128)}, f32[8,128]{1,0:T(8,128)}) custom-call(s32[1]{0:T(128)} %bitcast.refs_0_, bf16[1536,256]{1,0:T(8,128)(2,1)S(1)} %get-tuple-element.33.refs_1_, bf16[256,1536]{1,0:T(8,128)(2,1)S(1)} %get-tuple-element.34.refs_2_, ...), custom_call_target="tpu_custom_call", output_to_operand_aliasing={{0}: (15, {}), {1}: (16, {})} | custom-call | flops 40000000000 | tf_op jit(solution)/shard_map/weight_grads/pallas_call | solution.py:53
  72.4 3.7 %collective-permute-done.19 = bf16[64,1536]{1,0:T(8,128)(2,1)S(1)} collective-permute-done((bf16[64,1536]{1,0:T(8,128)(2,1)S(1)}, bf16[64,1536]{1,0:T(8,128)(2,1)S(1)}, u32[]{:S(2)}, u32[]{:S(2)}) %collective-permute-start.19) | collective-permute-done | bytes 196640 | tf_op jit(solution)/shard_map/ppermute | solution.py:329
  76.0 0.8 %add_convert_fusion.3 = bf16[64,1536]{1,0:T(8,128)(2,1)} fusion(bf16[64,1536]{1,0:T(8,128)(2,1)S(1)} %collective-permute-done.19, bf16[64,1536]{1,0:T(8,128)(2,1)S(1)} %collective-permute-done.14, bf16[64,1536]{1,0:T(8,128)(2,1)S(1)} %collective-permute-done.13, bf16[64,1536]{1,0:T(8,128)(2,1)S(1)} %get-tuple-element.37), kind=kLoop, calls=%fused_computation.3 | loop fusion | flops 786432 | bytes 983040 | tf_op jit(solution)/shard_map/convert_element_type | solution.py:399
  (31 shorter events, 2.0 us)
Async XLA Ops:
  1.7 16.2 %collective-permute-start = (bf16[2,64,1536]{2,1,0:T(8,128)(2,1)S(1)}, bf16[2,64,1536]{2,1,0:T(8,128)(2,1)S(1)}, u32[]{:S(2)}, u32[]{:S(2)}) collective-permute-start(bf16[2,64,1536]{2,1,0:T(8,128)(2,1)S(1)} %stacked.1.refs_1_.refs_4_.refs_0_), channel_id=1, source_target_pairs={{0,1},{1,2},{2,3},{3,0},{4,5},{5,6},{6,7},{7,4},{8,9},{9,10},{10,1... | collective-permute-start | bytes 1179656 | tf_op jit(solution)/shard_map/ppermute | solution.py:329
  9.3 6.7 %collective-permute-start.3 = (bf16[2,64,1536]{2,1,0:T(8,128)(2,1)S(1)}, bf16[2,64,1536]{2,1,0:T(8,128)(2,1)S(1)}, u32[]{:S(2)}, u32[]{:S(2)}) collective-permute-start(bf16[2,64,1536]{2,1,0:T(8,128)(2,1)S(1)} %get-tuple-element.26.refs_4_), channel_id=1, source_target_pairs={{0,4},{4,0},{8,12},{12,8},{1,5},{5,1},{9,13},{13,9},{2,6},{6,2},{1... | collective-permute-start | bytes 1179656 | tf_op jit(solution)/shard_map/ppermute | solution.py:326
  13.9 11.6 %collective-permute-start.1 = (bf16[2,64,1536]{2,1,0:T(8,128)(2,1)S(1)}, bf16[2,64,1536]{2,1,0:T(8,128)(2,1)S(1)}, u32[]{:S(2)}, u32[]{:S(2)}) collective-permute-start(bf16[2,64,1536]{2,1,0:T(8,128)(2,1)S(1)} %get-tuple-element.27), channel_id=1, source_target_pairs={{0,3},{1,0},{2,1},{3,2},{4,7},{5,4},{6,5},{7,6},{8,11},{9,8},{10,9... | collective-permute-start | bytes 1179656 | tf_op jit(solution)/shard_map/ppermute | solution.py:329
  16.1 12.0 %collective-permute-start.4 = (bf16[2,64,1536]{2,1,0:T(8,128)(2,1)S(1)}, bf16[2,64,1536]{2,1,0:T(8,128)(2,1)S(1)}, u32[]{:S(2)}, u32[]{:S(2)}) collective-permute-start(bf16[2,64,1536]{2,1,0:T(8,128)(2,1)S(1)} %add_convert_fusion.2.refs_3_.refs_0_), channel_id=1, source_target_pairs={{0,8},{4,12},{8,0},{12,4},{1,9},{5,13},{9,1},{13,5},{2,10},{6,14},... | collective-permute-start | bytes 1179656 | tf_op jit(solution)/shard_map/ppermute | solution.py:335
  20.2 2.7 %collective-permute-start.5 = (bf16[2,64,1536]{2,1,0:T(8,128)(2,1)S(1)}, bf16[2,64,1536]{2,1,0:T(8,128)(2,1)S(1)}, u32[]{:S(2)}, u32[]{:S(2)}) collective-permute-start(bf16[2,64,1536]{2,1,0:T(8,128)(2,1)S(1)} %give.3.refs_3_), channel_id=1, source_target_pairs={{0,4},{4,0},{8,12},{12,8},{1,5},{5,1},{9,13},{13,9},{2,6},{6,2},{1... | collective-permute-start | bytes 1179656 | tf_op jit(solution)/shard_map/ppermute | solution.py:326
  20.3 15.6 %collective-permute-start.2 = (bf16[2,64,1536]{2,1,0:T(8,128)(2,1)S(1)}, bf16[2,64,1536]{2,1,0:T(8,128)(2,1)S(1)}, u32[]{:S(2)}, u32[]{:S(2)}) collective-permute-start(bf16[2,64,1536]{2,1,0:T(8,128)(2,1)S(1)} %collective-permute-done.refs_0_.refs_1_), channel_id=1, source_target_pairs={{0,1},{1,2},{2,3},{3,0},{4,5},{5,6},{6,7},{7,4},{8,9},{9,10},{10,1... | collective-permute-start | bytes 1179656 | tf_op jit(solution)/shard_map/ppermute | solution.py:329
  23.0 15.3 %collective-permute-start.6 = (bf16[2,64,1536]{2,1,0:T(8,128)(2,1)S(1)}, bf16[2,64,1536]{2,1,0:T(8,128)(2,1)S(1)}, u32[]{:S(2)}, u32[]{:S(2)}) collective-permute-start(bf16[2,64,1536]{2,1,0:T(8,128)(2,1)S(1)} %add_convert_fusion.1.refs_3_.refs_2_), channel_id=1, source_target_pairs={{0,8},{4,12},{8,0},{12,4},{1,9},{5,13},{9,1},{13,5},{2,10},{6,14},... | collective-permute-start | bytes 1179656 | tf_op jit(solution)/shard_map/ppermute | solution.py:335
  30.5 2.4 %collective-permute-start.7 = (bf16[2,64,1536]{2,1,0:T(8,128)(2,1)S(1)}, bf16[2,64,1536]{2,1,0:T(8,128)(2,1)S(1)}, u32[]{:S(2)}, u32[]{:S(2)}) collective-permute-start(bf16[2,64,1536]{2,1,0:T(8,128)(2,1)S(1)} %give.4.refs_3_), channel_id=1, source_target_pairs={{0,4},{4,0},{8,12},{12,8},{1,5},{5,1},{9,13},{13,9},{2,6},{6,2},{1... | collective-permute-start | bytes 1179656 | tf_op jit(solution)/shard_map/ppermute | solution.py:326
  33.0 11.6 %collective-permute-start.9 = (bf16[2,64,1536]{2,1,0:T(8,128)(2,1)S(1)}, bf16[2,64,1536]{2,1,0:T(8,128)(2,1)S(1)}, u32[]{:S(2)}, u32[]{:S(2)}) collective-permute-start(bf16[2,64,1536]{2,1,0:T(8,128)(2,1)S(1)} %add_convert_fusion.refs_3_.refs_0_), channel_id=1, source_target_pairs={{0,8},{4,12},{8,0},{12,4},{1,9},{5,13},{9,1},{13,5},{2,10},{6,14},... | collective-permute-start | bytes 1179656 | tf_op jit(solution)/shard_map/ppermute | solution.py:335
  38.3 3.5 %collective-permute-start.8 = (bf16[2,64,1536]{2,1,0:T(8,128)(2,1)S(1)}, bf16[2,64,1536]{2,1,0:T(8,128)(2,1)S(1)}, u32[]{:S(2)}, u32[]{:S(2)}) collective-permute-start(bf16[2,64,1536]{2,1,0:T(8,128)(2,1)S(1)} %give.5.refs_4_), channel_id=1, source_target_pairs={{0,4},{4,0},{8,12},{12,8},{1,5},{5,1},{9,13},{13,9},{2,6},{6,2},{1... | collective-permute-start | bytes 1179656 | tf_op jit(solution)/shard_map/ppermute | solution.py:326
  38.9 10.8 %collective-permute-start.11 = (bf16[2,128,1536]{2,1,0:T(8,128)(2,1)S(1)}, bf16[2,128,1536]{2,1,0:T(8,128)(2,1)S(1)}, u32[]{:S(2)}, u32[]{:S(2)}) collective-permute-start(bf16[2,128,1536]{2,1,0:T(8,128)(2,1)S(1)} %gelu.4.refs_3_.refs_7_), channel_id=1, source_target_pairs={{0,4},{4,0},{8,12},{12,8},{1,5},{5,1},{9,13},{13,9},{2,6},{6,2},{1... | collective-permute-start | bytes 2359304 | tf_op jit(solution)/shard_map/ppermute | solution.py:326
  41.9 7.5 %collective-permute-start.10 = (bf16[2,64,768]{2,1,0:T(8,128)(2,1)S(1)}, bf16[2,64,768]{2,1,0:T(8,128)(2,1)S(1)}, u32[]{:S(2)}, u32[]{:S(2)}) collective-permute-start(bf16[2,64,768]{2,1,0:T(8,128)(2,1)S(1)} %get-tuple-element.49.refs_4_.refs_0_), channel_id=1, source_target_pairs={{0,8},{4,12},{8,0},{12,4},{1,9},{5,13},{9,1},{13,5},{2,10},{6,14},... | collective-permute-start | bytes 589832 | tf_op jit(solution)/shard_map/ppermute | solution.py:335
  44.9 4.8 %collective-permute-start.12 = (bf16[64,1536]{1,0:T(8,128)(2,1)S(1)}, bf16[64,1536]{1,0:T(8,128)(2,1)S(1)}, u32[]{:S(2)}, u32[]{:S(2)}) collective-permute-start(bf16[64,1536]{1,0:T(8,128)(2,1)S(1)} %get-tuple-element.35.refs_4_.refs_8_), channel_id=1, source_target_pairs={{0,4},{4,0},{8,12},{12,8},{1,5},{5,1},{9,13},{13,9},{2,6},{6,2},{1... | collective-permute-start | bytes 589832 | tf_op jit(solution)/shard_map/ppermute | solution.py:326
  44.9 10.2 %collective-permute-start.15 = (bf16[2,64,768]{2,1,0:T(8,128)(2,1)S(1)}, bf16[2,64,768]{2,1,0:T(8,128)(2,1)S(1)}, u32[]{:S(2)}, u32[]{:S(2)}) collective-permute-start(bf16[2,64,768]{2,1,0:T(8,128)(2,1)S(1)} %get-tuple-element.50.refs_5_.refs_0_), channel_id=1, source_target_pairs={{0,8},{4,12},{8,0},{12,4},{1,9},{5,13},{9,1},{13,5},{2,10},{6,14},... | collective-permute-start | bytes 589832 | tf_op jit(solution)/shard_map/ppermute | solution.py:335
  46.8 11.1 %collective-permute-start.17 = (bf16[64,1536]{1,0:T(8,128)(2,1)S(1)}, bf16[64,1536]{1,0:T(8,128)(2,1)S(1)}, u32[]{:S(2)}, u32[]{:S(2)}) collective-permute-start(bf16[64,1536]{1,0:T(8,128)(2,1)S(1)} %get-tuple-element.36.refs_2_.refs_5_.refs_9_), channel_id=1, source_target_pairs={{0,4},{4,0},{8,12},{12,8},{1,5},{5,1},{9,13},{13,9},{2,6},{6,2},{1... | collective-permute-start | bytes 589832 | tf_op jit(solution)/shard_map/ppermute | solution.py:326
  49.6 8.3 %collective-permute-start.18 = (bf16[2,64,768]{2,1,0:T(8,128)(2,1)S(1)}, bf16[2,64,768]{2,1,0:T(8,128)(2,1)S(1)}, u32[]{:S(2)}, u32[]{:S(2)}) collective-permute-start(bf16[2,64,768]{2,1,0:T(8,128)(2,1)S(1)} %gelu.6.refs_6_.refs_13_.refs_7_), channel_id=1, source_target_pairs={{0,4},{4,0},{8,12},{12,8},{1,5},{5,1},{9,13},{13,9},{2,6},{6,2},{1... | collective-permute-start | bytes 589832 | tf_op jit(solution)/shard_map/ppermute | solution.py:326
  55.3 6.0 %collective-permute-start.16 = (bf16[2,64,768]{2,1,0:T(8,128)(2,1)S(1)}, bf16[2,64,768]{2,1,0:T(8,128)(2,1)S(1)}, u32[]{:S(2)}, u32[]{:S(2)}) collective-permute-start(bf16[2,64,768]{2,1,0:T(8,128)(2,1)S(1)} %gelu.7.refs_11_.refs_15_.refs_10_), channel_id=1, source_target_pairs={{0,4},{4,0},{8,12},{12,8},{1,5},{5,1},{9,13},{13,9},{2,6},{6,2},{1... | collective-permute-start | bytes 589832 | tf_op jit(solution)/shard_map/ppermute | solution.py:326
  55.9 16.5 %collective-permute-start.13 = (bf16[64,1536]{1,0:T(8,128)(2,1)S(1)}, bf16[64,1536]{1,0:T(8,128)(2,1)S(1)}, u32[]{:S(2)}, u32[]{:S(2)}) collective-permute-start(bf16[64,1536]{1,0:T(8,128)(2,1)S(1)} %get-tuple-element.38), channel_id=1, source_target_pairs={{0,3},{1,0},{2,1},{3,2},{4,7},{5,4},{6,5},{7,6},{8,11},{9,8},{10,9... | collective-permute-start | bytes 589832 | tf_op jit(solution)/shard_map/ppermute | solution.py:329
  57.9 14.5 %collective-permute-start.14 = (bf16[64,1536]{1,0:T(8,128)(2,1)S(1)}, bf16[64,1536]{1,0:T(8,128)(2,1)S(1)}, u32[]{:S(2)}, u32[]{:S(2)}) collective-permute-start(bf16[64,1536]{1,0:T(8,128)(2,1)S(1)} %get-tuple-element.39), channel_id=1, source_target_pairs={{0,1},{1,2},{2,3},{3,0},{4,5},{5,6},{6,7},{7,4},{8,9},{9,10},{10,1... | collective-permute-start | bytes 589832 | tf_op jit(solution)/shard_map/ppermute | solution.py:329
  62.1 13.9 %collective-permute-start.19 = (bf16[64,1536]{1,0:T(8,128)(2,1)S(1)}, bf16[64,1536]{1,0:T(8,128)(2,1)S(1)}, u32[]{:S(2)}, u32[]{:S(2)}) collective-permute-start(bf16[64,1536]{1,0:T(8,128)(2,1)S(1)} %input_product.1.refs_17_), channel_id=1, source_target_pairs={{0,2},{1,3},{2,0},{3,1},{4,6},{5,7},{6,4},{7,5},{8,10},{9,11},{10,... | collective-permute-start | bytes 589832 | tf_op jit(solution)/shard_map/ppermute | solution.py:329

commit v10 on v7

--- a/solution.py
+++ b/solution.py
@@ -101,8 +101,8 @@
             part = pl.ds(i * tile, tile)
             copies.append(pltpu.make_async_copy(up_hbm.at[:, units], up_ref.at[:, part], sems.at[0, i]))
             copies.append(pltpu.make_async_copy(down_hbm.at[units, :], down_ref.at[part, :], sems.at[1, i]))
-        for copy in copies:
-            copy.start()
+        for i, copy in enumerate(copies):
+            copy.start(priority=i % 2)
         if not other:
             refs[0][...] = chunk_ref[...]
         for i in range(pieces):
@@ -238,7 +238,7 @@
                 busy[kind, slot].wait()
             stage[slot] = value * scale
             copy = pltpu.make_async_copy(stage.at[slot], target, sems.at[kind, slot])
-            copy.start()
+            copy.start(priority=kind)
             busy[kind, slot] = copy
 
         left = refs[: len(flat)]

time: 74.2 us -> 76.1 us (1.026)
  Pallas kernels: 46.3 us -> 48.4 us
    pallas_call x19, Pallas kernels: 46.3 us -> 48.4 us  [__call__(): pl.pallas_call(kernel, out_shape=outs, in_specs=specs, out_specs=[pl.Bloc...]
  transfers between devices with their start and end apart: 20 -> 20, of which waited for: 4 -> 4; matrix products, arithmetic and copies ran while one was open for 1% -> 0% of each run, Pallas kernels for 61% -> 62%
where the time goes in v10:
time: 76.1 us; the launch traced here: 75.9 us
  Pallas kernels  48.4 us (64%)
  starting transfers between devices  17.1 us (22%)
  waiting for transfers between devices  8.4 us (11%)
  other arithmetic  1.11 us (1%)
  between operations  0.94 us (1%)
    pallas_call x19, Pallas kernels, __call__(): pl.pallas_call(kernel, out_shape=outs, in_specs=specs, out_specs=[pl.Bloc...  48.4 us
    ppermute x6, starting transfers between devices, shift(): lax.ppermute(x, 'narrow', [(i, (i + places) % narrow) for i in range(narr...  9.41 us
    ppermute x5, starting transfers between devices, across_chips(): lax.ppermute(partial, 'wide', [(i, i ^ 2 * hop) for i in range(wide)])  6.08 us
    ppermute x6, waiting for transfers between devices, shift(): lax.ppermute(x, 'narrow', [(i, (i + places) % narrow) for i in range(narr...  5.72 us
    ppermute x5, waiting for transfers between devices, across_chips(): lax.ppermute(partial, 'wide', [(i, i ^ 2 * hop) for i in range(wide)])  2.65 us
    ppermute x9, starting transfers between devices, swap_cores(): return lax.ppermute(x, 'wide', [(i, i ^ 1) for i in range(wide)])  1.57 us
  transfers between devices with their start and end apart: 20, of which 4 were waited for; matrix products, arithmetic and copies ran while one was open for 0% of the time, Pallas kernels for 62%

profile of v10, /device:TPU:0, one launch (start us, length us, event | category | flops | bytes accessed | tf_op | source)
XLA Modules:
  0.0 75.9 jit_solution(12369667875678761067)
XLA Ops:
  0.6 1.0 %stacked.1.refs_1_.refs_4_.refs_0_ = bf16[2,64,1536]{2,1,0:T(8,128)(2,1)S(1)} custom-call(bf16[64,1536]{1,0:T(8,128)(2,1)} %refs_0_.1, bf16[64,1536]{1,0:T(8,128)(2,1)} %refs_1_.1), custom_call_target="tpu_custom_call" | custom-call | flops 2000000000 | tf_op jit(solution)/shard_map/stacked/pallas_call | solution.py:53
  1.7 3.1 %collective-permute-start = (bf16[2,64,1536]{2,1,0:T(8,128)(2,1)S(1)}, bf16[2,64,1536]{2,1,0:T(8,128)(2,1)S(1)}, u32[]{:S(2)}, u32[]{:S(2)}) collective-permute-start(bf16[2,64,1536]{2,1,0:T(8,128)(2,1)S(1)} %stacked.1.refs_1_.refs_4_.refs_0_), channel_id=1, source_target_pairs={{0,1},{1,2},{2,3},{3,0},{4,5},{5,6},{6,7},{7,4},{8,9},{9,10},{10,1... | collective-permute-start | bytes 1179656 | tf_op jit(solution)/shard_map/ppermute | solution.py:320
  4.8 5.5 %give_first.1 = (bf16[1536,1536]{1,0:T(8,128)(2,1)S(1)}, bf16[1536,1536]{1,0:T(8,128)(2,1)S(1)}, bf16[2,64,1536]{2,1,0:T(8,128)(2,1)S(1)}) custom-call(s32[1]{0:T(128)} %bitcast.refs_0_, bf16[2,64,1536]{2,1,0:T(8,128)(2,1)S(1)} %stacked.1.refs_1_.refs_4_.refs_0_, bf16[1536,3072]{1,0:T(8,128)(2,1)} %refs_2_.3, bf16[3072,1536]{1,0:T(8,128)(2,1)} %refs_3_.3, ...), custom_call_target="tpu_custom_call" | custom-call | flops 17999998976 | tf_op jit(solution)/shard_map/give_first/pallas_call | solution.py:53
  10.3 5.5 %keep_first.1 = (bf16[1536,1536]{1,0:T(8,128)(2,1)S(1)}, bf16[1536,1536]{1,0:T(8,128)(2,1)S(1)}, bf16[2,64,1536]{2,1,0:T(8,128)(2,1)S(1)}, bf16[2,64,1536]{2,1,0:T(8,128)(2,1)S(1)}) custom-call(s32[1]{0:T(128)} %bitcast.refs_0_, bf16[2,64,1536]{2,1,0:T(8,128)(2,1)S(1)} %stacked.1.refs_1_.refs_4_.refs_0_, bf16[1536,3072]{1,0:T(8,128)(2,1)} %refs_2_.3, ...), custom_call_target="tpu_custom_call" | custom-call | flops 17999998976 | tf_op jit(solution)/shard_map/keep_first/pallas_call | solution.py:53
  15.8 2.1 %collective-permute-start.6 = (bf16[2,64,1536]{2,1,0:T(8,128)(2,1)S(1)}, bf16[2,64,1536]{2,1,0:T(8,128)(2,1)S(1)}, u32[]{:S(2)}, u32[]{:S(2)}) collective-permute-start(bf16[2,64,1536]{2,1,0:T(8,128)(2,1)S(1)} %get-tuple-element.34), channel_id=1, source_target_pairs={{0,3},{1,0},{2,1},{3,2},{4,7},{5,4},{6,5},{7,6},{8,11},{9,8},{10,9... | collective-permute-start | bytes 1179656 | tf_op jit(solution)/shard_map/ppermute | solution.py:320
  18.0 1.8 %collective-permute-start.3 = (bf16[2,64,1536]{2,1,0:T(8,128)(2,1)S(1)}, bf16[2,64,1536]{2,1,0:T(8,128)(2,1)S(1)}, u32[]{:S(2)}, u32[]{:S(2)}) collective-permute-start(bf16[2,64,1536]{2,1,0:T(8,128)(2,1)S(1)} %add_convert_fusion.2.refs_3_.refs_0_), channel_id=1, source_target_pairs={{0,8},{4,12},{8,0},{12,4},{1,9},{5,13},{9,1},{13,5},{2,10},{6,14},... | collective-permute-start | bytes 1179656 | tf_op jit(solution)/shard_map/ppermute | solution.py:326
  19.8 2.3 %give.3.refs_3_ = bf16[2,64,1536]{2,1,0:T(8,128)(2,1)S(1)} custom-call(bf16[2,64,1536]{2,1,0:T(8,128)(2,1)S(1)} %collective-permute-done.refs_0_.refs_1_, bf16[1536,1536]{1,0:T(8,128)(2,1)S(1)} %get-tuple-element.32.refs_1_.refs_3_.refs_10_.refs_11_, bf16[1536,1536]{1,0:T(8,128)(2,1)S(1)} %get-tuple-element.33.refs_2_, ...), custom_call_target="tpu_custom_call" | custom-call | flops 9600000000 | tf_op jit(solution)/shard_map/give/pallas_call | solution.py:53
  22.5 2.3 %keep.3.refs_5_ = bf16[2,64,1536]{2,1,0:T(8,128)(2,1)S(1)} custom-call(bf16[2,64,1536]{2,1,0:T(8,128)(2,1)S(1)} %collective-permute-done.refs_0_.refs_1_, bf16[1536,1536]{1,0:T(8,128)(2,1)S(1)} %get-tuple-element.29.refs_1_.refs_2_.refs_9_.refs_10_.refs_12_, bf16[1536,1536]{1,0:T(8,128)(2,1)S(1)} %get-tuple-element.30.refs_2_, ...), custom_call_target="tpu_custom_call" | custom-call | flops 9600000000 | tf_op jit(solution)/shard_map/keep/pallas_call | solution.py:53
  24.9 0.4 collective-permute-start.5
  25.3 2.1 %collective-permute-done.6.refs_0_.refs_2_ = bf16[2,64,1536]{2,1,0:T(8,128)(2,1)S(1)} collective-permute-done((bf16[2,64,1536]{2,1,0:T(8,128)(2,1)S(1)}, bf16[2,64,1536]{2,1,0:T(8,128)(2,1)S(1)}, u32[]{:S(2)}, u32[]{:S(2)}) %collective-permute-start.6) | collective-permute-done | bytes 393248 | tf_op jit(solution)/shard_map/ppermute | solution.py:320
  27.4 2.6 %collective-permute-done.3.refs_4_.refs_1_ = bf16[2,64,1536]{2,1,0:T(8,128)(2,1)S(1)} collective-permute-done((bf16[2,64,1536]{2,1,0:T(8,128)(2,1)S(1)}, bf16[2,64,1536]{2,1,0:T(8,128)(2,1)S(1)}, u32[]{:S(2)}, u32[]{:S(2)}) %collective-permute-start.3) | collective-permute-done | bytes 393248 | tf_op jit(solution)/shard_map/ppermute | solution.py:326
  30.0 2.3 %give.4.refs_3_ = bf16[2,64,1536]{2,1,0:T(8,128)(2,1)S(1)} custom-call(bf16[2,64,1536]{2,1,0:T(8,128)(2,1)S(1)} %collective-permute-done.6.refs_0_.refs_2_, bf16[1536,1536]{1,0:T(8,128)(2,1)S(1)} %get-tuple-element.32.refs_1_.refs_3_.refs_10_.refs_11_, bf16[1536,1536]{1,0:T(8,128)(2,1)S(1)} %get-tuple-element.33.refs_2_, ...), custom_call_target="tpu_custom_call" | custom-call | flops 9600000000 | tf_op jit(solution)/shard_map/give/pallas_call | solution.py:53
  32.5 2.3 %keep.4.refs_4_ = bf16[2,64,1536]{2,1,0:T(8,128)(2,1)S(1)} custom-call(bf16[2,64,1536]{2,1,0:T(8,128)(2,1)S(1)} %collective-permute-done.6.refs_0_.refs_2_, bf16[1536,1536]{1,0:T(8,128)(2,1)S(1)} %get-tuple-element.29.refs_1_.refs_2_.refs_9_.refs_10_.refs_12_, bf16[1536,1536]{1,0:T(8,128)(2,1)S(1)} %get-tuple-element.30.refs_2_, ...), custom_call_target="tpu_custom_call" | custom-call | flops 9600000000 | tf_op jit(solution)/shard_map/keep/pallas_call | solution.py:53
  34.9 1.8 %collective-permute-start.10 = (bf16[2,64,1536]{2,1,0:T(8,128)(2,1)S(1)}, bf16[2,64,1536]{2,1,0:T(8,128)(2,1)S(1)}, u32[]{:S(2)}, u32[]{:S(2)}) collective-permute-start(bf16[2,64,1536]{2,1,0:T(8,128)(2,1)S(1)} %add_convert_fusion.refs_3_.refs_0_), channel_id=1, source_target_pairs={{0,8},{4,12},{8,0},{12,4},{1,9},{5,13},{9,1},{13,5},{2,10},{6,14},... | collective-permute-start | bytes 1179656 | tf_op jit(solution)/shard_map/ppermute | solution.py:326
  36.7 1.1 %collective-permute-done.1.refs_0_.refs_3_ = bf16[2,64,1536]{2,1,0:T(8,128)(2,1)S(1)} collective-permute-done((bf16[2,64,1536]{2,1,0:T(8,128)(2,1)S(1)}, bf16[2,64,1536]{2,1,0:T(8,128)(2,1)S(1)}, u32[]{:S(2)}, u32[]{:S(2)}) %collective-permute-start.1) | collective-permute-done | bytes 393248 | tf_op jit(solution)/shard_map/ppermute | solution.py:320
  37.9 2.3 %give.5.refs_4_ = bf16[2,64,1536]{2,1,0:T(8,128)(2,1)S(1)} custom-call(bf16[2,64,1536]{2,1,0:T(8,128)(2,1)S(1)} %collective-permute-done.1.refs_0_.refs_3_, bf16[1536,1536]{1,0:T(8,128)(2,1)S(1)} %get-tuple-element.32.refs_1_.refs_3_.refs_10_.refs_11_, bf16[1536,1536]{1,0:T(8,128)(2,1)S(1)} %get-tuple-element.33.refs_2_, ...), custom_call_target="tpu_custom_call" | custom-call | flops 9600000000 | tf_op jit(solution)/shard_map/give/pallas_call | solution.py:53
  40.3 0.5 gelu.4.refs_3_.refs_0_
  40.8 0.5 collective-permute-start.11
  41.4 2.3 %keep.5.refs_6_ = bf16[2,64,1536]{2,1,0:T(8,128)(2,1)S(1)} custom-call(bf16[2,64,1536]{2,1,0:T(8,128)(2,1)S(1)} %collective-permute-done.1.refs_0_.refs_3_, bf16[1536,1536]{1,0:T(8,128)(2,1)S(1)} %get-tuple-element.29.refs_1_.refs_2_.refs_9_.refs_10_.refs_12_, bf16[1536,1536]{1,0:T(8,128)(2,1)S(1)} %get-tuple-element.30.refs_2_, ...), custom_call_target="tpu_custom_call" | custom-call | flops 9600000000 | tf_op jit(solution)/shard_map/keep/pallas_call | solution.py:53
  43.8 1.5 %collective-permute-start.12 = (bf16[2,64,768]{2,1,0:T(8,128)(2,1)S(1)}, bf16[2,64,768]{2,1,0:T(8,128)(2,1)S(1)}, u32[]{:S(2)}, u32[]{:S(2)}) collective-permute-start(bf16[2,64,768]{2,1,0:T(8,128)(2,1)S(1)} %get-tuple-element.53.refs_4_.refs_0_), channel_id=1, source_target_pairs={{0,8},{4,12},{8,0},{12,4},{1,9},{5,13},{9,1},{13,5},{2,10},{6,14},... | collective-permute-start | bytes 589832 | tf_op jit(solution)/shard_map/ppermute | solution.py:326
  45.7 3.1 %input_product.2 = (bf16[64,1536]{1,0:T(8,128)(2,1)S(1)}, bf16[64,1536]{1,0:T(8,128)(2,1)S(1)}) custom-call(bf16[2,128,1536]{2,1,0:T(8,128)(2,1)S(1)} %gelu.4.refs_3_.refs_0_, bf16[2,128,1536]{2,1,0:T(8,128)(2,1)S(1)} %collective-permute-done.11.refs_1_.refs_3_.refs_7_, bf16[1536,1536]{1,0:T(8,128)(2,1)S(1)} %get-tuple-element.29.refs_1_.refs_2_.refs_9_.refs_10_.refs_12_, ...), custom_call_target="tpu_custom_call" | custom-call | flops 400000000 | tf_op jit(solution)/shard_map/input_product/pallas_call | solution.py:53
  49.1 0.6 collective-permute-start.9
  49.7 1.8 %collective-permute-start.15 = (bf16[64,1536]{1,0:T(8,128)(2,1)S(1)}, bf16[64,1536]{1,0:T(8,128)(2,1)S(1)}, u32[]{:S(2)}, u32[]{:S(2)}) collective-permute-start(bf16[64,1536]{1,0:T(8,128)(2,1)S(1)} %get-tuple-element.37.refs_2_), channel_id=1, source_target_pairs={{0,3},{1,0},{2,1},{3,2},{4,7},{5,4},{6,5},{7,6},{8,11},{9,8},{10,9... | collective-permute-start | bytes 589832 | tf_op jit(solution)/shard_map/ppermute | solution.py:320
  51.7 0.6 collective-permute-start.17
  52.3 4.9 %weight_grads.3 = (f32[1536,3072]{1,0:T(8,128)}, f32[3072,1536]{1,0:T(8,128)}, bf16[64,1536]{1,0:T(8,128)(2,1)S(1)}, f32[8,128]{1,0:T(8,128)S(1)}) custom-call(s32[1]{0:T(128)} %bitcast.refs_0_, bf16[1536,256]{1,0:T(8,128)(2,1)S(1)} %get-tuple-element.35.refs_1_, bf16[256,1536]{1,0:T(8,128)(2,1)S(1)} %get-tuple-element.36.refs_4_.refs_2_, ...), custom_call_target="tpu_custom_call" | custom-call | flops 16000000000 | tf_op jit(solution)/shard_map/weight_grads/pallas_call | solution.py:53
  57.4 0.5 collective-permute-start.18
  57.9 4.4 %weight_grads.4 = (f32[1536,3072]{1,0:T(8,128)}, f32[3072,1536]{1,0:T(8,128)}, f32[64,1536]{1,0:T(8,128)S(1)}, f32[8,128]{1,0:T(8,128)S(1)}) custom-call(s32[1]{0:T(128)} %bitcast.refs_0_, bf16[1536,256]{1,0:T(8,128)(2,1)S(1)} %get-tuple-element.35.refs_1_, ...), custom_call_target="tpu_custom_call", output_to_operand_aliasing={{0}: (13, {}), {1}: (14, {})} | custom-call | flops 16000000000 | tf_op jit(solution)/shard_map/weight_grads/pallas_call | solution.py:53
  62.3 0.9 %input_product.3 = (f32[64,1536]{1,0:T(8,128)S(1)}, bf16[64,1536]{1,0:T(8,128)(2,1)S(1)}) custom-call(bf16[2,64,768]{2,1,0:T(8,128)(2,1)S(1)} %collective-permute-done.14.refs_0_.refs_10_, bf16[1536,1536]{1,0:T(8,128)(2,1)S(1)} %get-tuple-element.32.refs_1_.refs_3_.refs_10_.refs_11_, bf16[64,1536]{1,0:T(8,128)(2,1)S(1)} %get-tuple-element.41.refs_2_, ...), custom_call_target="tpu_custom_call" | custom-call | flops 12000000000 | tf_op jit(solution)/shard_map/input_product/pallas_call | solution.py:53
  63.2 1.7 %collective-permute-start.19 = (bf16[64,1536]{1,0:T(8,128)(2,1)S(1)}, bf16[64,1536]{1,0:T(8,128)(2,1)S(1)}, u32[]{:S(2)}, u32[]{:S(2)}) collective-permute-start(bf16[64,1536]{1,0:T(8,128)(2,1)S(1)} %get-tuple-element.48.refs_13_), channel_id=1, source_target_pairs={{0,2},{1,3},{2,0},{3,1},{4,6},{5,7},{6,4},{7,5},{8,10},{9,11},{10,... | collective-permute-start | bytes 589832 | tf_op jit(solution)/shard_map/ppermute | solution.py:320
  64.9 7.8 %weight_grads.5 = (f32[1536,3072]{1,0:T(8,128)}, f32[3072,1536]{1,0:T(8,128)}, f32[8,128]{1,0:T(8,128)}) custom-call(s32[1]{0:T(128)} %bitcast.refs_0_, bf16[1536,256]{1,0:T(8,128)(2,1)S(1)} %get-tuple-element.35.refs_1_, bf16[256,1536]{1,0:T(8,128)(2,1)S(1)} %get-tuple-element.36.refs_4_.refs_2_, ...), custom_call_target="tpu_custom_call", output_to_operand_aliasing={{0}: (11, {}), {1}: (12, {})} | custom-call | flops 32000000000 | tf_op jit(solution)/shard_map/weight_grads/pallas_call | solution.py:53
  72.7 2.5 %collective-permute-done.19 = bf16[64,1536]{1,0:T(8,128)(2,1)S(1)} collective-permute-done((bf16[64,1536]{1,0:T(8,128)(2,1)S(1)}, bf16[64,1536]{1,0:T(8,128)(2,1)S(1)}, u32[]{:S(2)}, u32[]{:S(2)}) %collective-permute-start.19) | collective-permute-done | bytes 196640 | tf_op jit(solution)/shard_map/ppermute | solution.py:320
  75.2 0.7 add_convert_fusion.3
  (32 shorter events, 1.9 us)
Async XLA Ops:
  1.7 18.1 %collective-permute-start = (bf16[2,64,1536]{2,1,0:T(8,128)(2,1)S(1)}, bf16[2,64,1536]{2,1,0:T(8,128)(2,1)S(1)}, u32[]{:S(2)}, u32[]{:S(2)}) collective-permute-start(bf16[2,64,1536]{2,1,0:T(8,128)(2,1)S(1)} %stacked.1.refs_1_.refs_4_.refs_0_), channel_id=1, source_target_pairs={{0,1},{1,2},{2,3},{3,0},{4,5},{5,6},{6,7},{7,4},{8,9},{9,10},{10,1... | collective-permute-start | bytes 1179656 | tf_op jit(solution)/shard_map/ppermute | solution.py:320
  10.2 7.7 %collective-permute-start.2 = (bf16[2,64,1536]{2,1,0:T(8,128)(2,1)S(1)}, bf16[2,64,1536]{2,1,0:T(8,128)(2,1)S(1)}, u32[]{:S(2)}, u32[]{:S(2)}) collective-permute-start(bf16[2,64,1536]{2,1,0:T(8,128)(2,1)S(1)} %get-tuple-element.28.refs_4_), channel_id=1, source_target_pairs={{0,4},{4,0},{8,12},{12,8},{1,5},{5,1},{9,13},{13,9},{2,6},{6,2},{1... | collective-permute-start | bytes 1179656 | tf_op jit(solution)/shard_map/ppermute | solution.py:317
  15.8 11.6 %collective-permute-start.6 = (bf16[2,64,1536]{2,1,0:T(8,128)(2,1)S(1)}, bf16[2,64,1536]{2,1,0:T(8,128)(2,1)S(1)}, u32[]{:S(2)}, u32[]{:S(2)}) collective-permute-start(bf16[2,64,1536]{2,1,0:T(8,128)(2,1)S(1)} %get-tuple-element.34), channel_id=1, source_target_pairs={{0,3},{1,0},{2,1},{3,2},{4,7},{5,4},{6,5},{7,6},{8,11},{9,8},{10,9... | collective-permute-start | bytes 1179656 | tf_op jit(solution)/shard_map/ppermute | solution.py:320
  18.0 12.0 %collective-permute-start.3 = (bf16[2,64,1536]{2,1,0:T(8,128)(2,1)S(1)}, bf16[2,64,1536]{2,1,0:T(8,128)(2,1)S(1)}, u32[]{:S(2)}, u32[]{:S(2)}) collective-permute-start(bf16[2,64,1536]{2,1,0:T(8,128)(2,1)S(1)} %add_convert_fusion.2.refs_3_.refs_0_), channel_id=1, source_target_pairs={{0,8},{4,12},{8,0},{12,4},{1,9},{5,13},{9,1},{13,5},{2,10},{6,14},... | collective-permute-start | bytes 1179656 | tf_op jit(solution)/shard_map/ppermute | solution.py:326
  22.1 2.7 %collective-permute-start.4 = (bf16[2,64,1536]{2,1,0:T(8,128)(2,1)S(1)}, bf16[2,64,1536]{2,1,0:T(8,128)(2,1)S(1)}, u32[]{:S(2)}, u32[]{:S(2)}) collective-permute-start(bf16[2,64,1536]{2,1,0:T(8,128)(2,1)S(1)} %give.3.refs_3_), channel_id=1, source_target_pairs={{0,4},{4,0},{8,12},{12,8},{1,5},{5,1},{9,13},{13,9},{2,6},{6,2},{1... | collective-permute-start | bytes 1179656 | tf_op jit(solution)/shard_map/ppermute | solution.py:317
  22.2 15.6 %collective-permute-start.1 = (bf16[2,64,1536]{2,1,0:T(8,128)(2,1)S(1)}, bf16[2,64,1536]{2,1,0:T(8,128)(2,1)S(1)}, u32[]{:S(2)}, u32[]{:S(2)}) collective-permute-start(bf16[2,64,1536]{2,1,0:T(8,128)(2,1)S(1)} %collective-permute-done.refs_0_.refs_1_), channel_id=1, source_target_pairs={{0,1},{1,2},{2,3},{3,0},{4,5},{5,6},{6,7},{7,4},{8,9},{9,10},{10,1... | collective-permute-start | bytes 1179656 | tf_op jit(solution)/shard_map/ppermute | solution.py:320
  24.9 15.3 %collective-permute-start.5 = (bf16[2,64,1536]{2,1,0:T(8,128)(2,1)S(1)}, bf16[2,64,1536]{2,1,0:T(8,128)(2,1)S(1)}, u32[]{:S(2)}, u32[]{:S(2)}) collective-permute-start(bf16[2,64,1536]{2,1,0:T(8,128)(2,1)S(1)} %add_convert_fusion.1.refs_3_.refs_2_), channel_id=1, source_target_pairs={{0,8},{4,12},{8,0},{12,4},{1,9},{5,13},{9,1},{13,5},{2,10},{6,14},... | collective-permute-start | bytes 1179656 | tf_op jit(solution)/shard_map/ppermute | solution.py:326
  32.4 2.4 %collective-permute-start.7 = (bf16[2,64,1536]{2,1,0:T(8,128)(2,1)S(1)}, bf16[2,64,1536]{2,1,0:T(8,128)(2,1)S(1)}, u32[]{:S(2)}, u32[]{:S(2)}) collective-permute-start(bf16[2,64,1536]{2,1,0:T(8,128)(2,1)S(1)} %give.4.refs_3_), channel_id=1, source_target_pairs={{0,4},{4,0},{8,12},{12,8},{1,5},{5,1},{9,13},{13,9},{2,6},{6,2},{1... | collective-permute-start | bytes 1179656 | tf_op jit(solution)/shard_map/ppermute | solution.py:317
  34.9 13.8 %collective-permute-start.10 = (bf16[2,64,1536]{2,1,0:T(8,128)(2,1)S(1)}, bf16[2,64,1536]{2,1,0:T(8,128)(2,1)S(1)}, u32[]{:S(2)}, u32[]{:S(2)}) collective-permute-start(bf16[2,64,1536]{2,1,0:T(8,128)(2,1)S(1)} %add_convert_fusion.refs_3_.refs_0_), channel_id=1, source_target_pairs={{0,8},{4,12},{8,0},{12,4},{1,9},{5,13},{9,1},{13,5},{2,10},{6,14},... | collective-permute-start | bytes 1179656 | tf_op jit(solution)/shard_map/ppermute | solution.py:326
  40.2 3.5 %collective-permute-start.8 = (bf16[2,64,1536]{2,1,0:T(8,128)(2,1)S(1)}, bf16[2,64,1536]{2,1,0:T(8,128)(2,1)S(1)}, u32[]{:S(2)}, u32[]{:S(2)}) collective-permute-start(bf16[2,64,1536]{2,1,0:T(8,128)(2,1)S(1)} %give.5.refs_4_), channel_id=1, source_target_pairs={{0,4},{4,0},{8,12},{12,8},{1,5},{5,1},{9,13},{13,9},{2,6},{6,2},{1... | collective-permute-start | bytes 1179656 | tf_op jit(solution)/shard_map/ppermute | solution.py:317
  40.8 4.8 %collective-permute-start.11 = (bf16[2,128,1536]{2,1,0:T(8,128)(2,1)S(1)}, bf16[2,128,1536]{2,1,0:T(8,128)(2,1)S(1)}, u32[]{:S(2)}, u32[]{:S(2)}) collective-permute-start(bf16[2,128,1536]{2,1,0:T(8,128)(2,1)S(1)} %gelu.4.refs_3_.refs_0_), channel_id=1, source_target_pairs={{0,4},{4,0},{8,12},{12,8},{1,5},{5,1},{9,13},{13,9},{2,6},{6,2},{1... | collective-permute-start | bytes 2359304 | tf_op jit(solution)/shard_map/ppermute | solution.py:317
  43.8 7.7 %collective-permute-start.12 = (bf16[2,64,768]{2,1,0:T(8,128)(2,1)S(1)}, bf16[2,64,768]{2,1,0:T(8,128)(2,1)S(1)}, u32[]{:S(2)}, u32[]{:S(2)}) collective-permute-start(bf16[2,64,768]{2,1,0:T(8,128)(2,1)S(1)} %get-tuple-element.53.refs_4_.refs_0_), channel_id=1, source_target_pairs={{0,8},{4,12},{8,0},{12,4},{1,9},{5,13},{9,1},{13,5},{2,10},{6,14},... | collective-permute-start | bytes 589832 | tf_op jit(solution)/shard_map/ppermute | solution.py:326
  49.0 3.2 %collective-permute-start.13 = (bf16[64,1536]{1,0:T(8,128)(2,1)S(1)}, bf16[64,1536]{1,0:T(8,128)(2,1)S(1)}, u32[]{:S(2)}, u32[]{:S(2)}) collective-permute-start(bf16[64,1536]{1,0:T(8,128)(2,1)S(1)} %get-tuple-element.38.refs_4_.refs_7_), channel_id=1, source_target_pairs={{0,4},{4,0},{8,12},{12,8},{1,5},{5,1},{9,13},{13,9},{2,6},{6,2},{1... | collective-permute-start | bytes 589832 | tf_op jit(solution)/shard_map/ppermute | solution.py:317
  49.1 8.0 %collective-permute-start.9 = (bf16[2,64,768]{2,1,0:T(8,128)(2,1)S(1)}, bf16[2,64,768]{2,1,0:T(8,128)(2,1)S(1)}, u32[]{:S(2)}, u32[]{:S(2)}) collective-permute-start(bf16[2,64,768]{2,1,0:T(8,128)(2,1)S(1)} %get-tuple-element.54.refs_5_.refs_0_), channel_id=1, source_target_pairs={{0,8},{4,12},{8,0},{12,4},{1,9},{5,13},{9,1},{13,5},{2,10},{6,14},... | collective-permute-start | bytes 589832 | tf_op jit(solution)/shard_map/ppermute | solution.py:326
  49.7 12.6 %collective-permute-start.15 = (bf16[64,1536]{1,0:T(8,128)(2,1)S(1)}, bf16[64,1536]{1,0:T(8,128)(2,1)S(1)}, u32[]{:S(2)}, u32[]{:S(2)}) collective-permute-start(bf16[64,1536]{1,0:T(8,128)(2,1)S(1)} %get-tuple-element.37.refs_2_), channel_id=1, source_target_pairs={{0,3},{1,0},{2,1},{3,2},{4,7},{5,4},{6,5},{7,6},{8,11},{9,8},{10,9... | collective-permute-start | bytes 589832 | tf_op jit(solution)/shard_map/ppermute | solution.py:320
  51.6 6.3 %collective-permute-start.16 = (bf16[64,1536]{1,0:T(8,128)(2,1)S(1)}, bf16[64,1536]{1,0:T(8,128)(2,1)S(1)}, u32[]{:S(2)}, u32[]{:S(2)}) collective-permute-start(bf16[64,1536]{1,0:T(8,128)(2,1)S(1)} %get-tuple-element.39.refs_2_.refs_5_), channel_id=1, source_target_pairs={{0,4},{4,0},{8,12},{12,8},{1,5},{5,1},{9,13},{13,9},{2,6},{6,2},{1... | collective-permute-start | bytes 589832 | tf_op jit(solution)/shard_map/ppermute | solution.py:317
  51.7 6.2 %collective-permute-start.17 = (bf16[2,64,768]{2,1,0:T(8,128)(2,1)S(1)}, bf16[2,64,768]{2,1,0:T(8,128)(2,1)S(1)}, u32[]{:S(2)}, u32[]{:S(2)}) collective-permute-start(bf16[2,64,768]{2,1,0:T(8,128)(2,1)S(1)} %gelu.6.refs_6_.refs_11_.refs_7_), channel_id=1, source_target_pairs={{0,4},{4,0},{8,12},{12,8},{1,5},{5,1},{9,13},{13,9},{2,6},{6,2},{1... | collective-permute-start | bytes 589832 | tf_op jit(solution)/shard_map/ppermute | solution.py:317
  57.3 5.0 %collective-permute-start.14 = (bf16[2,64,768]{2,1,0:T(8,128)(2,1)S(1)}, bf16[2,64,768]{2,1,0:T(8,128)(2,1)S(1)}, u32[]{:S(2)}, u32[]{:S(2)}) collective-permute-start(bf16[2,64,768]{2,1,0:T(8,128)(2,1)S(1)} %gelu.7.refs_9_.refs_15_.refs_6_), channel_id=1, source_target_pairs={{0,4},{4,0},{8,12},{12,8},{1,5},{5,1},{9,13},{13,9},{2,6},{6,2},{1... | collective-permute-start | bytes 589832 | tf_op jit(solution)/shard_map/ppermute | solution.py:317
  57.4 15.3 %collective-permute-start.18 = (bf16[64,1536]{1,0:T(8,128)(2,1)S(1)}, bf16[64,1536]{1,0:T(8,128)(2,1)S(1)}, u32[]{:S(2)}, u32[]{:S(2)}) collective-permute-start(bf16[64,1536]{1,0:T(8,128)(2,1)S(1)} %get-tuple-element.47), channel_id=1, source_target_pairs={{0,1},{1,2},{2,3},{3,0},{4,5},{5,6},{6,7},{7,4},{8,9},{9,10},{10,1... | collective-permute-start | bytes 589832 | tf_op jit(solution)/shard_map/ppermute | solution.py:320
  63.2 12.0 %collective-permute-start.19 = (bf16[64,1536]{1,0:T(8,128)(2,1)S(1)}, bf16[64,1536]{1,0:T(8,128)(2,1)S(1)}, u32[]{:S(2)}, u32[]{:S(2)}) collective-permute-start(bf16[64,1536]{1,0:T(8,128)(2,1)S(1)} %get-tuple-element.48.refs_13_), channel_id=1, source_target_pairs={{0,2},{1,3},{2,0},{3,1},{4,6},{5,7},{6,4},{7,5},{8,10},{9,11},{10,... | collective-permute-start | bytes 589832 | tf_op jit(solution)/shard_map/ppermute | solution.py:320

commit v11 on v7

--- a/solution.py
+++ b/solution.py
@@ -316,8 +316,10 @@
     def swap_cores(x):
         return lax.ppermute(x, "wide", [(i, i ^ 1) for i in range(wide)])
 
+    ring = [*range(0, narrow, 2), *range(narrow - 1, 0, -2)]
+
     def shift(x, places):
-        return lax.ppermute(x, "narrow", [(i, (i + places) % narrow) for i in range(narrow)])
+        return lax.ppermute(x, "narrow", [(ring[i], ring[(i + places) % narrow]) for i in range(narrow)])
 
     def across_chips(keep, got):
         partial = (keep.astype(F32) + got.astype(F32)).astype(BF16)

time: 74.2 us -> 78.9 us (1.063)
  starting transfers between devices: 17.1 us -> 25.6 us
  waiting for transfers between devices: 8.67 us -> 4.87 us
    ppermute x6, starting transfers between devices: 9.42 us -> 18.2 us  [shift(): lax.ppermute(x, 'narrow', [(ring[i], ring[(i + places) % narrow]) for i i...]
    ppermute x6, waiting for transfers between devices: 5.99 us -> 4.05 us  [shift(): lax.ppermute(x, 'narrow', [(ring[i], ring[(i + places) % narrow]) for i i...]
    ppermute x5, waiting for transfers between devices: 2.65 us -> 0.8 us  [across_chips(): lax.ppermute(partial, 'wide', [(i, i ^ 2 * hop) for i in range(wide)])]
  transfers between devices with their start and end apart: 20 -> 20, of which waited for: 4 -> 4; matrix products, arithmetic and copies ran while one was open for 1% -> 0% of each run, Pallas kernels for 61% -> 57%
where the time goes in v11:
time: 78.9 us; the launch traced here: 78.7 us
  Pallas kernels  46.2 us (59%)
  starting transfers between devices  25.6 us (32%)
  waiting for transfers between devices  4.87 us (6%)
  other arithmetic  1.11 us (1%)
  between operations  0.92 us (1%)
    pallas_call x19, Pallas kernels, __call__(): pl.pallas_call(kernel, out_shape=outs, in_specs=specs, out_specs=[pl.Bloc...  46.2 us
    ppermute x6, starting transfers between devices, shift(): lax.ppermute(x, 'narrow', [(ring[i], ring[(i + places) % narrow]) for i i...  18.2 us
    ppermute x5, starting transfers between devices, across_chips(): lax.ppermute(partial, 'wide', [(i, i ^ 2 * hop) for i in range(wide)])  5.91 us
    ppermute x6, waiting for transfers between devices, shift(): lax.ppermute(x, 'narrow', [(ring[i], ring[(i + places) % narrow]) for i i...  4.05 us
  transfers between devices with their start and end apart: 20, of which 4 were waited for; matrix products, arithmetic and copies ran while one was open for 0% of the time, Pallas kernels for 57%

profile of v11, /device:TPU:0, one launch (start us, length us, event | category | flops | bytes accessed | tf_op | source)
XLA Modules:
  0.0 78.7 jit_solution(17501631931205462460)
XLA Ops:
  0.6 1.0 %stacked.1.refs_1_.refs_4_.refs_0_ = bf16[2,64,1536]{2,1,0:T(8,128)(2,1)S(1)} custom-call(bf16[64,1536]{1,0:T(8,128)(2,1)} %refs_0_.1, bf16[64,1536]{1,0:T(8,128)(2,1)} %refs_1_.1), custom_call_target="tpu_custom_call" | custom-call | flops 2000000000 | tf_op jit(solution)/shard_map/stacked/pallas_call | solution.py:53
  1.7 4.1 %collective-permute-start = (bf16[2,64,1536]{2,1,0:T(8,128)(2,1)S(1)}, bf16[2,64,1536]{2,1,0:T(8,128)(2,1)S(1)}, u32[]{:S(2)}, u32[]{:S(2)}) collective-permute-start(bf16[2,64,1536]{2,1,0:T(8,128)(2,1)S(1)} %stacked.1.refs_1_.refs_4_.refs_0_), channel_id=1, source_target_pairs={{0,2},{2,3},{3,1},{1,0},{4,6},{6,7},{7,5},{5,4},{8,10},{10,11},{11... | collective-permute-start | bytes 1179656 | tf_op jit(solution)/shard_map/ppermute | solution.py:322
  5.8 4.5 %give_first.1 = (bf16[1536,1536]{1,0:T(8,128)(2,1)S(1)}, bf16[1536,1536]{1,0:T(8,128)(2,1)S(1)}, bf16[2,64,1536]{2,1,0:T(8,128)(2,1)S(1)}) custom-call(s32[1]{0:T(128)} %bitcast.refs_0_, bf16[2,64,1536]{2,1,0:T(8,128)(2,1)S(1)} %stacked.1.refs_1_.refs_4_.refs_0_, bf16[1536,3072]{1,0:T(8,128)(2,1)} %refs_2_.3, bf16[3072,1536]{1,0:T(8,128)(2,1)} %refs_3_.3, ...), custom_call_target="tpu_custom_call" | custom-call | flops 17999998976 | tf_op jit(solution)/shard_map/give_first/pallas_call | solution.py:53
  10.4 4.5 %keep_first.1 = (bf16[1536,1536]{1,0:T(8,128)(2,1)S(1)}, bf16[1536,1536]{1,0:T(8,128)(2,1)S(1)}, bf16[2,64,1536]{2,1,0:T(8,128)(2,1)S(1)}, bf16[2,64,1536]{2,1,0:T(8,128)(2,1)S(1)}) custom-call(s32[1]{0:T(128)} %bitcast.refs_0_, bf16[2,64,1536]{2,1,0:T(8,128)(2,1)S(1)} %stacked.1.refs_1_.refs_4_.refs_0_, bf16[1536,3072]{1,0:T(8,128)(2,1)} %refs_2_.3, ...), custom_call_target="tpu_custom_call" | custom-call | flops 17999998976 | tf_op jit(solution)/shard_map/keep_first/pallas_call | solution.py:53
  15.1 1.6 %collective-permute-start.3 = (bf16[2,64,1536]{2,1,0:T(8,128)(2,1)S(1)}, bf16[2,64,1536]{2,1,0:T(8,128)(2,1)S(1)}, u32[]{:S(2)}, u32[]{:S(2)}) collective-permute-start(bf16[2,64,1536]{2,1,0:T(8,128)(2,1)S(1)} %add_convert_fusion.2.refs_3_.refs_0_), channel_id=1, source_target_pairs={{0,8},{4,12},{8,0},{12,4},{1,9},{5,13},{9,1},{13,5},{2,10},{6,14},... | collective-permute-start | bytes 1179656 | tf_op jit(solution)/shard_map/ppermute | solution.py:328
  16.6 2.3 %give.3.refs_3_ = bf16[2,64,1536]{2,1,0:T(8,128)(2,1)S(1)} custom-call(bf16[2,64,1536]{2,1,0:T(8,128)(2,1)S(1)} %collective-permute-done.refs_0_.refs_1_, bf16[1536,1536]{1,0:T(8,128)(2,1)S(1)} %get-tuple-element.32.refs_1_.refs_3_.refs_10_.refs_11_, bf16[1536,1536]{1,0:T(8,128)(2,1)S(1)} %get-tuple-element.33.refs_2_, ...), custom_call_target="tpu_custom_call" | custom-call | flops 9600000000 | tf_op jit(solution)/shard_map/give/pallas_call | solution.py:53
  19.0 0.3 collective-permute-start.4
  19.3 2.9 %collective-permute-start.1 = (bf16[2,64,1536]{2,1,0:T(8,128)(2,1)S(1)}, bf16[2,64,1536]{2,1,0:T(8,128)(2,1)S(1)}, u32[]{:S(2)}, u32[]{:S(2)}) collective-permute-start(bf16[2,64,1536]{2,1,0:T(8,128)(2,1)S(1)} %collective-permute-done.refs_0_.refs_1_), channel_id=1, source_target_pairs={{0,2},{2,3},{3,1},{1,0},{4,6},{6,7},{7,5},{5,4},{8,10},{10,11},{11... | collective-permute-start | bytes 1179656 | tf_op jit(solution)/shard_map/ppermute | solution.py:322
  22.2 2.3 %keep.3.refs_5_ = bf16[2,64,1536]{2,1,0:T(8,128)(2,1)S(1)} custom-call(bf16[2,64,1536]{2,1,0:T(8,128)(2,1)S(1)} %collective-permute-done.refs_0_.refs_1_, bf16[1536,1536]{1,0:T(8,128)(2,1)S(1)} %get-tuple-element.29.refs_1_.refs_2_.refs_9_.refs_10_.refs_12_, bf16[1536,1536]{1,0:T(8,128)(2,1)S(1)} %get-tuple-element.30.refs_2_, ...), custom_call_target="tpu_custom_call" | custom-call | flops 9600000000 | tf_op jit(solution)/shard_map/keep/pallas_call | solution.py:53
  24.7 0.6 collective-permute-start.5
  25.3 2.5 %collective-permute-done.6.refs_0_.refs_2_ = bf16[2,64,1536]{2,1,0:T(8,128)(2,1)S(1)} collective-permute-done((bf16[2,64,1536]{2,1,0:T(8,128)(2,1)S(1)}, bf16[2,64,1536]{2,1,0:T(8,128)(2,1)S(1)}, u32[]{:S(2)}, u32[]{:S(2)}) %collective-permute-start.6) | collective-permute-done | bytes 393248 | tf_op jit(solution)/shard_map/ppermute | solution.py:322
  27.7 2.3 %give.4.refs_3_ = bf16[2,64,1536]{2,1,0:T(8,128)(2,1)S(1)} custom-call(bf16[2,64,1536]{2,1,0:T(8,128)(2,1)S(1)} %collective-permute-done.6.refs_0_.refs_2_, bf16[1536,1536]{1,0:T(8,128)(2,1)S(1)} %get-tuple-element.32.refs_1_.refs_3_.refs_10_.refs_11_, bf16[1536,1536]{1,0:T(8,128)(2,1)S(1)} %get-tuple-element.33.refs_2_, ...), custom_call_target="tpu_custom_call" | custom-call | flops 9600000000 | tf_op jit(solution)/shard_map/give/pallas_call | solution.py:53
  30.1 2.3 %keep.4.refs_4_ = bf16[2,64,1536]{2,1,0:T(8,128)(2,1)S(1)} custom-call(bf16[2,64,1536]{2,1,0:T(8,128)(2,1)S(1)} %collective-permute-done.6.refs_0_.refs_2_, bf16[1536,1536]{1,0:T(8,128)(2,1)S(1)} %get-tuple-element.29.refs_1_.refs_2_.refs_9_.refs_10_.refs_12_, bf16[1536,1536]{1,0:T(8,128)(2,1)S(1)} %get-tuple-element.30.refs_2_, ...), custom_call_target="tpu_custom_call" | custom-call | flops 9600000000 | tf_op jit(solution)/shard_map/keep/pallas_call | solution.py:53
  32.6 1.6 %collective-permute-start.10 = (bf16[2,64,1536]{2,1,0:T(8,128)(2,1)S(1)}, bf16[2,64,1536]{2,1,0:T(8,128)(2,1)S(1)}, u32[]{:S(2)}, u32[]{:S(2)}) collective-permute-start(bf16[2,64,1536]{2,1,0:T(8,128)(2,1)S(1)} %add_convert_fusion.refs_3_.refs_0_), channel_id=1, source_target_pairs={{0,8},{4,12},{8,0},{12,4},{1,9},{5,13},{9,1},{13,5},{2,10},{6,14},... | collective-permute-start | bytes 1179656 | tf_op jit(solution)/shard_map/ppermute | solution.py:328
  34.2 1.6 %collective-permute-done.1.refs_0_.refs_3_ = bf16[2,64,1536]{2,1,0:T(8,128)(2,1)S(1)} collective-permute-done((bf16[2,64,1536]{2,1,0:T(8,128)(2,1)S(1)}, bf16[2,64,1536]{2,1,0:T(8,128)(2,1)S(1)}, u32[]{:S(2)}, u32[]{:S(2)}) %collective-permute-start.1) | collective-permute-done | bytes 393248 | tf_op jit(solution)/shard_map/ppermute | solution.py:322
  35.8 2.3 %give.5.refs_4_ = bf16[2,64,1536]{2,1,0:T(8,128)(2,1)S(1)} custom-call(bf16[2,64,1536]{2,1,0:T(8,128)(2,1)S(1)} %collective-permute-done.1.refs_0_.refs_3_, bf16[1536,1536]{1,0:T(8,128)(2,1)S(1)} %get-tuple-element.32.refs_1_.refs_3_.refs_10_.refs_11_, bf16[1536,1536]{1,0:T(8,128)(2,1)S(1)} %get-tuple-element.33.refs_2_, ...), custom_call_target="tpu_custom_call" | custom-call | flops 9600000000 | tf_op jit(solution)/shard_map/give/pallas_call | solution.py:53
  38.3 0.5 gelu.4.refs_3_.refs_0_
  38.8 0.5 collective-permute-start.11
  39.3 2.3 %keep.5.refs_6_ = bf16[2,64,1536]{2,1,0:T(8,128)(2,1)S(1)} custom-call(bf16[2,64,1536]{2,1,0:T(8,128)(2,1)S(1)} %collective-permute-done.1.refs_0_.refs_3_, bf16[1536,1536]{1,0:T(8,128)(2,1)S(1)} %get-tuple-element.29.refs_1_.refs_2_.refs_9_.refs_10_.refs_12_, bf16[1536,1536]{1,0:T(8,128)(2,1)S(1)} %get-tuple-element.30.refs_2_, ...), custom_call_target="tpu_custom_call" | custom-call | flops 9600000000 | tf_op jit(solution)/shard_map/keep/pallas_call | solution.py:53
  41.8 1.6 %collective-permute-start.12 = (bf16[2,64,768]{2,1,0:T(8,128)(2,1)S(1)}, bf16[2,64,768]{2,1,0:T(8,128)(2,1)S(1)}, u32[]{:S(2)}, u32[]{:S(2)}) collective-permute-start(bf16[2,64,768]{2,1,0:T(8,128)(2,1)S(1)} %get-tuple-element.53.refs_4_.refs_0_), channel_id=1, source_target_pairs={{0,8},{4,12},{8,0},{12,4},{1,9},{5,13},{9,1},{13,5},{2,10},{6,14},... | collective-permute-start | bytes 589832 | tf_op jit(solution)/shard_map/ppermute | solution.py:328
  43.6 3.1 %input_product.2 = (bf16[64,1536]{1,0:T(8,128)(2,1)S(1)}, bf16[64,1536]{1,0:T(8,128)(2,1)S(1)}) custom-call(bf16[2,128,1536]{2,1,0:T(8,128)(2,1)S(1)} %gelu.4.refs_3_.refs_0_, bf16[2,128,1536]{2,1,0:T(8,128)(2,1)S(1)} %collective-permute-done.11.refs_1_.refs_3_.refs_7_, bf16[1536,1536]{1,0:T(8,128)(2,1)S(1)} %get-tuple-element.29.refs_1_.refs_2_.refs_9_.refs_10_.refs_12_, ...), custom_call_target="tpu_custom_call" | custom-call | flops 400000000 | tf_op jit(solution)/shard_map/input_product/pallas_call | solution.py:53
  47.1 0.6 collective-permute-start.9
  47.7 0.7 collective-permute-start.15
  48.4 0.3 collective-permute-done.12.refs_1_
  49.1 4.9 %weight_grads.3 = (f32[1536,3072]{1,0:T(8,128)}, f32[3072,1536]{1,0:T(8,128)}, bf16[64,1536]{1,0:T(8,128)(2,1)S(1)}, f32[8,128]{1,0:T(8,128)S(1)}) custom-call(s32[1]{0:T(128)} %bitcast.refs_0_, bf16[1536,256]{1,0:T(8,128)(2,1)S(1)} %get-tuple-element.35.refs_1_, bf16[256,1536]{1,0:T(8,128)(2,1)S(1)} %get-tuple-element.36.refs_4_.refs_2_, ...), custom_call_target="tpu_custom_call" | custom-call | flops 16000000000 | tf_op jit(solution)/shard_map/weight_grads/pallas_call | solution.py:53
  54.0 0.4 collective-permute-done.9.refs_1_
  54.6 2.1 %collective-permute-start.18 = (bf16[64,1536]{1,0:T(8,128)(2,1)S(1)}, bf16[64,1536]{1,0:T(8,128)(2,1)S(1)}, u32[]{:S(2)}, u32[]{:S(2)}) collective-permute-start(bf16[64,1536]{1,0:T(8,128)(2,1)S(1)} %get-tuple-element.47), channel_id=1, source_target_pairs={{0,2},{2,3},{3,1},{1,0},{4,6},{6,7},{7,5},{5,4},{8,10},{10,11},{11... | collective-permute-start | bytes 589832 | tf_op jit(solution)/shard_map/ppermute | solution.py:322
  56.7 4.4 %weight_grads.4 = (f32[1536,3072]{1,0:T(8,128)}, f32[3072,1536]{1,0:T(8,128)}, f32[64,1536]{1,0:T(8,128)S(1)}, f32[8,128]{1,0:T(8,128)S(1)}) custom-call(s32[1]{0:T(128)} %bitcast.refs_0_, bf16[1536,256]{1,0:T(8,128)(2,1)S(1)} %get-tuple-element.35.refs_1_, ...), custom_call_target="tpu_custom_call", output_to_operand_aliasing={{0}: (13, {}), {1}: (14, {})} | custom-call | flops 16000000000 | tf_op jit(solution)/shard_map/weight_grads/pallas_call | solution.py:53
  61.1 0.9 %input_product.3 = (f32[64,1536]{1,0:T(8,128)S(1)}, bf16[64,1536]{1,0:T(8,128)(2,1)S(1)}) custom-call(bf16[2,64,768]{2,1,0:T(8,128)(2,1)S(1)} %collective-permute-done.14.refs_0_.refs_10_, bf16[1536,1536]{1,0:T(8,128)(2,1)S(1)} %get-tuple-element.32.refs_1_.refs_3_.refs_10_.refs_11_, bf16[64,1536]{1,0:T(8,128)(2,1)S(1)} %get-tuple-element.41.refs_2_, ...), custom_call_target="tpu_custom_call" | custom-call | flops 12000000000 | tf_op jit(solution)/shard_map/input_product/pallas_call | solution.py:53
  62.0 8.4 %collective-permute-start.19 = (bf16[64,1536]{1,0:T(8,128)(2,1)S(1)}, bf16[64,1536]{1,0:T(8,128)(2,1)S(1)}, u32[]{:S(2)}, u32[]{:S(2)}) collective-permute-start(bf16[64,1536]{1,0:T(8,128)(2,1)S(1)} %get-tuple-element.48.refs_13_), channel_id=1, source_target_pairs={{0,3},{2,1},{3,0},{1,2},{4,7},{6,5},{7,4},{5,6},{8,11},{10,9},{11,... | collective-permute-start | bytes 589832 | tf_op jit(solution)/shard_map/ppermute | solution.py:322
  70.4 7.6 %weight_grads.5 = (f32[1536,3072]{1,0:T(8,128)}, f32[3072,1536]{1,0:T(8,128)}, f32[8,128]{1,0:T(8,128)}) custom-call(s32[1]{0:T(128)} %bitcast.refs_0_, bf16[1536,256]{1,0:T(8,128)(2,1)S(1)} %get-tuple-element.35.refs_1_, bf16[256,1536]{1,0:T(8,128)(2,1)S(1)} %get-tuple-element.36.refs_4_.refs_2_, ...), custom_call_target="tpu_custom_call", output_to_operand_aliasing={{0}: (11, {}), {1}: (12, {})} | custom-call | flops 32000000000 | tf_op jit(solution)/shard_map/weight_grads/pallas_call | solution.py:53
  78.0 0.7 add_convert_fusion.3
  (32 shorter events, 1.9 us)
Async XLA Ops:
  1.7 15.0 %collective-permute-start = (bf16[2,64,1536]{2,1,0:T(8,128)(2,1)S(1)}, bf16[2,64,1536]{2,1,0:T(8,128)(2,1)S(1)}, u32[]{:S(2)}, u32[]{:S(2)}) collective-permute-start(bf16[2,64,1536]{2,1,0:T(8,128)(2,1)S(1)} %stacked.1.refs_1_.refs_4_.refs_0_), channel_id=1, source_target_pairs={{0,2},{2,3},{3,1},{1,0},{4,6},{6,7},{7,5},{5,4},{8,10},{10,11},{11... | collective-permute-start | bytes 1179656 | tf_op jit(solution)/shard_map/ppermute | solution.py:322
  10.3 4.7 %collective-permute-start.2 = (bf16[2,64,1536]{2,1,0:T(8,128)(2,1)S(1)}, bf16[2,64,1536]{2,1,0:T(8,128)(2,1)S(1)}, u32[]{:S(2)}, u32[]{:S(2)}) collective-permute-start(bf16[2,64,1536]{2,1,0:T(8,128)(2,1)S(1)} %get-tuple-element.28.refs_4_), channel_id=1, source_target_pairs={{0,4},{4,0},{8,12},{12,8},{1,5},{5,1},{9,13},{13,9},{2,6},{6,2},{1... | collective-permute-start | bytes 1179656 | tf_op jit(solution)/shard_map/ppermute | solution.py:317
  14.9 12.8 %collective-permute-start.6 = (bf16[2,64,1536]{2,1,0:T(8,128)(2,1)S(1)}, bf16[2,64,1536]{2,1,0:T(8,128)(2,1)S(1)}, u32[]{:S(2)}, u32[]{:S(2)}) collective-permute-start(bf16[2,64,1536]{2,1,0:T(8,128)(2,1)S(1)} %get-tuple-element.34), channel_id=1, source_target_pairs={{0,1},{2,0},{3,2},{1,3},{4,5},{6,4},{7,6},{5,7},{8,9},{10,8},{11,1... | collective-permute-start | bytes 1179656 | tf_op jit(solution)/shard_map/ppermute | solution.py:322
  15.1 12.6 %collective-permute-start.3 = (bf16[2,64,1536]{2,1,0:T(8,128)(2,1)S(1)}, bf16[2,64,1536]{2,1,0:T(8,128)(2,1)S(1)}, u32[]{:S(2)}, u32[]{:S(2)}) collective-permute-start(bf16[2,64,1536]{2,1,0:T(8,128)(2,1)S(1)} %add_convert_fusion.2.refs_3_.refs_0_), channel_id=1, source_target_pairs={{0,8},{4,12},{8,0},{12,4},{1,9},{5,13},{9,1},{13,5},{2,10},{6,14},... | collective-permute-start | bytes 1179656 | tf_op jit(solution)/shard_map/ppermute | solution.py:328
  19.0 5.6 %collective-permute-start.4 = (bf16[2,64,1536]{2,1,0:T(8,128)(2,1)S(1)}, bf16[2,64,1536]{2,1,0:T(8,128)(2,1)S(1)}, u32[]{:S(2)}, u32[]{:S(2)}) collective-permute-start(bf16[2,64,1536]{2,1,0:T(8,128)(2,1)S(1)} %give.3.refs_3_), channel_id=1, source_target_pairs={{0,4},{4,0},{8,12},{12,8},{1,5},{5,1},{9,13},{13,9},{2,6},{6,2},{1... | collective-permute-start | bytes 1179656 | tf_op jit(solution)/shard_map/ppermute | solution.py:317
  19.3 16.5 %collective-permute-start.1 = (bf16[2,64,1536]{2,1,0:T(8,128)(2,1)S(1)}, bf16[2,64,1536]{2,1,0:T(8,128)(2,1)S(1)}, u32[]{:S(2)}, u32[]{:S(2)}) collective-permute-start(bf16[2,64,1536]{2,1,0:T(8,128)(2,1)S(1)} %collective-permute-done.refs_0_.refs_1_), channel_id=1, source_target_pairs={{0,2},{2,3},{3,1},{1,0},{4,6},{6,7},{7,5},{5,4},{8,10},{10,11},{11... | collective-permute-start | bytes 1179656 | tf_op jit(solution)/shard_map/ppermute | solution.py:322
  24.7 13.6 %collective-permute-start.5 = (bf16[2,64,1536]{2,1,0:T(8,128)(2,1)S(1)}, bf16[2,64,1536]{2,1,0:T(8,128)(2,1)S(1)}, u32[]{:S(2)}, u32[]{:S(2)}) collective-permute-start(bf16[2,64,1536]{2,1,0:T(8,128)(2,1)S(1)} %add_convert_fusion.1.refs_3_.refs_2_), channel_id=1, source_target_pairs={{0,8},{4,12},{8,0},{12,4},{1,9},{5,13},{9,1},{13,5},{2,10},{6,14},... | collective-permute-start | bytes 1179656 | tf_op jit(solution)/shard_map/ppermute | solution.py:328
  30.1 2.4 %collective-permute-start.7 = (bf16[2,64,1536]{2,1,0:T(8,128)(2,1)S(1)}, bf16[2,64,1536]{2,1,0:T(8,128)(2,1)S(1)}, u32[]{:S(2)}, u32[]{:S(2)}) collective-permute-start(bf16[2,64,1536]{2,1,0:T(8,128)(2,1)S(1)} %give.4.refs_3_), channel_id=1, source_target_pairs={{0,4},{4,0},{8,12},{12,8},{1,5},{5,1},{9,13},{13,9},{2,6},{6,2},{1... | collective-permute-start | bytes 1179656 | tf_op jit(solution)/shard_map/ppermute | solution.py:317
  32.6 14.1 %collective-permute-start.10 = (bf16[2,64,1536]{2,1,0:T(8,128)(2,1)S(1)}, bf16[2,64,1536]{2,1,0:T(8,128)(2,1)S(1)}, u32[]{:S(2)}, u32[]{:S(2)}) collective-permute-start(bf16[2,64,1536]{2,1,0:T(8,128)(2,1)S(1)} %add_convert_fusion.refs_3_.refs_0_), channel_id=1, source_target_pairs={{0,8},{4,12},{8,0},{12,4},{1,9},{5,13},{9,1},{13,5},{2,10},{6,14},... | collective-permute-start | bytes 1179656 | tf_op jit(solution)/shard_map/ppermute | solution.py:328
  38.1 3.5 %collective-permute-start.8 = (bf16[2,64,1536]{2,1,0:T(8,128)(2,1)S(1)}, bf16[2,64,1536]{2,1,0:T(8,128)(2,1)S(1)}, u32[]{:S(2)}, u32[]{:S(2)}) collective-permute-start(bf16[2,64,1536]{2,1,0:T(8,128)(2,1)S(1)} %give.5.refs_4_), channel_id=1, source_target_pairs={{0,4},{4,0},{8,12},{12,8},{1,5},{5,1},{9,13},{13,9},{2,6},{6,2},{1... | collective-permute-start | bytes 1179656 | tf_op jit(solution)/shard_map/ppermute | solution.py:317
  38.8 4.8 %collective-permute-start.11 = (bf16[2,128,1536]{2,1,0:T(8,128)(2,1)S(1)}, bf16[2,128,1536]{2,1,0:T(8,128)(2,1)S(1)}, u32[]{:S(2)}, u32[]{:S(2)}) collective-permute-start(bf16[2,128,1536]{2,1,0:T(8,128)(2,1)S(1)} %gelu.4.refs_3_.refs_0_), channel_id=1, source_target_pairs={{0,4},{4,0},{8,12},{12,8},{1,5},{5,1},{9,13},{13,9},{2,6},{6,2},{1... | collective-permute-start | bytes 2359304 | tf_op jit(solution)/shard_map/ppermute | solution.py:317
  41.8 6.9 %collective-permute-start.12 = (bf16[2,64,768]{2,1,0:T(8,128)(2,1)S(1)}, bf16[2,64,768]{2,1,0:T(8,128)(2,1)S(1)}, u32[]{:S(2)}, u32[]{:S(2)}) collective-permute-start(bf16[2,64,768]{2,1,0:T(8,128)(2,1)S(1)} %get-tuple-element.53.refs_4_.refs_0_), channel_id=1, source_target_pairs={{0,8},{4,12},{8,0},{12,4},{1,9},{5,13},{9,1},{13,5},{2,10},{6,14},... | collective-permute-start | bytes 589832 | tf_op jit(solution)/shard_map/ppermute | solution.py:328
  47.0 2.1 %collective-permute-start.13 = (bf16[64,1536]{1,0:T(8,128)(2,1)S(1)}, bf16[64,1536]{1,0:T(8,128)(2,1)S(1)}, u32[]{:S(2)}, u32[]{:S(2)}) collective-permute-start(bf16[64,1536]{1,0:T(8,128)(2,1)S(1)} %get-tuple-element.38.refs_4_.refs_7_), channel_id=1, source_target_pairs={{0,4},{4,0},{8,12},{12,8},{1,5},{5,1},{9,13},{13,9},{2,6},{6,2},{1... | collective-permute-start | bytes 589832 | tf_op jit(solution)/shard_map/ppermute | solution.py:317
  47.1 7.3 %collective-permute-start.9 = (bf16[2,64,768]{2,1,0:T(8,128)(2,1)S(1)}, bf16[2,64,768]{2,1,0:T(8,128)(2,1)S(1)}, u32[]{:S(2)}, u32[]{:S(2)}) collective-permute-start(bf16[2,64,768]{2,1,0:T(8,128)(2,1)S(1)} %get-tuple-element.54.refs_5_.refs_0_), channel_id=1, source_target_pairs={{0,8},{4,12},{8,0},{12,4},{1,9},{5,13},{9,1},{13,5},{2,10},{6,14},... | collective-permute-start | bytes 589832 | tf_op jit(solution)/shard_map/ppermute | solution.py:328
  47.7 13.5 %collective-permute-start.15 = (bf16[64,1536]{1,0:T(8,128)(2,1)S(1)}, bf16[64,1536]{1,0:T(8,128)(2,1)S(1)}, u32[]{:S(2)}, u32[]{:S(2)}) collective-permute-start(bf16[64,1536]{1,0:T(8,128)(2,1)S(1)} %get-tuple-element.37.refs_2_), channel_id=1, source_target_pairs={{0,1},{2,0},{3,2},{1,3},{4,5},{6,4},{7,6},{5,7},{8,9},{10,8},{11,1... | collective-permute-start | bytes 589832 | tf_op jit(solution)/shard_map/ppermute | solution.py:322
  48.3 8.3 %collective-permute-start.16 = (bf16[64,1536]{1,0:T(8,128)(2,1)S(1)}, bf16[64,1536]{1,0:T(8,128)(2,1)S(1)}, u32[]{:S(2)}, u32[]{:S(2)}) collective-permute-start(bf16[64,1536]{1,0:T(8,128)(2,1)S(1)} %get-tuple-element.39.refs_2_.refs_5_), channel_id=1, source_target_pairs={{0,4},{4,0},{8,12},{12,8},{1,5},{5,1},{9,13},{13,9},{2,6},{6,2},{1... | collective-permute-start | bytes 589832 | tf_op jit(solution)/shard_map/ppermute | solution.py:317
  48.8 7.9 %collective-permute-start.17 = (bf16[2,64,768]{2,1,0:T(8,128)(2,1)S(1)}, bf16[2,64,768]{2,1,0:T(8,128)(2,1)S(1)}, u32[]{:S(2)}, u32[]{:S(2)}) collective-permute-start(bf16[2,64,768]{2,1,0:T(8,128)(2,1)S(1)} %gelu.6.refs_6_.refs_11_.refs_7_), channel_id=1, source_target_pairs={{0,4},{4,0},{8,12},{12,8},{1,5},{5,1},{9,13},{13,9},{2,6},{6,2},{1... | collective-permute-start | bytes 589832 | tf_op jit(solution)/shard_map/ppermute | solution.py:317
  54.5 6.6 %collective-permute-start.14 = (bf16[2,64,768]{2,1,0:T(8,128)(2,1)S(1)}, bf16[2,64,768]{2,1,0:T(8,128)(2,1)S(1)}, u32[]{:S(2)}, u32[]{:S(2)}) collective-permute-start(bf16[2,64,768]{2,1,0:T(8,128)(2,1)S(1)} %gelu.7.refs_9_.refs_15_.refs_6_), channel_id=1, source_target_pairs={{0,4},{4,0},{8,12},{12,8},{1,5},{5,1},{9,13},{13,9},{2,6},{6,2},{1... | collective-permute-start | bytes 589832 | tf_op jit(solution)/shard_map/ppermute | solution.py:317
  54.6 23.4 %collective-permute-start.18 = (bf16[64,1536]{1,0:T(8,128)(2,1)S(1)}, bf16[64,1536]{1,0:T(8,128)(2,1)S(1)}, u32[]{:S(2)}, u32[]{:S(2)}) collective-permute-start(bf16[64,1536]{1,0:T(8,128)(2,1)S(1)} %get-tuple-element.47), channel_id=1, source_target_pairs={{0,2},{2,3},{3,1},{1,0},{4,6},{6,7},{7,5},{5,4},{8,10},{10,11},{11... | collective-permute-start | bytes 589832 | tf_op jit(solution)/shard_map/ppermute | solution.py:322
  62.0 16.0 %collective-permute-start.19 = (bf16[64,1536]{1,0:T(8,128)(2,1)S(1)}, bf16[64,1536]{1,0:T(8,128)(2,1)S(1)}, u32[]{:S(2)}, u32[]{:S(2)}) collective-permute-start(bf16[64,1536]{1,0:T(8,128)(2,1)S(1)} %get-tuple-element.48.refs_13_), channel_id=1, source_target_pairs={{0,3},{2,1},{3,0},{1,2},{4,7},{6,5},{7,4},{5,6},{8,11},{10,9},{11,... | collective-permute-start | bytes 589832 | tf_op jit(solution)/shard_map/ppermute | solution.py:322

commit v12 on v11

--- a/solution.py
+++ b/solution.py
@@ -84,6 +84,13 @@
         spaces=[pl.ANY, pl.ANY],
         scratch=[pltpu.SemaphoreType.DMA((2,))],
     )[0]
+
+
+def copied(ordered, chunk):
+    def body(chunk_ref, out_ref):
+        out_ref[...] = chunk_ref[...]
+
+    return ordered(body, (chunk,), [jax.ShapeDtypeStruct(chunk.shape, BF16)], "copied", 0.1)[0]
 
 
 def first_product(ordered, core, other, chunk, up_weight, down_weight, name):
@@ -338,6 +345,7 @@
     got = swap_cores(give)
     up_mine, down_mine, sent_back, keep = first_product(ordered, core, False, chunks[0], up_weight, down_weight, "keep_first")
     sums = [across_chips(keep, got)]
+    forward = {-1: sent_back}
 
     def acts_of(sums, apart=False):
         mine = gelu(ordered, sums, apart)
@@ -347,12 +355,14 @@
     width = half // slices
     for offset in offsets[1:]:
         places = 1 if offset > 0 else -1
-        chunk = chunks[offset] = shift(sent_back if offset == -1 else chunks[offset - places], places)
+        chunk = chunks[offset] = shift(forward.get(offset, chunks[offset - places]), places)
         give = product(ordered, chunk, up_other, down_other, "give", after=[sums[-1][0]] + [sums[0][1]] * (len(sums) == 2))
         got = swap_cores(give)
         if offset == offsets[-1]:
             early = acts_of(sums[:-1])
         keep = product(ordered, chunk, up_mine, down_mine, "keep")
+        if offset == 1:
+            forward[2] = copied(ordered, chunk)
         if offset != offsets[-1]:
             sums.append(across_chips(keep, got))
         else:

time: 78.9 us -> 78.9 us (level)
    pallas_call x19 -> x20, Pallas kernels: 46.2 us -> 46.3 us  [__call__(): pl.pallas_call(kernel, out_shape=outs, in_specs=specs, out_specs=[pl.Bloc...]
where the time goes in v12:
time: 78.9 us; the launch traced here: 78.7 us
  Pallas kernels  46.3 us (59%)
  starting transfers between devices  25.5 us (32%)
  waiting for transfers between devices  4.85 us (6%)
  other arithmetic  1.11 us (1%)
  between operations  0.92 us (1%)
    pallas_call x20, Pallas kernels, __call__(): pl.pallas_call(kernel, out_shape=outs, in_specs=specs, out_specs=[pl.Bloc...  46.3 us
    ppermute x6, starting transfers between devices, shift(): lax.ppermute(x, 'narrow', [(ring[i], ring[(i + places) % narrow]) for i i...  18.2 us
    ppermute x5, starting transfers between devices, across_chips(): lax.ppermute(partial, 'wide', [(i, i ^ 2 * hop) for i in range(wide)])  5.91 us
    ppermute x6, waiting for transfers between devices, shift(): lax.ppermute(x, 'narrow', [(ring[i], ring[(i + places) % narrow]) for i i...  4.02 us
  transfers between devices with their start and end apart: 20, of which 4 were waited for; matrix products, arithmetic and copies ran while one was open for 0% of the time, Pallas kernels for 57%

profile of v12, /device:TPU:0, one launch (start us, length us, event | category | flops | bytes accessed | tf_op | source)
XLA Modules:
  0.0 78.7 jit_solution(18306875353222094332)
XLA Ops:
  0.6 1.0 %stacked.1.refs_1_.refs_4_.refs_0_ = bf16[2,64,1536]{2,1,0:T(8,128)(2,1)S(1)} custom-call(bf16[64,1536]{1,0:T(8,128)(2,1)} %refs_0_.1, bf16[64,1536]{1,0:T(8,128)(2,1)} %refs_1_.1), custom_call_target="tpu_custom_call" | custom-call | flops 2000000000 | tf_op jit(solution)/shard_map/stacked/pallas_call | solution.py:53
  1.7 4.1 %collective-permute-start = (bf16[2,64,1536]{2,1,0:T(8,128)(2,1)S(1)}, bf16[2,64,1536]{2,1,0:T(8,128)(2,1)S(1)}, u32[]{:S(2)}, u32[]{:S(2)}) collective-permute-start(bf16[2,64,1536]{2,1,0:T(8,128)(2,1)S(1)} %stacked.1.refs_1_.refs_4_.refs_0_), channel_id=1, source_target_pairs={{0,2},{2,3},{3,1},{1,0},{4,6},{6,7},{7,5},{5,4},{8,10},{10,11},{11... | collective-permute-start | bytes 1179656 | tf_op jit(solution)/shard_map/ppermute | solution.py:329
  5.8 4.5 %give_first.1 = (bf16[1536,1536]{1,0:T(8,128)(2,1)S(1)}, bf16[1536,1536]{1,0:T(8,128)(2,1)S(1)}, bf16[2,64,1536]{2,1,0:T(8,128)(2,1)S(1)}) custom-call(s32[1]{0:T(128)} %bitcast.refs_0_, bf16[2,64,1536]{2,1,0:T(8,128)(2,1)S(1)} %stacked.1.refs_1_.refs_4_.refs_0_, bf16[1536,3072]{1,0:T(8,128)(2,1)} %refs_2_.3, bf16[3072,1536]{1,0:T(8,128)(2,1)} %refs_3_.3, ...), custom_call_target="tpu_custom_call" | custom-call | flops 17999998976 | tf_op jit(solution)/shard_map/give_first/pallas_call | solution.py:53
  10.4 4.5 %keep_first.1 = (bf16[1536,1536]{1,0:T(8,128)(2,1)S(1)}, bf16[1536,1536]{1,0:T(8,128)(2,1)S(1)}, bf16[2,64,1536]{2,1,0:T(8,128)(2,1)S(1)}, bf16[2,64,1536]{2,1,0:T(8,128)(2,1)S(1)}) custom-call(s32[1]{0:T(128)} %bitcast.refs_0_, bf16[2,64,1536]{2,1,0:T(8,128)(2,1)S(1)} %stacked.1.refs_1_.refs_4_.refs_0_, bf16[1536,3072]{1,0:T(8,128)(2,1)} %refs_2_.3, ...), custom_call_target="tpu_custom_call" | custom-call | flops 17999998976 | tf_op jit(solution)/shard_map/keep_first/pallas_call | solution.py:53
  15.1 1.6 %collective-permute-start.3 = (bf16[2,64,1536]{2,1,0:T(8,128)(2,1)S(1)}, bf16[2,64,1536]{2,1,0:T(8,128)(2,1)S(1)}, u32[]{:S(2)}, u32[]{:S(2)}) collective-permute-start(bf16[2,64,1536]{2,1,0:T(8,128)(2,1)S(1)} %add_convert_fusion.2.refs_3_.refs_0_), channel_id=1, source_target_pairs={{0,8},{4,12},{8,0},{12,4},{1,9},{5,13},{9,1},{13,5},{2,10},{6,14},... | collective-permute-start | bytes 1179656 | tf_op jit(solution)/shard_map/ppermute | solution.py:335
  16.6 2.3 %give.3.refs_3_ = bf16[2,64,1536]{2,1,0:T(8,128)(2,1)S(1)} custom-call(bf16[2,64,1536]{2,1,0:T(8,128)(2,1)S(1)} %collective-permute-done.refs_0_.refs_1_, bf16[1536,1536]{1,0:T(8,128)(2,1)S(1)} %get-tuple-element.31.refs_1_.refs_3_.refs_10_.refs_11_, bf16[1536,1536]{1,0:T(8,128)(2,1)S(1)} %get-tuple-element.32.refs_2_, ...), custom_call_target="tpu_custom_call" | custom-call | flops 9600000000 | tf_op jit(solution)/shard_map/give/pallas_call | solution.py:53
  19.0 0.3 collective-permute-start.4
  19.3 2.3 %keep.3.refs_1_ = bf16[2,64,1536]{2,1,0:T(8,128)(2,1)S(1)} custom-call(bf16[2,64,1536]{2,1,0:T(8,128)(2,1)S(1)} %collective-permute-done.refs_0_.refs_1_, bf16[1536,1536]{1,0:T(8,128)(2,1)S(1)} %get-tuple-element.29.refs_1_.refs_2_.refs_9_.refs_10_.refs_12_, bf16[1536,1536]{1,0:T(8,128)(2,1)S(1)} %get-tuple-element.30.refs_2_, ...), custom_call_target="tpu_custom_call" | custom-call | flops 9600000000 | tf_op jit(solution)/shard_map/keep/pallas_call | solution.py:53
  21.7 2.9 %collective-permute-start.2 = (bf16[2,64,1536]{2,1,0:T(8,128)(2,1)S(1)}, bf16[2,64,1536]{2,1,0:T(8,128)(2,1)S(1)}, u32[]{:S(2)}, u32[]{:S(2)}) collective-permute-start(bf16[2,64,1536]{2,1,0:T(8,128)(2,1)S(1)} %copied.1.refs_5_), channel_id=1, source_target_pairs={{0,2},{2,3},{3,1},{1,0},{4,6},{6,7},{7,5},{5,4},{8,10},{10,11},{11... | collective-permute-start | bytes 1179656 | tf_op jit(solution)/shard_map/ppermute | solution.py:329
  24.7 0.6 collective-permute-start.5
  25.3 2.4 %collective-permute-done.6.refs_0_.refs_2_ = bf16[2,64,1536]{2,1,0:T(8,128)(2,1)S(1)} collective-permute-done((bf16[2,64,1536]{2,1,0:T(8,128)(2,1)S(1)}, bf16[2,64,1536]{2,1,0:T(8,128)(2,1)S(1)}, u32[]{:S(2)}, u32[]{:S(2)}) %collective-permute-start.6) | collective-permute-done | bytes 393248 | tf_op jit(solution)/shard_map/ppermute | solution.py:329
  27.7 2.3 %give.4.refs_3_ = bf16[2,64,1536]{2,1,0:T(8,128)(2,1)S(1)} custom-call(bf16[2,64,1536]{2,1,0:T(8,128)(2,1)S(1)} %collective-permute-done.6.refs_0_.refs_2_, bf16[1536,1536]{1,0:T(8,128)(2,1)S(1)} %get-tuple-element.31.refs_1_.refs_3_.refs_10_.refs_11_, bf16[1536,1536]{1,0:T(8,128)(2,1)S(1)} %get-tuple-element.32.refs_2_, ...), custom_call_target="tpu_custom_call" | custom-call | flops 9600000000 | tf_op jit(solution)/shard_map/give/pallas_call | solution.py:53
  30.1 2.3 %keep.4.refs_4_ = bf16[2,64,1536]{2,1,0:T(8,128)(2,1)S(1)} custom-call(bf16[2,64,1536]{2,1,0:T(8,128)(2,1)S(1)} %collective-permute-done.6.refs_0_.refs_2_, bf16[1536,1536]{1,0:T(8,128)(2,1)S(1)} %get-tuple-element.29.refs_1_.refs_2_.refs_9_.refs_10_.refs_12_, bf16[1536,1536]{1,0:T(8,128)(2,1)S(1)} %get-tuple-element.30.refs_2_, ...), custom_call_target="tpu_custom_call" | custom-call | flops 9600000000 | tf_op jit(solution)/shard_map/keep/pallas_call | solution.py:53
  32.6 1.6 %collective-permute-start.10 = (bf16[2,64,1536]{2,1,0:T(8,128)(2,1)S(1)}, bf16[2,64,1536]{2,1,0:T(8,128)(2,1)S(1)}, u32[]{:S(2)}, u32[]{:S(2)}) collective-permute-start(bf16[2,64,1536]{2,1,0:T(8,128)(2,1)S(1)} %add_convert_fusion.refs_3_.refs_0_), channel_id=1, source_target_pairs={{0,8},{4,12},{8,0},{12,4},{1,9},{5,13},{9,1},{13,5},{2,10},{6,14},... | collective-permute-start | bytes 1179656 | tf_op jit(solution)/shard_map/ppermute | solution.py:335
  34.2 1.6 %collective-permute-done.2.refs_0_.refs_3_ = bf16[2,64,1536]{2,1,0:T(8,128)(2,1)S(1)} collective-permute-done((bf16[2,64,1536]{2,1,0:T(8,128)(2,1)S(1)}, bf16[2,64,1536]{2,1,0:T(8,128)(2,1)S(1)}, u32[]{:S(2)}, u32[]{:S(2)}) %collective-permute-start.2) | collective-permute-done | bytes 393248 | tf_op jit(solution)/shard_map/ppermute | solution.py:329
  35.8 2.3 %give.5.refs_4_ = bf16[2,64,1536]{2,1,0:T(8,128)(2,1)S(1)} custom-call(bf16[2,64,1536]{2,1,0:T(8,128)(2,1)S(1)} %collective-permute-done.2.refs_0_.refs_3_, bf16[1536,1536]{1,0:T(8,128)(2,1)S(1)} %get-tuple-element.31.refs_1_.refs_3_.refs_10_.refs_11_, bf16[1536,1536]{1,0:T(8,128)(2,1)S(1)} %get-tuple-element.32.refs_2_, ...), custom_call_target="tpu_custom_call" | custom-call | flops 9600000000 | tf_op jit(solution)/shard_map/give/pallas_call | solution.py:53
  38.3 0.5 gelu.4.refs_3_.refs_0_
  38.8 0.5 collective-permute-start.11
  39.3 2.3 %keep.5.refs_6_ = bf16[2,64,1536]{2,1,0:T(8,128)(2,1)S(1)} custom-call(bf16[2,64,1536]{2,1,0:T(8,128)(2,1)S(1)} %collective-permute-done.2.refs_0_.refs_3_, bf16[1536,1536]{1,0:T(8,128)(2,1)S(1)} %get-tuple-element.29.refs_1_.refs_2_.refs_9_.refs_10_.refs_12_, bf16[1536,1536]{1,0:T(8,128)(2,1)S(1)} %get-tuple-element.30.refs_2_, ...), custom_call_target="tpu_custom_call" | custom-call | flops 9600000000 | tf_op jit(solution)/shard_map/keep/pallas_call | solution.py:53
  41.8 1.6 %collective-permute-start.12 = (bf16[2,64,768]{2,1,0:T(8,128)(2,1)S(1)}, bf16[2,64,768]{2,1,0:T(8,128)(2,1)S(1)}, u32[]{:S(2)}, u32[]{:S(2)}) collective-permute-start(bf16[2,64,768]{2,1,0:T(8,128)(2,1)S(1)} %get-tuple-element.53.refs_4_.refs_0_), channel_id=1, source_target_pairs={{0,8},{4,12},{8,0},{12,4},{1,9},{5,13},{9,1},{13,5},{2,10},{6,14},... | collective-permute-start | bytes 589832 | tf_op jit(solution)/shard_map/ppermute | solution.py:335
  43.6 3.1 %input_product.2 = (bf16[64,1536]{1,0:T(8,128)(2,1)S(1)}, bf16[64,1536]{1,0:T(8,128)(2,1)S(1)}) custom-call(bf16[2,128,1536]{2,1,0:T(8,128)(2,1)S(1)} %gelu.4.refs_3_.refs_0_, bf16[2,128,1536]{2,1,0:T(8,128)(2,1)S(1)} %collective-permute-done.11.refs_1_.refs_3_.refs_7_, bf16[1536,1536]{1,0:T(8,128)(2,1)S(1)} %get-tuple-element.29.refs_1_.refs_2_.refs_9_.refs_10_.refs_12_, ...), custom_call_target="tpu_custom_call" | custom-call | flops 400000000 | tf_op jit(solution)/shard_map/input_product/pallas_call | solution.py:53
  47.1 0.6 collective-permute-start.9
  47.7 0.7 collective-permute-start.15
  48.4 0.4 collective-permute-done.12.refs_1_
  49.1 4.9 %weight_grads.3 = (f32[1536,3072]{1,0:T(8,128)}, f32[3072,1536]{1,0:T(8,128)}, bf16[64,1536]{1,0:T(8,128)(2,1)S(1)}, f32[8,128]{1,0:T(8,128)S(1)}) custom-call(s32[1]{0:T(128)} %bitcast.refs_0_, bf16[1536,256]{1,0:T(8,128)(2,1)S(1)} %get-tuple-element.35.refs_1_, bf16[256,1536]{1,0:T(8,128)(2,1)S(1)} %get-tuple-element.36.refs_4_.refs_2_, ...), custom_call_target="tpu_custom_call" | custom-call | flops 16000000000 | tf_op jit(solution)/shard_map/weight_grads/pallas_call | solution.py:53
  54.0 0.4 collective-permute-done.9.refs_1_
  54.6 2.1 %collective-permute-start.18 = (bf16[64,1536]{1,0:T(8,128)(2,1)S(1)}, bf16[64,1536]{1,0:T(8,128)(2,1)S(1)}, u32[]{:S(2)}, u32[]{:S(2)}) collective-permute-start(bf16[64,1536]{1,0:T(8,128)(2,1)S(1)} %get-tuple-element.47), channel_id=1, source_target_pairs={{0,2},{2,3},{3,1},{1,0},{4,6},{6,7},{7,5},{5,4},{8,10},{10,11},{11... | collective-permute-start | bytes 589832 | tf_op jit(solution)/shard_map/ppermute | solution.py:329
  56.7 4.4 %weight_grads.4 = (f32[1536,3072]{1,0:T(8,128)}, f32[3072,1536]{1,0:T(8,128)}, f32[64,1536]{1,0:T(8,128)S(1)}, f32[8,128]{1,0:T(8,128)S(1)}) custom-call(s32[1]{0:T(128)} %bitcast.refs_0_, bf16[1536,256]{1,0:T(8,128)(2,1)S(1)} %get-tuple-element.35.refs_1_, ...), custom_call_target="tpu_custom_call", output_to_operand_aliasing={{0}: (13, {}), {1}: (14, {})} | custom-call | flops 16000000000 | tf_op jit(solution)/shard_map/weight_grads/pallas_call | solution.py:53
  61.1 0.9 %input_product.3 = (f32[64,1536]{1,0:T(8,128)S(1)}, bf16[64,1536]{1,0:T(8,128)(2,1)S(1)}) custom-call(bf16[2,64,768]{2,1,0:T(8,128)(2,1)S(1)} %collective-permute-done.14.refs_0_.refs_10_, bf16[1536,1536]{1,0:T(8,128)(2,1)S(1)} %get-tuple-element.31.refs_1_.refs_3_.refs_10_.refs_11_, bf16[64,1536]{1,0:T(8,128)(2,1)S(1)} %get-tuple-element.41.refs_2_, ...), custom_call_target="tpu_custom_call" | custom-call | flops 12000000000 | tf_op jit(solution)/shard_map/input_product/pallas_call | solution.py:53
  62.0 8.4 %collective-permute-start.19 = (bf16[64,1536]{1,0:T(8,128)(2,1)S(1)}, bf16[64,1536]{1,0:T(8,128)(2,1)S(1)}, u32[]{:S(2)}, u32[]{:S(2)}) collective-permute-start(bf16[64,1536]{1,0:T(8,128)(2,1)S(1)} %get-tuple-element.48.refs_13_), channel_id=1, source_target_pairs={{0,3},{2,1},{3,0},{1,2},{4,7},{6,5},{7,4},{5,6},{8,11},{10,9},{11,... | collective-permute-start | bytes 589832 | tf_op jit(solution)/shard_map/ppermute | solution.py:329
  70.4 7.6 %weight_grads.5 = (f32[1536,3072]{1,0:T(8,128)}, f32[3072,1536]{1,0:T(8,128)}, f32[8,128]{1,0:T(8,128)}) custom-call(s32[1]{0:T(128)} %bitcast.refs_0_, bf16[1536,256]{1,0:T(8,128)(2,1)S(1)} %get-tuple-element.35.refs_1_, bf16[256,1536]{1,0:T(8,128)(2,1)S(1)} %get-tuple-element.36.refs_4_.refs_2_, ...), custom_call_target="tpu_custom_call", output_to_operand_aliasing={{0}: (11, {}), {1}: (12, {})} | custom-call | flops 32000000000 | tf_op jit(solution)/shard_map/weight_grads/pallas_call | solution.py:53
  78.0 0.7 add_convert_fusion.3
  (33 shorter events, 1.9 us)
Async XLA Ops:
  1.7 15.0 %collective-permute-start = (bf16[2,64,1536]{2,1,0:T(8,128)(2,1)S(1)}, bf16[2,64,1536]{2,1,0:T(8,128)(2,1)S(1)}, u32[]{:S(2)}, u32[]{:S(2)}) collective-permute-start(bf16[2,64,1536]{2,1,0:T(8,128)(2,1)S(1)} %stacked.1.refs_1_.refs_4_.refs_0_), channel_id=1, source_target_pairs={{0,2},{2,3},{3,1},{1,0},{4,6},{6,7},{7,5},{5,4},{8,10},{10,11},{11... | collective-permute-start | bytes 1179656 | tf_op jit(solution)/shard_map/ppermute | solution.py:329
  10.3 4.7 %collective-permute-start.1 = (bf16[2,64,1536]{2,1,0:T(8,128)(2,1)S(1)}, bf16[2,64,1536]{2,1,0:T(8,128)(2,1)S(1)}, u32[]{:S(2)}, u32[]{:S(2)}) collective-permute-start(bf16[2,64,1536]{2,1,0:T(8,128)(2,1)S(1)} %get-tuple-element.28.refs_4_), channel_id=1, source_target_pairs={{0,4},{4,0},{8,12},{12,8},{1,5},{5,1},{9,13},{13,9},{2,6},{6,2},{1... | collective-permute-start | bytes 1179656 | tf_op jit(solution)/shard_map/ppermute | solution.py:324
  14.9 12.8 %collective-permute-start.6 = (bf16[2,64,1536]{2,1,0:T(8,128)(2,1)S(1)}, bf16[2,64,1536]{2,1,0:T(8,128)(2,1)S(1)}, u32[]{:S(2)}, u32[]{:S(2)}) collective-permute-start(bf16[2,64,1536]{2,1,0:T(8,128)(2,1)S(1)} %get-tuple-element.34), channel_id=1, source_target_pairs={{0,1},{2,0},{3,2},{1,3},{4,5},{6,4},{7,6},{5,7},{8,9},{10,8},{11,1... | collective-permute-start | bytes 1179656 | tf_op jit(solution)/shard_map/ppermute | solution.py:329
  15.1 12.6 %collective-permute-start.3 = (bf16[2,64,1536]{2,1,0:T(8,128)(2,1)S(1)}, bf16[2,64,1536]{2,1,0:T(8,128)(2,1)S(1)}, u32[]{:S(2)}, u32[]{:S(2)}) collective-permute-start(bf16[2,64,1536]{2,1,0:T(8,128)(2,1)S(1)} %add_convert_fusion.2.refs_3_.refs_0_), channel_id=1, source_target_pairs={{0,8},{4,12},{8,0},{12,4},{1,9},{5,13},{9,1},{13,5},{2,10},{6,14},... | collective-permute-start | bytes 1179656 | tf_op jit(solution)/shard_map/ppermute | solution.py:335
  19.0 5.6 %collective-permute-start.4 = (bf16[2,64,1536]{2,1,0:T(8,128)(2,1)S(1)}, bf16[2,64,1536]{2,1,0:T(8,128)(2,1)S(1)}, u32[]{:S(2)}, u32[]{:S(2)}) collective-permute-start(bf16[2,64,1536]{2,1,0:T(8,128)(2,1)S(1)} %give.3.refs_3_), channel_id=1, source_target_pairs={{0,4},{4,0},{8,12},{12,8},{1,5},{5,1},{9,13},{13,9},{2,6},{6,2},{1... | collective-permute-start | bytes 1179656 | tf_op jit(solution)/shard_map/ppermute | solution.py:324
  21.7 14.1 %collective-permute-start.2 = (bf16[2,64,1536]{2,1,0:T(8,128)(2,1)S(1)}, bf16[2,64,1536]{2,1,0:T(8,128)(2,1)S(1)}, u32[]{:S(2)}, u32[]{:S(2)}) collective-permute-start(bf16[2,64,1536]{2,1,0:T(8,128)(2,1)S(1)} %copied.1.refs_5_), channel_id=1, source_target_pairs={{0,2},{2,3},{3,1},{1,0},{4,6},{6,7},{7,5},{5,4},{8,10},{10,11},{11... | collective-permute-start | bytes 1179656 | tf_op jit(solution)/shard_map/ppermute | solution.py:329
  24.7 13.6 %collective-permute-start.5 = (bf16[2,64,1536]{2,1,0:T(8,128)(2,1)S(1)}, bf16[2,64,1536]{2,1,0:T(8,128)(2,1)S(1)}, u32[]{:S(2)}, u32[]{:S(2)}) collective-permute-start(bf16[2,64,1536]{2,1,0:T(8,128)(2,1)S(1)} %add_convert_fusion.1.refs_3_.refs_2_), channel_id=1, source_target_pairs={{0,8},{4,12},{8,0},{12,4},{1,9},{5,13},{9,1},{13,5},{2,10},{6,14},... | collective-permute-start | bytes 1179656 | tf_op jit(solution)/shard_map/ppermute | solution.py:335
  30.1 2.4 %collective-permute-start.7 = (bf16[2,64,1536]{2,1,0:T(8,128)(2,1)S(1)}, bf16[2,64,1536]{2,1,0:T(8,128)(2,1)S(1)}, u32[]{:S(2)}, u32[]{:S(2)}) collective-permute-start(bf16[2,64,1536]{2,1,0:T(8,128)(2,1)S(1)} %give.4.refs_3_), channel_id=1, source_target_pairs={{0,4},{4,0},{8,12},{12,8},{1,5},{5,1},{9,13},{13,9},{2,6},{6,2},{1... | collective-permute-start | bytes 1179656 | tf_op jit(solution)/shard_map/ppermute | solution.py:324
  32.6 14.1 %collective-permute-start.10 = (bf16[2,64,1536]{2,1,0:T(8,128)(2,1)S(1)}, bf16[2,64,1536]{2,1,0:T(8,128)(2,1)S(1)}, u32[]{:S(2)}, u32[]{:S(2)}) collective-permute-start(bf16[2,64,1536]{2,1,0:T(8,128)(2,1)S(1)} %add_convert_fusion.refs_3_.refs_0_), channel_id=1, source_target_pairs={{0,8},{4,12},{8,0},{12,4},{1,9},{5,13},{9,1},{13,5},{2,10},{6,14},... | collective-permute-start | bytes 1179656 | tf_op jit(solution)/shard_map/ppermute | solution.py:335
  38.1 3.5 %collective-permute-start.8 = (bf16[2,64,1536]{2,1,0:T(8,128)(2,1)S(1)}, bf16[2,64,1536]{2,1,0:T(8,128)(2,1)S(1)}, u32[]{:S(2)}, u32[]{:S(2)}) collective-permute-start(bf16[2,64,1536]{2,1,0:T(8,128)(2,1)S(1)} %give.5.refs_4_), channel_id=1, source_target_pairs={{0,4},{4,0},{8,12},{12,8},{1,5},{5,1},{9,13},{13,9},{2,6},{6,2},{1... | collective-permute-start | bytes 1179656 | tf_op jit(solution)/shard_map/ppermute | solution.py:324
  38.8 4.8 %collective-permute-start.11 = (bf16[2,128,1536]{2,1,0:T(8,128)(2,1)S(1)}, bf16[2,128,1536]{2,1,0:T(8,128)(2,1)S(1)}, u32[]{:S(2)}, u32[]{:S(2)}) collective-permute-start(bf16[2,128,1536]{2,1,0:T(8,128)(2,1)S(1)} %gelu.4.refs_3_.refs_0_), channel_id=1, source_target_pairs={{0,4},{4,0},{8,12},{12,8},{1,5},{5,1},{9,13},{13,9},{2,6},{6,2},{1... | collective-permute-start | bytes 2359304 | tf_op jit(solution)/shard_map/ppermute | solution.py:324
  41.8 6.9 %collective-permute-start.12 = (bf16[2,64,768]{2,1,0:T(8,128)(2,1)S(1)}, bf16[2,64,768]{2,1,0:T(8,128)(2,1)S(1)}, u32[]{:S(2)}, u32[]{:S(2)}) collective-permute-start(bf16[2,64,768]{2,1,0:T(8,128)(2,1)S(1)} %get-tuple-element.53.refs_4_.refs_0_), channel_id=1, source_target_pairs={{0,8},{4,12},{8,0},{12,4},{1,9},{5,13},{9,1},{13,5},{2,10},{6,14},... | collective-permute-start | bytes 589832 | tf_op jit(solution)/shard_map/ppermute | solution.py:335
  47.0 2.1 %collective-permute-start.13 = (bf16[64,1536]{1,0:T(8,128)(2,1)S(1)}, bf16[64,1536]{1,0:T(8,128)(2,1)S(1)}, u32[]{:S(2)}, u32[]{:S(2)}) collective-permute-start(bf16[64,1536]{1,0:T(8,128)(2,1)S(1)} %get-tuple-element.38.refs_4_.refs_7_), channel_id=1, source_target_pairs={{0,4},{4,0},{8,12},{12,8},{1,5},{5,1},{9,13},{13,9},{2,6},{6,2},{1... | collective-permute-start | bytes 589832 | tf_op jit(solution)/shard_map/ppermute | solution.py:324
  47.1 7.3 %collective-permute-start.9 = (bf16[2,64,768]{2,1,0:T(8,128)(2,1)S(1)}, bf16[2,64,768]{2,1,0:T(8,128)(2,1)S(1)}, u32[]{:S(2)}, u32[]{:S(2)}) collective-permute-start(bf16[2,64,768]{2,1,0:T(8,128)(2,1)S(1)} %get-tuple-element.54.refs_5_.refs_0_), channel_id=1, source_target_pairs={{0,8},{4,12},{8,0},{12,4},{1,9},{5,13},{9,1},{13,5},{2,10},{6,14},... | collective-permute-start | bytes 589832 | tf_op jit(solution)/shard_map/ppermute | solution.py:335
  47.7 13.5 %collective-permute-start.15 = (bf16[64,1536]{1,0:T(8,128)(2,1)S(1)}, bf16[64,1536]{1,0:T(8,128)(2,1)S(1)}, u32[]{:S(2)}, u32[]{:S(2)}) collective-permute-start(bf16[64,1536]{1,0:T(8,128)(2,1)S(1)} %get-tuple-element.37.refs_2_), channel_id=1, source_target_pairs={{0,1},{2,0},{3,2},{1,3},{4,5},{6,4},{7,6},{5,7},{8,9},{10,8},{11,1... | collective-permute-start | bytes 589832 | tf_op jit(solution)/shard_map/ppermute | solution.py:329
  48.3 8.3 %collective-permute-start.16 = (bf16[64,1536]{1,0:T(8,128)(2,1)S(1)}, bf16[64,1536]{1,0:T(8,128)(2,1)S(1)}, u32[]{:S(2)}, u32[]{:S(2)}) collective-permute-start(bf16[64,1536]{1,0:T(8,128)(2,1)S(1)} %get-tuple-element.39.refs_2_.refs_5_), channel_id=1, source_target_pairs={{0,4},{4,0},{8,12},{12,8},{1,5},{5,1},{9,13},{13,9},{2,6},{6,2},{1... | collective-permute-start | bytes 589832 | tf_op jit(solution)/shard_map/ppermute | solution.py:324
  48.8 7.9 %collective-permute-start.17 = (bf16[2,64,768]{2,1,0:T(8,128)(2,1)S(1)}, bf16[2,64,768]{2,1,0:T(8,128)(2,1)S(1)}, u32[]{:S(2)}, u32[]{:S(2)}) collective-permute-start(bf16[2,64,768]{2,1,0:T(8,128)(2,1)S(1)} %gelu.6.refs_6_.refs_11_.refs_7_), channel_id=1, source_target_pairs={{0,4},{4,0},{8,12},{12,8},{1,5},{5,1},{9,13},{13,9},{2,6},{6,2},{1... | collective-permute-start | bytes 589832 | tf_op jit(solution)/shard_map/ppermute | solution.py:324
  54.5 6.6 %collective-permute-start.14 = (bf16[2,64,768]{2,1,0:T(8,128)(2,1)S(1)}, bf16[2,64,768]{2,1,0:T(8,128)(2,1)S(1)}, u32[]{:S(2)}, u32[]{:S(2)}) collective-permute-start(bf16[2,64,768]{2,1,0:T(8,128)(2,1)S(1)} %gelu.7.refs_9_.refs_15_.refs_6_), channel_id=1, source_target_pairs={{0,4},{4,0},{8,12},{12,8},{1,5},{5,1},{9,13},{13,9},{2,6},{6,2},{1... | collective-permute-start | bytes 589832 | tf_op jit(solution)/shard_map/ppermute | solution.py:324
  54.6 23.3 %collective-permute-start.18 = (bf16[64,1536]{1,0:T(8,128)(2,1)S(1)}, bf16[64,1536]{1,0:T(8,128)(2,1)S(1)}, u32[]{:S(2)}, u32[]{:S(2)}) collective-permute-start(bf16[64,1536]{1,0:T(8,128)(2,1)S(1)} %get-tuple-element.47), channel_id=1, source_target_pairs={{0,2},{2,3},{3,1},{1,0},{4,6},{6,7},{7,5},{5,4},{8,10},{10,11},{11... | collective-permute-start | bytes 589832 | tf_op jit(solution)/shard_map/ppermute | solution.py:329
  62.0 15.9 %collective-permute-start.19 = (bf16[64,1536]{1,0:T(8,128)(2,1)S(1)}, bf16[64,1536]{1,0:T(8,128)(2,1)S(1)}, u32[]{:S(2)}, u32[]{:S(2)}) collective-permute-start(bf16[64,1536]{1,0:T(8,128)(2,1)S(1)} %get-tuple-element.48.refs_13_), channel_id=1, source_target_pairs={{0,3},{2,1},{3,0},{1,2},{4,7},{6,5},{7,4},{5,6},{8,11},{10,9},{11,... | collective-permute-start | bytes 589832 | tf_op jit(solution)/shard_map/ppermute | solution.py:329

commit v13 on v12

--- a/solution.py
+++ b/solution.py
@@ -86,11 +86,11 @@
     )[0]
 
 
-def copied(ordered, chunk):
+def copied(ordered, chunk, after):
     def body(chunk_ref, out_ref):
         out_ref[...] = chunk_ref[...]
 
-    return ordered(body, (chunk,), [jax.ShapeDtypeStruct(chunk.shape, BF16)], "copied", 0.1)[0]
+    return ordered(body, (chunk,), [jax.ShapeDtypeStruct(chunk.shape, BF16)], "copied", 0.1, after=after)[0]
 
 
 def first_product(ordered, core, other, chunk, up_weight, down_weight, name):
@@ -361,10 +361,10 @@
         if offset == offsets[-1]:
             early = acts_of(sums[:-1])
         keep = product(ordered, chunk, up_mine, down_mine, "keep")
-        if offset == 1:
-            forward[2] = copied(ordered, chunk)
         if offset != offsets[-1]:
             sums.append(across_chips(keep, got))
+            if offset == 1:
+                forward[2] = copied(ordered, chunk, [sums[1][0]])
         else:
             parts = [slice(i * width, (i + 1) * width) for i in range(slices)]
             late = [across_chips(keep[:, :, part], got[:, :, part]) for part in parts]

time: 78.9 us -> 71.9 us (0.911)
  starting transfers between devices: 25.5 us -> 18.6 us
    ppermute x6, starting transfers between devices: 18.2 us -> 11.3 us  [shift(): lax.ppermute(x, 'narrow', [(ring[i], ring[(i + places) % narrow]) for i i...]
  transfers between devices with their start and end apart: 20 -> 20, of which waited for: 4 -> 4; matrix products, arithmetic and copies ran while one was open for 0% -> 1% of each run, Pallas kernels for 57% -> 63%
where the time goes in v13:
time: 71.9 us; the launch traced here: 71.8 us
  Pallas kernels  46.3 us (64%)
  starting transfers between devices  18.6 us (26%)
  waiting for transfers between devices  4.84 us (7%)
  other arithmetic  1.11 us (2%)
  between operations  0.93 us (1%)
    pallas_call x20, Pallas kernels, __call__(): pl.pallas_call(kernel, out_shape=outs, in_specs=specs, out_specs=[pl.Bloc...  46.3 us
    ppermute x6, starting transfers between devices, shift(): lax.ppermute(x, 'narrow', [(ring[i], ring[(i + places) % narrow]) for i i...  11.3 us
    ppermute x5, starting transfers between devices, across_chips(): lax.ppermute(partial, 'wide', [(i, i ^ 2 * hop) for i in range(wide)])  5.88 us
    ppermute x6, waiting for transfers between devices, shift(): lax.ppermute(x, 'narrow', [(ring[i], ring[(i + places) % narrow]) for i i...  4.04 us
    ppermute x9, starting transfers between devices, swap_cores(): return lax.ppermute(x, 'wide', [(i, i ^ 1) for i in range(wide)])  1.46 us
  transfers between devices with their start and end apart: 20, of which 4 were waited for; matrix products, arithmetic and copies ran while one was open for 1% of the time, Pallas kernels for 63%

profile of v13, /device:TPU:0, one launch (start us, length us, event | category | flops | bytes accessed | tf_op | source)
XLA Modules:
  0.0 71.8 jit_solution(10958254455611447822)
XLA Ops:
  0.6 1.0 %stacked.1.refs_1_.refs_4_.refs_0_ = bf16[2,64,1536]{2,1,0:T(8,128)(2,1)S(1)} custom-call(bf16[64,1536]{1,0:T(8,128)(2,1)} %refs_0_.1, bf16[64,1536]{1,0:T(8,128)(2,1)} %refs_1_.1), custom_call_target="tpu_custom_call" | custom-call | flops 2000000000 | tf_op jit(solution)/shard_map/stacked/pallas_call | solution.py:53
  1.7 4.1 %collective-permute-start = (bf16[2,64,1536]{2,1,0:T(8,128)(2,1)S(1)}, bf16[2,64,1536]{2,1,0:T(8,128)(2,1)S(1)}, u32[]{:S(2)}, u32[]{:S(2)}) collective-permute-start(bf16[2,64,1536]{2,1,0:T(8,128)(2,1)S(1)} %stacked.1.refs_1_.refs_4_.refs_0_), channel_id=1, source_target_pairs={{0,2},{2,3},{3,1},{1,0},{4,6},{6,7},{7,5},{5,4},{8,10},{10,11},{11... | collective-permute-start | bytes 1179656 | tf_op jit(solution)/shard_map/ppermute | solution.py:329
  5.8 4.5 %give_first.1 = (bf16[1536,1536]{1,0:T(8,128)(2,1)S(1)}, bf16[1536,1536]{1,0:T(8,128)(2,1)S(1)}, bf16[2,64,1536]{2,1,0:T(8,128)(2,1)S(1)}) custom-call(s32[1]{0:T(128)} %bitcast.refs_0_, bf16[2,64,1536]{2,1,0:T(8,128)(2,1)S(1)} %stacked.1.refs_1_.refs_4_.refs_0_, bf16[1536,3072]{1,0:T(8,128)(2,1)} %refs_2_.3, bf16[3072,1536]{1,0:T(8,128)(2,1)} %refs_3_.3, ...), custom_call_target="tpu_custom_call" | custom-call | flops 17999998976 | tf_op jit(solution)/shard_map/give_first/pallas_call | solution.py:53
  10.4 4.5 %keep_first.1 = (bf16[1536,1536]{1,0:T(8,128)(2,1)S(1)}, bf16[1536,1536]{1,0:T(8,128)(2,1)S(1)}, bf16[2,64,1536]{2,1,0:T(8,128)(2,1)S(1)}, bf16[2,64,1536]{2,1,0:T(8,128)(2,1)S(1)}) custom-call(s32[1]{0:T(128)} %bitcast.refs_0_, bf16[2,64,1536]{2,1,0:T(8,128)(2,1)S(1)} %stacked.1.refs_1_.refs_4_.refs_0_, bf16[1536,3072]{1,0:T(8,128)(2,1)} %refs_2_.3, ...), custom_call_target="tpu_custom_call" | custom-call | flops 17999998976 | tf_op jit(solution)/shard_map/keep_first/pallas_call | solution.py:53
  15.1 1.6 %collective-permute-start.4 = (bf16[2,64,1536]{2,1,0:T(8,128)(2,1)S(1)}, bf16[2,64,1536]{2,1,0:T(8,128)(2,1)S(1)}, u32[]{:S(2)}, u32[]{:S(2)}) collective-permute-start(bf16[2,64,1536]{2,1,0:T(8,128)(2,1)S(1)} %add_convert_fusion.2.refs_3_.refs_0_), channel_id=1, source_target_pairs={{0,8},{4,12},{8,0},{12,4},{1,9},{5,13},{9,1},{13,5},{2,10},{6,14},... | collective-permute-start | bytes 1179656 | tf_op jit(solution)/shard_map/ppermute | solution.py:335
  16.6 2.3 %give.3.refs_3_ = bf16[2,64,1536]{2,1,0:T(8,128)(2,1)S(1)} custom-call(bf16[2,64,1536]{2,1,0:T(8,128)(2,1)S(1)} %collective-permute-done.refs_0_.refs_1_, bf16[1536,1536]{1,0:T(8,128)(2,1)S(1)} %get-tuple-element.31.refs_1_.refs_3_.refs_10_.refs_11_, bf16[1536,1536]{1,0:T(8,128)(2,1)S(1)} %get-tuple-element.32.refs_2_, ...), custom_call_target="tpu_custom_call" | custom-call | flops 9600000000 | tf_op jit(solution)/shard_map/give/pallas_call | solution.py:53
  19.0 0.3 collective-permute-start.2
  19.3 2.3 %keep.3.refs_2_ = bf16[2,64,1536]{2,1,0:T(8,128)(2,1)S(1)} custom-call(bf16[2,64,1536]{2,1,0:T(8,128)(2,1)S(1)} %collective-permute-done.refs_0_.refs_1_, bf16[1536,1536]{1,0:T(8,128)(2,1)S(1)} %get-tuple-element.29.refs_1_.refs_2_.refs_9_.refs_10_.refs_12_, bf16[1536,1536]{1,0:T(8,128)(2,1)S(1)} %get-tuple-element.30.refs_2_, ...), custom_call_target="tpu_custom_call" | custom-call | flops 9600000000 | tf_op jit(solution)/shard_map/keep/pallas_call | solution.py:53
  21.7 0.6 collective-permute-start.5
  22.4 2.9 %collective-permute-start.3 = (bf16[2,64,1536]{2,1,0:T(8,128)(2,1)S(1)}, bf16[2,64,1536]{2,1,0:T(8,128)(2,1)S(1)}, u32[]{:S(2)}, u32[]{:S(2)}) collective-permute-start(bf16[2,64,1536]{2,1,0:T(8,128)(2,1)S(1)} %copied.1.refs_5_), channel_id=1, source_target_pairs={{0,2},{2,3},{3,1},{1,0},{4,6},{6,7},{7,5},{5,4},{8,10},{10,11},{11... | collective-permute-start | bytes 1179656 | tf_op jit(solution)/shard_map/ppermute | solution.py:329
  25.3 2.2 %collective-permute-done.6.refs_0_.refs_2_ = bf16[2,64,1536]{2,1,0:T(8,128)(2,1)S(1)} collective-permute-done((bf16[2,64,1536]{2,1,0:T(8,128)(2,1)S(1)}, bf16[2,64,1536]{2,1,0:T(8,128)(2,1)S(1)}, u32[]{:S(2)}, u32[]{:S(2)}) %collective-permute-start.6) | collective-permute-done | bytes 393248 | tf_op jit(solution)/shard_map/ppermute | solution.py:329
  27.5 2.3 %give.4.refs_3_ = bf16[2,64,1536]{2,1,0:T(8,128)(2,1)S(1)} custom-call(bf16[2,64,1536]{2,1,0:T(8,128)(2,1)S(1)} %collective-permute-done.6.refs_0_.refs_2_, bf16[1536,1536]{1,0:T(8,128)(2,1)S(1)} %get-tuple-element.31.refs_1_.refs_3_.refs_10_.refs_11_, bf16[1536,1536]{1,0:T(8,128)(2,1)S(1)} %get-tuple-element.32.refs_2_, ...), custom_call_target="tpu_custom_call" | custom-call | flops 9600000000 | tf_op jit(solution)/shard_map/give/pallas_call | solution.py:53
  29.9 2.3 %keep.4.refs_4_ = bf16[2,64,1536]{2,1,0:T(8,128)(2,1)S(1)} custom-call(bf16[2,64,1536]{2,1,0:T(8,128)(2,1)S(1)} %collective-permute-done.6.refs_0_.refs_2_, bf16[1536,1536]{1,0:T(8,128)(2,1)S(1)} %get-tuple-element.29.refs_1_.refs_2_.refs_9_.refs_10_.refs_12_, bf16[1536,1536]{1,0:T(8,128)(2,1)S(1)} %get-tuple-element.30.refs_2_, ...), custom_call_target="tpu_custom_call" | custom-call | flops 9600000000 | tf_op jit(solution)/shard_map/keep/pallas_call | solution.py:53
  32.4 1.6 %collective-permute-start.10 = (bf16[2,64,1536]{2,1,0:T(8,128)(2,1)S(1)}, bf16[2,64,1536]{2,1,0:T(8,128)(2,1)S(1)}, u32[]{:S(2)}, u32[]{:S(2)}) collective-permute-start(bf16[2,64,1536]{2,1,0:T(8,128)(2,1)S(1)} %add_convert_fusion.refs_3_.refs_0_), channel_id=1, source_target_pairs={{0,8},{4,12},{8,0},{12,4},{1,9},{5,13},{9,1},{13,5},{2,10},{6,14},... | collective-permute-start | bytes 1179656 | tf_op jit(solution)/shard_map/ppermute | solution.py:335
  33.9 1.9 %collective-permute-done.3.refs_0_.refs_3_ = bf16[2,64,1536]{2,1,0:T(8,128)(2,1)S(1)} collective-permute-done((bf16[2,64,1536]{2,1,0:T(8,128)(2,1)S(1)}, bf16[2,64,1536]{2,1,0:T(8,128)(2,1)S(1)}, u32[]{:S(2)}, u32[]{:S(2)}) %collective-permute-start.3) | collective-permute-done | bytes 393248 | tf_op jit(solution)/shard_map/ppermute | solution.py:329
  35.8 2.3 %give.5.refs_4_ = bf16[2,64,1536]{2,1,0:T(8,128)(2,1)S(1)} custom-call(bf16[2,64,1536]{2,1,0:T(8,128)(2,1)S(1)} %collective-permute-done.3.refs_0_.refs_3_, bf16[1536,1536]{1,0:T(8,128)(2,1)S(1)} %get-tuple-element.31.refs_1_.refs_3_.refs_10_.refs_11_, bf16[1536,1536]{1,0:T(8,128)(2,1)S(1)} %get-tuple-element.32.refs_2_, ...), custom_call_target="tpu_custom_call" | custom-call | flops 9600000000 | tf_op jit(solution)/shard_map/give/pallas_call | solution.py:53
  38.2 0.5 gelu.4.refs_3_.refs_0_
  38.8 0.5 collective-permute-start.11
  39.3 2.3 %keep.5.refs_6_ = bf16[2,64,1536]{2,1,0:T(8,128)(2,1)S(1)} custom-call(bf16[2,64,1536]{2,1,0:T(8,128)(2,1)S(1)} %collective-permute-done.3.refs_0_.refs_3_, bf16[1536,1536]{1,0:T(8,128)(2,1)S(1)} %get-tuple-element.29.refs_1_.refs_2_.refs_9_.refs_10_.refs_12_, bf16[1536,1536]{1,0:T(8,128)(2,1)S(1)} %get-tuple-element.30.refs_2_, ...), custom_call_target="tpu_custom_call" | custom-call | flops 9600000000 | tf_op jit(solution)/shard_map/keep/pallas_call | solution.py:53
  41.8 1.6 %collective-permute-start.12 = (bf16[2,64,768]{2,1,0:T(8,128)(2,1)S(1)}, bf16[2,64,768]{2,1,0:T(8,128)(2,1)S(1)}, u32[]{:S(2)}, u32[]{:S(2)}) collective-permute-start(bf16[2,64,768]{2,1,0:T(8,128)(2,1)S(1)} %get-tuple-element.53.refs_4_.refs_0_), channel_id=1, source_target_pairs={{0,8},{4,12},{8,0},{12,4},{1,9},{5,13},{9,1},{13,5},{2,10},{6,14},... | collective-permute-start | bytes 589832 | tf_op jit(solution)/shard_map/ppermute | solution.py:335
  43.6 3.1 %input_product.2 = (bf16[64,1536]{1,0:T(8,128)(2,1)S(1)}, bf16[64,1536]{1,0:T(8,128)(2,1)S(1)}) custom-call(bf16[2,128,1536]{2,1,0:T(8,128)(2,1)S(1)} %gelu.4.refs_3_.refs_0_, bf16[2,128,1536]{2,1,0:T(8,128)(2,1)S(1)} %collective-permute-done.11.refs_1_.refs_3_.refs_7_, bf16[1536,1536]{1,0:T(8,128)(2,1)S(1)} %get-tuple-element.29.refs_1_.refs_2_.refs_9_.refs_10_.refs_12_, ...), custom_call_target="tpu_custom_call" | custom-call | flops 400000000 | tf_op jit(solution)/shard_map/input_product/pallas_call | solution.py:53
  47.1 0.6 collective-permute-start.9
  47.7 0.7 collective-permute-start.15
  48.4 0.3 collective-permute-done.12.refs_1_
  49.1 4.9 %weight_grads.3 = (f32[1536,3072]{1,0:T(8,128)}, f32[3072,1536]{1,0:T(8,128)}, bf16[64,1536]{1,0:T(8,128)(2,1)S(1)}, f32[8,128]{1,0:T(8,128)S(1)}) custom-call(s32[1]{0:T(128)} %bitcast.refs_0_, bf16[1536,256]{1,0:T(8,128)(2,1)S(1)} %get-tuple-element.35.refs_1_, bf16[256,1536]{1,0:T(8,128)(2,1)S(1)} %get-tuple-element.36.refs_4_.refs_2_, ...), custom_call_target="tpu_custom_call" | custom-call | flops 16000000000 | tf_op jit(solution)/shard_map/weight_grads/pallas_call | solution.py:53
  54.0 0.4 collective-permute-done.9.refs_1_
  54.6 2.1 %collective-permute-start.18 = (bf16[64,1536]{1,0:T(8,128)(2,1)S(1)}, bf16[64,1536]{1,0:T(8,128)(2,1)S(1)}, u32[]{:S(2)}, u32[]{:S(2)}) collective-permute-start(bf16[64,1536]{1,0:T(8,128)(2,1)S(1)} %get-tuple-element.47), channel_id=1, source_target_pairs={{0,2},{2,3},{3,1},{1,0},{4,6},{6,7},{7,5},{5,4},{8,10},{10,11},{11... | collective-permute-start | bytes 589832 | tf_op jit(solution)/shard_map/ppermute | solution.py:329
  56.7 4.4 %weight_grads.4 = (f32[1536,3072]{1,0:T(8,128)}, f32[3072,1536]{1,0:T(8,128)}, f32[64,1536]{1,0:T(8,128)S(1)}, f32[8,128]{1,0:T(8,128)S(1)}) custom-call(s32[1]{0:T(128)} %bitcast.refs_0_, bf16[1536,256]{1,0:T(8,128)(2,1)S(1)} %get-tuple-element.35.refs_1_, ...), custom_call_target="tpu_custom_call", output_to_operand_aliasing={{0}: (13, {}), {1}: (14, {})} | custom-call | flops 16000000000 | tf_op jit(solution)/shard_map/weight_grads/pallas_call | solution.py:53
  61.1 0.9 %input_product.3 = (f32[64,1536]{1,0:T(8,128)S(1)}, bf16[64,1536]{1,0:T(8,128)(2,1)S(1)}) custom-call(bf16[2,64,768]{2,1,0:T(8,128)(2,1)S(1)} %collective-permute-done.14.refs_0_.refs_10_, bf16[1536,1536]{1,0:T(8,128)(2,1)S(1)} %get-tuple-element.31.refs_1_.refs_3_.refs_10_.refs_11_, bf16[64,1536]{1,0:T(8,128)(2,1)S(1)} %get-tuple-element.41.refs_2_, ...), custom_call_target="tpu_custom_call" | custom-call | flops 12000000000 | tf_op jit(solution)/shard_map/input_product/pallas_call | solution.py:53
  62.0 1.4 %collective-permute-start.19 = (bf16[64,1536]{1,0:T(8,128)(2,1)S(1)}, bf16[64,1536]{1,0:T(8,128)(2,1)S(1)}, u32[]{:S(2)}, u32[]{:S(2)}) collective-permute-start(bf16[64,1536]{1,0:T(8,128)(2,1)S(1)} %get-tuple-element.48.refs_13_), channel_id=1, source_target_pairs={{0,3},{2,1},{3,0},{1,2},{4,7},{6,5},{7,4},{5,6},{8,11},{10,9},{11,... | collective-permute-start | bytes 589832 | tf_op jit(solution)/shard_map/ppermute | solution.py:329
  63.4 7.6 %weight_grads.5 = (f32[1536,3072]{1,0:T(8,128)}, f32[3072,1536]{1,0:T(8,128)}, f32[8,128]{1,0:T(8,128)}) custom-call(s32[1]{0:T(128)} %bitcast.refs_0_, bf16[1536,256]{1,0:T(8,128)(2,1)S(1)} %get-tuple-element.35.refs_1_, bf16[256,1536]{1,0:T(8,128)(2,1)S(1)} %get-tuple-element.36.refs_4_.refs_2_, ...), custom_call_target="tpu_custom_call", output_to_operand_aliasing={{0}: (11, {}), {1}: (12, {})} | custom-call | flops 32000000000 | tf_op jit(solution)/shard_map/weight_grads/pallas_call | solution.py:53
  71.0 0.7 %add_convert_fusion.3 = bf16[64,1536]{1,0:T(8,128)(2,1)} fusion(bf16[64,1536]{1,0:T(8,128)(2,1)S(1)} %collective-permute-done.19, f32[64,1536]{1,0:T(8,128)S(1)} %get-tuple-element.46, bf16[64,1536]{1,0:T(8,128)(2,1)S(1)} %collective-permute-done.18), kind=kLoop, calls=%fused_computation.3 | loop fusion | flops 491520 | bytes 983040 | tf_op jit(solution)/shard_map/convert_element_type | solution.py:402
  (33 shorter events, 1.9 us)
Async XLA Ops:
  1.7 15.0 %collective-permute-start = (bf16[2,64,1536]{2,1,0:T(8,128)(2,1)S(1)}, bf16[2,64,1536]{2,1,0:T(8,128)(2,1)S(1)}, u32[]{:S(2)}, u32[]{:S(2)}) collective-permute-start(bf16[2,64,1536]{2,1,0:T(8,128)(2,1)S(1)} %stacked.1.refs_1_.refs_4_.refs_0_), channel_id=1, source_target_pairs={{0,2},{2,3},{3,1},{1,0},{4,6},{6,7},{7,5},{5,4},{8,10},{10,11},{11... | collective-permute-start | bytes 1179656 | tf_op jit(solution)/shard_map/ppermute | solution.py:329
  10.3 4.7 %collective-permute-start.1 = (bf16[2,64,1536]{2,1,0:T(8,128)(2,1)S(1)}, bf16[2,64,1536]{2,1,0:T(8,128)(2,1)S(1)}, u32[]{:S(2)}, u32[]{:S(2)}) collective-permute-start(bf16[2,64,1536]{2,1,0:T(8,128)(2,1)S(1)} %get-tuple-element.28.refs_4_), channel_id=1, source_target_pairs={{0,4},{4,0},{8,12},{12,8},{1,5},{5,1},{9,13},{13,9},{2,6},{6,2},{1... | collective-permute-start | bytes 1179656 | tf_op jit(solution)/shard_map/ppermute | solution.py:324
  14.9 12.6 %collective-permute-start.6 = (bf16[2,64,1536]{2,1,0:T(8,128)(2,1)S(1)}, bf16[2,64,1536]{2,1,0:T(8,128)(2,1)S(1)}, u32[]{:S(2)}, u32[]{:S(2)}) collective-permute-start(bf16[2,64,1536]{2,1,0:T(8,128)(2,1)S(1)} %get-tuple-element.34), channel_id=1, source_target_pairs={{0,1},{2,0},{3,2},{1,3},{4,5},{6,4},{7,6},{5,7},{8,9},{10,8},{11,1... | collective-permute-start | bytes 1179656 | tf_op jit(solution)/shard_map/ppermute | solution.py:329
  15.1 12.4 %collective-permute-start.4 = (bf16[2,64,1536]{2,1,0:T(8,128)(2,1)S(1)}, bf16[2,64,1536]{2,1,0:T(8,128)(2,1)S(1)}, u32[]{:S(2)}, u32[]{:S(2)}) collective-permute-start(bf16[2,64,1536]{2,1,0:T(8,128)(2,1)S(1)} %add_convert_fusion.2.refs_3_.refs_0_), channel_id=1, source_target_pairs={{0,8},{4,12},{8,0},{12,4},{1,9},{5,13},{9,1},{13,5},{2,10},{6,14},... | collective-permute-start | bytes 1179656 | tf_op jit(solution)/shard_map/ppermute | solution.py:335
  19.0 2.6 %collective-permute-start.2 = (bf16[2,64,1536]{2,1,0:T(8,128)(2,1)S(1)}, bf16[2,64,1536]{2,1,0:T(8,128)(2,1)S(1)}, u32[]{:S(2)}, u32[]{:S(2)}) collective-permute-start(bf16[2,64,1536]{2,1,0:T(8,128)(2,1)S(1)} %give.3.refs_3_), channel_id=1, source_target_pairs={{0,4},{4,0},{8,12},{12,8},{1,5},{5,1},{9,13},{13,9},{2,6},{6,2},{1... | collective-permute-start | bytes 1179656 | tf_op jit(solution)/shard_map/ppermute | solution.py:324
  21.7 16.5 %collective-permute-start.5 = (bf16[2,64,1536]{2,1,0:T(8,128)(2,1)S(1)}, bf16[2,64,1536]{2,1,0:T(8,128)(2,1)S(1)}, u32[]{:S(2)}, u32[]{:S(2)}) collective-permute-start(bf16[2,64,1536]{2,1,0:T(8,128)(2,1)S(1)} %add_convert_fusion.1.refs_1_.refs_3_.refs_2_), channel_id=1, source_target_pairs={{0,8},{4,12},{8,0},{12,4},{1,9},{5,13},{9,1},{13,5},{2,10},{6,14},... | collective-permute-start | bytes 1179656 | tf_op jit(solution)/shard_map/ppermute | solution.py:335
  22.4 13.4 %collective-permute-start.3 = (bf16[2,64,1536]{2,1,0:T(8,128)(2,1)S(1)}, bf16[2,64,1536]{2,1,0:T(8,128)(2,1)S(1)}, u32[]{:S(2)}, u32[]{:S(2)}) collective-permute-start(bf16[2,64,1536]{2,1,0:T(8,128)(2,1)S(1)} %copied.1.refs_5_), channel_id=1, source_target_pairs={{0,2},{2,3},{3,1},{1,0},{4,6},{6,7},{7,5},{5,4},{8,10},{10,11},{11... | collective-permute-start | bytes 1179656 | tf_op jit(solution)/shard_map/ppermute | solution.py:329
  29.8 2.4 %collective-permute-start.7 = (bf16[2,64,1536]{2,1,0:T(8,128)(2,1)S(1)}, bf16[2,64,1536]{2,1,0:T(8,128)(2,1)S(1)}, u32[]{:S(2)}, u32[]{:S(2)}) collective-permute-start(bf16[2,64,1536]{2,1,0:T(8,128)(2,1)S(1)} %give.4.refs_3_), channel_id=1, source_target_pairs={{0,4},{4,0},{8,12},{12,8},{1,5},{5,1},{9,13},{13,9},{2,6},{6,2},{1... | collective-permute-start | bytes 1179656 | tf_op jit(solution)/shard_map/ppermute | solution.py:324
  32.4 14.4 %collective-permute-start.10 = (bf16[2,64,1536]{2,1,0:T(8,128)(2,1)S(1)}, bf16[2,64,1536]{2,1,0:T(8,128)(2,1)S(1)}, u32[]{:S(2)}, u32[]{:S(2)}) collective-permute-start(bf16[2,64,1536]{2,1,0:T(8,128)(2,1)S(1)} %add_convert_fusion.refs_3_.refs_0_), channel_id=1, source_target_pairs={{0,8},{4,12},{8,0},{12,4},{1,9},{5,13},{9,1},{13,5},{2,10},{6,14},... | collective-permute-start | bytes 1179656 | tf_op jit(solution)/shard_map/ppermute | solution.py:335
  38.1 3.5 %collective-permute-start.8 = (bf16[2,64,1536]{2,1,0:T(8,128)(2,1)S(1)}, bf16[2,64,1536]{2,1,0:T(8,128)(2,1)S(1)}, u32[]{:S(2)}, u32[]{:S(2)}) collective-permute-start(bf16[2,64,1536]{2,1,0:T(8,128)(2,1)S(1)} %give.5.refs_4_), channel_id=1, source_target_pairs={{0,4},{4,0},{8,12},{12,8},{1,5},{5,1},{9,13},{13,9},{2,6},{6,2},{1... | collective-permute-start | bytes 1179656 | tf_op jit(solution)/shard_map/ppermute | solution.py:324
  38.8 4.8 %collective-permute-start.11 = (bf16[2,128,1536]{2,1,0:T(8,128)(2,1)S(1)}, bf16[2,128,1536]{2,1,0:T(8,128)(2,1)S(1)}, u32[]{:S(2)}, u32[]{:S(2)}) collective-permute-start(bf16[2,128,1536]{2,1,0:T(8,128)(2,1)S(1)} %gelu.4.refs_3_.refs_0_), channel_id=1, source_target_pairs={{0,4},{4,0},{8,12},{12,8},{1,5},{5,1},{9,13},{13,9},{2,6},{6,2},{1... | collective-permute-start | bytes 2359304 | tf_op jit(solution)/shard_map/ppermute | solution.py:324
  41.8 6.9 %collective-permute-start.12 = (bf16[2,64,768]{2,1,0:T(8,128)(2,1)S(1)}, bf16[2,64,768]{2,1,0:T(8,128)(2,1)S(1)}, u32[]{:S(2)}, u32[]{:S(2)}) collective-permute-start(bf16[2,64,768]{2,1,0:T(8,128)(2,1)S(1)} %get-tuple-element.53.refs_4_.refs_0_), channel_id=1, source_target_pairs={{0,8},{4,12},{8,0},{12,4},{1,9},{5,13},{9,1},{13,5},{2,10},{6,14},... | collective-permute-start | bytes 589832 | tf_op jit(solution)/shard_map/ppermute | solution.py:335
  47.0 2.1 %collective-permute-start.13 = (bf16[64,1536]{1,0:T(8,128)(2,1)S(1)}, bf16[64,1536]{1,0:T(8,128)(2,1)S(1)}, u32[]{:S(2)}, u32[]{:S(2)}) collective-permute-start(bf16[64,1536]{1,0:T(8,128)(2,1)S(1)} %get-tuple-element.38.refs_4_.refs_7_), channel_id=1, source_target_pairs={{0,4},{4,0},{8,12},{12,8},{1,5},{5,1},{9,13},{13,9},{2,6},{6,2},{1... | collective-permute-start | bytes 589832 | tf_op jit(solution)/shard_map/ppermute | solution.py:324
  47.1 7.3 %collective-permute-start.9 = (bf16[2,64,768]{2,1,0:T(8,128)(2,1)S(1)}, bf16[2,64,768]{2,1,0:T(8,128)(2,1)S(1)}, u32[]{:S(2)}, u32[]{:S(2)}) collective-permute-start(bf16[2,64,768]{2,1,0:T(8,128)(2,1)S(1)} %get-tuple-element.54.refs_5_.refs_0_), channel_id=1, source_target_pairs={{0,8},{4,12},{8,0},{12,4},{1,9},{5,13},{9,1},{13,5},{2,10},{6,14},... | collective-permute-start | bytes 589832 | tf_op jit(solution)/shard_map/ppermute | solution.py:335
  47.7 13.5 %collective-permute-start.15 = (bf16[64,1536]{1,0:T(8,128)(2,1)S(1)}, bf16[64,1536]{1,0:T(8,128)(2,1)S(1)}, u32[]{:S(2)}, u32[]{:S(2)}) collective-permute-start(bf16[64,1536]{1,0:T(8,128)(2,1)S(1)} %get-tuple-element.37.refs_2_), channel_id=1, source_target_pairs={{0,1},{2,0},{3,2},{1,3},{4,5},{6,4},{7,6},{5,7},{8,9},{10,8},{11,1... | collective-permute-start | bytes 589832 | tf_op jit(solution)/shard_map/ppermute | solution.py:329
  48.3 8.3 %collective-permute-start.16 = (bf16[64,1536]{1,0:T(8,128)(2,1)S(1)}, bf16[64,1536]{1,0:T(8,128)(2,1)S(1)}, u32[]{:S(2)}, u32[]{:S(2)}) collective-permute-start(bf16[64,1536]{1,0:T(8,128)(2,1)S(1)} %get-tuple-element.39.refs_2_.refs_5_), channel_id=1, source_target_pairs={{0,4},{4,0},{8,12},{12,8},{1,5},{5,1},{9,13},{13,9},{2,6},{6,2},{1... | collective-permute-start | bytes 589832 | tf_op jit(solution)/shard_map/ppermute | solution.py:324
  48.8 7.9 %collective-permute-start.17 = (bf16[2,64,768]{2,1,0:T(8,128)(2,1)S(1)}, bf16[2,64,768]{2,1,0:T(8,128)(2,1)S(1)}, u32[]{:S(2)}, u32[]{:S(2)}) collective-permute-start(bf16[2,64,768]{2,1,0:T(8,128)(2,1)S(1)} %gelu.6.refs_6_.refs_11_.refs_7_), channel_id=1, source_target_pairs={{0,4},{4,0},{8,12},{12,8},{1,5},{5,1},{9,13},{13,9},{2,6},{6,2},{1... | collective-permute-start | bytes 589832 | tf_op jit(solution)/shard_map/ppermute | solution.py:324
  54.5 6.6 %collective-permute-start.14 = (bf16[2,64,768]{2,1,0:T(8,128)(2,1)S(1)}, bf16[2,64,768]{2,1,0:T(8,128)(2,1)S(1)}, u32[]{:S(2)}, u32[]{:S(2)}) collective-permute-start(bf16[2,64,768]{2,1,0:T(8,128)(2,1)S(1)} %gelu.7.refs_9_.refs_15_.refs_6_), channel_id=1, source_target_pairs={{0,4},{4,0},{8,12},{12,8},{1,5},{5,1},{9,13},{13,9},{2,6},{6,2},{1... | collective-permute-start | bytes 589832 | tf_op jit(solution)/shard_map/ppermute | solution.py:324
  54.6 16.4 %collective-permute-start.18 = (bf16[64,1536]{1,0:T(8,128)(2,1)S(1)}, bf16[64,1536]{1,0:T(8,128)(2,1)S(1)}, u32[]{:S(2)}, u32[]{:S(2)}) collective-permute-start(bf16[64,1536]{1,0:T(8,128)(2,1)S(1)} %get-tuple-element.47), channel_id=1, source_target_pairs={{0,2},{2,3},{3,1},{1,0},{4,6},{6,7},{7,5},{5,4},{8,10},{10,11},{11... | collective-permute-start | bytes 589832 | tf_op jit(solution)/shard_map/ppermute | solution.py:329
  62.0 9.0 %collective-permute-start.19 = (bf16[64,1536]{1,0:T(8,128)(2,1)S(1)}, bf16[64,1536]{1,0:T(8,128)(2,1)S(1)}, u32[]{:S(2)}, u32[]{:S(2)}) collective-permute-start(bf16[64,1536]{1,0:T(8,128)(2,1)S(1)} %get-tuple-element.48.refs_13_), channel_id=1, source_target_pairs={{0,3},{2,1},{3,0},{1,2},{4,7},{6,5},{7,4},{5,6},{8,11},{10,9},{11,... | collective-permute-start | bytes 589832 | tf_op jit(solution)/shard_map/ppermute | solution.py:329

commit v14 on v13

--- a/solution.py
+++ b/solution.py
@@ -323,7 +323,7 @@
     def swap_cores(x):
         return lax.ppermute(x, "wide", [(i, i ^ 1) for i in range(wide)])
 
-    ring = [*range(0, narrow, 2), *range(narrow - 1, 0, -2)]
+    ring = [0, *range(1, narrow, 2), *range(narrow - 2, 0, -2)]
 
     def shift(x, places):
         return lax.ppermute(x, "narrow", [(ring[i], ring[(i + places) % narrow]) for i in range(narrow)])
@@ -356,6 +356,8 @@
     for offset in offsets[1:]:
         places = 1 if offset > 0 else -1
         chunk = chunks[offset] = shift(forward.get(offset, chunks[offset - places]), places)
+        if offset == -1:
+            forward[2] = copied(ordered, chunks[1], [sums[1][0], chunk])
         give = product(ordered, chunk, up_other, down_other, "give", after=[sums[-1][0]] + [sums[0][1]] * (len(sums) == 2))
         got = swap_cores(give)
         if offset == offsets[-1]:
@@ -363,8 +365,6 @@
         keep = product(ordered, chunk, up_mine, down_mine, "keep")
         if offset != offsets[-1]:
             sums.append(across_chips(keep, got))
-            if offset == 1:
-                forward[2] = copied(ordered, chunk, [sums[1][0]])
         else:
             parts = [slice(i * width, (i + 1) * width) for i in range(slices)]
             late = [across_chips(keep[:, :, part], got[:, :, part]) for part in parts]

time: 71.9 us -> 75.1 us (1.045)
  waiting for transfers between devices: 4.84 us -> 8.4 us
  starting transfers between devices: 18.6 us -> 17.6 us
    ppermute x6, waiting for transfers between devices: 4.04 us -> 6.95 us  [shift(): lax.ppermute(x, 'narrow', [(ring[i], ring[(i + places) % narrow]) for i i...]
    ppermute x6, starting transfers between devices: 11.3 us -> 10.5 us  [shift(): lax.ppermute(x, 'narrow', [(ring[i], ring[(i + places) % narrow]) for i i...]
  transfers between devices with their start and end apart: 20 -> 20, of which waited for: 4 -> 4; matrix products, arithmetic and copies ran while one was open for 1% -> 1% of each run, Pallas kernels for 63% -> 61%
where the time goes in v14:
time: 75.1 us; the launch traced here: 74.3 us
  Pallas kernels  46.3 us (62%)
  starting transfers between devices  17.6 us (23%)
  waiting for transfers between devices  8.4 us (11%)
  other arithmetic  1.11 us (1%)
  between operations  0.95 us (1%)
    pallas_call x20, Pallas kernels, __call__(): pl.pallas_call(kernel, out_shape=outs, in_specs=specs, out_specs=[pl.Bloc...  46.3 us
    ppermute x6, starting transfers between devices, shift(): lax.ppermute(x, 'narrow', [(ring[i], ring[(i + places) % narrow]) for i i...  10.5 us
    ppermute x6, waiting for transfers between devices, shift(): lax.ppermute(x, 'narrow', [(ring[i], ring[(i + places) % narrow]) for i i...  6.95 us
    ppermute x5, starting transfers between devices, across_chips(): lax.ppermute(partial, 'wide', [(i, i ^ 2 * hop) for i in range(wide)])  5.88 us
  transfers between devices with their start and end apart: 20, of which 4 were waited for; matrix products, arithmetic and copies ran while one was open for 1% of the time, Pallas kernels for 61%

profile of v14, /device:TPU:0, one launch (start us, length us, event | category | flops | bytes accessed | tf_op | source)
XLA Modules:
  0.0 74.3 jit_solution(13939452950814611485)
XLA Ops:
  0.6 1.0 %stacked.1.refs_1_.refs_4_.refs_0_ = bf16[2,64,1536]{2,1,0:T(8,128)(2,1)S(1)} custom-call(bf16[64,1536]{1,0:T(8,128)(2,1)} %refs_0_.1, bf16[64,1536]{1,0:T(8,128)(2,1)} %refs_1_.1), custom_call_target="tpu_custom_call" | custom-call | flops 2000000000 | tf_op jit(solution)/shard_map/stacked/pallas_call | solution.py:53
  1.7 3.1 %collective-permute-start = (bf16[2,64,1536]{2,1,0:T(8,128)(2,1)S(1)}, bf16[2,64,1536]{2,1,0:T(8,128)(2,1)S(1)}, u32[]{:S(2)}, u32[]{:S(2)}) collective-permute-start(bf16[2,64,1536]{2,1,0:T(8,128)(2,1)S(1)} %stacked.1.refs_1_.refs_4_.refs_0_), channel_id=1, source_target_pairs={{0,1},{1,3},{3,2},{2,0},{4,5},{5,7},{7,6},{6,4},{8,9},{9,11},{11,1... | collective-permute-start | bytes 1179656 | tf_op jit(solution)/shard_map/ppermute | solution.py:329
  4.8 4.5 %give_first.1 = (bf16[1536,1536]{1,0:T(8,128)(2,1)S(1)}, bf16[1536,1536]{1,0:T(8,128)(2,1)S(1)}, bf16[2,64,1536]{2,1,0:T(8,128)(2,1)S(1)}) custom-call(s32[1]{0:T(128)} %bitcast.refs_0_, bf16[2,64,1536]{2,1,0:T(8,128)(2,1)S(1)} %stacked.1.refs_1_.refs_4_.refs_0_, bf16[1536,3072]{1,0:T(8,128)(2,1)} %refs_2_.3, bf16[3072,1536]{1,0:T(8,128)(2,1)} %refs_3_.3, ...), custom_call_target="tpu_custom_call" | custom-call | flops 17999998976 | tf_op jit(solution)/shard_map/give_first/pallas_call | solution.py:53
  9.4 4.5 %keep_first.1 = (bf16[1536,1536]{1,0:T(8,128)(2,1)S(1)}, bf16[1536,1536]{1,0:T(8,128)(2,1)S(1)}, bf16[2,64,1536]{2,1,0:T(8,128)(2,1)S(1)}, bf16[2,64,1536]{2,1,0:T(8,128)(2,1)S(1)}) custom-call(s32[1]{0:T(128)} %bitcast.refs_0_, bf16[2,64,1536]{2,1,0:T(8,128)(2,1)S(1)} %stacked.1.refs_1_.refs_4_.refs_0_, bf16[1536,3072]{1,0:T(8,128)(2,1)} %refs_2_.3, ...), custom_call_target="tpu_custom_call" | custom-call | flops 17999998976 | tf_op jit(solution)/shard_map/keep_first/pallas_call | solution.py:53
  13.9 1.1 %collective-permute-start.3 = (bf16[2,64,1536]{2,1,0:T(8,128)(2,1)S(1)}, bf16[2,64,1536]{2,1,0:T(8,128)(2,1)S(1)}, u32[]{:S(2)}, u32[]{:S(2)}) collective-permute-start(bf16[2,64,1536]{2,1,0:T(8,128)(2,1)S(1)} %get-tuple-element.34), channel_id=1, source_target_pairs={{0,2},{1,0},{3,1},{2,3},{4,6},{5,4},{7,5},{6,7},{8,10},{9,8},{11,9... | collective-permute-start | bytes 1179656 | tf_op jit(solution)/shard_map/ppermute | solution.py:329
  15.1 1.9 %collective-permute-start.5 = (bf16[2,64,1536]{2,1,0:T(8,128)(2,1)S(1)}, bf16[2,64,1536]{2,1,0:T(8,128)(2,1)S(1)}, u32[]{:S(2)}, u32[]{:S(2)}) collective-permute-start(bf16[2,64,1536]{2,1,0:T(8,128)(2,1)S(1)} %add_convert_fusion.2.refs_3_.refs_0_), channel_id=1, source_target_pairs={{0,8},{4,12},{8,0},{12,4},{1,9},{5,13},{9,1},{13,5},{2,10},{6,14},... | collective-permute-start | bytes 1179656 | tf_op jit(solution)/shard_map/ppermute | solution.py:335
  16.9 2.3 %give.3.refs_3_ = bf16[2,64,1536]{2,1,0:T(8,128)(2,1)S(1)} custom-call(bf16[2,64,1536]{2,1,0:T(8,128)(2,1)S(1)} %collective-permute-done.refs_0_.refs_1_, bf16[1536,1536]{1,0:T(8,128)(2,1)S(1)} %get-tuple-element.31.refs_1_.refs_3_.refs_10_.refs_11_, bf16[1536,1536]{1,0:T(8,128)(2,1)S(1)} %get-tuple-element.32.refs_2_, ...), custom_call_target="tpu_custom_call" | custom-call | flops 9600000000 | tf_op jit(solution)/shard_map/give/pallas_call | solution.py:53
  19.4 2.3 %keep.3.refs_3_ = bf16[2,64,1536]{2,1,0:T(8,128)(2,1)S(1)} custom-call(bf16[2,64,1536]{2,1,0:T(8,128)(2,1)S(1)} %collective-permute-done.refs_0_.refs_1_, bf16[1536,1536]{1,0:T(8,128)(2,1)S(1)} %get-tuple-element.29.refs_1_.refs_2_.refs_9_.refs_10_.refs_12_, bf16[1536,1536]{1,0:T(8,128)(2,1)S(1)} %get-tuple-element.30.refs_2_, ...), custom_call_target="tpu_custom_call" | custom-call | flops 9600000000 | tf_op jit(solution)/shard_map/keep/pallas_call | solution.py:53
  21.8 0.3 collective-permute-start.6
  22.1 4.2 %collective-permute-done.3.refs_2_.refs_0_ = bf16[2,64,1536]{2,1,0:T(8,128)(2,1)S(1)} collective-permute-done((bf16[2,64,1536]{2,1,0:T(8,128)(2,1)S(1)}, bf16[2,64,1536]{2,1,0:T(8,128)(2,1)S(1)}, u32[]{:S(2)}, u32[]{:S(2)}) %collective-permute-start.3) | collective-permute-done | bytes 393248 | tf_op jit(solution)/shard_map/ppermute | solution.py:329
  26.3 2.9 %collective-permute-start.4 = (bf16[2,64,1536]{2,1,0:T(8,128)(2,1)S(1)}, bf16[2,64,1536]{2,1,0:T(8,128)(2,1)S(1)}, u32[]{:S(2)}, u32[]{:S(2)}) collective-permute-start(bf16[2,64,1536]{2,1,0:T(8,128)(2,1)S(1)} %copied.1.refs_5_), channel_id=1, source_target_pairs={{0,1},{1,3},{3,2},{2,0},{4,5},{5,7},{7,6},{6,4},{8,9},{9,11},{11,1... | collective-permute-start | bytes 1179656 | tf_op jit(solution)/shard_map/ppermute | solution.py:329
  29.2 2.3 %give.4.refs_3_ = bf16[2,64,1536]{2,1,0:T(8,128)(2,1)S(1)} custom-call(bf16[2,64,1536]{2,1,0:T(8,128)(2,1)S(1)} %collective-permute-done.3.refs_2_.refs_0_, bf16[1536,1536]{1,0:T(8,128)(2,1)S(1)} %get-tuple-element.31.refs_1_.refs_3_.refs_10_.refs_11_, bf16[1536,1536]{1,0:T(8,128)(2,1)S(1)} %get-tuple-element.32.refs_2_, ...), custom_call_target="tpu_custom_call" | custom-call | flops 9600000000 | tf_op jit(solution)/shard_map/give/pallas_call | solution.py:53
  31.6 2.3 %keep.4.refs_4_ = bf16[2,64,1536]{2,1,0:T(8,128)(2,1)S(1)} custom-call(bf16[2,64,1536]{2,1,0:T(8,128)(2,1)S(1)} %collective-permute-done.3.refs_2_.refs_0_, bf16[1536,1536]{1,0:T(8,128)(2,1)S(1)} %get-tuple-element.29.refs_1_.refs_2_.refs_9_.refs_10_.refs_12_, bf16[1536,1536]{1,0:T(8,128)(2,1)S(1)} %get-tuple-element.30.refs_2_, ...), custom_call_target="tpu_custom_call" | custom-call | flops 9600000000 | tf_op jit(solution)/shard_map/keep/pallas_call | solution.py:53
  34.1 1.6 %collective-permute-start.10 = (bf16[2,64,1536]{2,1,0:T(8,128)(2,1)S(1)}, bf16[2,64,1536]{2,1,0:T(8,128)(2,1)S(1)}, u32[]{:S(2)}, u32[]{:S(2)}) collective-permute-start(bf16[2,64,1536]{2,1,0:T(8,128)(2,1)S(1)} %add_convert_fusion.refs_3_.refs_0_), channel_id=1, source_target_pairs={{0,8},{4,12},{8,0},{12,4},{1,9},{5,13},{9,1},{13,5},{2,10},{6,14},... | collective-permute-start | bytes 1179656 | tf_op jit(solution)/shard_map/ppermute | solution.py:335
  35.7 2.8 %collective-permute-done.4.refs_0_.refs_3_ = bf16[2,64,1536]{2,1,0:T(8,128)(2,1)S(1)} collective-permute-done((bf16[2,64,1536]{2,1,0:T(8,128)(2,1)S(1)}, bf16[2,64,1536]{2,1,0:T(8,128)(2,1)S(1)}, u32[]{:S(2)}, u32[]{:S(2)}) %collective-permute-start.4) | collective-permute-done | bytes 393248 | tf_op jit(solution)/shard_map/ppermute | solution.py:329
  38.4 2.3 %give.5.refs_4_ = bf16[2,64,1536]{2,1,0:T(8,128)(2,1)S(1)} custom-call(bf16[2,64,1536]{2,1,0:T(8,128)(2,1)S(1)} %collective-permute-done.4.refs_0_.refs_3_, bf16[1536,1536]{1,0:T(8,128)(2,1)S(1)} %get-tuple-element.31.refs_1_.refs_3_.refs_10_.refs_11_, bf16[1536,1536]{1,0:T(8,128)(2,1)S(1)} %get-tuple-element.32.refs_2_, ...), custom_call_target="tpu_custom_call" | custom-call | flops 9600000000 | tf_op jit(solution)/shard_map/give/pallas_call | solution.py:53
  40.9 0.5 gelu.4.refs_3_.refs_0_
  41.4 0.5 collective-permute-start.11
  41.9 2.3 %keep.5.refs_6_ = bf16[2,64,1536]{2,1,0:T(8,128)(2,1)S(1)} custom-call(bf16[2,64,1536]{2,1,0:T(8,128)(2,1)S(1)} %collective-permute-done.4.refs_0_.refs_3_, bf16[1536,1536]{1,0:T(8,128)(2,1)S(1)} %get-tuple-element.29.refs_1_.refs_2_.refs_9_.refs_10_.refs_12_, bf16[1536,1536]{1,0:T(8,128)(2,1)S(1)} %get-tuple-element.30.refs_2_, ...), custom_call_target="tpu_custom_call" | custom-call | flops 9600000000 | tf_op jit(solution)/shard_map/keep/pallas_call | solution.py:53
  44.4 1.6 %collective-permute-start.12 = (bf16[2,64,768]{2,1,0:T(8,128)(2,1)S(1)}, bf16[2,64,768]{2,1,0:T(8,128)(2,1)S(1)}, u32[]{:S(2)}, u32[]{:S(2)}) collective-permute-start(bf16[2,64,768]{2,1,0:T(8,128)(2,1)S(1)} %get-tuple-element.53.refs_4_.refs_0_), channel_id=1, source_target_pairs={{0,8},{4,12},{8,0},{12,4},{1,9},{5,13},{9,1},{13,5},{2,10},{6,14},... | collective-permute-start | bytes 589832 | tf_op jit(solution)/shard_map/ppermute | solution.py:335
  46.2 3.1 %input_product.2 = (bf16[64,1536]{1,0:T(8,128)(2,1)S(1)}, bf16[64,1536]{1,0:T(8,128)(2,1)S(1)}) custom-call(bf16[2,128,1536]{2,1,0:T(8,128)(2,1)S(1)} %gelu.4.refs_3_.refs_0_, bf16[2,128,1536]{2,1,0:T(8,128)(2,1)S(1)} %collective-permute-done.11.refs_1_.refs_3_.refs_7_, bf16[1536,1536]{1,0:T(8,128)(2,1)S(1)} %get-tuple-element.29.refs_1_.refs_2_.refs_9_.refs_10_.refs_12_, ...), custom_call_target="tpu_custom_call" | custom-call | flops 400000000 | tf_op jit(solution)/shard_map/input_product/pallas_call | solution.py:53
  49.3 0.3 gelu.5
  49.7 0.6 collective-permute-start.9
  50.5 0.8 %collective-permute-done.12.refs_1_ = bf16[2,64,768]{2,1,0:T(8,128)(2,1)S(1)} collective-permute-done((bf16[2,64,768]{2,1,0:T(8,128)(2,1)S(1)}, bf16[2,64,768]{2,1,0:T(8,128)(2,1)S(1)}, u32[]{:S(2)}, u32[]{:S(2)}) %collective-permute-start.12) | collective-permute-done | bytes 196640 | tf_op jit(solution)/shard_map/ppermute | solution.py:335
  51.5 4.9 %weight_grads.3 = (f32[1536,3072]{1,0:T(8,128)}, f32[3072,1536]{1,0:T(8,128)}, bf16[64,1536]{1,0:T(8,128)(2,1)S(1)}, f32[8,128]{1,0:T(8,128)S(1)}) custom-call(s32[1]{0:T(128)} %bitcast.refs_0_, bf16[1536,256]{1,0:T(8,128)(2,1)S(1)} %get-tuple-element.35.refs_1_, bf16[256,1536]{1,0:T(8,128)(2,1)S(1)} %get-tuple-element.36.refs_4_.refs_2_, ...), custom_call_target="tpu_custom_call" | custom-call | flops 16000000000 | tf_op jit(solution)/shard_map/weight_grads/pallas_call | solution.py:53
  56.4 0.6 collective-permute-done.9.refs_1_
  57.2 1.8 %collective-permute-start.18 = (bf16[64,1536]{1,0:T(8,128)(2,1)S(1)}, bf16[64,1536]{1,0:T(8,128)(2,1)S(1)}, u32[]{:S(2)}, u32[]{:S(2)}) collective-permute-start(bf16[64,1536]{1,0:T(8,128)(2,1)S(1)} %get-tuple-element.47), channel_id=1, source_target_pairs={{0,1},{1,3},{3,2},{2,0},{4,5},{5,7},{7,6},{6,4},{8,9},{9,11},{11,1... | collective-permute-start | bytes 589832 | tf_op jit(solution)/shard_map/ppermute | solution.py:329
  59.0 4.4 %weight_grads.4 = (f32[1536,3072]{1,0:T(8,128)}, f32[3072,1536]{1,0:T(8,128)}, f32[64,1536]{1,0:T(8,128)S(1)}, f32[8,128]{1,0:T(8,128)S(1)}) custom-call(s32[1]{0:T(128)} %bitcast.refs_0_, bf16[1536,256]{1,0:T(8,128)(2,1)S(1)} %get-tuple-element.35.refs_1_, ...), custom_call_target="tpu_custom_call", output_to_operand_aliasing={{0}: (13, {}), {1}: (14, {})} | custom-call | flops 16000000000 | tf_op jit(solution)/shard_map/weight_grads/pallas_call | solution.py:53
  63.5 0.9 %input_product.3 = (f32[64,1536]{1,0:T(8,128)S(1)}, bf16[64,1536]{1,0:T(8,128)(2,1)S(1)}) custom-call(bf16[2,64,768]{2,1,0:T(8,128)(2,1)S(1)} %collective-permute-done.14.refs_0_.refs_10_, bf16[1536,1536]{1,0:T(8,128)(2,1)S(1)} %get-tuple-element.31.refs_1_.refs_3_.refs_10_.refs_11_, bf16[64,1536]{1,0:T(8,128)(2,1)S(1)} %get-tuple-element.41.refs_2_, ...), custom_call_target="tpu_custom_call" | custom-call | flops 12000000000 | tf_op jit(solution)/shard_map/input_product/pallas_call | solution.py:53
  64.3 1.6 %collective-permute-start.19 = (bf16[64,1536]{1,0:T(8,128)(2,1)S(1)}, bf16[64,1536]{1,0:T(8,128)(2,1)S(1)}, u32[]{:S(2)}, u32[]{:S(2)}) collective-permute-start(bf16[64,1536]{1,0:T(8,128)(2,1)S(1)} %get-tuple-element.48.refs_13_), channel_id=1, source_target_pairs={{0,3},{1,2},{3,0},{2,1},{4,7},{5,6},{7,4},{6,5},{8,11},{9,10},{11,... | collective-permute-start | bytes 589832 | tf_op jit(solution)/shard_map/ppermute | solution.py:329
  66.0 7.6 %weight_grads.5 = (f32[1536,3072]{1,0:T(8,128)}, f32[3072,1536]{1,0:T(8,128)}, f32[8,128]{1,0:T(8,128)}) custom-call(s32[1]{0:T(128)} %bitcast.refs_0_, bf16[1536,256]{1,0:T(8,128)(2,1)S(1)} %get-tuple-element.35.refs_1_, bf16[256,1536]{1,0:T(8,128)(2,1)S(1)} %get-tuple-element.36.refs_4_.refs_2_, ...), custom_call_target="tpu_custom_call", output_to_operand_aliasing={{0}: (11, {}), {1}: (12, {})} | custom-call | flops 32000000000 | tf_op jit(solution)/shard_map/weight_grads/pallas_call | solution.py:53
  73.6 0.7 add_convert_fusion.3
  (33 shorter events, 1.6 us)
Async XLA Ops:
  1.7 15.3 %collective-permute-start = (bf16[2,64,1536]{2,1,0:T(8,128)(2,1)S(1)}, bf16[2,64,1536]{2,1,0:T(8,128)(2,1)S(1)}, u32[]{:S(2)}, u32[]{:S(2)}) collective-permute-start(bf16[2,64,1536]{2,1,0:T(8,128)(2,1)S(1)} %stacked.1.refs_1_.refs_4_.refs_0_), channel_id=1, source_target_pairs={{0,1},{1,3},{3,2},{2,0},{4,5},{5,7},{7,6},{6,4},{8,9},{9,11},{11,1... | collective-permute-start | bytes 1179656 | tf_op jit(solution)/shard_map/ppermute | solution.py:329
  9.3 5.7 %collective-permute-start.1 = (bf16[2,64,1536]{2,1,0:T(8,128)(2,1)S(1)}, bf16[2,64,1536]{2,1,0:T(8,128)(2,1)S(1)}, u32[]{:S(2)}, u32[]{:S(2)}) collective-permute-start(bf16[2,64,1536]{2,1,0:T(8,128)(2,1)S(1)} %get-tuple-element.28.refs_4_), channel_id=1, source_target_pairs={{0,4},{4,0},{8,12},{12,8},{1,5},{5,1},{9,13},{13,9},{2,6},{6,2},{1... | collective-permute-start | bytes 1179656 | tf_op jit(solution)/shard_map/ppermute | solution.py:324
  13.9 12.4 %collective-permute-start.3 = (bf16[2,64,1536]{2,1,0:T(8,128)(2,1)S(1)}, bf16[2,64,1536]{2,1,0:T(8,128)(2,1)S(1)}, u32[]{:S(2)}, u32[]{:S(2)}) collective-permute-start(bf16[2,64,1536]{2,1,0:T(8,128)(2,1)S(1)} %get-tuple-element.34), channel_id=1, source_target_pairs={{0,2},{1,0},{3,1},{2,3},{4,6},{5,4},{7,5},{6,7},{8,10},{9,8},{11,9... | collective-permute-start | bytes 1179656 | tf_op jit(solution)/shard_map/ppermute | solution.py:329
  15.1 14.1 %collective-permute-start.5 = (bf16[2,64,1536]{2,1,0:T(8,128)(2,1)S(1)}, bf16[2,64,1536]{2,1,0:T(8,128)(2,1)S(1)}, u32[]{:S(2)}, u32[]{:S(2)}) collective-permute-start(bf16[2,64,1536]{2,1,0:T(8,128)(2,1)S(1)} %add_convert_fusion.2.refs_3_.refs_0_), channel_id=1, source_target_pairs={{0,8},{4,12},{8,0},{12,4},{1,9},{5,13},{9,1},{13,5},{2,10},{6,14},... | collective-permute-start | bytes 1179656 | tf_op jit(solution)/shard_map/ppermute | solution.py:335
  19.3 2.4 %collective-permute-start.2 = (bf16[2,64,1536]{2,1,0:T(8,128)(2,1)S(1)}, bf16[2,64,1536]{2,1,0:T(8,128)(2,1)S(1)}, u32[]{:S(2)}, u32[]{:S(2)}) collective-permute-start(bf16[2,64,1536]{2,1,0:T(8,128)(2,1)S(1)} %give.3.refs_3_), channel_id=1, source_target_pairs={{0,4},{4,0},{8,12},{12,8},{1,5},{5,1},{9,13},{13,9},{2,6},{6,2},{1... | collective-permute-start | bytes 1179656 | tf_op jit(solution)/shard_map/ppermute | solution.py:324
  21.8 19.0 %collective-permute-start.6 = (bf16[2,64,1536]{2,1,0:T(8,128)(2,1)S(1)}, bf16[2,64,1536]{2,1,0:T(8,128)(2,1)S(1)}, u32[]{:S(2)}, u32[]{:S(2)}) collective-permute-start(bf16[2,64,1536]{2,1,0:T(8,128)(2,1)S(1)} %add_convert_fusion.1.refs_1_.refs_3_.refs_2_), channel_id=1, source_target_pairs={{0,8},{4,12},{8,0},{12,4},{1,9},{5,13},{9,1},{13,5},{2,10},{6,14},... | collective-permute-start | bytes 1179656 | tf_op jit(solution)/shard_map/ppermute | solution.py:335
  26.3 12.1 %collective-permute-start.4 = (bf16[2,64,1536]{2,1,0:T(8,128)(2,1)S(1)}, bf16[2,64,1536]{2,1,0:T(8,128)(2,1)S(1)}, u32[]{:S(2)}, u32[]{:S(2)}) collective-permute-start(bf16[2,64,1536]{2,1,0:T(8,128)(2,1)S(1)} %copied.1.refs_5_), channel_id=1, source_target_pairs={{0,1},{1,3},{3,2},{2,0},{4,5},{5,7},{7,6},{6,4},{8,9},{9,11},{11,1... | collective-permute-start | bytes 1179656 | tf_op jit(solution)/shard_map/ppermute | solution.py:329
  31.6 2.4 %collective-permute-start.7 = (bf16[2,64,1536]{2,1,0:T(8,128)(2,1)S(1)}, bf16[2,64,1536]{2,1,0:T(8,128)(2,1)S(1)}, u32[]{:S(2)}, u32[]{:S(2)}) collective-permute-start(bf16[2,64,1536]{2,1,0:T(8,128)(2,1)S(1)} %give.4.refs_3_), channel_id=1, source_target_pairs={{0,4},{4,0},{8,12},{12,8},{1,5},{5,1},{9,13},{13,9},{2,6},{6,2},{1... | collective-permute-start | bytes 1179656 | tf_op jit(solution)/shard_map/ppermute | solution.py:324
  34.1 15.2 %collective-permute-start.10 = (bf16[2,64,1536]{2,1,0:T(8,128)(2,1)S(1)}, bf16[2,64,1536]{2,1,0:T(8,128)(2,1)S(1)}, u32[]{:S(2)}, u32[]{:S(2)}) collective-permute-start(bf16[2,64,1536]{2,1,0:T(8,128)(2,1)S(1)} %add_convert_fusion.refs_3_.refs_0_), channel_id=1, source_target_pairs={{0,8},{4,12},{8,0},{12,4},{1,9},{5,13},{9,1},{13,5},{2,10},{6,14},... | collective-permute-start | bytes 1179656 | tf_op jit(solution)/shard_map/ppermute | solution.py:335
  40.8 3.5 %collective-permute-start.8 = (bf16[2,64,1536]{2,1,0:T(8,128)(2,1)S(1)}, bf16[2,64,1536]{2,1,0:T(8,128)(2,1)S(1)}, u32[]{:S(2)}, u32[]{:S(2)}) collective-permute-start(bf16[2,64,1536]{2,1,0:T(8,128)(2,1)S(1)} %give.5.refs_4_), channel_id=1, source_target_pairs={{0,4},{4,0},{8,12},{12,8},{1,5},{5,1},{9,13},{13,9},{2,6},{6,2},{1... | collective-permute-start | bytes 1179656 | tf_op jit(solution)/shard_map/ppermute | solution.py:324
  41.4 4.8 %collective-permute-start.11 = (bf16[2,128,1536]{2,1,0:T(8,128)(2,1)S(1)}, bf16[2,128,1536]{2,1,0:T(8,128)(2,1)S(1)}, u32[]{:S(2)}, u32[]{:S(2)}) collective-permute-start(bf16[2,128,1536]{2,1,0:T(8,128)(2,1)S(1)} %gelu.4.refs_3_.refs_0_), channel_id=1, source_target_pairs={{0,4},{4,0},{8,12},{12,8},{1,5},{5,1},{9,13},{13,9},{2,6},{6,2},{1... | collective-permute-start | bytes 2359304 | tf_op jit(solution)/shard_map/ppermute | solution.py:324
  44.4 6.9 %collective-permute-start.12 = (bf16[2,64,768]{2,1,0:T(8,128)(2,1)S(1)}, bf16[2,64,768]{2,1,0:T(8,128)(2,1)S(1)}, u32[]{:S(2)}, u32[]{:S(2)}) collective-permute-start(bf16[2,64,768]{2,1,0:T(8,128)(2,1)S(1)} %get-tuple-element.53.refs_4_.refs_0_), channel_id=1, source_target_pairs={{0,8},{4,12},{8,0},{12,4},{1,9},{5,13},{9,1},{13,5},{2,10},{6,14},... | collective-permute-start | bytes 589832 | tf_op jit(solution)/shard_map/ppermute | solution.py:335
  49.6 1.9 %collective-permute-start.13 = (bf16[64,1536]{1,0:T(8,128)(2,1)S(1)}, bf16[64,1536]{1,0:T(8,128)(2,1)S(1)}, u32[]{:S(2)}, u32[]{:S(2)}) collective-permute-start(bf16[64,1536]{1,0:T(8,128)(2,1)S(1)} %get-tuple-element.38.refs_4_.refs_7_), channel_id=1, source_target_pairs={{0,4},{4,0},{8,12},{12,8},{1,5},{5,1},{9,13},{13,9},{2,6},{6,2},{1... | collective-permute-start | bytes 589832 | tf_op jit(solution)/shard_map/ppermute | solution.py:324
  49.7 7.3 %collective-permute-start.9 = (bf16[2,64,768]{2,1,0:T(8,128)(2,1)S(1)}, bf16[2,64,768]{2,1,0:T(8,128)(2,1)S(1)}, u32[]{:S(2)}, u32[]{:S(2)}) collective-permute-start(bf16[2,64,768]{2,1,0:T(8,128)(2,1)S(1)} %get-tuple-element.54.refs_5_.refs_0_), channel_id=1, source_target_pairs={{0,8},{4,12},{8,0},{12,4},{1,9},{5,13},{9,1},{13,5},{2,10},{6,14},... | collective-permute-start | bytes 589832 | tf_op jit(solution)/shard_map/ppermute | solution.py:335
  50.3 13.2 %collective-permute-start.15 = (bf16[64,1536]{1,0:T(8,128)(2,1)S(1)}, bf16[64,1536]{1,0:T(8,128)(2,1)S(1)}, u32[]{:S(2)}, u32[]{:S(2)}) collective-permute-start(bf16[64,1536]{1,0:T(8,128)(2,1)S(1)} %get-tuple-element.37.refs_2_), channel_id=1, source_target_pairs={{0,2},{1,0},{3,1},{2,3},{4,6},{5,4},{7,5},{6,7},{8,10},{9,8},{11,9... | collective-permute-start | bytes 589832 | tf_op jit(solution)/shard_map/ppermute | solution.py:329
  50.3 8.7 %collective-permute-start.16 = (bf16[64,1536]{1,0:T(8,128)(2,1)S(1)}, bf16[64,1536]{1,0:T(8,128)(2,1)S(1)}, u32[]{:S(2)}, u32[]{:S(2)}) collective-permute-start(bf16[64,1536]{1,0:T(8,128)(2,1)S(1)} %get-tuple-element.39.refs_2_.refs_5_), channel_id=1, source_target_pairs={{0,4},{4,0},{8,12},{12,8},{1,5},{5,1},{9,13},{13,9},{2,6},{6,2},{1... | collective-permute-start | bytes 589832 | tf_op jit(solution)/shard_map/ppermute | solution.py:324
  51.4 7.6 %collective-permute-start.17 = (bf16[2,64,768]{2,1,0:T(8,128)(2,1)S(1)}, bf16[2,64,768]{2,1,0:T(8,128)(2,1)S(1)}, u32[]{:S(2)}, u32[]{:S(2)}) collective-permute-start(bf16[2,64,768]{2,1,0:T(8,128)(2,1)S(1)} %gelu.6.refs_6_.refs_11_.refs_7_), channel_id=1, source_target_pairs={{0,4},{4,0},{8,12},{12,8},{1,5},{5,1},{9,13},{13,9},{2,6},{6,2},{1... | collective-permute-start | bytes 589832 | tf_op jit(solution)/shard_map/ppermute | solution.py:324
  57.1 6.3 %collective-permute-start.14 = (bf16[2,64,768]{2,1,0:T(8,128)(2,1)S(1)}, bf16[2,64,768]{2,1,0:T(8,128)(2,1)S(1)}, u32[]{:S(2)}, u32[]{:S(2)}) collective-permute-start(bf16[2,64,768]{2,1,0:T(8,128)(2,1)S(1)} %gelu.7.refs_9_.refs_15_.refs_6_), channel_id=1, source_target_pairs={{0,4},{4,0},{8,12},{12,8},{1,5},{5,1},{9,13},{13,9},{2,6},{6,2},{1... | collective-permute-start | bytes 589832 | tf_op jit(solution)/shard_map/ppermute | solution.py:324
  57.2 16.3 %collective-permute-start.18 = (bf16[64,1536]{1,0:T(8,128)(2,1)S(1)}, bf16[64,1536]{1,0:T(8,128)(2,1)S(1)}, u32[]{:S(2)}, u32[]{:S(2)}) collective-permute-start(bf16[64,1536]{1,0:T(8,128)(2,1)S(1)} %get-tuple-element.47), channel_id=1, source_target_pairs={{0,1},{1,3},{3,2},{2,0},{4,5},{5,7},{7,6},{6,4},{8,9},{9,11},{11,1... | collective-permute-start | bytes 589832 | tf_op jit(solution)/shard_map/ppermute | solution.py:329
  64.3 9.2 %collective-permute-start.19 = (bf16[64,1536]{1,0:T(8,128)(2,1)S(1)}, bf16[64,1536]{1,0:T(8,128)(2,1)S(1)}, u32[]{:S(2)}, u32[]{:S(2)}) collective-permute-start(bf16[64,1536]{1,0:T(8,128)(2,1)S(1)} %get-tuple-element.48.refs_13_), channel_id=1, source_target_pairs={{0,3},{1,2},{3,0},{2,1},{4,7},{5,6},{7,4},{6,5},{8,11},{9,10},{11,... | collective-permute-start | bytes 589832 | tf_op jit(solution)/shard_map/ppermute | solution.py:329
